TPU v7x, 128 devices: a whole 4x4x4 slice. The times are simulated.
128 devices in a mesh: dp: 8 (over x, core), context: 8 (over y, z_lo), tensor: 2 (over z_hi).
Axes of the slice: x: 4, y: 4, z: 4 (z_hi: 2, z_lo: 2; z = z_hi * 2 + z_lo), core: 2. Of those that a mesh axis runs over, the one named last changes fastest.
Arguments:
- tokens_in: float32 [16, 1024, 512], P('dp', 'context'), may hold values from -6 to 6
- cotangent: float32 [16, 1024, 512], P('dp', 'context'), may hold values from -6 to 6
- positions: int32 [16, 1024], P('dp', 'context'), may hold values from 0 to 1023, as said below
- w_qkv: bfloat16 [2, 512, 3, 512], P(None, None, None, 'tensor'), may hold values from -0.25 to 0.25
- b_qkv: float32 [2, 3, 512], P(None, None, 'tensor'), may hold values from -3 to 3
- w_out: bfloat16 [2, 512, 512], P(None, 'tensor'), may hold values from -1.5 to 1.5
- w_up: bfloat16 [2, 512, 2048], P(None, None, 'tensor'), may hold values from -0.25 to 0.25
- b_up: float32 [2, 2048], P(None, 'tensor'), may hold values from -3 to 3
- w_down: bfloat16 [2, 2048, 512], P(None, 'tensor'), may hold values from -0.125 to 0.125
- out_bias: float32 [2, 2, 512], replicated, may hold values from -3 to 3
- ln_gain: float32 [2, 2, 512], replicated, may hold values from 0.5 to 1.5
- ln_bias: float32 [2, 2, 512], replicated, may hold values from -3 to 3
Outputs:
- block_out: float32 [16, 1024, 512], P('dp', 'context')
- in_grad: float32 [16, 1024, 512], P('dp', 'context')
- grad_w_qkv: float32 [2, 512, 3, 512], P(None, None, None, 'tensor')
- grad_b_qkv: float32 [2, 3, 512], P(None, None, 'tensor')
- grad_w_out: float32 [2, 512, 512], P(None, 'tensor')
- grad_w_up: float32 [2, 512, 2048], P(None, None, 'tensor')
- grad_b_up: float32 [2, 2048], P(None, 'tensor')
- grad_w_down: float32 [2, 2048, 512], P(None, 'tensor')
- grad_out_bias: float32 [2, 2, 512], replicated
- grad_ln_gain: float32 [2, 2, 512], replicated
- grad_ln_bias: float32 [2, 2, 512], replicated
Inputs may be any that keep to these rules, and one draw needn't show every extreme that they name: Each row is a pack of documents: from token to token the position rises by one, or falls to 0 where a new document begins; the first document of a row may have begun before the row. In each aligned block of 2 rows one row, drawn from the seed, is a single document with positions 0 to 1023.
All inputs are finite; a program needn't handle non-finite values.
Results may differ from a plain program's by a relative error of at most 0.017.
Values may be sent and summed in bfloat16 or wider, within the bound.
No kernel may reach another device: no remote copies, remote signals or barrier semaphores. Data moves between devices by JAX's collectives and lax.ppermute only.
A program may use at most 128 MiB of HBM per device.

v0:
```python
from functools import partial

import jax
import jax.numpy as jnp
from jax import lax
from jax.sharding import PartitionSpec as P

HEADS = 8
ROT = 16


EPS = 1e-05


def rope_tables(token_pos, rot_dims):
    half_rot = rot_dims // 2
    freqs = 10000.0 ** (-jnp.arange(half_rot).astype(jnp.float32) * 2.0 / rot_dims)
    angles = token_pos.astype(jnp.float32)[..., None] * freqs
    cosine = jnp.concatenate([jnp.cos(angles), jnp.cos(angles)], -1)[..., None, :]
    sine = jnp.concatenate([jnp.sin(angles), jnp.sin(angles)], -1)[..., None, :]
    return (cosine, sine)


def rope_apply(tensor, cosine, sine, rot_dims):
    half_rot = rot_dims // 2
    rotary_part = tensor[..., :rot_dims]
    turned = jnp.concatenate([-rotary_part[..., half_rot:], rotary_part[..., :half_rot]], -1)
    return jnp.concatenate([rotary_part * cosine + turned * sine, tensor[..., rot_dims:]], -1)


def rope_back(gradient, cosine, sine, rot_dims):
    half_rot = rot_dims // 2
    rotary_part = gradient[..., :rot_dims]
    with_sine = rotary_part * sine
    turned_back = jnp.concatenate([with_sine[..., half_rot:], -with_sine[..., :half_rot]], -1)
    return jnp.concatenate([rotary_part * cosine + turned_back, gradient[..., rot_dims:]], -1)


def shards(
    tokens_in,
    cotangent,
    positions,
    w_qkv,
    b_qkv,
    w_out,
    w_up,
    b_up,
    w_down,
    out_bias,
    ln_gain,
    ln_bias,
):
    seq_count, block_len, model_width = tokens_in.shape
    row_count = seq_count * block_len
    layer_count = w_qkv.shape[0]
    local_width = w_qkv.shape[3]
    heads_local = HEADS // lax.axis_size("tensor")
    head_dim = local_width // heads_local
    score_scale = head_dim ** (-0.5)
    seq_length = block_len * lax.axis_size("context")
    cosine, sine = rope_tables(positions, ROT)
    query_index = lax.axis_index("context") * block_len + jnp.arange(block_len, dtype=jnp.int32)
    key_index = jnp.arange(seq_length, dtype=jnp.int32)
    doc_start = jnp.maximum(query_index[None, :] - positions, 0)
    visible = (key_index[None, None, :] <= query_index[None, :, None]) & (
        key_index[None, None, :] >= doc_start[:, :, None]
    )

    def scores_of(query_b, key_all):
        raw_scores = (
            jnp.einsum("sqhd,skhd->shqk", query_b, key_all, preferred_element_type=jnp.float32)
            * score_scale
        )
        return jnp.where(visible[:, None], raw_scores, -1e30)

    def split_kv(kv_all):
        key_all = kv_all[:, :, 0].reshape(seq_count, seq_length, heads_local, head_dim)
        value_all = kv_all[:, :, 1].reshape(seq_count, seq_length, heads_local, head_dim)
        return (key_all, value_all)

    stream = tokens_in.reshape(row_count, model_width)
    kept_state = []
    for layer_idx in range(layer_count):
        row_mean = jnp.mean(stream, -1, keepdims=True)
        centred = stream - row_mean
        variance = jnp.mean(centred * centred, -1, keepdims=True)
        inv_std = lax.rsqrt(variance + EPS)
        normed = centred * inv_std
        attn_in = (normed * ln_gain[layer_idx, 0] + ln_bias[layer_idx, 0]).astype(jnp.bfloat16)
        mlp_in = (normed * ln_gain[layer_idx, 1] + ln_bias[layer_idx, 1]).astype(jnp.bfloat16)
        joined = jnp.dot(
            attn_in,
            w_qkv[layer_idx].reshape(model_width, 3 * local_width),
            preferred_element_type=jnp.float32,
        )
        joined = joined.reshape(row_count, 3, local_width) + b_qkv[layer_idx]
        query_b = rope_apply(
            joined[:, 0].reshape(seq_count, block_len, heads_local, head_dim), cosine, sine, ROT
        ).astype(jnp.bfloat16)
        key_b = rope_apply(
            joined[:, 1].reshape(seq_count, block_len, heads_local, head_dim), cosine, sine, ROT
        ).astype(jnp.bfloat16)
        value_b = joined[:, 2].astype(jnp.bfloat16)
        kv_local = jnp.stack(
            [
                key_b.reshape(seq_count, block_len, local_width),
                value_b.reshape(seq_count, block_len, local_width),
            ],
            axis=2,
        )
        kv_full = lax.all_gather(kv_local, "context", axis=1, tiled=True)
        key_all, value_all = split_kv(kv_full)
        scores = scores_of(query_b, key_all)
        row_peak = jnp.max(scores, -1, keepdims=True)
        shifted = jnp.exp(scores - row_peak)
        row_total = jnp.sum(shifted, -1, keepdims=True)
        probs_b = (shifted / row_total).astype(jnp.bfloat16)
        attended = jnp.einsum(
            "shqk,skhd->sqhd", probs_b, value_all, preferred_element_type=jnp.float32
        )
        context = attended.astype(jnp.bfloat16).reshape(row_count, local_width)
        pre_act = (
            jnp.dot(mlp_in, w_up[layer_idx], preferred_element_type=jnp.float32) + b_up[layer_idx]
        )
        act = jax.nn.gelu(pre_act, approximate=False).astype(jnp.bfloat16)
        partial_branch = jnp.dot(
            context, w_out[layer_idx], preferred_element_type=jnp.float32
        ) + jnp.dot(act, w_down[layer_idx], preferred_element_type=jnp.float32)
        branch = lax.psum(partial_branch.astype(jnp.bfloat16), "tensor").astype(jnp.float32)
        stream = stream + branch + out_bias[layer_idx, 0] + out_bias[layer_idx, 1]
        kept_state.append(
            (
                normed,
                inv_std,
                attn_in,
                mlp_in,
                query_b,
                kv_local,
                kv_full,
                row_peak,
                row_total,
                context,
                pre_act,
                act,
            )
        )
    block_out = stream.reshape(seq_count, block_len, model_width)
    residual_grad = cotangent.reshape(row_count, model_width)
    per_layer = [None] * layer_count
    for layer_idx in reversed(range(layer_count)):
        (
            normed,
            inv_std,
            attn_in,
            mlp_in,
            query_b,
            kv_local,
            kv_full,
            row_peak,
            row_total,
            context,
            pre_act,
            act,
        ) = kept_state[layer_idx]
        grad_b = residual_grad.astype(jnp.bfloat16)
        grad_total = jnp.sum(residual_grad, 0)
        d_out_bias = jnp.stack([grad_total, grad_total])
        d_w_out = jnp.dot(context.T, grad_b, preferred_element_type=jnp.float32)
        d_context = jnp.dot(grad_b, w_out[layer_idx].T, preferred_element_type=jnp.float32)
        d_context_b = d_context.astype(jnp.bfloat16).reshape(
            seq_count, block_len, heads_local, head_dim
        )
        d_w_down = jnp.dot(act.T, grad_b, preferred_element_type=jnp.float32)
        d_act = jnp.dot(grad_b, w_down[layer_idx].T, preferred_element_type=jnp.float32)
        unused_value, gelu_pullback = jax.vjp(partial(jax.nn.gelu, approximate=False), pre_act)
        d_pre = gelu_pullback(d_act)[0].astype(jnp.bfloat16)
        d_b_up = jnp.sum(d_pre.astype(jnp.float32), 0)
        d_w_up = jnp.dot(mlp_in.T, d_pre, preferred_element_type=jnp.float32)
        d_mlp_in = jnp.dot(d_pre, w_up[layer_idx].T, preferred_element_type=jnp.float32)
        kv_all = lax.all_gather(kv_local, "context", axis=1, tiled=True)
        key_all, value_all = split_kv(kv_all)
        scores = scores_of(query_b, key_all)
        probs = jnp.exp(scores - row_peak) / row_total
        probs_b = probs.astype(jnp.bfloat16)
        d_probs = jnp.einsum(
            "sqhd,skhd->shqk", d_context_b, value_all, preferred_element_type=jnp.float32
        )
        delta = jnp.sum(probs * d_probs, -1, keepdims=True)
        d_scores = (score_scale * (probs * (d_probs - delta))).astype(jnp.bfloat16)
        d_query_r = jnp.einsum(
            "shqk,skhd->sqhd", d_scores, key_all, preferred_element_type=jnp.float32
        )
        row_num = block_len * lax.axis_size("context")
        key_term = jnp.einsum(
            "shqk,sqhd->kshd", d_scores, query_b, preferred_element_type=jnp.float32
        )
        value_term = jnp.einsum(
            "shqk,sqhd->kshd", probs_b, d_context_b, preferred_element_type=jnp.float32
        )
        kv_grad = lax.psum_scatter(
            jnp.stack(
                [
                    key_term.reshape(row_num, seq_count, local_width),
                    value_term.reshape(row_num, seq_count, local_width),
                ],
                axis=2,
            ).astype(jnp.bfloat16),
            "context",
            scatter_dimension=0,
            tiled=True,
        ).astype(jnp.float32)
        kv_grad = jnp.transpose(kv_grad, (1, 0, 2, 3))
        d_key_r = kv_grad[:, :, 0].reshape(seq_count, block_len, heads_local, head_dim)
        d_value = kv_grad[:, :, 1].reshape(row_count, local_width)
        d_query = rope_back(d_query_r, cosine, sine, ROT).reshape(row_count, local_width)
        d_key = rope_back(d_key_r, cosine, sine, ROT).reshape(row_count, local_width)
        d_qkv = jnp.stack([d_query, d_key, d_value], 1).astype(jnp.bfloat16)
        d_b_qkv = jnp.sum(d_qkv.astype(jnp.float32), 0)
        d_flat = d_qkv.reshape(row_count, 3 * local_width)
        d_w_qkv = jnp.dot(attn_in.T, d_flat, preferred_element_type=jnp.float32).reshape(
            model_width, 3, local_width
        )
        d_attn_in = jnp.dot(
            d_flat,
            w_qkv[layer_idx].reshape(model_width, 3 * local_width).T,
            preferred_element_type=jnp.float32,
        )
        d_attn_in, d_mlp_in = (
            lax.psum(d_attn_in.astype(jnp.bfloat16), "tensor").astype(jnp.float32),
            lax.psum(d_mlp_in.astype(jnp.bfloat16), "tensor").astype(jnp.float32),
        )
        d_gain = jnp.stack([jnp.sum(d_attn_in * normed, 0), jnp.sum(d_mlp_in * normed, 0)])
        d_ln_bias = jnp.stack([jnp.sum(d_attn_in, 0), jnp.sum(d_mlp_in, 0)])
        d_normed = d_attn_in * ln_gain[layer_idx, 0] + d_mlp_in * ln_gain[layer_idx, 1]
        residual_grad = residual_grad + inv_std * (
            d_normed
            - jnp.mean(d_normed, -1, keepdims=True)
            - normed * jnp.mean(d_normed * normed, -1, keepdims=True)
        )
        layer_result = (
            d_w_qkv,
            d_b_qkv,
            d_w_out,
            d_w_up,
            d_b_up,
            d_w_down,
            d_out_bias,
            d_gain,
            d_ln_bias,
        )
        per_layer[layer_idx] = layer_result
    stacked = tuple(
        (
            jnp.stack([per_layer[layer_idx][member] for layer_idx in range(layer_count)])
            for member in range(9)
        )
    )
    stacked = lax.psum(stacked, ("dp", "context"))
    in_grad = residual_grad.reshape(seq_count, block_len, model_width)
    return (
        block_out,
        in_grad,
        stacked[0],
        stacked[1],
        stacked[2],
        stacked[3],
        stacked[4],
        stacked[5],
        stacked[6],
        stacked[7],
        stacked[8],
    )


def solution(mesh):
    return jax.shard_map(
        shards,
        mesh=mesh,
        in_specs=(
            P("dp", "context", None),
            P("dp", "context", None),
            P("dp", "context"),
            P(None, None, None, "tensor"),
            P(None, None, "tensor"),
            P(None, "tensor", None),
            P(None, None, "tensor"),
            P(None, "tensor"),
            P(None, "tensor", None),
            P(),
            P(),
            P(),
        ),
        out_specs=(
            P("dp", "context", None),
            P("dp", "context", None),
            P(None, None, None, "tensor"),
            P(None, None, "tensor"),
            P(None, "tensor", None),
            P(None, None, "tensor"),
            P(None, "tensor"),
            P(None, "tensor", None),
            P(),
            P(),
            P(),
        ),
        check_vma=False,
    )
```

profile of v0, /device:TPU:1, one launch (start us, length us, event | category | flops | bytes accessed | tf_op | source)
XLA Modules:
  0.0 1109.8 jit_solution(16911518953325362103)
XLA Ops:
  31.3 5.4 multiply_convert_fusion.3
  36.6 52.4 %all-gather.3.cloned.1.call-done = bf16[2,1024,2,256]{1,3,0,2:T(8,128)(2,1)} async-done(((bf16[2,128,2,256]{1,3,0,2:T(8,128)(2,1)}), bf16[2,1024,2,256]{1,3,0,2:T(8,128)(2,1)}) %all-gather.3.cloned.1.call-update) | async-done | bytes 2097168 | tf_op jit(solution)/shard_map/all_gather | solution.py:111
  89.1 2.8 fusion.168
  91.9 5.3 fusion.186
  97.8 3.2 fusion.52
  103.9 32.6 %all-reduce.9.cloned.1.call-done = bf16[256,512]{1,0:T(8,128)(2,1)} async-done(((bf16[256,512]{1,0:T(8,128)(2,1)}), bf16[256,512]{1,0:T(8,128)(2,1)}) %all-reduce.9.cloned.1.call-update) | async-done | bytes 262160 | tf_op jit(solution)/shard_map/psum | solution.py:129
  159.4 45.4 %all-gather.5.cloned.1.call-done = bf16[2,1024,2,256]{3,1,0,2:T(8,128)(2,1)} async-done(((bf16[2,128,2,256]{3,1,0,2:T(8,128)(2,1)}), bf16[2,1024,2,256]{3,1,0,2:T(8,128)(2,1)}) %all-gather.5.cloned.1.call-update) | async-done | bytes 2097168 | tf_op jit(solution)/shard_map/all_gather | solution.py:111
  210.3 3.7 fusion.188
  214.0 5.3 fusion.187
  219.4 3.7 convolution_convert_fusion.1
  223.1 11.7 %fusion.37 = bf16[2,4,64,1024]{3,2,1,0:T(8,128)(2,1)S(1)} fusion(f32[2,4,128,1024]{3,2,1,0:T(8,128)} %fusion.188, bf16[2,128,4,48]{1,3,2,0:T(8,128)(2,1)S(1)} %copy-done.46, bf16[2,128,4,16]{1,3,2,0:T(8,128)(2,1)S(1)} %copy-done.59, f32[2,4,128,1024]{3,2,1,0:T(8,128)} %get-tuple-element.133, f32[2,4,128]{2,1,0:T(4,128)S(1)} %copy-done.92), kind=kOutput, calls=%fused_computation.44 | convolution fusion | flops 142346240 | bytes 9572352 | tf_op jit(solution)/shard_map/shqk,sqhd->kshd/dot_general | solution.py:194
  238.7 4.7 multiply_convert_fusion.2
  246.3 10.8 fusion.49
  257.1 34.0 %reduce-scatter.3.cloned.1.call-done = bf16[128,2,2,256]{3,0,1,2:T(8,128)(2,1)} async-done(((bf16[1024,2,2,256]{3,0,1,2:T(8,128)(2,1)}), bf16[128,2,2,256]{3,0,1,2:T(8,128)(2,1)}) %reduce-scatter.3.cloned.1.call-update) | async-done | bytes 262160 | tf_op jit(solution)/shard_map/reduce_scatter | solution.py:200
  297.4 38.7 %all-reduce.15.cloned.1.call-done = (bf16[256,512]{1,0:T(8,128)(2,1)}, bf16[256,512]{1,0:T(8,128)(2,1)}) async-done(((bf16[256,512]{1,0:T(8,128)(2,1)}, bf16[256,512]{1,0:T(8,128)(2,1)}), (bf16[256,512]{1,0:T(8,128)(2,1)}, bf16[256,512]{1,0:T(8,128)(2,1)})) %all-reduce.15.cloned.1.call-update) | async-done | bytes 524304 | tf_op jit(solution)/shard_map/psum | solution.py:230
  347.5 11.7 %fusion.34 = bf16[2,4,64,1024]{3,2,1,0:T(8,128)(2,1)S(1)} fusion(f32[2,4,128,1024]{3,2,1,0:T(8,128)} %fusion.189, bf16[2,128,4,48]{1,3,2,0:T(8,128)(2,1)S(1)} %copy-done.45, bf16[2,128,4,16]{1,3,2,0:T(8,128)(2,1)S(1)} %copy-done.58, f32[2,4,128,1024]{3,2,1,0:T(8,128)} %get-tuple-element.129, f32[2,4,128]{2,1,0:T(4,128)S(1)} %copy-done.91), kind=kOutput, calls=%fused_computation.43 | convolution fusion | flops 142346240 | bytes 9572352 | tf_op jit(solution)/shard_map/shqk,sqhd->kshd/dot_general | solution.py:194
  363.1 3.1 convolution_bitcast_fusion
  374.4 11.8 %fusion.46 = f32[2,128,4,64]{1,3,2,0:T(8,128)S(1)} fusion(bf16[2,1024,4,64]{1,3,2,0:T(8,128)(2,1)} %bitcast.316, f32[2,4,128,1024]{3,2,1,0:T(8,128)} %fusion.189, f32[2,4,128,1024]{3,2,1,0:T(8,128)} %get-tuple-element.129, f32[2,4,128]{2,1,0:T(4,128)} %copy-done.89), kind=kOutput, calls=%fused_computation.65 | convolution fusion | flops 141559808 | bytes 9703424 | tf_op jit(solution)/shard_map/shqk,skhd->sqhd/dot_general | solution.py:190
  387.9 3.2 convert_reduce_fusion.1
  393.1 19.5 %reduce-scatter.5.cloned.1.call-done = bf16[128,2,2,256]{3,0,1,2:T(8,128)(2,1)} async-done(((bf16[1024,2,2,256]{3,0,1,2:T(8,128)(2,1)}), bf16[128,2,2,256]{3,0,1,2:T(8,128)(2,1)}) %reduce-scatter.5.cloned.1.call-update) | async-done | bytes 262160 | tf_op jit(solution)/shard_map/reduce_scatter | solution.py:200
  442.4 35.7 %all-reduce.13.cloned.1.call-done = (bf16[256,512]{1,0:T(8,128)(2,1)}, bf16[256,512]{1,0:T(8,128)(2,1)}, bf16[256,512]{1,0:T(8,128)(2,1)}) async-done(((bf16[256,512]{1,0:T(8,128)(2,1)}, bf16[256,512]{1,0:T(8,128)(2,1)}, bf16[256,512]{1,0:T(8,128)(2,1)}), (bf16[256,512]{1,0:T(8,128)(2,1)}, bf16[256,512]{1,0:T(8,128)(2,1)}, bf16[256,512]{1,0:T(8,128)(2,1)})) %all-reduce.13.cloned.1.call-update) | async-done | bytes 786448 | tf_op jit(solution)/shard_map/psum | solution.py:129
  485.9 272.1 %all-reduce = (f32[2,3,256]{2,1,0:T(4,128)S(1)}, f32[2,1024]{1,0:T(2,128)}, f32[2,2,512]{2,1,0:T(2,128)}, f32[2,2,512]{2,1,0:T(2,128)}, f32[2,2,512]{2,1,0:T(2,128)}) all-reduce(f32[2,3,256]{2,1,0:T(4,128)S(1)} %pad_maximum_fusion.32, ...), channel_id=1, replica_groups=mesh['dp'=8,'context'=8,'tensor'=2] {'dp','context'}, use_global_device_ids=true, to_apply=%region_25.26 | all-reduce | flops 9728 | bytes 77824 | tf_op jit(solution)/shard_map/psum | solution.py:258
  758.6 333.1 %all-reduce.11.cloned.1.call-done = (f32[2,512,3,256]{3,1,2,0:T(8,128)}, f32[2,256,512]{2,1,0:T(8,128)}, f32[2,512,1024]{2,1,0:T(8,128)}, f32[2,1024,512]{2,1,0:T(8,128)}) async-done(((f32[2,512,3,256]{3,1,2,0:T(8,128)}, f32[2,256,512]{2,1,0:T(8,128)}, f32[2,512,1024]{2,1,0:T(8,128)}, f32[2,1024,512]{2,1,0:T(8,128)}), (f32[2,512,3,256]{3,1,2,0:T(8,128)}, f32[2,256,512]{2,1,0:T(8,128)}, ...) | async-done | bytes 12582928 | tf_op jit(solution)/shard_map/psum | solution.py:258
  1091.7 4.1 copy.160
  (381 shorter events, 139.6 us)
Async XLA Ops:
  7.2 81.9 %all-gather.3.cloned.1.call-start = ((), (), s32[]{:S(2)}) async-start(), calls=%async_computation.2 | async-start | bytes 2359296 | tf_op jit(solution)/shard_map/all_gather | solution.py:111
  27.9 63.9 %copy-start.57 = (bf16[2,128,4,16]{1,3,2,0:T(8,128)(2,1)}, bf16[2,128,4,16]{1,3,2,0:T(8,128)(2,1)S(1)}, u32[]{:S(2)}) copy-start(bf16[2,128,4,16]{1,3,2,0:T(8,128)(2,1)S(1)} %get-tuple-element.94) | copy-start | bytes 98308
  29.1 107.4 %all-reduce.9.cloned.1.call-start = ((), (), s32[]{:S(2)}) async-start(), calls=%async_computation.3 | async-start | bytes 524288 | tf_op jit(solution)/shard_map/psum | solution.py:129
  29.5 62.4 %copy-start.44 = (bf16[2,128,4,48]{1,3,2,0:T(8,128)(2,1)}, bf16[2,128,4,48]{1,3,2,0:T(8,128)(2,1)S(1)}, u32[]{:S(2)}) copy-start(bf16[2,128,4,48]{1,3,2,0:T(8,128)(2,1)S(1)} %copy.115) | copy-start | bytes 294916
  31.3 60.6 %copy-start.41 = (pred[2,128,1024]{2,1,0:T(8,128)(4,1)}, pred[2,128,1024]{2,1,0:T(8,128)(4,1)S(1)}, u32[]{:S(2)}) copy-start(pred[2,128,1024]{2,1,0:T(8,128)(4,1)S(1)} %fusion.84) | copy-start | bytes 786436
  101.1 38.9 %copy-start.51 = (f32[1,1,512]{2,1,0:T(1,128)S(1)}, f32[1,1,512]{2,1,0:T(1,128)}, u32[]{:S(2)}) copy-start(f32[1,1,512]{2,1,0:T(1,128)} %get-tuple-element.111) | copy-start | bytes 6148
  102.7 102.1 %all-gather.5.cloned.1.call-start = ((), (), s32[]{:S(2)}) async-start(), calls=%async_computation.4 | async-start | bytes 2359296 | tf_op jit(solution)/shard_map/all_gather | solution.py:111
  103.2 45.2 %copy-start.12 = (bf16[1,512,3,256]{1,3,2,0:T(8,128)(2,1)}, bf16[1,512,3,256]{1,3,2,0:T(8,128)(2,1)S(1)}, u32[]{:S(2)}) copy-start(bf16[1,512,3,256]{1,3,2,0:T(8,128)(2,1)S(1)} %copy.108) | copy-start | bytes 2359300
  155.8 135.3 %reduce-scatter.3.cloned.1.call-start = ((), (), s32[]{:S(2)}) async-start(), calls=%async_computation.5 | async-start | bytes 2359296 | tf_op jit(solution)/shard_map/reduce_scatter | solution.py:200
  157.2 86.3 %copy-start.16 = (bf16[2,128,512]{2,1,0:T(8,128)(2,1)}, bf16[2,128,512]{2,1,0:T(8,128)(2,1)S(1)}, u32[]{:S(2)}) copy-start(bf16[2,128,512]{2,1,0:T(8,128)(2,1)S(1)} %get-tuple-element.74) | copy-start | bytes 786436
  238.4 97.7 %all-reduce.15.cloned.1.call-start = ((), (), s32[]{:S(2)}) async-start(), calls=%async_computation.9 | async-start | bytes 1048576 | tf_op jit(solution)/shard_map/psum | solution.py:230
  257.1 39.2 %copy-start.13 = (bf16[1,512,3,256]{1,3,2,0:T(8,128)(2,1)S(1)}, bf16[1,512,3,256]{1,3,2,0:T(8,128)(2,1)}, u32[]{:S(2)}) copy-start(bf16[1,512,3,256]{1,3,2,0:T(8,128)(2,1)} %copy-done.12) | copy-start | bytes 2359300
  294.7 47.8 %copy-start.10 = (bf16[2,1024,1,256]{1,3,0,2:T(8,128)(2,1)S(1)}, bf16[2,1024,1,256]{1,3,0,2:T(8,128)(2,1)}, u32[]{:S(2)}) copy-start(bf16[2,1024,1,256]{1,3,0,2:T(8,128)(2,1)} %copy-done.9) | copy-start | bytes 3145732
  297.4 115.2 %reduce-scatter.5.cloned.1.call-start = ((), (), s32[]{:S(2)}) async-start(), calls=%async_computation.6 | async-start | bytes 2359296 | tf_op jit(solution)/shard_map/reduce_scatter | solution.py:200
  362.8 115.2 %all-reduce.13.cloned.1.call-start = ((), (), s32[]{:S(2)}) async-start(), calls=%async_computation.8 | async-start | bytes 1572864 | tf_op jit(solution)/shard_map/psum | solution.py:129
  393.1 40.5 %copy-start.20 = (f32[1,256,512]{2,1,0:T(8,128)S(1)}, f32[1,256,512]{2,1,0:T(8,128)}, u32[]{:S(2)}) copy-start(f32[1,256,512]{2,1,0:T(8,128)} %convolution_bitcast_fusion.6) | copy-start | bytes 1572868
  433.6 658.1 %all-reduce.11.cloned.1.call-start = ((), (), s32[]{:S(2)}) async-start(), calls=%async_computation.7 | async-start | bytes 25165824 | tf_op jit(solution)/shard_map/psum | solution.py:258
  440.3 39.3 %copy-start.4 = (f32[256,512]{1,0:T(8,128)S(1)}, f32[256,512]{1,0:T(8,128)}, u32[]{:S(2)}) copy-start(f32[256,512]{1,0:T(8,128)} %copy-done.3) | copy-start | bytes 1572868
  440.3 39.3 %copy-start.5 = (bf16[256,512]{1,0:T(8,128)(2,1)S(1)}, bf16[256,512]{1,0:T(8,128)(2,1)}, u32[]{:S(2)}) copy-start(bf16[256,512]{1,0:T(8,128)(2,1)} %all-reduce.9.cloned.1.call-done) | copy-start | bytes 786436
  440.3 39.3 %copy-start.48 = (f32[1,1,512]{2,1,0:T(1,128)S(1)}, f32[1,1,512]{2,1,0:T(1,128)}, u32[]{:S(2)}) copy-start(f32[1,1,512]{2,1,0:T(1,128)} %copy-done.47) | copy-start | bytes 6148
  440.4 39.3 %copy-start.50 = (f32[1,1,512]{2,1,0:T(1,128)S(1)}, f32[1,1,512]{2,1,0:T(1,128)}, u32[]{:S(2)}) copy-start(f32[1,1,512]{2,1,0:T(1,128)} %copy-done.49) | copy-start | bytes 6148
  440.4 39.3 %copy-start.61 = (f32[1,1,512]{2,1,0:T(1,128)S(1)}, f32[1,1,512]{2,1,0:T(1,128)}, u32[]{:S(2)}) copy-start(f32[1,1,512]{2,1,0:T(1,128)} %copy-done.60) | copy-start | bytes 6148
  440.4 39.3 %copy-start.74 = (f32[1,1,512]{2,1,0:T(1,128)S(1)}, f32[1,1,512]{2,1,0:T(1,128)}, u32[]{:S(2)}) copy-start(f32[1,1,512]{2,1,0:T(1,128)} %get-tuple-element.104) | copy-start | bytes 6148
  440.4 39.3 %copy-start.75 = (f32[1,1,512]{2,1,0:T(1,128)S(1)}, f32[1,1,512]{2,1,0:T(1,128)}, u32[]{:S(2)}) copy-start(f32[1,1,512]{2,1,0:T(1,128)} %get-tuple-element.107) | copy-start | bytes 6148
  (80 other events, 576.0 us)
Sparse Core Ops, SparseCore 0:
  29.2 59.8 all-gather.2
  102.8 33.6 all-reduce.8
  155.9 48.8 all-gather.4
  238.5 52.5 reduce-scatter.2
  297.5 38.5 all-reduce.14
  362.9 49.6 reduce-scatter.4
  433.7 44.3 all-reduce.12
  485.2 606.4 all-reduce.10
where the time goes:
time: 1120 us; the launch traced here: 1110 us
  waiting for transfers between devices  591 us (53%)
  blocking collectives  272 us (24%)
  matrix products  110 us (10%)
  local copies, waits for them, and re-layouts  75.9 us (7%)
  other arithmetic  43.1 us (4%)
  between operations  16.1 us (1%)
    psum x1, waiting for transfers between devices, shards(): stacked = lax.psum(stacked, ('dp', 'context'))  333 us
    psum x1, blocking collectives, shards(): stacked = lax.psum(stacked, ('dp', 'context'))  272 us
    all_gather x2, waiting for transfers between devices, shards(): kv_full = lax.all_gather(kv_local, 'context', axis=1, tiled=True)  97.9 us
    psum x2, waiting for transfers between devices, shards(): lax.psum(partial_branch.astype(jnp.bfloat16), 'tensor').astype(jnp.float32)  68.2 us
    reduce_scatter x2, waiting for transfers between devices, shards(): lax.psum_scatter(jnp.stack([key_term.reshape(row_num, seq_count, local_wi...  53.5 us
    psum x1, waiting for transfers between devices, shards(): lax.psum(d_mlp_in.astype(jnp.bfloat16), 'tensor').astype(jnp.float32)  38.7 us
    unnamed x207, local copies, waits for them, and re-layouts  24.1 us
    dot_general x2, matrix products, shards(): jnp.einsum('shqk,sqhd->kshd', d_scores, query_b, preferred_element_type=j...  23.5 us
  transfers between devices with their start and end apart: 8, of which 8 were waited for; matrix products, arithmetic and copies ran while one was open for 6% of the time, Pallas kernels for 0%

commit v1 on v0

v1 whole, which is shorter than its diff:
```python
from functools import partial

import numpy as np

import jax
import jax.numpy as jnp
from jax import lax
from jax.experimental import pallas as pl
from jax.experimental.pallas import tpu as pltpu
from jax.sharding import PartitionSpec as P

EPS = 1e-05
HALF = 8
HEAD = 64
BLK = 128
CHUNK = 256
NEG = -1e30
BF = jnp.bfloat16
F32 = jnp.float32

FREQS = (10000.0 ** (-np.arange(HALF, dtype=np.float64) * 2.0 / 16.0)).astype(np.float32)


def mm(a, b, ca=1, cb=0):
    return lax.dot_general(a, b, (((ca,), (cb,)), ((), ())), preferred_element_type=F32)


def call(body, out_shape, args, name, scratch=(), smem_first=False):
    specs = [pl.BlockSpec(memory_space=pltpu.VMEM) for _ in args]
    if smem_first:
        specs[0] = pl.BlockSpec(memory_space=pltpu.SMEM)
    return pl.pallas_call(
        body,
        out_shape=[jax.ShapeDtypeStruct(s, d) for s, d in out_shape],
        in_specs=specs,
        out_specs=[pl.BlockSpec(memory_space=pltpu.VMEM) for _ in out_shape],
        scratch_shapes=list(scratch),
        compiler_params=pltpu.CompilerParams(vmem_limit_bytes=56 * 1024 * 1024),
        name=name,
    )(*args)


def norm_rows(x):
    mean = jnp.mean(x, -1, keepdims=True)
    cen = x - mean
    inv = lax.rsqrt(jnp.mean(cen * cen, -1, keepdims=True) + EPS)
    return cen * inv, inv


def turn(t, cos, sin):
    a, b = t[:HALF], t[HALF : 2 * HALF]
    return jnp.concatenate([a * cos - b * sin, b * cos + a * sin, t[2 * HALF :]], 0)


def turn_back(u, cos, sin):
    a, b = u[:HALF], u[HALF : 2 * HALF]
    return jnp.concatenate([a * cos + b * sin, b * cos - a * sin, u[2 * HALF :]], 0)


def send_qkv(send, attn_in, w_qkv, b_qkv, cs):
    qkv = mm(attn_in, w_qkv[...]) + b_qkv[...]
    qkv_t = qkv.T
    wide = w_qkv.shape[1] // 3
    heads = wide // HEAD
    for s in range(2):
        cos, sin = cs[s, 0], cs[s, 1]
        cols = slice(s * BLK, (s + 1) * BLK)
        for h in range(heads):
            j = s * heads + h
            for e in range(3):
                part = qkv_t[e * wide + h * HEAD : e * wide + (h + 1) * HEAD, cols]
                if e < 2:
                    part = turn(part, cos, sin)
                if e == 0:
                    part = part * (HEAD**-0.5)
                send[j, e * HEAD : (e + 1) * HEAD, :] = part.astype(BF)


def feed_forward(mlp_in, w_up, b_up, w_down, act, slope):
    width = w_up.shape[1]
    total = None
    for c in range(0, width, 256):
        cols = slice(c, c + 256)
        pre = mm(mlp_in, w_up[:, cols]) + b_up[:, cols]
        cdf = 0.5 + 0.5 * lax.erf(pre * np.float32(0.7071067811865476))
        a = (pre * cdf).astype(BF)
        act[:, cols] = a
        slope[:, cols] = cdf + pre * (jnp.exp(-0.5 * pre * pre) * np.float32(0.3989422804014327))
        term = mm(a, w_down[cols, :])
        total = term if total is None else total + term
    return total


def feed_back(g_b, act, slope, mlp_in, w_up, w_down, d_up, d_down, d_b_up):
    width = w_up.shape[1]
    total = None
    mlp_t = mlp_in.astype(F32).T.astype(BF)
    for c in range(0, width, 256):
        cols = slice(c, c + 256)
        d_act = mm(g_b, w_down[cols, :], 1, 1)
        d_pre = d_act * slope[:, cols]
        d_pre_b = d_pre.astype(BF)
        d_b_up[:, cols] = jnp.sum(d_pre_b.astype(F32), 0, keepdims=True)
        d_up(c // 256, mm(mlp_t, d_pre_b))
        d_down(c, mm(act[:, cols].astype(F32).T.astype(BF), g_b))
        term = mm(d_pre_b, w_up[:, cols], 1, 1)
        total = term if total is None else total + term
    return total


def pack_up(out, row):
    def put(c, value):
        for p in range(8):
            out[p, row + 64 * c : row + 64 * (c + 1), :] = value[64 * p : 64 * (p + 1)].astype(BF)

    return put


def pack_down(out, row):
    def put(c, value):
        for half in range(2):
            for k in range(2):
                out[c // 128 + k, row + 128 * half : row + 128 * (half + 1), :] = value[
                    128 * k : 128 * (k + 1), 256 * half : 256 * (half + 1)
                ].astype(BF)

    return put


def pack_qkv(out, row, value):
    for p in range(8):
        for c in range(3):
            out[p, row + 64 * c : row + 64 * (c + 1), :] = value[
                64 * p : 64 * (p + 1), 256 * c : 256 * (c + 1)
            ].astype(BF)


def pack_out(out, row, value):
    for p in range(8):
        for half in range(2):
            out[p, row + 32 * half : row + 32 * (half + 1), :] = value[
                32 * p : 32 * (p + 1), 256 * half : 256 * (half + 1)
            ].astype(BF)


def first_body(
    at, pos, freqs, x, gain, bias, w_qkv, b_qkv, w_up, b_up, w_down, send, part, act, slope, cs
):
    for s in range(2):
        p = pos[s : s + 1, :].astype(F32)
        angle = freqs[...] * p
        cs[s, 0] = jnp.cos(angle)
        cs[s, 1] = jnp.sin(angle)
    normed, _ = norm_rows(x[...])
    attn_in = (normed * gain[0, 0:1] + bias[0, 0:1]).astype(BF)
    mlp_in = (normed * gain[0, 1:2] + bias[0, 1:2]).astype(BF)
    send_qkv(send, attn_in, w_qkv, b_qkv, cs)
    heads = w_qkv.shape[1] // 3 // HEAD
    row = lax.broadcasted_iota(jnp.int32, (16, BLK), 0)
    token = at[0] * BLK + lax.broadcasted_iota(jnp.int32, (1, BLK), 1)
    for s in range(2):
        start = jnp.maximum(token - pos[s : s + 1, :], 0)
        high = (start // 8).astype(F32)
        low = (start % 8).astype(F32)
        block = jnp.where(row == 0, high, jnp.where(row == 1, low, 0.0)).astype(BF)
        for h in range(heads):
            send[s * heads + h, 3 * HEAD : 3 * HEAD + 16, :] = block
    part[...] = feed_forward(mlp_in, w_up, b_up, w_down, act, slope).astype(BF)


def load_rows(recv, lo, hi):
    return jnp.concatenate([recv[i, lo:hi, :] for i in range(8)], 1)


def starts_of(recv):
    rows = load_rows(recv, 3 * HEAD, 3 * HEAD + 16).astype(F32)
    return rows[0:1] * 8.0 + rows[1:2]


def visible_of(start, c, length):
    key = lax.broadcasted_iota(jnp.int32, (length, CHUNK), 0)
    query = lax.broadcasted_iota(jnp.int32, (length, CHUNK), 1) + c * CHUNK
    return (key <= query) & (key >= start[:, c * CHUNK : (c + 1) * CHUNK])


def attend_body(recv, send, lse, ctx, start_out):
    q = load_rows(recv, 0, HEAD)
    k_t = load_rows(recv, HEAD, 2 * HEAD)
    v_t = load_rows(recv, 2 * HEAD, 3 * HEAD)
    k = k_t.astype(F32).T.astype(BF)
    start = starts_of(recv).astype(jnp.int32)
    start_out[...] = start
    for c in range(4):
        cols = slice(c * CHUNK, (c + 1) * CHUNK)
        length = (c + 1) * CHUNK
        scores = mm(k[:length], q[:, cols])
        scores = jnp.where(visible_of(start, c, length), scores, NEG)
        peak = jnp.max(scores, 0, keepdims=True)
        shifted = jnp.exp(scores - peak)
        total = jnp.sum(shifted, 0, keepdims=True)
        lse[:, cols] = peak + jnp.log(total)
        out = mm(v_t[:, :length], shifted.astype(BF)) / total
        ctx[:, cols] = out
        for i in range(CHUNK // BLK):
            block = out[:, i * BLK : (i + 1) * BLK].astype(BF)
            for t in range(2):
                send[c * (CHUNK // BLK) + i, t] = block


def attend_both_body(recv, start, send, dk, dv):
    q = load_rows(recv, 0, HEAD)
    k_t = load_rows(recv, HEAD, 2 * HEAD)
    v_t = load_rows(recv, 2 * HEAD, 3 * HEAD)
    d_ctx = load_rows(recv, 3 * HEAD, 4 * HEAD)
    k = k_t.astype(F32).T.astype(BF)
    v = v_t.astype(F32).T.astype(BF)
    dk[...] = jnp.zeros_like(dk)
    dv[...] = jnp.zeros_like(dv)
    for c in range(4):
        cols = slice(c * CHUNK, (c + 1) * CHUNK)
        length = (c + 1) * CHUNK
        scores = mm(k[:length], q[:, cols])
        scores = jnp.where(visible_of(start[...], c, length), scores, NEG)
        peak = jnp.max(scores, 0, keepdims=True)
        shifted = jnp.exp(scores - peak)
        probs = shifted * (1.0 / jnp.sum(shifted, 0, keepdims=True))
        probs_b = probs.astype(BF)
        out = mm(v_t[:, :length], probs_b)
        dq = backward_chunk(q, k_t, v, d_ctx, probs, probs_b, out, cols, length, dk, dv)
        for i in range(CHUNK // BLK):
            b = c * (CHUNK // BLK) + i
            for t in range(2):
                send[b, t, 0:HEAD] = out[:, i * BLK : (i + 1) * BLK].astype(BF)
                send[b, t, HEAD : 2 * HEAD] = dq[:, i * BLK : (i + 1) * BLK].astype(BF)
    put_kv(send, dk, dv, 2 * HEAD)


def backward_chunk(q, k_t, v, d_ctx, probs, probs_b, out, cols, length, dk, dv):
    d_out = d_ctx[:, cols]
    d_probs = mm(v[:length], d_out)
    delta = jnp.sum(d_out.astype(F32) * out, 0, keepdims=True)
    d_scores = (probs * (d_probs - delta)).astype(BF)
    dk[:, :length] += mm(q[:, cols], d_scores, 1, 1)
    dv[:, :length] += mm(d_out, probs_b, 1, 1)
    return mm(k_t[:, :length], d_scores) * (HEAD**-0.5)


def put_kv(send, dk, dv, row):
    for b in range(8):
        for t in range(2):
            send[b, t, row : row + HEAD] = dk[:, b * BLK : (b + 1) * BLK].astype(BF)
            send[b, t, row + HEAD : row + 2 * HEAD] = dv[:, b * BLK : (b + 1) * BLK].astype(BF)


def attend_back_body(recv, recv_d, start, lse, ctx, send, dk, dv):
    q = load_rows(recv, 0, HEAD)
    k_t = load_rows(recv, HEAD, 2 * HEAD)
    v_t = load_rows(recv, 2 * HEAD, 3 * HEAD)
    d_ctx = load_rows(recv_d, 0, HEAD)
    k = k_t.astype(F32).T.astype(BF)
    v = v_t.astype(F32).T.astype(BF)
    dk[...] = jnp.zeros_like(dk)
    dv[...] = jnp.zeros_like(dv)
    for c in range(4):
        cols = slice(c * CHUNK, (c + 1) * CHUNK)
        length = (c + 1) * CHUNK
        scores = mm(k[:length], q[:, cols])
        scores = jnp.where(visible_of(start[...], c, length), scores, NEG)
        probs = jnp.exp(scores - lse[:, cols])
        probs_b = probs.astype(BF)
        dq = backward_chunk(q, k_t, v, d_ctx, probs, probs_b, ctx[:, cols], cols, length, dk, dv)
        for i in range(CHUNK // BLK):
            for t in range(2):
                send[c * (CHUNK // BLK) + i, t, 0:HEAD] = dq[:, i * BLK : (i + 1) * BLK].astype(BF)
    put_kv(send, dk, dv, HEAD)


def gather_ctx(recv, s):
    return jnp.concatenate([recv[s * 4 + h, t, 0:HEAD, :] for t in range(2) for h in range(4)], 0)


def ordered(t, own, other):
    first = jnp.where(t == 0, own[...], other[...])
    second = jnp.where(t == 0, other[...], own[...])
    return first, second


def branch_of(t, recv, w_own, w_other):
    first, second = ordered(t, w_own, w_other)
    w = jnp.concatenate([first, second], 0)
    rows = []
    for s in range(2):
        rows.append(mm(gather_ctx(recv, s).astype(F32).T.astype(BF), w))
    return jnp.concatenate(rows, 0)


def middle_body(
    at, x, part, part_other, recv, w_out_own, w_out_other, out_bias, gain, bias,
    w_qkv, b_qkv, w_up, b_up, w_down, w_out, cot, cs,
    stream, send, grads, parts, d_b_up, d_sum, act, slope,
):
    branch = part[...].astype(F32) + part_other[...].astype(F32)
    branch = branch + branch_of(at[1], recv, w_out_own, w_out_other)
    out = x[...] + branch + out_bias[0, 0:1] + out_bias[0, 1:2]
    stream[...] = out
    normed, _ = norm_rows(out)
    attn_in = (normed * gain[1, 0:1] + bias[1, 0:1]).astype(BF)
    mlp_in = (normed * gain[1, 1:2] + bias[1, 1:2]).astype(BF)
    send_qkv(send, attn_in, w_qkv, b_qkv, cs)
    g_b = cot[...].astype(BF)
    d_ctx = mm(w_out[...], g_b, 1, 1)
    for s in range(2):
        for h in range(4):
            send[s * 4 + h, 3 * HEAD : 4 * HEAD, :] = d_ctx[
                h * HEAD : (h + 1) * HEAD, s * BLK : (s + 1) * BLK
            ].astype(BF)
    d_sum[...] = jnp.sum(cot[...], 0, keepdims=True)
    parts[0:256] = feed_forward(mlp_in, w_up, b_up, w_down, act, slope).astype(BF)
    parts[256:512] = feed_back(
        g_b, act, slope, mlp_in, w_up, w_down, pack_up(grads, 0), pack_down(grads, 256), d_b_up
    ).astype(BF)


def norm_back(
    t, x, g, d_mlp_in, recv, row, w_own, w_other, cs, gain, bias, layer, d_qkv, d_b_qkv, d_norm
):
    normed, inv = norm_rows(x)
    attn_in = (normed * gain[layer, 0:1] + bias[layer, 0:1]).astype(BF)
    halves = [[], []]
    for tt in range(2):
        for e in range(3):
            for h in range(4):
                pieces = []
                for s in range(2):
                    lo = row + e * HEAD
                    u = recv[s * 4 + h, tt, lo : lo + HEAD, :]
                    if e < 2:
                        u = turn_back(u.astype(F32), cs[s, 0], cs[s, 1]).astype(BF)
                    pieces.append(u)
                halves[tt].append(jnp.concatenate(pieces, 1))
    halves = [jnp.concatenate(half, 0) for half in halves]
    first, second = ordered(t, w_own, w_other)
    d_attn_t = mm(first, halves[0]) + mm(second, halves[1])
    d_attn_in = d_attn_t.T
    own = jnp.where(t == 0, halves[0], halves[1])
    d_qkv(mm(attn_in.astype(F32).T.astype(BF), own, 1, 1))
    d_b_qkv[...] = mm(jnp.ones((8, own.shape[1]), BF), own, 1, 1)[0:1]
    d_norm[0:1] = jnp.sum(d_attn_in * normed, 0, keepdims=True)
    d_norm[1:2] = jnp.sum(d_mlp_in * normed, 0, keepdims=True)
    d_norm[2:3] = jnp.sum(d_attn_in, 0, keepdims=True)
    d_norm[3:4] = jnp.sum(d_mlp_in, 0, keepdims=True)
    d_normed = d_attn_in * gain[layer, 0:1] + d_mlp_in * gain[layer, 1:2]
    return g + inv * (
        d_normed
        - jnp.mean(d_normed, -1, keepdims=True)
        - normed * jnp.mean(d_normed * normed, -1, keepdims=True)
    )


def turn_point_body(
    at, stream, parts, parts_other, recv, w_out_own, w_out_other, w_qkv, w_qkv_other, out_bias,
    gain, bias, cot, cs, x, act, slope, w_up, w_down, w_out, recv_first,
    block_out, g_out, send, grads, part, d_b_up, d_b_qkv, d_norm, d_sum,
):
    t = at[1]
    branch = parts[0:256].astype(F32) + parts_other[0:256].astype(F32)
    branch = branch + branch_of(t, recv, w_out_own, w_out_other)
    block_out[...] = stream[...] + branch + out_bias[1, 0:1] + out_bias[1, 1:2]
    d_mlp_in = parts[256:512].astype(F32) + parts_other[256:512].astype(F32)
    g = norm_back(
        t, stream[...], cot[...], d_mlp_in, recv, HEAD, w_qkv, w_qkv_other, cs, gain, bias, 1,
        lambda value: pack_qkv(grads, 0, value), d_b_qkv, d_norm,
    )
    g_out[...] = g
    g_b = g.astype(BF)
    d_sum[...] = jnp.sum(g, 0, keepdims=True)
    d_ctx = mm(w_out[...], g_b, 1, 1)
    for s in range(2):
        for h in range(4):
            send[s * 4 + h] = d_ctx[h * HEAD : (h + 1) * HEAD, s * BLK : (s + 1) * BLK].astype(BF)
    cot_b = cot[...].astype(BF)
    for which, (source, upstream, place) in enumerate(
        ((recv, cot_b, 192), (recv_first, g_b, 768))
    ):
        full = [gather_ctx(source, s) for s in range(2)]
        full = jnp.concatenate(full, 1)
        own = jnp.where(t == 0, full[0:256], full[256:512])
        pack_out(grads, place, mm(own, upstream))
    normed, _ = norm_rows(x[...])
    mlp_in = (normed * gain[0, 1:2] + bias[0, 1:2]).astype(BF)
    part[...] = feed_back(
        g_b, act, slope, mlp_in, w_up, w_down, pack_up(grads, 256), pack_down(grads, 512), d_b_up
    ).astype(BF)


def last_body(
    at, x, g, part, part_other, recv, w_qkv, w_qkv_other, cs, gain, bias,
    in_grad, grads, d_b_qkv, d_norm,
):
    d_mlp_in = part[...].astype(F32) + part_other[...].astype(F32)
    in_grad[...] = norm_back(
        at[1], x[...], g[...], d_mlp_in, recv, 0, w_qkv, w_qkv_other, cs, gain, bias, 0,
        lambda value: pack_qkv(grads, 0, value), d_b_qkv, d_norm,
    )


def swap(value):
    return lax.ppermute(value, "tensor", [(0, 1), (1, 0)])


def exchange(value, axes):
    return lax.all_to_all(value, axes, 0, 0)


def both(value):
    flat = value.reshape((16,) + value.shape[2:])
    return exchange(flat, ("context", "tensor")).reshape(value.shape)


def reduce_all(packed):
    rows = packed.shape[1]
    got = exchange(packed, "dp")
    one = jnp.sum(got.astype(F32), 0).astype(BF)
    got = exchange(one.reshape(8, rows // 8, 256), "context")
    one = jnp.sum(got.astype(F32), 0).astype(BF)
    back = exchange(jnp.broadcast_to(one[None], (8,) + one.shape), "context").reshape(rows, 256)
    return exchange(jnp.broadcast_to(back[None], (8,) + back.shape), "dp")


def shards(
    tokens_in, cotangent, positions, w_qkv, b_qkv, w_out, w_up, b_up, w_down, out_bias, ln_gain, ln_bias
):
    rows, width = 256, 512
    x = tokens_in.reshape(rows, width)
    cot = cotangent.reshape(rows, width)
    wq = w_qkv.reshape(2, width, 768)
    bq = b_qkv.reshape(2, 1, 768)
    bu = b_up.reshape(2, 1, 1024)
    at = jnp.stack([lax.axis_index("context"), lax.axis_index("tensor")]).astype(jnp.int32)
    freqs = jnp.asarray(FREQS).reshape(HALF, 1)
    w_out_other = swap(w_out)
    wq_other = swap(wq)

    send, part, act, slope, cs = call(
        first_body,
        [
            ((8, 208, BLK), BF),
            ((rows, width), BF),
            ((rows, 1024), BF),
            ((rows, 1024), F32),
            ((2, 2, HALF, BLK), F32),
        ],
        (at, positions, freqs, x, ln_gain, ln_bias, wq[0], bq[0], w_up[0], bu[0], w_down[0]),
        "norm_qkv_feed",
        smem_first=True,
    )
    part_other = swap(part)
    recv = exchange(send, "context")
    ctx_send, lse, ctx, start = call(
        attend_body,
        [((8, 2, HEAD, BLK), BF), ((1, 1024), F32), ((HEAD, 1024), F32), ((1, 1024), jnp.int32)],
        (recv,),
        "attend",
    )
    recv_ctx = both(ctx_send)
    stream, send, grads_a, parts, d_b_up1, d_sum1 = call(
        middle_body,
        [
            ((rows, width), F32),
            ((8, 256, BLK), BF),
            ((8, 512, 256), BF),
            ((2 * rows, width), BF),
            ((1, 1024), F32),
            ((1, width), F32),
        ],
        (
            at, x, part, part_other, recv_ctx, w_out[0], w_out_other[0], out_bias, ln_gain, ln_bias,
            wq[1], bq[1], w_up[1], bu[1], w_down[1], w_out[1], cot, cs,
        ),
        "middle",
        scratch=[pltpu.VMEM((rows, 1024), BF), pltpu.VMEM((rows, 1024), F32)],
        smem_first=True,
    )
    parts_other = swap(parts)
    recv_both = exchange(send, "context")
    (both_send,) = call(
        attend_both_body,
        [((8, 2, 256, BLK), BF)],
        (recv_both, start),
        "attend_both",
        scratch=[pltpu.VMEM((HEAD, 1024), F32), pltpu.VMEM((HEAD, 1024), F32)],
    )
    recv_grad = both(both_send)
    block_out, g, send, grads_b, part_g, d_b_up0, d_b_qkv1, d_norm1, d_sum0 = call(
        turn_point_body,
        [
            ((rows, width), F32),
            ((rows, width), F32),
            ((8, HEAD, BLK), BF),
            ((8, 832, 256), BF),
            ((rows, width), BF),
            ((1, 1024), F32),
            ((1, 768), F32),
            ((4, width), F32),
            ((1, width), F32),
        ],
        (
            at, stream, parts, parts_other, recv_grad, w_out[1], w_out_other[1], wq[1], wq_other[1],
            out_bias, ln_gain, ln_bias, cot, cs, x, act, slope, w_up[0], w_down[0], w_out[0], recv_ctx,
        ),
        "turn_point",
        smem_first=True,
    )
    part_g_other = swap(part_g)
    recv_d = exchange(send, "context")
    (back_send,) = call(
        attend_back_body,
        [((8, 2, 192, BLK), BF)],
        (recv, recv_d, start, lse, ctx),
        "attend_back",
        scratch=[pltpu.VMEM((HEAD, 1024), F32), pltpu.VMEM((HEAD, 1024), F32)],
    )
    recv_grad0 = both(back_send)
    in_grad, grads_c, d_b_qkv0, d_norm0 = call(
        last_body,
        [((rows, width), F32), ((8, 192, 256), BF), ((1, 768), F32), ((4, width), F32)],
        (at, x, g, part_g, part_g_other, recv_grad0, wq[0], wq_other[0], cs, ln_gain, ln_bias),
        "last",
        smem_first=True,
    )

    small = jnp.concatenate(
        [
            v.reshape(-1)
            for v in (d_b_up0, d_b_up1, d_b_qkv0, d_b_qkv1, d_sum0, d_sum1, d_norm0, d_norm1)
        ]
    )
    used = small.shape[0]
    small = jnp.pad(small, (0, 8 * 16 * 256 - used)).astype(BF).reshape(8, 16, 256)
    pad = jnp.zeros((8, 48, 256), BF)
    packed = jnp.concatenate([grads_a, grads_b, grads_c, small, pad], 1)
    total = reduce_all(packed)

    def up(row):
        v = total[:, row : row + 256].reshape(8, 4, 64, 256)
        return jnp.transpose(v, (0, 2, 1, 3)).reshape(512, 1024)

    def down(row):
        v = total[:, row : row + 256].reshape(8, 2, 128, 256)
        return jnp.transpose(v, (0, 2, 1, 3)).reshape(1024, 512)

    def qkv(row):
        v = total[:, row : row + 192].reshape(8, 3, 64, 256)
        return jnp.transpose(v, (0, 2, 1, 3)).reshape(512, 3, 256)

    def out(row):
        v = total[:, row : row + 64].reshape(8, 2, 32, 256)
        return jnp.transpose(v, (0, 2, 1, 3)).reshape(256, 512)

    def pair(first, second):
        return jnp.stack([first, second]).astype(F32)

    base = 512
    tiny = total[:, 1536:1552].reshape(-1).astype(F32)
    g_b_up = tiny[0:2048].reshape(2, 1024)
    g_b_qkv = tiny[2048:3584].reshape(2, 3, 256)
    g_sum = tiny[3584:4608].reshape(2, 1, 512)
    g_norm = tiny[4608:8704].reshape(2, 2, 2, 512)
    return (
        block_out.reshape(tokens_in.shape),
        in_grad.reshape(tokens_in.shape),
        pair(qkv(1344), qkv(base)),
        g_b_qkv,
        pair(out(base + 768), out(base + 192)),
        pair(up(base + 256), up(0)),
        g_b_up,
        pair(down(base + 512), down(256)),
        jnp.concatenate([g_sum, g_sum], 1),
        g_norm[:, 0],
        g_norm[:, 1],
    )


def solution(mesh):
    return jax.shard_map(
        shards,
        mesh=mesh,
        in_specs=(
            P("dp", "context", None),
            P("dp", "context", None),
            P("dp", "context"),
            P(None, None, None, "tensor"),
            P(None, None, "tensor"),
            P(None, "tensor", None),
            P(None, None, "tensor"),
            P(None, "tensor"),
            P(None, "tensor", None),
            P(),
            P(),
            P(),
        ),
        out_specs=(
            P("dp", "context", None),
            P("dp", "context", None),
            P(None, None, None, "tensor"),
            P(None, None, "tensor"),
            P(None, "tensor", None),
            P(None, None, "tensor"),
            P(None, "tensor"),
            P(None, "tensor", None),
            P(),
            P(),
            P(),
        ),
        check_vma=False,
    )
```

time: 1120 us -> 431 us (0.38)
  waiting for transfers between devices: 591 us -> 69 us
  matrix products: 110 us -> 0 us
  blocking collectives: 272 us -> 207 us
  Pallas kernels: 0 us -> 39.4 us
  starting transfers between devices: 0.97 us -> 37.6 us
  other arithmetic: 43.1 us -> 18.7 us
  local copies, waits for them, and re-layouts: 75.9 us -> 56.1 us
  between operations: 16.1 us -> 0.94 us
    psum x4 -> x0, waiting for transfers between devices: 440 us -> none  [the longest x1 333 us: shards(): stacked = lax.psum(stacked, ('dp', 'context'))]
    psum x1 -> x0, blocking collectives: 272 us -> none  [shards(): stacked = lax.psum(stacked, ('dp', 'context'))]
    all_to_all x0 -> x5, blocking collectives: none -> 207 us  [exchange(): return lax.all_to_all(value, axes, 0, 0)]
    dot_general x34 -> x0, matrix products: 99.5 us -> none  [the longest x2 23.5 us: shards(): jnp.einsum('shqk,sqhd->kshd', d_scores, query_b, preferred_element_type=j...]
    all_gather x2 -> x0, waiting for transfers between devices: 97.9 us -> none  [shards(): kv_full = lax.all_gather(kv_local, 'context', axis=1, tiled=True)]
    reduce_scatter x2 -> x0, waiting for transfers between devices: 53.5 us -> none  [shards(): lax.psum_scatter(jnp.stack([key_term.reshape(row_num, seq_count, local_wi...]
    all_to_all x0 -> x5, waiting for transfers between devices: none -> 46.7 us  [exchange(): return lax.all_to_all(value, axes, 0, 0)]
    pallas_call x0 -> x7, Pallas kernels: none -> 39.4 us  [call(): pl.pallas_call(body, out_shape=[jax.ShapeDtypeStruct(s, d) for s, d in ou...]
  transfers between devices with their start and end apart: 8 -> 10, of which waited for: 8 -> 5; matrix products, arithmetic and copies ran while one was open for 6% -> 3% of each run, Pallas kernels for 0% -> 5%
where the time goes in v1:
time: 431 us; the launch traced here: 429 us
  blocking collectives  207 us (48%)
  waiting for transfers between devices  69 us (16%)
  local copies, waits for them, and re-layouts  56.1 us (13%)
  Pallas kernels  39.4 us (9%)
  starting transfers between devices  37.6 us (9%)
  other arithmetic  18.7 us (4%)
    all_to_all x5, blocking collectives, exchange(): return lax.all_to_all(value, axes, 0, 0)  207 us
    all_to_all x5, waiting for transfers between devices, exchange(): return lax.all_to_all(value, axes, 0, 0)  46.7 us
    pallas_call x7, Pallas kernels, call(): pl.pallas_call(body, out_shape=[jax.ShapeDtypeStruct(s, d) for s, d in ou...  39.4 us
    all_to_all x5, starting transfers between devices, exchange(): return lax.all_to_all(value, axes, 0, 0)  25.4 us
    ppermute x5, waiting for transfers between devices, swap(): return lax.ppermute(value, 'tensor', [(0, 1), (1, 0)])  22.4 us
    unnamed x49, local copies, waits for them, and re-layouts  16.1 us
    ppermute x5, starting transfers between devices, swap(): return lax.ppermute(value, 'tensor', [(0, 1), (1, 0)])  12.3 us
    convert_element_type x4, other arithmetic, pair(): return jnp.stack([first, second]).astype(F32)  8.85 us
  transfers between devices with their start and end apart: 10, of which 5 were waited for; matrix products, arithmetic and copies ran while one was open for 3% of the time, Pallas kernels for 5%

profile of v1, /device:TPU:1, one launch (start us, length us, event | category | flops | bytes accessed | tf_op | source)
XLA Modules:
  0.0 429.3 jit_solution(10701576718888131149)
XLA Ops:
  12.1 4.7 %norm_qkv_feed.1 = (bf16[8,208,128]{2,1,0:T(8,128)(2,1)}, bf16[256,512]{1,0:T(8,128)(2,1)}, bf16[256,1024]{1,0:T(8,128)(2,1)}, f32[256,1024]{1,0:T(8,128)}, f32[2,2,8,128]{3,2,1,0:T(8,128)}) custom-call(s32[2]{0:T(128)} %pad_add_fusion.at, s32[2,128]{1,0:T(2,128)} %pos.1, f32[8,1]{1,0:T(8,128)} %constant.24.freqs, f32[256,512]{1,0:T(8,128)} %bitcast.84, ...), custom_call_target="tpu_custom_call" | custom-call | tf_op jit(solution)/shard_map/norm_qkv_feed/pallas_call | solution.py:32
  16.8 6.4 %all-to-all-start = ((bf16[8,208,128]{2,1,0:T(8,128)(2,1)}), bf16[8,208,128]{2,1,0:T(8,128)(2,1)S(1)}, u32[]{:S(2)}, u32[]{:S(2)}) async-start(bf16[8,208,128]{2,1,0:T(8,128)(2,1)} %get-tuple-element.40), calls=%async_computation | async-start | bytes 851968 | tf_op jit(solution)/shard_map/all_to_all | solution.py:412
  31.8 3.8 attend.1
  35.6 5.6 %all-to-all-start.1 = ((bf16[16,64,128]{2,1,0:T(8,128)(2,1)}), bf16[16,64,128]{2,1,0:T(8,128)(2,1)S(1)}, u32[]{:S(2)}, u32[]{:S(2)}) async-start(bf16[16,64,128]{2,1,0:T(8,128)(2,1)} %bitcast.116), calls=%async_computation.1 | async-start | bytes 524288 | tf_op jit(solution)/shard_map/all_to_all | solution.py:412
  45.1 4.0 collective-permute-done.part_other
  49.2 35.5 %all-to-all-done.1 = bf16[16,64,128]{2,1,0:T(8,128)(2,1)S(1)} async-done(((bf16[16,64,128]{2,1,0:T(8,128)(2,1)}), bf16[16,64,128]{2,1,0:T(8,128)(2,1)S(1)}, u32[]{:S(2)}, u32[]{:S(2)}) %all-to-all-start.1) | async-done | bytes 262176 | tf_op jit(solution)/shard_map/all_to_all | solution.py:412
  85.3 7.5 %middle.1 = (f32[256,512]{1,0:T(8,128)}, bf16[8,256,128]{2,1,0:T(8,128)(2,1)}, bf16[8,512,256]{2,1,0:T(8,128)(2,1)}, bf16[512,512]{1,0:T(8,128)(2,1)}, f32[1,1024]{1,0:T(1,128)}, /*index=5*/f32[1,512]{1,0:T(1,128)}) custom-call(s32[2]{0:T(128)} %pad_add_fusion.at, f32[256,512]{1,0:T(8,128)} %bitcast.85, bf16[256,512]{1,0:T(8,128)(2,1)} %get-tuple-element.39.part, ...), custom_call_target="tpu_custom_call" | custom-call | tf_op jit(solution)/shard_map/middle/pallas_call | solution.py:32
  92.9 13.7 %all_to_all.50.recv = bf16[8,256,128]{2,1,0:T(8,128)(2,1)} all-to-all(bf16[8,256,128]{2,1,0:T(8,128)(2,1)} %get-tuple-element.45), channel_id=1, replica_groups=mesh['dp'=8,'context'=8,'tensor'=2] {'context'}, dimensions={0} | all-to-all | bytes 1048576 | tf_op jit(solution)/shard_map/all_to_all | solution.py:412
  106.5 6.2 %attend_both.1 = bf16[8,2,256,128]{3,2,1,0:T(8,128)(2,1)} custom-call(bf16[8,256,128]{2,1,0:T(8,128)(2,1)} %all_to_all.50.recv, s32[1,1024]{1,0:T(1,128)} %get-tuple-element.46.start), custom_call_target="tpu_custom_call" | custom-call | tf_op jit(solution)/shard_map/attend_both/pallas_call | solution.py:32
  112.7 4.5 %all-to-all-start.3 = ((bf16[16,256,128]{2,1,0:T(8,128)(2,1)}), bf16[16,256,128]{2,1,0:T(8,128)(2,1)S(1)}, u32[]{:S(2)}, u32[]{:S(2)}) async-start(bf16[16,256,128]{2,1,0:T(8,128)(2,1)} %bitcast.89), calls=%async_computation.3 | async-start | bytes 2097152 | tf_op jit(solution)/shard_map/all_to_all | solution.py:412
  124.3 18.3 %collective-permute-done.2.parts_other = bf16[512,512]{1,0:T(8,128)(2,1)} collective-permute-done((bf16[512,512]{1,0:T(8,128)(2,1)}, bf16[512,512]{1,0:T(8,128)(2,1)}, u32[]{:S(2)}, u32[]{:S(2)}) %collective-permute-start.2) | collective-permute-done | bytes 524320 | tf_op jit(solution)/shard_map/ppermute | solution.py:408
  143.6 8.9 %turn_point.1 = (f32[256,512]{1,0:T(8,128)}, f32[256,512]{1,0:T(8,128)}, bf16[8,64,128]{2,1,0:T(8,128)(2,1)}, bf16[8,832,256]{2,1,0:T(8,128)(2,1)}, bf16[256,512...) custom-call(s32[2]{0:T(128)} %pad_add_fusion.at, ...), custom_call_target="tpu_custom_call" | custom-call | tf_op jit(solution)/shard_map/turn_point/pallas_call | solution.py:32
  155.5 4.0 all-to-all-start.4
  160.2 4.5 %all-to-all-done.4.recv_d = bf16[8,64,128]{2,1,0:T(8,128)(2,1)S(1)} async-done(((bf16[8,64,128]{2,1,0:T(8,128)(2,1)}), bf16[8,64,128]{2,1,0:T(8,128)(2,1)S(1)}, u32[]{:S(2)}, u32[]{:S(2)}) %all-to-all-start.4) | async-done | bytes 131104 | tf_op jit(solution)/shard_map/all_to_all | solution.py:412
  165.4 4.3 %attend_back.1 = bf16[8,2,192,128]{3,2,1,0:T(8,128)(2,1)} custom-call(bf16[8,208,128]{2,1,0:T(8,128)(2,1)} %copy-done.4, bf16[8,64,128]{2,1,0:T(8,128)(2,1)} %copy-done.10, s32[1,1024]{1,0:T(1,128)} %get-tuple-element.46.start, f32[1,1024]{1,0:T(1,128)} %get-tuple-element.53.lse, f32[64,1024]{1,0:T(8,128)} %get-tuple-element.54.ctx), custom_call_target="tpu_custom_call" | custom-call | tf_op jit(solution)/shard_map/attend_back/pallas_call | solution.py:32
  169.7 4.9 %all-to-all-start.5 = ((bf16[16,192,128]{2,1,0:T(8,128)(2,1)}), bf16[16,192,128]{2,1,0:T(8,128)(2,1)}, u32[]{:S(2)}, u32[]{:S(2)}) async-start(bf16[16,192,128]{2,1,0:T(8,128)(2,1)} %bitcast.102), calls=%async_computation.5 | async-start | bytes 1572864 | tf_op jit(solution)/shard_map/all_to_all | solution.py:412
  178.7 6.7 %all-to-all-done.5 = bf16[16,192,128]{2,1,0:T(8,128)(2,1)} async-done(((bf16[16,192,128]{2,1,0:T(8,128)(2,1)}), bf16[16,192,128]{2,1,0:T(8,128)(2,1)}, u32[]{:S(2)}, u32[]{:S(2)}) %all-to-all-start.5) | async-done | bytes 786464 | tf_op jit(solution)/shard_map/all_to_all | solution.py:412
  185.4 4.1 last.1
  195.7 85.1 %all_to_all.51 = bf16[8,1600,256]{2,1,0:T(8,128)(2,1)} all-to-all(bf16[8,1600,256]{2,1,0:T(8,128)(2,1)} %broadcast_dynamic-update-slice_fusion), channel_id=1, replica_groups=mesh['dp'=8,'context'=8,'tensor'=2] {'dp'}, dimensions={0} | all-to-all | bytes 13107200 | tf_op jit(solution)/shard_map/all_to_all | solution.py:412
  280.8 4.3 reduce_sum.24
  285.0 14.4 %all_to_all.52 = bf16[8,200,256]{2,1,0:T(8,128)(2,1)S(1)} all-to-all(bf16[8,200,256]{2,1,0:T(8,128)(2,1)S(1)} %bitcast.99), channel_id=1, replica_groups=mesh['dp'=8,'context'=8,'tensor'=2] {'context'}, dimensions={0} | all-to-all | bytes 1638400 | tf_op jit(solution)/shard_map/all_to_all | solution.py:412
  299.6 13.0 %all_to_all.53 = bf16[8,200,256]{2,1,0:T(8,128)(2,1)S(1)} all-to-all(bf16[8,200,256]{2,1,0:T(8,128)(2,1)S(1)} %broadcast_in_dim.17), channel_id=1, replica_groups=mesh['dp'=8,'context'=8,'tensor'=2] {'context'}, dimensions={0} | all-to-all | bytes 1638400 | tf_op jit(solution)/shard_map/all_to_all | solution.py:412
  313.0 81.3 %all_to_all.54 = bf16[8,1600,256]{2,1,0:T(8,128)(2,1)S(1)} all-to-all(bf16[8,1600,256]{2,1,0:T(8,128)(2,1)S(1)} %broadcast_in_dim.19), channel_id=1, replica_groups=mesh['dp'=8,'context'=8,'tensor'=2] {'dp'}, dimensions={0} | all-to-all | bytes 13107200 | tf_op jit(solution)/shard_map/all_to_all | solution.py:412
  403.9 3.8 fusion
  (117 shorter events, 78.9 us)
Async XLA Ops:
  0.6 5.1 %copy-start.13 = (f32[2,3,256]{2,0,1:T(2,128)S(1)}, f32[2,3,256]{2,0,1:T(2,128)}, u32[]{:S(2)}) copy-start(f32[2,3,256]{2,0,1:T(2,128)} %param.17) | copy-start | bytes 18436
  2.4 7.0 %copy-start.12 = (f32[2,1024]{1,0:T(2,128)S(1)}, f32[2,1024]{1,0:T(2,128)}, u32[]{:S(2)}) copy-start(f32[2,1024]{1,0:T(2,128)} %param.20) | copy-start | bytes 24580
  5.7 4.3 copy-start.7
  10.0 13.2 %copy-start.11 = (bf16[2,256,512]{2,1,0:T(8,128)(2,1)S(1)}, bf16[2,256,512]{2,1,0:T(8,128)(2,1)}, u32[]{:S(2)}) copy-start(bf16[2,256,512]{2,1,0:T(8,128)(2,1)} %param.18) | copy-start | bytes 1572868
  16.8 14.3 %all-to-all-start = ((bf16[8,208,128]{2,1,0:T(8,128)(2,1)}), bf16[8,208,128]{2,1,0:T(8,128)(2,1)S(1)}, u32[]{:S(2)}, u32[]{:S(2)}) async-start(bf16[8,208,128]{2,1,0:T(8,128)(2,1)} %get-tuple-element.40), calls=%async_computation | async-start | bytes 851968 | tf_op jit(solution)/shard_map/all_to_all | solution.py:412
  23.1 20.1 %collective-permute-start.1 = (bf16[2,256,512]{2,1,0:T(8,128)(2,1)S(1)}, bf16[2,256,512]{2,1,0:T(8,128)(2,1)}, u32[]{:S(2)}, u32[]{:S(2)}) collective-permute-start(bf16[2,256,512]{2,1,0:T(8,128)(2,1)S(1)} %copy-done.11), channel_id=1, source_target_pairs={{0,1},{1,0},{2,3},{3,2},{4,5},{5,4},{6,7},{7,6},{8,9},{9,8},{10,11... | collective-permute-start | bytes 1572872 | tf_op jit(solution)/shard_map/ppermute | solution.py:408
  26.5 22.6 %collective-permute-start = (bf16[256,512]{1,0:T(8,128)(2,1)}, bf16[256,512]{1,0:T(8,128)(2,1)}, u32[]{:S(2)}, u32[]{:S(2)}) collective-permute-start(bf16[256,512]{1,0:T(8,128)(2,1)} %get-tuple-element.39.part), channel_id=1, source_target_pairs={{0,1},{1,0},{2,3},{3,2},{4,5},{5,4},{6,7},{7,6},{8,9},{9,8},{10,11... | collective-permute-start | bytes 786440 | tf_op jit(solution)/shard_map/ppermute | solution.py:408
  28.2 93.5 %collective-permute-start.3 = (bf16[2,512,768]{2,1,0:T(8,128)(2,1)}, bf16[2,512,768]{2,1,0:T(8,128)(2,1)}, u32[]{:S(2)}, u32[]{:S(2)}) collective-permute-start(bf16[2,512,768]{2,1,0:T(8,128)(2,1)} %copy.58), channel_id=1, source_target_pairs={{0,1},{1,0},{2,3},{3,2},{4,5},{5,4},{6,7},{7,6},{8,9},{9,8},{10,11... | collective-permute-start | bytes 4718600 | tf_op jit(solution)/shard_map/ppermute | solution.py:408
  31.1 0.8 copy-start.4
  35.6 49.0 %all-to-all-start.1 = ((bf16[16,64,128]{2,1,0:T(8,128)(2,1)}), bf16[16,64,128]{2,1,0:T(8,128)(2,1)S(1)}, u32[]{:S(2)}, u32[]{:S(2)}) async-start(bf16[16,64,128]{2,1,0:T(8,128)(2,1)} %bitcast.116), calls=%async_computation.1 | async-start | bytes 524288 | tf_op jit(solution)/shard_map/all_to_all | solution.py:412
  92.8 27.3 %copy-start.14 = (f32[1,1024]{1,0:T(1,128)S(1)}, f32[1,1024]{1,0:T(1,128)}, u32[]{:S(2)}) copy-start(f32[1,1024]{1,0:T(1,128)} %get-tuple-element.60) | copy-start | bytes 12292
  92.8 27.3 %copy-start.15 = (f32[1,512]{1,0:T(1,128)S(1)}, f32[1,512]{1,0:T(1,128)}, u32[]{:S(2)}) copy-start(f32[1,512]{1,0:T(1,128)} %get-tuple-element.64) | copy-start | bytes 6148
  92.8 27.4 %copy-start.8 = (bf16[8,512,256]{2,1,0:T(8,128)(2,1)S(1)}, bf16[8,512,256]{2,1,0:T(8,128)(2,1)}, u32[]{:S(2)}) copy-start(bf16[8,512,256]{2,1,0:T(8,128)(2,1)} %get-tuple-element.56) | copy-start | bytes 6291460
  112.7 29.9 %all-to-all-start.3 = ((bf16[16,256,128]{2,1,0:T(8,128)(2,1)}), bf16[16,256,128]{2,1,0:T(8,128)(2,1)S(1)}, u32[]{:S(2)}, u32[]{:S(2)}) async-start(bf16[16,256,128]{2,1,0:T(8,128)(2,1)} %bitcast.89), calls=%async_computation.3 | async-start | bytes 2097152 | tf_op jit(solution)/shard_map/all_to_all | solution.py:412
  117.3 25.4 %collective-permute-start.2 = (bf16[512,512]{1,0:T(8,128)(2,1)}, bf16[512,512]{1,0:T(8,128)(2,1)}, u32[]{:S(2)}, u32[]{:S(2)}) collective-permute-start(bf16[512,512]{1,0:T(8,128)(2,1)} %get-tuple-element.44.parts), channel_id=1, source_target_pairs={{0,1},{1,0},{2,3},{3,2},{4,5},{5,4},{6,7},{7,6},{8,9},{9,8},{10,11... | collective-permute-start | bytes 1572872 | tf_op jit(solution)/shard_map/ppermute | solution.py:408
  142.6 1.0 copy-start.1
  152.5 24.2 %copy-start.5 = (bf16[8,832,256]{2,1,0:T(8,128)(2,1)S(1)}, bf16[8,832,256]{2,1,0:T(8,128)(2,1)}, u32[]{:S(2)}) copy-start(bf16[8,832,256]{2,1,0:T(8,128)(2,1)} %get-tuple-element.57) | copy-start | bytes 10223620
  152.5 26.3 %collective-permute-start.4 = (bf16[256,512]{1,0:T(8,128)(2,1)}, bf16[256,512]{1,0:T(8,128)(2,1)}, u32[]{:S(2)}, u32[]{:S(2)}) collective-permute-start(bf16[256,512]{1,0:T(8,128)(2,1)} %get-tuple-element.51.part), channel_id=1, source_target_pairs={{0,1},{1,0},{2,3},{3,2},{4,5},{5,4},{6,7},{7,6},{8,9},{9,8},{10,11... | collective-permute-start | bytes 786440 | tf_op jit(solution)/shard_map/ppermute | solution.py:408
  155.5 9.2 %all-to-all-start.4 = ((bf16[8,64,128]{2,1,0:T(8,128)(2,1)}), bf16[8,64,128]{2,1,0:T(8,128)(2,1)S(1)}, u32[]{:S(2)}, u32[]{:S(2)}) async-start(bf16[8,64,128]{2,1,0:T(8,128)(2,1)} %get-tuple-element.52), calls=%async_computation.4 | async-start | bytes 262144 | tf_op jit(solution)/shard_map/all_to_all | solution.py:412
  169.7 15.7 %all-to-all-start.5 = ((bf16[16,192,128]{2,1,0:T(8,128)(2,1)}), bf16[16,192,128]{2,1,0:T(8,128)(2,1)}, u32[]{:S(2)}, u32[]{:S(2)}) async-start(bf16[16,192,128]{2,1,0:T(8,128)(2,1)} %bitcast.102), calls=%async_computation.5 | async-start | bytes 1572864 | tf_op jit(solution)/shard_map/all_to_all | solution.py:412
  394.4 2.7 copy-start
  419.2 4.5 %copy-start.9 = (bf16[1,256,512]{2,1,0:T(8,128)(2,1)S(1)}, bf16[1,256,512]{2,1,0:T(8,128)(2,1)}, u32[]{:S(2)}) copy-start(bf16[1,256,512]{2,1,0:T(8,128)(2,1)} %stack_reshape.26) | copy-start | bytes 786436
  423.7 3.3 copy-start.2
  423.7 3.3 copy-start.3
  (2 other events, 1.4 us)

commit v2 on v1

--- a/solution.py
+++ b/solution.py
@@ -25,15 +25,33 @@
     return lax.dot_general(a, b, (((ca,), (cb,)), ((), ())), preferred_element_type=F32)
 
 
+class Layer:
+    def __init__(self, array, index):
+        self.array, self.index = array, index
+
+    def spec(self):
+        rest = self.array.shape[1:]
+        place = (self.index,) + (0,) * len(rest)
+        return pl.BlockSpec((None,) + rest, lambda i: place)
+
+
+def whole(shape):
+    return pl.BlockSpec(shape, lambda i: (0,) * len(shape))
+
+
 def call(body, out_shape, args, name, scratch=(), smem_first=False):
-    specs = [pl.BlockSpec(memory_space=pltpu.VMEM) for _ in args]
+    specs = [
+        a.spec() if isinstance(a, Layer) else whole(a.shape) for a in args
+    ]
+    args = [a.array if isinstance(a, Layer) else a for a in args]
     if smem_first:
         specs[0] = pl.BlockSpec(memory_space=pltpu.SMEM)
     return pl.pallas_call(
         body,
+        grid=(1,),
         out_shape=[jax.ShapeDtypeStruct(s, d) for s, d in out_shape],
         in_specs=specs,
-        out_specs=[pl.BlockSpec(memory_space=pltpu.VMEM) for _ in out_shape],
+        out_specs=[whole(s) for s, _ in out_shape],
         scratch_shapes=list(scratch),
         compiler_params=pltpu.CompilerParams(vmem_limit_bytes=56 * 1024 * 1024),
         name=name,
@@ -57,18 +75,14 @@
     return jnp.concatenate([a * cos + b * sin, b * cos - a * sin, u[2 * HALF :]], 0)
 
 
-def send_qkv(send, attn_in, w_qkv, b_qkv, cs):
-    qkv = mm(attn_in, w_qkv[...]) + b_qkv[...]
-    qkv_t = qkv.T
-    wide = w_qkv.shape[1] // 3
-    heads = wide // HEAD
-    for s in range(2):
-        cos, sin = cs[s, 0], cs[s, 1]
-        cols = slice(s * BLK, (s + 1) * BLK)
-        for h in range(heads):
-            j = s * heads + h
-            for e in range(3):
-                part = qkv_t[e * wide + h * HEAD : e * wide + (h + 1) * HEAD, cols]
+def send_qkv(send, attn_in, w_qkv, b_qkv, layer, cs):
+    for e in range(3):
+        turned = (mm(attn_in, w_qkv[e]) + b_qkv[e, layer : layer + 1]).T
+        for s in range(2):
+            cos, sin = cs[s, 0], cs[s, 1]
+            for h in range(4):
+                j = s * 4 + h
+                part = turned[h * HEAD : (h + 1) * HEAD, s * BLK : (s + 1) * BLK]
                 if e < 2:
                     part = turn(part, cos, sin)
                 if e == 0:
@@ -76,12 +90,12 @@
                 send[j, e * HEAD : (e + 1) * HEAD, :] = part.astype(BF)
 
 
-def feed_forward(mlp_in, w_up, b_up, w_down, act, slope):
+def feed_forward(mlp_in, w_up, b_up, layer, w_down, act, slope):
     width = w_up.shape[1]
     total = None
     for c in range(0, width, 256):
         cols = slice(c, c + 256)
-        pre = mm(mlp_in, w_up[:, cols]) + b_up[:, cols]
+        pre = mm(mlp_in, w_up[:, cols]) + b_up[layer : layer + 1, cols]
         cdf = 0.5 + 0.5 * lax.erf(pre * np.float32(0.7071067811865476))
         a = (pre * cdf).astype(BF)
         act[:, cols] = a
@@ -127,15 +141,21 @@
     return put
 
 
-def pack_qkv(out, row, value):
-    for p in range(8):
-        for c in range(3):
-            out[p, row + 64 * c : row + 64 * (c + 1), :] = value[
-                64 * p : 64 * (p + 1), 256 * c : 256 * (c + 1)
-            ].astype(BF)
-
-
-def pack_out(out, row, value):
+def pack_qkv(out, row):
+    def put(e, value):
+        for p in range(8):
+            out[p, row + 64 * e : row + 64 * (e + 1), :] = value[64 * p : 64 * (p + 1)].astype(BF)
+
+    return put
+
+
+def own_ctx(t, recv):
+    full = jnp.concatenate([gather_ctx(recv, s) for s in range(2)], 1)
+    return jnp.where(t == 0, full[0:256], full[256:512])
+
+
+def pack_out(out, row, ctx, upstream):
+    value = mm(ctx, upstream)
     for p in range(8):
         for half in range(2):
             out[p, row + 32 * half : row + 32 * (half + 1), :] = value[
@@ -154,8 +174,7 @@
     normed, _ = norm_rows(x[...])
     attn_in = (normed * gain[0, 0:1] + bias[0, 0:1]).astype(BF)
     mlp_in = (normed * gain[0, 1:2] + bias[0, 1:2]).astype(BF)
-    send_qkv(send, attn_in, w_qkv, b_qkv, cs)
-    heads = w_qkv.shape[1] // 3 // HEAD
+    send_qkv(send, attn_in, w_qkv, b_qkv, 0, cs)
     row = lax.broadcasted_iota(jnp.int32, (16, BLK), 0)
     token = at[0] * BLK + lax.broadcasted_iota(jnp.int32, (1, BLK), 1)
     for s in range(2):
@@ -163,9 +182,9 @@
         high = (start // 8).astype(F32)
         low = (start % 8).astype(F32)
         block = jnp.where(row == 0, high, jnp.where(row == 1, low, 0.0)).astype(BF)
-        for h in range(heads):
-            send[s * heads + h, 3 * HEAD : 3 * HEAD + 16, :] = block
-    part[...] = feed_forward(mlp_in, w_up, b_up, w_down, act, slope).astype(BF)
+        for h in range(4):
+            send[s * 4 + h, 3 * HEAD : 3 * HEAD + 16, :] = block
+    part[...] = feed_forward(mlp_in, w_up, b_up, 0, w_down, act, slope).astype(BF)
 
 
 def load_rows(recv, lo, hi):
@@ -280,13 +299,19 @@
 
 
 def ordered(t, own, other):
-    first = jnp.where(t == 0, own[...], other[...])
-    second = jnp.where(t == 0, other[...], own[...])
-    return first, second
-
-
-def branch_of(t, recv, w_own, w_other):
-    first, second = ordered(t, w_own, w_other)
+    return jnp.where(t == 0, own, other), jnp.where(t == 0, other, own)
+
+
+def out_other(others):
+    halves = [
+        jnp.concatenate([others[3, 64 * p + 32 * c : 64 * p + 32 * (c + 1), :] for p in range(8)], 0)
+        for c in range(2)
+    ]
+    return jnp.concatenate(halves, 1)
+
+
+def branch_of(t, recv, w_own, others):
+    first, second = ordered(t, w_own[...], out_other(others))
     w = jnp.concatenate([first, second], 0)
     rows = []
     for s in range(2):
@@ -295,18 +320,18 @@
 
 
 def middle_body(
-    at, x, part, part_other, recv, w_out_own, w_out_other, out_bias, gain, bias,
+    at, x, part, part_other, recv, w_out_own, others, out_bias, gain, bias,
     w_qkv, b_qkv, w_up, b_up, w_down, w_out, cot, cs,
     stream, send, grads, parts, d_b_up, d_sum, act, slope,
 ):
     branch = part[...].astype(F32) + part_other[...].astype(F32)
-    branch = branch + branch_of(at[1], recv, w_out_own, w_out_other)
+    branch = branch + branch_of(at[1], recv, w_out_own, others)
     out = x[...] + branch + out_bias[0, 0:1] + out_bias[0, 1:2]
     stream[...] = out
     normed, _ = norm_rows(out)
     attn_in = (normed * gain[1, 0:1] + bias[1, 0:1]).astype(BF)
     mlp_in = (normed * gain[1, 1:2] + bias[1, 1:2]).astype(BF)
-    send_qkv(send, attn_in, w_qkv, b_qkv, cs)
+    send_qkv(send, attn_in, w_qkv, b_qkv, 1, cs)
     g_b = cot[...].astype(BF)
     d_ctx = mm(w_out[...], g_b, 1, 1)
     for s in range(2):
@@ -315,20 +340,23 @@
                 h * HEAD : (h + 1) * HEAD, s * BLK : (s + 1) * BLK
             ].astype(BF)
     d_sum[...] = jnp.sum(cot[...], 0, keepdims=True)
-    parts[0:256] = feed_forward(mlp_in, w_up, b_up, w_down, act, slope).astype(BF)
+    parts[0:256] = feed_forward(mlp_in, w_up, b_up, 1, w_down, act, slope).astype(BF)
     parts[256:512] = feed_back(
         g_b, act, slope, mlp_in, w_up, w_down, pack_up(grads, 0), pack_down(grads, 256), d_b_up
     ).astype(BF)
 
 
 def norm_back(
-    t, x, g, d_mlp_in, recv, row, w_own, w_other, cs, gain, bias, layer, d_qkv, d_b_qkv, d_norm
+    t, x, g, d_mlp_in, recv, row, w_own, others, cs, gain, bias, layer, d_qkv, d_b_qkv, d_norm
 ):
     normed, inv = norm_rows(x)
     attn_in = (normed * gain[layer, 0:1] + bias[layer, 0:1]).astype(BF)
-    halves = [[], []]
-    for tt in range(2):
-        for e in range(3):
+    attn_t = attn_in.astype(F32).T.astype(BF)
+    d_attn_t = None
+    for e in range(3):
+        halves = []
+        for tt in range(2):
+            blocks = []
             for h in range(4):
                 pieces = []
                 for s in range(2):
@@ -337,14 +365,15 @@
                     if e < 2:
                         u = turn_back(u.astype(F32), cs[s, 0], cs[s, 1]).astype(BF)
                     pieces.append(u)
-                halves[tt].append(jnp.concatenate(pieces, 1))
-    halves = [jnp.concatenate(half, 0) for half in halves]
-    first, second = ordered(t, w_own, w_other)
-    d_attn_t = mm(first, halves[0]) + mm(second, halves[1])
+                blocks.append(jnp.concatenate(pieces, 1))
+            halves.append(jnp.concatenate(blocks, 0))
+        first, second = ordered(t, w_own[e], others[e])
+        term = mm(first, halves[0]) + mm(second, halves[1])
+        d_attn_t = term if d_attn_t is None else d_attn_t + term
+        own = jnp.where(t == 0, halves[0], halves[1])
+        d_qkv(e, mm(attn_t, own, 1, 1))
+        d_b_qkv[e : e + 1] = mm(jnp.ones((8, own.shape[1]), BF), own, 1, 1)[0:1]
     d_attn_in = d_attn_t.T
-    own = jnp.where(t == 0, halves[0], halves[1])
-    d_qkv(mm(attn_in.astype(F32).T.astype(BF), own, 1, 1))
-    d_b_qkv[...] = mm(jnp.ones((8, own.shape[1]), BF), own, 1, 1)[0:1]
     d_norm[0:1] = jnp.sum(d_attn_in * normed, 0, keepdims=True)
     d_norm[1:2] = jnp.sum(d_mlp_in * normed, 0, keepdims=True)
     d_norm[2:3] = jnp.sum(d_attn_in, 0, keepdims=True)
@@ -358,50 +387,180 @@
 
 
 def turn_point_body(
-    at, stream, parts, parts_other, recv, w_out_own, w_out_other, w_qkv, w_qkv_other, out_bias,
-    gain, bias, cot, cs, x, act, slope, w_up, w_down, w_out, recv_first,
+    at, stream, parts, parts_other, recv, w_out, w_qkv, others, out_bias,
+    gain, bias, cot, cs, x, act, slope, w_up, w_down, w_out_first,
     block_out, g_out, send, grads, part, d_b_up, d_b_qkv, d_norm, d_sum,
 ):
     t = at[1]
     branch = parts[0:256].astype(F32) + parts_other[0:256].astype(F32)
-    branch = branch + branch_of(t, recv, w_out_own, w_out_other)
+    branch = branch + branch_of(t, recv, w_out, others)
     block_out[...] = stream[...] + branch + out_bias[1, 0:1] + out_bias[1, 1:2]
     d_mlp_in = parts[256:512].astype(F32) + parts_other[256:512].astype(F32)
     g = norm_back(
-        t, stream[...], cot[...], d_mlp_in, recv, HEAD, w_qkv, w_qkv_other, cs, gain, bias, 1,
-        lambda value: pack_qkv(grads, 0, value), d_b_qkv, d_norm,
+        t, stream[...], cot[...], d_mlp_in, recv, HEAD, w_qkv, others, cs, gain, bias, 1,
+        pack_qkv(grads, 0), d_b_qkv, d_norm,
     )
     g_out[...] = g
     g_b = g.astype(BF)
     d_sum[...] = jnp.sum(g, 0, keepdims=True)
-    d_ctx = mm(w_out[...], g_b, 1, 1)
+    d_ctx = mm(w_out_first[...], g_b, 1, 1)
     for s in range(2):
         for h in range(4):
             send[s * 4 + h] = d_ctx[h * HEAD : (h + 1) * HEAD, s * BLK : (s + 1) * BLK].astype(BF)
-    cot_b = cot[...].astype(BF)
-    for which, (source, upstream, place) in enumerate(
-        ((recv, cot_b, 192), (recv_first, g_b, 768))
-    ):
-        full = [gather_ctx(source, s) for s in range(2)]
-        full = jnp.concatenate(full, 1)
-        own = jnp.where(t == 0, full[0:256], full[256:512])
-        pack_out(grads, place, mm(own, upstream))
+    pack_out(grads, 704, own_ctx(t, recv), cot[...].astype(BF))
     normed, _ = norm_rows(x[...])
     mlp_in = (normed * gain[0, 1:2] + bias[0, 1:2]).astype(BF)
     part[...] = feed_back(
-        g_b, act, slope, mlp_in, w_up, w_down, pack_up(grads, 256), pack_down(grads, 512), d_b_up
+        g_b, act, slope, mlp_in, w_up, w_down, pack_up(grads, 192), pack_down(grads, 448), d_b_up
     ).astype(BF)
 
 
 def last_body(
-    at, x, g, part, part_other, recv, w_qkv, w_qkv_other, cs, gain, bias,
-    in_grad, grads, d_b_qkv, d_norm,
+    at, x, g, part, part_other, recv, recv_ctx, w_qkv, others, cs, gain, bias,
+    d_b_up0, d_b_up1, d_b_qkv1, d_norm1, d_sum0, d_sum1,
+    in_grad, grads, d_b_qkv0, d_norm0,
 ):
     d_mlp_in = part[...].astype(F32) + part_other[...].astype(F32)
     in_grad[...] = norm_back(
-        at[1], x[...], g[...], d_mlp_in, recv, 0, w_qkv, w_qkv_other, cs, gain, bias, 0,
-        lambda value: pack_qkv(grads, 0, value), d_b_qkv, d_norm,
-    )
+        at[1], x[...], g[...], d_mlp_in, recv, 0, w_qkv, others, cs, gain, bias, 0,
+        pack_qkv(grads, 0), d_b_qkv0, d_norm0,
+    )
+    pack_out(grads, 192, own_ctx(at[1], recv_ctx), g[...].astype(BF))
+
+    def lanes(ref, row, count):
+        return [ref[row : row + 1, 256 * c : 256 * (c + 1)] for c in range(count)]
+
+    def norms(ref):
+        return [v for r in range(4) for v in lanes(ref, r, 2)]
+
+    rows = [
+        lanes(d_b_up0, 0, 4)
+        + lanes(d_b_up1, 0, 4)
+        + [v for e in range(3) for ref in (d_b_qkv0, d_b_qkv1) for v in lanes(ref, e, 1)],
+        lanes(d_sum0, 0, 2) + lanes(d_sum1, 0, 2) + norms(d_norm0),
+        norms(d_norm1),
+    ]
+    for p in range(8):
+        have = rows[p] if p < len(rows) else []
+        fill = [jnp.zeros((16 - len(have), 256), F32)]
+        grads[p, 256:272, :] = jnp.concatenate(have + fill, 0).astype(BF)
+
+
+def chunk_body(at, w_qkv, w_out, out):
+    for layer in range(2):
+        for e in range(3):
+            out[layer, e] = w_qkv[layer, e, pl.ds(pl.multiple_of(at[2] * 64, 64), 64), :]
+        rows = w_out[layer, pl.ds(pl.multiple_of(at[2] * 32, 32), 32), :]
+        out[layer, 3, 0:32] = rows[:, 0:256]
+        out[layer, 3, 32:64] = rows[:, 256:512]
+
+
+def mix_body(got, early, out):
+    total = got[0].astype(F32)
+    for i in range(1, 8):
+        total = total + got[i].astype(F32)
+    for q in range(8):
+        out[q, 0:96] = early[96 * q : 96 * (q + 1)]
+        out[q, 96:128] = total[32 * q : 32 * (q + 1)].astype(BF)
+        if q == 0:
+            out[q, 128:144] = total[256:272].astype(BF)
+        else:
+            out[q, 128:144] = jnp.zeros((16, 256), BF)
+
+
+def sum_body(got, out):
+    total = got[0].astype(F32)
+    for i in range(1, 8):
+        total = total + got[i].astype(F32)
+    out[...] = total.astype(BF)
+
+
+def unpack_body(first, rest, g_qkv, g_out, g_up, g_down, g_b_up, g_b_qkv, g_sum, g_gain, g_bias):
+    p = pl.program_id(0)
+
+    def early(row):
+        return rest[row // 96, row % 96 : row % 96 + 32].astype(F32)
+
+    def late(row):
+        return rest[row // 32, 96:128].astype(F32)
+
+    for e in range(3):
+        for k in range(2):
+            g_qkv[0, e, 32 * k : 32 * (k + 1)] = late(64 * e + 32 * k)
+            g_qkv[1, e, 32 * k : 32 * (k + 1)] = early(64 * e + 32 * k)
+    for c in range(2):
+        g_out[0, :, 256 * c : 256 * (c + 1)] = late(192 + 32 * c)
+        g_out[1, :, 256 * c : 256 * (c + 1)] = early(704 + 32 * c)
+    for c in range(4):
+        cols = slice(256 * c, 256 * (c + 1))
+        for k in range(2):
+            g_up[0, 32 * k : 32 * (k + 1), cols] = early(192 + 64 * c + 32 * k)
+        g_up[1, :, cols] = first[64 * c : 64 * (c + 1)].astype(F32)
+    for c in range(2):
+        cols = slice(256 * c, 256 * (c + 1))
+        for k in range(4):
+            g_down[0, 32 * k : 32 * (k + 1), cols] = early(448 + 128 * c + 32 * k)
+        g_down[1, :, cols] = first[256 + 128 * c : 256 + 128 * (c + 1)].astype(F32)
+
+    tiny = rest[0, 128:144].astype(F32)
+
+    @pl.when(p == 0)
+    def _():
+        for layer in range(2):
+            for c in range(4):
+                r = 4 * layer + c
+                g_b_up[layer : layer + 1, 256 * c : 256 * (c + 1)] = tiny[r : r + 1]
+        for e in range(3):
+            for layer in range(2):
+                r = 8 + 2 * e + layer
+                g_b_qkv[e, layer : layer + 1, :] = tiny[r : r + 1]
+
+    def norms(layer, base):
+        for which in range(2):
+            for c in range(2):
+                cols = slice(256 * c, 256 * (c + 1))
+                r = base + 2 * which + c
+                g_gain[layer, which : which + 1, cols] = tiny[r : r + 1]
+                g_bias[layer, which : which + 1, cols] = tiny[r + 4 : r + 5]
+
+    @pl.when(p == 1)
+    def _():
+        for layer in range(2):
+            for c in range(2):
+                r = 2 * layer + c
+                for which in range(2):
+                    g_sum[layer, which : which + 1, 256 * c : 256 * (c + 1)] = tiny[r : r + 1]
+        norms(0, 4)
+
+    @pl.when(p == 2)
+    def _():
+        norms(1, 0)
+
+
+def unpack(first, rest):
+    outs = [
+        ((2, 3, 512, 256), pl.BlockSpec((2, 3, 64, 256), lambda p: (0, 0, p, 0))),
+        ((2, 256, 512), pl.BlockSpec((2, 32, 512), lambda p: (0, p, 0))),
+        ((2, 512, 1024), pl.BlockSpec((2, 64, 1024), lambda p: (0, p, 0))),
+        ((2, 1024, 512), pl.BlockSpec((2, 128, 512), lambda p: (0, p, 0))),
+        ((2, 1024), whole((2, 1024))),
+        ((3, 2, 256), whole((3, 2, 256))),
+        ((2, 2, 512), whole((2, 2, 512))),
+        ((2, 2, 512), whole((2, 2, 512))),
+        ((2, 2, 512), whole((2, 2, 512))),
+    ]
+    return pl.pallas_call(
+        unpack_body,
+        grid=(8,),
+        out_shape=[jax.ShapeDtypeStruct(shape, F32) for shape, _ in outs],
+        in_specs=[
+            pl.BlockSpec((None, 512, 256), lambda p: (p, 0, 0)),
+            pl.BlockSpec((None, 8, 144, 256), lambda p: (p, 0, 0, 0)),
+        ],
+        out_specs=[spec for _, spec in outs],
+        compiler_params=pltpu.CompilerParams(vmem_limit_bytes=56 * 1024 * 1024),
+        name="unpack",
+    )(first, rest)
 
 
 def swap(value):
@@ -415,16 +574,6 @@
 def both(value):
     flat = value.reshape((16,) + value.shape[2:])
     return exchange(flat, ("context", "tensor")).reshape(value.shape)
-
-
-def reduce_all(packed):
-    rows = packed.shape[1]
-    got = exchange(packed, "dp")
-    one = jnp.sum(got.astype(F32), 0).astype(BF)
-    got = exchange(one.reshape(8, rows // 8, 256), "context")
-    one = jnp.sum(got.astype(F32), 0).astype(BF)
-    back = exchange(jnp.broadcast_to(one[None], (8,) + one.shape), "context").reshape(rows, 256)
-    return exchange(jnp.broadcast_to(back[None], (8,) + back.shape), "dp")
 
 
 def shards(
@@ -433,13 +582,14 @@
     rows, width = 256, 512
     x = tokens_in.reshape(rows, width)
     cot = cotangent.reshape(rows, width)
-    wq = w_qkv.reshape(2, width, 768)
-    bq = b_qkv.reshape(2, 1, 768)
-    bu = b_up.reshape(2, 1, 1024)
-    at = jnp.stack([lax.axis_index("context"), lax.axis_index("tensor")]).astype(jnp.int32)
+    wq = jnp.transpose(w_qkv, (0, 2, 1, 3))
+    bq = jnp.transpose(b_qkv, (1, 0, 2))
+    at = jnp.stack(
+        [lax.axis_index("context"), lax.axis_index("tensor"), lax.axis_index("dp")]
+    ).astype(jnp.int32)
     freqs = jnp.asarray(FREQS).reshape(HALF, 1)
-    w_out_other = swap(w_out)
-    wq_other = swap(wq)
+    (chunk,) = call(chunk_body, [((2, 4, 64, 256), BF)], (at, wq, w_out), "chunk", smem_first=True)
+    others = lax.all_gather(swap(chunk), "dp", axis=2, tiled=True)
 
     send, part, act, slope, cs = call(
         first_body,
@@ -450,7 +600,10 @@
             ((rows, 1024), F32),
             ((2, 2, HALF, BLK), F32),
         ],
-        (at, positions, freqs, x, ln_gain, ln_bias, wq[0], bq[0], w_up[0], bu[0], w_down[0]),
+        (
+            at, positions, freqs, x, ln_gain, ln_bias, Layer(wq, 0), bq, Layer(w_up, 0), b_up,
+            Layer(w_down, 0),
+        ),
         "norm_qkv_feed",
         smem_first=True,
     )
@@ -474,13 +627,16 @@
             ((1, width), F32),
         ],
         (
-            at, x, part, part_other, recv_ctx, w_out[0], w_out_other[0], out_bias, ln_gain, ln_bias,
-            wq[1], bq[1], w_up[1], bu[1], w_down[1], w_out[1], cot, cs,
+            at, x, part, part_other, recv_ctx, Layer(w_out, 0), Layer(others, 0), out_bias, ln_gain,
+            ln_bias, Layer(wq, 1), bq, Layer(w_up, 1), b_up, Layer(w_down, 1), Layer(w_out, 1), cot, cs,
         ),
         "middle",
         scratch=[pltpu.VMEM((rows, 1024), BF), pltpu.VMEM((rows, 1024), F32)],
         smem_first=True,
     )
+    sums_a = lax.psum_scatter(grads_a, "dp", scatter_dimension=0)
+    sums_a = lax.psum(sums_a, "context")
+    full_a = lax.all_gather(sums_a, "dp")
     parts_other = swap(parts)
     recv_both = exchange(send, "context")
     (both_send,) = call(
@@ -497,20 +653,22 @@
             ((rows, width), F32),
             ((rows, width), F32),
             ((8, HEAD, BLK), BF),
-            ((8, 832, 256), BF),
+            ((8, 768, 256), BF),
             ((rows, width), BF),
             ((1, 1024), F32),
-            ((1, 768), F32),
+            ((3, 256), F32),
             ((4, width), F32),
             ((1, width), F32),
         ],
         (
-            at, stream, parts, parts_other, recv_grad, w_out[1], w_out_other[1], wq[1], wq_other[1],
-            out_bias, ln_gain, ln_bias, cot, cs, x, act, slope, w_up[0], w_down[0], w_out[0], recv_ctx,
+            at, stream, parts, parts_other, recv_grad, Layer(w_out, 1), Layer(wq, 1), Layer(others, 1),
+            out_bias, ln_gain, ln_bias, cot, cs, x, act, slope, Layer(w_up, 0), Layer(w_down, 0),
+            Layer(w_out, 0),
         ),
         "turn_point",
         smem_first=True,
     )
+    sums_b = lax.psum_scatter(grads_b, "dp", scatter_dimension=0)
     part_g_other = swap(part_g)
     recv_d = exchange(send, "context")
     (back_send,) = call(
@@ -521,63 +679,33 @@
         scratch=[pltpu.VMEM((HEAD, 1024), F32), pltpu.VMEM((HEAD, 1024), F32)],
     )
     recv_grad0 = both(back_send)
-    in_grad, grads_c, d_b_qkv0, d_norm0 = call(
+    in_grad, grads_c, _, _ = call(
         last_body,
-        [((rows, width), F32), ((8, 192, 256), BF), ((1, 768), F32), ((4, width), F32)],
-        (at, x, g, part_g, part_g_other, recv_grad0, wq[0], wq_other[0], cs, ln_gain, ln_bias),
+        [((rows, width), F32), ((8, 272, 256), BF), ((3, 256), F32), ((4, width), F32)],
+        (
+            at, x, g, part_g, part_g_other, recv_grad0, recv_ctx, Layer(wq, 0), Layer(others, 0), cs,
+            ln_gain, ln_bias, d_b_up0, d_b_up1, d_b_qkv1, d_norm1, d_sum0, d_sum1,
+        ),
         "last",
         smem_first=True,
     )
-
-    small = jnp.concatenate(
-        [
-            v.reshape(-1)
-            for v in (d_b_up0, d_b_up1, d_b_qkv0, d_b_qkv1, d_sum0, d_sum1, d_norm0, d_norm1)
-        ]
-    )
-    used = small.shape[0]
-    small = jnp.pad(small, (0, 8 * 16 * 256 - used)).astype(BF).reshape(8, 16, 256)
-    pad = jnp.zeros((8, 48, 256), BF)
-    packed = jnp.concatenate([grads_a, grads_b, grads_c, small, pad], 1)
-    total = reduce_all(packed)
-
-    def up(row):
-        v = total[:, row : row + 256].reshape(8, 4, 64, 256)
-        return jnp.transpose(v, (0, 2, 1, 3)).reshape(512, 1024)
-
-    def down(row):
-        v = total[:, row : row + 256].reshape(8, 2, 128, 256)
-        return jnp.transpose(v, (0, 2, 1, 3)).reshape(1024, 512)
-
-    def qkv(row):
-        v = total[:, row : row + 192].reshape(8, 3, 64, 256)
-        return jnp.transpose(v, (0, 2, 1, 3)).reshape(512, 3, 256)
-
-    def out(row):
-        v = total[:, row : row + 64].reshape(8, 2, 32, 256)
-        return jnp.transpose(v, (0, 2, 1, 3)).reshape(256, 512)
-
-    def pair(first, second):
-        return jnp.stack([first, second]).astype(F32)
-
-    base = 512
-    tiny = total[:, 1536:1552].reshape(-1).astype(F32)
-    g_b_up = tiny[0:2048].reshape(2, 1024)
-    g_b_qkv = tiny[2048:3584].reshape(2, 3, 256)
-    g_sum = tiny[3584:4608].reshape(2, 1, 512)
-    g_norm = tiny[4608:8704].reshape(2, 2, 2, 512)
+    (mixed,) = call(mix_body, [((8, 144, 256), BF)], (exchange(grads_c, "dp"), sums_b), "mix")
+    (summed,) = call(sum_body, [((144, 256), BF)], (exchange(mixed, "context"),), "sum")
+    summed = exchange(jnp.broadcast_to(summed[None], (8, 144, 256)), "context")
+    full_bc = lax.all_gather(summed, "dp")
+    g_qkv, g_out, g_up, g_down, g_b_up, g_b_qkv, g_sum, g_gain, g_bias = unpack(full_a, full_bc)
     return (
         block_out.reshape(tokens_in.shape),
         in_grad.reshape(tokens_in.shape),
-        pair(qkv(1344), qkv(base)),
-        g_b_qkv,
-        pair(out(base + 768), out(base + 192)),
-        pair(up(base + 256), up(0)),
+        jnp.transpose(g_qkv, (0, 2, 1, 3)),
+        jnp.transpose(g_b_qkv, (1, 0, 2)),
+        g_out,
+        g_up,
         g_b_up,
-        pair(down(base + 512), down(256)),
-        jnp.concatenate([g_sum, g_sum], 1),
-        g_norm[:, 0],
-        g_norm[:, 1],
+        g_down,
+        g_sum,
+        g_gain,
+        g_bias,
     )
 
 

time: 431 us -> 320 us (0.74)
  blocking collectives: 207 us -> 77.8 us
  waiting for transfers between devices: 69 us -> 131 us
  local copies, waits for them, and re-layouts: 56.1 us -> 6.2 us
  other arithmetic: 18.7 us -> 0.61 us
  Pallas kernels: 39.4 us -> 55.7 us
  between operations: 0.94 us -> 14.3 us
  starting transfers between devices: 37.6 us -> 33.1 us
    all_to_all x5, blocking collectives: 207 us -> 77.8 us  [exchange(): return lax.all_to_all(value, axes, 0, 0)]
    psum x0 -> x1, waiting for transfers between devices: none -> 49.3 us  [shards(): sums_a = lax.psum(sums_a, 'context')]
    all_to_all x5 -> x4, waiting for transfers between devices: 46.7 us -> 10.8 us  [exchange(): return lax.all_to_all(value, axes, 0, 0)]
    all_gather x0 -> x3, waiting for transfers between devices: none -> 34 us  [the longest x1 34 us: shards(): full_bc = lax.all_gather(summed, 'dp')]
    pallas_call x7 -> x11, Pallas kernels: 39.4 us -> 55.7 us  [the longest x10 46.7 us: call(): pl.pallas_call(body, grid=(1,), out_shape=[jax.ShapeDtypeStruct(s, d) for...]
    squeeze x8 -> x0, local copies, waits for them, and re-layouts: 13.9 us -> none  [the longest x1 3.07 us: shards(): w_up[1]]
    unnamed x49 -> x24, local copies, waits for them, and re-layouts: 16.1 us -> 5.27 us
    reshape x12 -> x0, local copies, waits for them, and re-layouts: 10.3 us -> none  [the longest x2 4.61 us: down(): v = total[:, row:row + 256].reshape(8, 2, 128, 256)]
  transfers between devices with their start and end apart: 10 -> 14, of which waited for: 5 -> 8; matrix products, arithmetic and copies ran while one was open for 3% -> 0% of each run, Pallas kernels for 5% -> 12%
where the time goes in v2:
time: 320 us; the launch traced here: 319 us
  waiting for transfers between devices  131 us (41%)
  blocking collectives  77.8 us (24%)
  Pallas kernels  55.7 us (17%)
  starting transfers between devices  33.1 us (10%)
  between operations  14.3 us (4%)
  local copies, waits for them, and re-layouts  6.2 us (2%)
    all_to_all x5, blocking collectives, exchange(): return lax.all_to_all(value, axes, 0, 0)  77.8 us
    psum x1, waiting for transfers between devices, shards(): sums_a = lax.psum(sums_a, 'context')  49.3 us
    pallas_call x10, Pallas kernels, call(): pl.pallas_call(body, grid=(1,), out_shape=[jax.ShapeDtypeStruct(s, d) for...  46.7 us
    all_gather x1, waiting for transfers between devices, shards(): full_bc = lax.all_gather(summed, 'dp')  34 us
    ppermute x4, waiting for transfers between devices, swap(): return lax.ppermute(value, 'tensor', [(0, 1), (1, 0)])  28.6 us
    all_to_all x4, starting transfers between devices, exchange(): return lax.all_to_all(value, axes, 0, 0)  19.2 us
    ppermute x4, starting transfers between devices, swap(): return lax.ppermute(value, 'tensor', [(0, 1), (1, 0)])  13.5 us
    all_to_all x4, waiting for transfers between devices, exchange(): return lax.all_to_all(value, axes, 0, 0)  10.8 us
  transfers between devices with their start and end apart: 14, of which 8 were waited for; matrix products, arithmetic and copies ran while one was open for 0% of the time, Pallas kernels for 12%

profile of v2, /device:TPU:1, one launch (start us, length us, event | category | flops | bytes accessed | tf_op | source)
XLA Modules:
  0.0 319.0 jit_solution(9361140620627196482)
XLA Ops:
  10.1 4.4 %collective-permute-start.1 = (bf16[2,4,64,256]{3,2,1,0:T(8,128)(2,1)}, bf16[2,4,64,256]{3,2,1,0:T(8,128)(2,1)S(1)}, u32[]{:S(2)}, u32[]{:S(2)}) collective-permute-start(bf16[2,4,64,256]{3,2,1,0:T(8,128)(2,1)} %chunk.1), channel_id=1, source_target_pairs={{0,1},{1,0},{2,3},{3,2},{4,5},{5,4},{6,7},{7,6},{8,9},{9,8},{10,11... | collective-permute-start | bytes 786440 | tf_op jit(solution)/shard_map/ppermute | solution.py:567
  14.5 6.2 %collective-permute-done.1 = bf16[2,4,64,256]{3,2,1,0:T(8,128)(2,1)S(1)} collective-permute-done((bf16[2,4,64,256]{3,2,1,0:T(8,128)(2,1)}, bf16[2,4,64,256]{3,2,1,0:T(8,128)(2,1)S(1)}, u32[]{:S(2)}, u32[]{:S(2)}) %collective-permute-start.1) | collective-permute-done | bytes 262176 | tf_op jit(solution)/shard_map/ppermute | solution.py:567
  21.5 4.7 %norm_qkv_feed.1 = (bf16[8,208,128]{2,1,0:T(8,128)(2,1)}, bf16[256,512]{1,0:T(8,128)(2,1)}, bf16[256,1024]{1,0:T(8,128)(2,1)}, f32[256,1024]{1,0:T(8,128)}, f32[2,2,8,128]{3,2,1,0:T(8,128)}) custom-call(s32[3]{0:T(128)} %pad_add_fusion.at, s32[2,128]{1,0:T(2,128)} %pos.1, f32[8,1]{1,0:T(8,128)} %constant.18.freqs, f32[256,512]{1,0:T(8,128)} %bitcast.24, ...), custom_call_target="tpu_custom_call" | custom-call | tf_op jit(solution)/shard_map/norm_qkv_feed/pallas_call | solution.py:49
  26.1 4.6 %all-to-all-start = ((bf16[8,208,128]{2,1,0:T(8,128)(2,1)}), bf16[8,208,128]{2,1,0:T(8,128)(2,1)S(1)}, u32[]{:S(2)}, u32[]{:S(2)}) async-start(bf16[8,208,128]{2,1,0:T(8,128)(2,1)} %get-tuple-element.47), calls=%async_computation | async-start | bytes 851968 | tf_op jit(solution)/shard_map/all_to_all | solution.py:571
  38.0 3.8 %attend.1 = (bf16[8,2,64,128]{3,2,1,0:T(8,128)(2,1)}, f32[1,1024]{1,0:T(1,128)}, f32[64,1024]{1,0:T(8,128)}, s32[1,1024]{1,0:T(1,128)}) custom-call(bf16[8,208,128]{2,1,0:T(8,128)(2,1)} %copy-done.1), custom_call_target="tpu_custom_call" | custom-call | tf_op jit(solution)/shard_map/attend/pallas_call | solution.py:49
  41.8 5.8 %all-to-all-start.1 = ((bf16[16,64,128]{2,1,0:T(8,128)(2,1)}), bf16[16,64,128]{2,1,0:T(8,128)(2,1)S(1)}, u32[]{:S(2)}, u32[]{:S(2)}) async-start(bf16[16,64,128]{2,1,0:T(8,128)(2,1)} %bitcast.38), calls=%async_computation.1 | async-start | bytes 524288 | tf_op jit(solution)/shard_map/all_to_all | solution.py:571
  47.7 7.6 %all-to-all-done.1 = bf16[16,64,128]{2,1,0:T(8,128)(2,1)S(1)} async-done(((bf16[16,64,128]{2,1,0:T(8,128)(2,1)}), bf16[16,64,128]{2,1,0:T(8,128)(2,1)S(1)}, u32[]{:S(2)}, u32[]{:S(2)}) %all-to-all-start.1) | async-done | bytes 262176 | tf_op jit(solution)/shard_map/all_to_all | solution.py:571
  56.0 7.7 %middle.1 = (f32[256,512]{1,0:T(8,128)}, bf16[8,256,128]{2,1,0:T(8,128)(2,1)}, bf16[8,512,256]{2,1,0:T(8,128)(2,1)}, bf16[512,512]{1,0:T(8,128)(2,1)}, f32[1,1024]{1,0:T(1,128)}, /*index=5*/f32[1,512]{1,0:T(1,128)}) custom-call(s32[3]{0:T(128)} %pad_add_fusion.at, f32[256,512]{1,0:T(8,128)} %bitcast.25, bf16[256,512]{1,0:T(8,128)(2,1)} %get-tuple-element.46.part, ...), custom_call_target="tpu_custom_call" | custom-call | tf_op jit(solution)/shard_map/middle/pallas_call | solution.py:49
  64.7 10.3 %all_to_all.45.recv = bf16[8,256,128]{2,1,0:T(8,128)(2,1)} all-to-all(bf16[8,256,128]{2,1,0:T(8,128)(2,1)S(1)} %copy-done.4), channel_id=1, replica_groups=mesh['dp'=8,'context'=8,'tensor'=2] {'context'}, dimensions={0} | all-to-all | bytes 1048576 | tf_op jit(solution)/shard_map/all_to_all | solution.py:571
  75.0 6.3 %attend_both.1 = bf16[8,2,256,128]{3,2,1,0:T(8,128)(2,1)} custom-call(bf16[8,256,128]{2,1,0:T(8,128)(2,1)} %all_to_all.45.recv, s32[1,1024]{1,0:T(1,128)} %get-tuple-element.53.start), custom_call_target="tpu_custom_call" | custom-call | tf_op jit(solution)/shard_map/attend_both/pallas_call | solution.py:49
  87.8 8.5 %reduce-scatter.3.cloned.1.call-done = bf16[1,512,256]{2,1,0:T(8,128)(2,1)} async-done(((bf16[8,512,256]{2,1,0:T(8,128)(2,1)}), bf16[1,512,256]{2,1,0:T(8,128)(2,1)}) %reduce-scatter.3.cloned.1.call-update) | async-done | bytes 262160 | tf_op jit(solution)/shard_map/reduce_scatter | solution.py:637
  96.5 13.4 %collective-permute-done.2.parts_other = bf16[512,512]{1,0:T(8,128)(2,1)S(1)} collective-permute-done((bf16[512,512]{1,0:T(8,128)(2,1)S(1)}, bf16[512,512]{1,0:T(8,128)(2,1)S(1)}, u32[]{:S(2)}, u32[]{:S(2)}) %collective-permute-start.2) | collective-permute-done | bytes 524320 | tf_op jit(solution)/shard_map/ppermute | solution.py:567
  111.1 8.8 %turn_point.1 = (f32[256,512]{1,0:T(8,128)}, f32[256,512]{1,0:T(8,128)}, bf16[8,64,128]{2,1,0:T(8,128)(2,1)}, bf16[8,768,256]{2,1,0:T(8,128)(2,1)}, bf16[256,512...) custom-call(s32[3]{0:T(128)} %pad_add_fusion.at, ...), custom_call_target="tpu_custom_call" | custom-call | tf_op jit(solution)/shard_map/turn_point/pallas_call | solution.py:49
  120.0 49.3 %all-reduce.2.cloned.1.call-done = bf16[1,512,256]{2,1,0:T(8,128)(2,1)} async-done(((bf16[1,512,256]{2,1,0:T(8,128)(2,1)}), bf16[1,512,256]{2,1,0:T(8,128)(2,1)}) %all-reduce.2.cloned.1.call-update) | async-done | bytes 262160 | tf_op jit(solution)/shard_map/psum | solution.py:638
  169.3 8.3 %all_to_all.46.recv_d = bf16[8,64,128]{2,1,0:T(8,128)(2,1)} all-to-all(bf16[8,64,128]{2,1,0:T(8,128)(2,1)S(1)} %copy-done.11), channel_id=1, replica_groups=mesh['dp'=8,'context'=8,'tensor'=2] {'context'}, dimensions={0} | all-to-all | bytes 262144 | tf_op jit(solution)/shard_map/all_to_all | solution.py:571
  177.6 4.3 %attend_back.1 = bf16[8,2,192,128]{3,2,1,0:T(8,128)(2,1)} custom-call(bf16[8,208,128]{2,1,0:T(8,128)(2,1)} %copy-done.1, bf16[8,64,128]{2,1,0:T(8,128)(2,1)} %all_to_all.46.recv_d, s32[1,1024]{1,0:T(1,128)} %get-tuple-element.53.start, f32[1,1024]{1,0:T(1,128)} %get-tuple-element.60.lse, f32[64,1024]{1,0:T(8,128)} %get-tuple-element.61.ctx), custom_call_target="tpu_custom_call" | custom-call | tf_op jit(solution)/shard_map/attend_back/pallas_call | solution.py:49
  181.9 5.1 %all-to-all-start.5 = ((bf16[16,192,128]{2,1,0:T(8,128)(2,1)}), bf16[16,192,128]{2,1,0:T(8,128)(2,1)S(1)}, u32[]{:S(2)}, u32[]{:S(2)}) async-start(bf16[16,192,128]{2,1,0:T(8,128)(2,1)} %bitcast.32), calls=%async_computation.5 | async-start | bytes 1572864 | tf_op jit(solution)/shard_map/all_to_all | solution.py:571
  190.1 9.0 %collective-permute-done.3.part_other = bf16[256,512]{1,0:T(8,128)(2,1)S(1)} collective-permute-done((bf16[256,512]{1,0:T(8,128)(2,1)S(1)}, bf16[256,512]{1,0:T(8,128)(2,1)S(1)}, u32[]{:S(2)}, u32[]{:S(2)}) %collective-permute-start.3) | collective-permute-done | bytes 262176 | tf_op jit(solution)/shard_map/ppermute | solution.py:567
  200.0 4.8 %last.1 = (f32[256,512]{1,0:T(8,128)}, bf16[8,272,256]{2,1,0:T(8,128)(2,1)}, f32[3,256]{1,0:T(4,128)}, f32[4,512]{1,0:T(4,128)}) custom-call(s32[3]{0:T(128)} %pad_add_fusion.at, f32[256,512]{1,0:T(8,128)} %bitcast.27, f32[256,512]{1,0:T(8,128)} %get-tuple-element.57.g, bf16[256,512]{1,0:T(8,128)(2,1)} %get-tuple-element.58.part, ...), custom_call_target="tpu_custom_call" | custom-call | tf_op jit(solution)/shard_map/last/pallas_call | solution.py:49
  204.8 34.8 %all_to_all.47.got = bf16[8,272,256]{2,1,0:T(8,128)(2,1)} all-to-all(bf16[8,272,256]{2,1,0:T(8,128)(2,1)} %get-tuple-element.70), channel_id=1, replica_groups=mesh['dp'=8,'context'=8,'tensor'=2] {'dp'}, dimensions={0} | all-to-all | bytes 2228224 | tf_op jit(solution)/shard_map/all_to_all | solution.py:571
  241.9 13.4 %all_to_all.48.got = bf16[8,144,256]{2,1,0:T(8,128)(2,1)} all-to-all(bf16[8,144,256]{2,1,0:T(8,128)(2,1)} %mix.1), channel_id=1, replica_groups=mesh['dp'=8,'context'=8,'tensor'=2] {'context'}, dimensions={0} | all-to-all | bytes 1179648 | tf_op jit(solution)/shard_map/all_to_all | solution.py:571
  258.0 11.0 %all_to_all.49 = bf16[8,144,256]{2,1,0:T(8,128)(2,1)} all-to-all(bf16[8,144,256]{2,1,0:T(8,128)(2,1)S(1)} %broadcast_in_dim.2), channel_id=1, replica_groups=mesh['dp'=8,'context'=8,'tensor'=2] {'context'}, dimensions={0} | all-to-all | bytes 1179648 | tf_op jit(solution)/shard_map/all_to_all | solution.py:571
  269.1 34.0 %all-gather.9.cloned.1.call-done = bf16[64,144,256]{2,1,0:T(8,128)(2,1)} async-done(((bf16[8,144,256]{2,1,0:T(8,128)(2,1)}), bf16[64,144,256]{2,1,0:T(8,128)(2,1)}) %all-gather.9.cloned.1.call-update) | async-done | bytes 4718608 | tf_op jit(solution)/shard_map/all_gather | solution.py:695
  303.1 9.1 %unpack.1 = (f32[2,3,512,256]{3,2,1,0:T(8,128)}, f32[2,256,512]{2,1,0:T(8,128)}, f32[2,512,1024]{2,1,0:T(8,128)}, f32[2,1024,512]{2,1,0:T(8,128)}, f32[2,1024]{1...) custom-call(bf16[8,512,256]{2,1,0:T(8,128)(2,1)} %all-gather.7.cloned.1., ...), custom_call_target="tpu_custom_call" | custom-call | tf_op jit(solution)/shard_map/unpack/pallas_call | solution.py:552
  (52 shorter events, 29.6 us)
Async XLA Ops:
  7.2 48.1 %all-gather.5.cloned.1.call-start = ((), (), s32[]{:S(2)}) async-start(), calls=%async_computation.11 | async-start | bytes 2359296 | tf_op jit(solution)/shard_map/all_gather | solution.py:592
  10.1 10.7 %collective-permute-start.1 = (bf16[2,4,64,256]{3,2,1,0:T(8,128)(2,1)}, bf16[2,4,64,256]{3,2,1,0:T(8,128)(2,1)S(1)}, u32[]{:S(2)}, u32[]{:S(2)}) collective-permute-start(bf16[2,4,64,256]{3,2,1,0:T(8,128)(2,1)} %chunk.1), channel_id=1, source_target_pairs={{0,1},{1,0},{2,3},{3,2},{4,5},{5,4},{6,7},{7,6},{8,9},{9,8},{10,11... | collective-permute-start | bytes 786440 | tf_op jit(solution)/shard_map/ppermute | solution.py:567
  20.7 0.7 copy-start.10
  26.1 11.1 %all-to-all-start = ((bf16[8,208,128]{2,1,0:T(8,128)(2,1)}), bf16[8,208,128]{2,1,0:T(8,128)(2,1)S(1)}, u32[]{:S(2)}, u32[]{:S(2)}) async-start(bf16[8,208,128]{2,1,0:T(8,128)(2,1)} %get-tuple-element.47), calls=%async_computation | async-start | bytes 851968 | tf_op jit(solution)/shard_map/all_to_all | solution.py:571
  30.7 17.0 %collective-permute-start = (bf16[256,512]{1,0:T(8,128)(2,1)}, bf16[256,512]{1,0:T(8,128)(2,1)S(1)}, u32[]{:S(2)}, u32[]{:S(2)}) collective-permute-start(bf16[256,512]{1,0:T(8,128)(2,1)} %get-tuple-element.46.part), channel_id=1, source_target_pairs={{0,1},{1,0},{2,3},{3,2},{4,5},{5,4},{6,7},{7,6},{8,9},{9,8},{10,11... | collective-permute-start | bytes 786440 | tf_op jit(solution)/shard_map/ppermute | solution.py:567
  37.2 0.8 copy-start.1
  41.8 13.5 %all-to-all-start.1 = ((bf16[16,64,128]{2,1,0:T(8,128)(2,1)}), bf16[16,64,128]{2,1,0:T(8,128)(2,1)S(1)}, u32[]{:S(2)}, u32[]{:S(2)}) async-start(bf16[16,64,128]{2,1,0:T(8,128)(2,1)} %bitcast.38), calls=%async_computation.1 | async-start | bytes 524288 | tf_op jit(solution)/shard_map/all_to_all | solution.py:571
  47.6 48.6 %reduce-scatter.3.cloned.1.call-start = ((), (), s32[]{:S(2)}) async-start(), calls=%async_computation.12 | async-start | bytes 2359296 | tf_op jit(solution)/shard_map/reduce_scatter | solution.py:637
  47.7 7.6 %copy-start.8 = (bf16[256,512]{1,0:T(8,128)(2,1)}, bf16[256,512]{1,0:T(8,128)(2,1)S(1)}, u32[]{:S(2)}) copy-start(bf16[256,512]{1,0:T(8,128)(2,1)S(1)} %collective-permute-done.part_other) | copy-start | bytes 786436
  63.7 1.0 copy-start.4
  75.0 10.0 %copy-start.5 = (bf16[512,512]{1,0:T(8,128)(2,1)S(1)}, bf16[512,512]{1,0:T(8,128)(2,1)}, u32[]{:S(2)}) copy-start(bf16[512,512]{1,0:T(8,128)(2,1)} %get-tuple-element.51.parts) | copy-start | bytes 1572868
  81.2 28.7 %all-to-all-start.3 = ((bf16[16,256,128]{2,1,0:T(8,128)(2,1)}), bf16[16,256,128]{2,1,0:T(8,128)(2,1)S(1)}, u32[]{:S(2)}, u32[]{:S(2)}) async-start(bf16[16,256,128]{2,1,0:T(8,128)(2,1)} %bitcast.29), calls=%async_computation.3 | async-start | bytes 2097152 | tf_op jit(solution)/shard_map/all_to_all | solution.py:571
  84.9 84.3 %all-reduce.2.cloned.1.call-start = ((), (), s32[]{:S(2)}) async-start(), calls=%async_computation.13 | async-start | bytes 524288 | tf_op jit(solution)/shard_map/psum | solution.py:638
  85.0 25.0 %collective-permute-start.2 = (bf16[512,512]{1,0:T(8,128)(2,1)S(1)}, bf16[512,512]{1,0:T(8,128)(2,1)S(1)}, u32[]{:S(2)}, u32[]{:S(2)}) collective-permute-start(bf16[512,512]{1,0:T(8,128)(2,1)S(1)} %copy-done.5), channel_id=1, source_target_pairs={{0,1},{1,0},{2,3},{3,2},{4,5},{5,4},{6,7},{7,6},{8,9},{9,8},{10,11... | collective-permute-start | bytes 1572872 | tf_op jit(solution)/shard_map/ppermute | solution.py:567
  96.3 143.3 %reduce-scatter.5.cloned.1.call-start = ((), (), s32[]{:S(2)}) async-start(), calls=%async_computation.15 | async-start | bytes 3538944 | tf_op jit(solution)/shard_map/reduce_scatter | solution.py:671
  110.0 0.8 copy-start.6
  110.0 1.1 copy-start
  119.9 49.4 %copy-start.11 = (bf16[8,64,128]{2,1,0:T(8,128)(2,1)S(1)}, bf16[8,64,128]{2,1,0:T(8,128)(2,1)}, u32[]{:S(2)}) copy-start(bf16[8,64,128]{2,1,0:T(8,128)(2,1)} %get-tuple-element.59) | copy-start | bytes 393220
  119.9 67.2 %copy-start.7 = (bf16[256,512]{1,0:T(8,128)(2,1)S(1)}, bf16[256,512]{1,0:T(8,128)(2,1)}, u32[]{:S(2)}) copy-start(bf16[256,512]{1,0:T(8,128)(2,1)} %get-tuple-element.58.part) | copy-start | bytes 786436
  119.9 149.2 %all-gather.7.cloned.1.call-start = ((), (), s32[]{:S(2)}) async-start(), calls=%async_computation.14 | async-start | bytes 2359296 | tf_op jit(solution)/shard_map/all_gather | solution.py:639
  181.9 17.1 %all-to-all-start.5 = ((bf16[16,192,128]{2,1,0:T(8,128)(2,1)}), bf16[16,192,128]{2,1,0:T(8,128)(2,1)S(1)}, u32[]{:S(2)}, u32[]{:S(2)}) async-start(bf16[16,192,128]{2,1,0:T(8,128)(2,1)} %bitcast.32), calls=%async_computation.5 | async-start | bytes 1572864 | tf_op jit(solution)/shard_map/all_to_all | solution.py:571
  187.0 116.0 %all-gather.9.cloned.1.call-start = ((), (), s32[]{:S(2)}) async-start(), calls=%async_computation.16 | async-start | bytes 5308416 | tf_op jit(solution)/shard_map/all_gather | solution.py:695
  187.1 11.9 %collective-permute-start.3 = (bf16[256,512]{1,0:T(8,128)(2,1)S(1)}, bf16[256,512]{1,0:T(8,128)(2,1)S(1)}, u32[]{:S(2)}, u32[]{:S(2)}) collective-permute-start(bf16[256,512]{1,0:T(8,128)(2,1)S(1)} %copy-done.7), channel_id=1, source_target_pairs={{0,1},{1,0},{2,3},{3,2},{4,5},{5,4},{6,7},{7,6},{8,9},{9,8},{10,11... | collective-permute-start | bytes 786440 | tf_op jit(solution)/shard_map/ppermute | solution.py:567
  199.0 1.0 copy-start.2
  (2 other events, 1.4 us)
Sparse Core Ops, SparseCore 0:
  21.6 27.8 all-gather.4
  63.8 32.4 reduce-scatter.2
  98.8 70.4 all-reduce.1
  172.2 37.3 reduce-scatter.4
  211.3 31.8 all-gather.6
  269.2 33.8 all-gather.8

commit v3 on v2

--- a/solution.py
+++ b/solution.py
@@ -25,6 +25,14 @@
     return lax.dot_general(a, b, (((ca,), (cb,)), ((), ())), preferred_element_type=F32)
 
 
+class After:
+    def __init__(self, array):
+        self.array = array
+
+    def spec(self):
+        return pl.BlockSpec(memory_space=pl.ANY)
+
+
 class Layer:
     def __init__(self, array, index):
         self.array, self.index = array, index
@@ -41,9 +49,9 @@
 
 def call(body, out_shape, args, name, scratch=(), smem_first=False):
     specs = [
-        a.spec() if isinstance(a, Layer) else whole(a.shape) for a in args
+        a.spec() if isinstance(a, (Layer, After)) else whole(a.shape) for a in args
     ]
-    args = [a.array if isinstance(a, Layer) else a for a in args]
+    args = [a.array if isinstance(a, (Layer, After)) else a for a in args]
     if smem_first:
         specs[0] = pl.BlockSpec(memory_space=pltpu.SMEM)
     return pl.pallas_call(
@@ -164,8 +172,11 @@
 
 
 def first_body(
-    at, pos, freqs, x, gain, bias, w_qkv, b_qkv, w_up, b_up, w_down, send, part, act, slope, cs
+    at, pos, freqs, x, gain, bias, w_qkv, b_qkv, w_up, b_up, w_down, w_out,
+    send, pair, act, slope, cs, chunk,
 ):
+    chunk_of(at, w_qkv, w_out, chunk)
+    pair[256:512] = w_out[0]
     for s in range(2):
         p = pos[s : s + 1, :].astype(F32)
         angle = freqs[...] * p
@@ -174,7 +185,7 @@
     normed, _ = norm_rows(x[...])
     attn_in = (normed * gain[0, 0:1] + bias[0, 0:1]).astype(BF)
     mlp_in = (normed * gain[0, 1:2] + bias[0, 1:2]).astype(BF)
-    send_qkv(send, attn_in, w_qkv, b_qkv, 0, cs)
+    send_qkv(send, attn_in, w_qkv.at[0], b_qkv, 0, cs)
     row = lax.broadcasted_iota(jnp.int32, (16, BLK), 0)
     token = at[0] * BLK + lax.broadcasted_iota(jnp.int32, (1, BLK), 1)
     for s in range(2):
@@ -184,7 +195,7 @@
         block = jnp.where(row == 0, high, jnp.where(row == 1, low, 0.0)).astype(BF)
         for h in range(4):
             send[s * 4 + h, 3 * HEAD : 3 * HEAD + 16, :] = block
-    part[...] = feed_forward(mlp_in, w_up, b_up, 0, w_down, act, slope).astype(BF)
+    pair[0:256] = feed_forward(mlp_in, w_up, b_up, 0, w_down, act, slope).astype(BF)
 
 
 def load_rows(recv, lo, hi):
@@ -226,7 +237,7 @@
                 send[c * (CHUNK // BLK) + i, t] = block
 
 
-def attend_both_body(recv, start, send, dk, dv):
+def attend_both_body(recv, start, _, send, dk, dv):
     q = load_rows(recv, 0, HEAD)
     k_t = load_rows(recv, HEAD, 2 * HEAD)
     v_t = load_rows(recv, 2 * HEAD, 3 * HEAD)
@@ -271,7 +282,14 @@
             send[b, t, row + HEAD : row + 2 * HEAD] = dv[:, b * BLK : (b + 1) * BLK].astype(BF)
 
 
-def attend_back_body(recv, recv_d, start, lse, ctx, send, dk, dv):
+def attend_back_body(recv, recv_d, start, lse, ctx, _, send, dk, dv):
+    ride = recv_d[0, 64:192].astype(F32)
+    for i in range(1, 8):
+        ride = ride + recv_d[i, 64:192].astype(F32)
+    ride = ride.astype(BF)
+    for b in range(8):
+        for t in range(2):
+            send[b, t, 192:320] = ride
     q = load_rows(recv, 0, HEAD)
     k_t = load_rows(recv, HEAD, 2 * HEAD)
     v_t = load_rows(recv, 2 * HEAD, 3 * HEAD)
@@ -310,8 +328,8 @@
     return jnp.concatenate(halves, 1)
 
 
-def branch_of(t, recv, w_own, others):
-    first, second = ordered(t, w_own[...], out_other(others))
+def branch_of(t, recv, w_own, w_other):
+    first, second = ordered(t, w_own, w_other)
     w = jnp.concatenate([first, second], 0)
     rows = []
     for s in range(2):
@@ -320,12 +338,12 @@
 
 
 def middle_body(
-    at, x, part, part_other, recv, w_out_own, others, out_bias, gain, bias,
+    at, x, pair, pair_other, recv, w_out_own, out_bias, gain, bias,
     w_qkv, b_qkv, w_up, b_up, w_down, w_out, cot, cs,
     stream, send, grads, parts, d_b_up, d_sum, act, slope,
 ):
-    branch = part[...].astype(F32) + part_other[...].astype(F32)
-    branch = branch + branch_of(at[1], recv, w_out_own, others)
+    branch = pair[0:256].astype(F32) + pair_other[0:256].astype(F32)
+    branch = branch + branch_of(at[1], recv, w_out_own[...], pair_other[256:512])
     out = x[...] + branch + out_bias[0, 0:1] + out_bias[0, 1:2]
     stream[...] = out
     normed, _ = norm_rows(out)
@@ -388,12 +406,12 @@
 
 def turn_point_body(
     at, stream, parts, parts_other, recv, w_out, w_qkv, others, out_bias,
-    gain, bias, cot, cs, x, act, slope, w_up, w_down, w_out_first,
+    gain, bias, cot, cs, x, act, slope, w_up, w_down, w_out_first, recv_first, sums_a,
     block_out, g_out, send, grads, part, d_b_up, d_b_qkv, d_norm, d_sum,
 ):
     t = at[1]
     branch = parts[0:256].astype(F32) + parts_other[0:256].astype(F32)
-    branch = branch + branch_of(t, recv, w_out, others)
+    branch = branch + branch_of(t, recv, w_out[...], out_other(others))
     block_out[...] = stream[...] + branch + out_bias[1, 0:1] + out_bias[1, 1:2]
     d_mlp_in = parts[256:512].astype(F32) + parts_other[256:512].astype(F32)
     g = norm_back(
@@ -406,8 +424,16 @@
     d_ctx = mm(w_out_first[...], g_b, 1, 1)
     for s in range(2):
         for h in range(4):
-            send[s * 4 + h] = d_ctx[h * HEAD : (h + 1) * HEAD, s * BLK : (s + 1) * BLK].astype(BF)
+            send[s * 4 + h, 0:HEAD] = d_ctx[
+                h * HEAD : (h + 1) * HEAD, s * BLK : (s + 1) * BLK
+            ].astype(BF)
+    for q in range(8):
+        for c in range(2):
+            send[q, 64 + 64 * c : 128 + 64 * c] = sums_a[
+                64 * q : 64 * (q + 1), BLK * c : BLK * (c + 1)
+            ]
     pack_out(grads, 704, own_ctx(t, recv), cot[...].astype(BF))
+    pack_out(grads, 768, own_ctx(t, recv_first), g_b)
     normed, _ = norm_rows(x[...])
     mlp_in = (normed * gain[0, 1:2] + bias[0, 1:2]).astype(BF)
     part[...] = feed_back(
@@ -416,16 +442,20 @@
 
 
 def last_body(
-    at, x, g, part, part_other, recv, recv_ctx, w_qkv, others, cs, gain, bias,
+    at, x, g, part, part_other, recv, w_qkv, others, cs, gain, bias,
     d_b_up0, d_b_up1, d_b_qkv1, d_norm1, d_sum0, d_sum1,
-    in_grad, grads, d_b_qkv0, d_norm0,
+    in_grad, grads, sums_a, d_b_qkv0, d_norm0,
 ):
     d_mlp_in = part[...].astype(F32) + part_other[...].astype(F32)
     in_grad[...] = norm_back(
         at[1], x[...], g[...], d_mlp_in, recv, 0, w_qkv, others, cs, gain, bias, 0,
         pack_qkv(grads, 0), d_b_qkv0, d_norm0,
     )
-    pack_out(grads, 192, own_ctx(at[1], recv_ctx), g[...].astype(BF))
+    for q in range(8):
+        both_planes = recv[q, :, 192:320]
+        block = jnp.where(at[1] == 0, both_planes[0], both_planes[1])
+        for c in range(2):
+            sums_a[64 * q : 64 * (q + 1), BLK * c : BLK * (c + 1)] = block[64 * c : 64 * (c + 1)]
 
     def lanes(ref, row, count):
         return [ref[row : row + 1, 256 * c : 256 * (c + 1)] for c in range(count)]
@@ -443,10 +473,10 @@
     for p in range(8):
         have = rows[p] if p < len(rows) else []
         fill = [jnp.zeros((16 - len(have), 256), F32)]
-        grads[p, 256:272, :] = jnp.concatenate(have + fill, 0).astype(BF)
-
-
-def chunk_body(at, w_qkv, w_out, out):
+        grads[p, 192:208, :] = jnp.concatenate(have + fill, 0).astype(BF)
+
+
+def chunk_of(at, w_qkv, w_out, out):
     for layer in range(2):
         for e in range(3):
             out[layer, e] = w_qkv[layer, e, pl.ds(pl.multiple_of(at[2] * 64, 64), 64), :]
@@ -460,12 +490,9 @@
     for i in range(1, 8):
         total = total + got[i].astype(F32)
     for q in range(8):
-        out[q, 0:96] = early[96 * q : 96 * (q + 1)]
-        out[q, 96:128] = total[32 * q : 32 * (q + 1)].astype(BF)
-        if q == 0:
-            out[q, 128:144] = total[256:272].astype(BF)
-        else:
-            out[q, 128:144] = jnp.zeros((16, 256), BF)
+        mine = [early[104 * q : 104 * (q + 1)].astype(F32), total[24 * q : 24 * (q + 1)]]
+        out[q, 0:128] = jnp.concatenate(mine, 0).astype(BF)
+        out[q, 128:144] = total[192:208].astype(BF) if q == 0 else jnp.zeros((16, 256), BF)
 
 
 def sum_body(got, out):
@@ -475,32 +502,36 @@
     out[...] = total.astype(BF)
 
 
-def unpack_body(first, rest, g_qkv, g_out, g_up, g_down, g_b_up, g_b_qkv, g_sum, g_gain, g_bias):
+def unpack_first_body(first, g_up, g_down):
+    for c in range(4):
+        g_up[0, :, 256 * c : 256 * (c + 1)] = first[64 * c : 64 * (c + 1)].astype(F32)
+    for c in range(2):
+        rows = first[256 + 128 * c : 256 + 128 * (c + 1)]
+        g_down[0, :, 256 * c : 256 * (c + 1)] = rows.astype(F32)
+
+
+def unpack_rest_body(rest, _, __, g_up, g_down, g_qkv, g_out, g_b_up, g_b_qkv, g_sum, g_gain, g_bias):
     p = pl.program_id(0)
 
     def early(row):
-        return rest[row // 96, row % 96 : row % 96 + 32].astype(F32)
+        return rest[row // 104, row % 104 : row % 104 + 8].astype(F32)
 
     def late(row):
-        return rest[row // 32, 96:128].astype(F32)
-
-    for e in range(3):
-        for k in range(2):
-            g_qkv[0, e, 32 * k : 32 * (k + 1)] = late(64 * e + 32 * k)
-            g_qkv[1, e, 32 * k : 32 * (k + 1)] = early(64 * e + 32 * k)
-    for c in range(2):
-        g_out[0, :, 256 * c : 256 * (c + 1)] = late(192 + 32 * c)
-        g_out[1, :, 256 * c : 256 * (c + 1)] = early(704 + 32 * c)
-    for c in range(4):
-        cols = slice(256 * c, 256 * (c + 1))
-        for k in range(2):
-            g_up[0, 32 * k : 32 * (k + 1), cols] = early(192 + 64 * c + 32 * k)
-        g_up[1, :, cols] = first[64 * c : 64 * (c + 1)].astype(F32)
-    for c in range(2):
-        cols = slice(256 * c, 256 * (c + 1))
-        for k in range(4):
-            g_down[0, 32 * k : 32 * (k + 1), cols] = early(448 + 128 * c + 32 * k)
-        g_down[1, :, cols] = first[256 + 128 * c : 256 + 128 * (c + 1)].astype(F32)
+        return rest[row // 24, 104 + row % 24 : 104 + row % 24 + 8].astype(F32)
+
+    for k in range(0, 64, 8):
+        for e in range(3):
+            g_qkv[0, e, k : k + 8] = late(64 * e + k)
+            g_qkv[1, e, k : k + 8] = early(64 * e + k)
+        for c in range(4):
+            g_up[0, k : k + 8, 256 * c : 256 * (c + 1)] = early(192 + 64 * c + k)
+    for k in range(0, 32, 8):
+        for c in range(2):
+            g_out[0, k : k + 8, 256 * c : 256 * (c + 1)] = early(768 + 32 * c + k)
+            g_out[1, k : k + 8, 256 * c : 256 * (c + 1)] = early(704 + 32 * c + k)
+    for k in range(0, 128, 8):
+        for c in range(2):
+            g_down[0, k : k + 8, 256 * c : 256 * (c + 1)] = early(448 + 128 * c + k)
 
     tiny = rest[0, 128:144].astype(F32)
 
@@ -537,12 +568,30 @@
         norms(1, 0)
 
 
+UP = (2, 512, 1024)
+DOWN = (2, 1024, 512)
+
+
 def unpack(first, rest):
+    def place(layer):
+        return [
+            pl.BlockSpec((1, 64, 1024), lambda p: (layer, p, 0)),
+            pl.BlockSpec((1, 128, 512), lambda p: (layer, p, 0)),
+        ]
+
+    params = pltpu.CompilerParams(vmem_limit_bytes=56 * 1024 * 1024)
+    g_up, g_down = pl.pallas_call(
+        unpack_first_body,
+        grid=(8,),
+        out_shape=[jax.ShapeDtypeStruct(UP, F32), jax.ShapeDtypeStruct(DOWN, F32)],
+        in_specs=[pl.BlockSpec((None, 512, 256), lambda p: (p, 0, 0))],
+        out_specs=place(1),
+        compiler_params=params,
+        name="unpack_first",
+    )(first)
     outs = [
         ((2, 3, 512, 256), pl.BlockSpec((2, 3, 64, 256), lambda p: (0, 0, p, 0))),
         ((2, 256, 512), pl.BlockSpec((2, 32, 512), lambda p: (0, p, 0))),
-        ((2, 512, 1024), pl.BlockSpec((2, 64, 1024), lambda p: (0, p, 0))),
-        ((2, 1024, 512), pl.BlockSpec((2, 128, 512), lambda p: (0, p, 0))),
         ((2, 1024), whole((2, 1024))),
         ((3, 2, 256), whole((3, 2, 256))),
         ((2, 2, 512), whole((2, 2, 512))),
@@ -550,17 +599,19 @@
         ((2, 2, 512), whole((2, 2, 512))),
     ]
     return pl.pallas_call(
-        unpack_body,
+        unpack_rest_body,
         grid=(8,),
-        out_shape=[jax.ShapeDtypeStruct(shape, F32) for shape, _ in outs],
+        out_shape=[jax.ShapeDtypeStruct(shape, F32) for shape in [UP, DOWN] + [o[0] for o in outs]],
         in_specs=[
-            pl.BlockSpec((None, 512, 256), lambda p: (p, 0, 0)),
             pl.BlockSpec((None, 8, 144, 256), lambda p: (p, 0, 0, 0)),
+            pl.BlockSpec(memory_space=pl.ANY),
+            pl.BlockSpec(memory_space=pl.ANY),
         ],
-        out_specs=[spec for _, spec in outs],
-        compiler_params=pltpu.CompilerParams(vmem_limit_bytes=56 * 1024 * 1024),
-        name="unpack",
-    )(first, rest)
+        out_specs=place(0) + [spec for _, spec in outs],
+        input_output_aliases={1: 0, 2: 1},
+        compiler_params=params,
+        name="unpack_rest",
+    )(rest, g_up, g_down)
 
 
 def swap(value):
@@ -588,26 +639,25 @@
         [lax.axis_index("context"), lax.axis_index("tensor"), lax.axis_index("dp")]
     ).astype(jnp.int32)
     freqs = jnp.asarray(FREQS).reshape(HALF, 1)
-    (chunk,) = call(chunk_body, [((2, 4, 64, 256), BF)], (at, wq, w_out), "chunk", smem_first=True)
-    others = lax.all_gather(swap(chunk), "dp", axis=2, tiled=True)
-
-    send, part, act, slope, cs = call(
+    send, pair, act, slope, cs, chunk = call(
         first_body,
         [
             ((8, 208, BLK), BF),
-            ((rows, width), BF),
+            ((2 * rows, width), BF),
             ((rows, 1024), BF),
             ((rows, 1024), F32),
             ((2, 2, HALF, BLK), F32),
+            ((2, 4, 64, 256), BF),
         ],
         (
-            at, positions, freqs, x, ln_gain, ln_bias, Layer(wq, 0), bq, Layer(w_up, 0), b_up,
-            Layer(w_down, 0),
+            at, positions, freqs, x, ln_gain, ln_bias, wq, bq, Layer(w_up, 0), b_up,
+            Layer(w_down, 0), w_out,
         ),
         "norm_qkv_feed",
         smem_first=True,
     )
-    part_other = swap(part)
+    pair_other = swap(pair)
+    others = lax.all_gather(swap(chunk), "dp", axis=2, tiled=True)
     recv = exchange(send, "context")
     ctx_send, lse, ctx, start = call(
         attend_body,
@@ -627,22 +677,20 @@
             ((1, width), F32),
         ],
         (
-            at, x, part, part_other, recv_ctx, Layer(w_out, 0), Layer(others, 0), out_bias, ln_gain,
-            ln_bias, Layer(wq, 1), bq, Layer(w_up, 1), b_up, Layer(w_down, 1), Layer(w_out, 1), cot, cs,
+            at, x, pair, pair_other, recv_ctx, Layer(w_out, 0), out_bias, ln_gain, ln_bias,
+            Layer(wq, 1), bq, Layer(w_up, 1), b_up, Layer(w_down, 1), Layer(w_out, 1), cot, cs,
         ),
         "middle",
         scratch=[pltpu.VMEM((rows, 1024), BF), pltpu.VMEM((rows, 1024), F32)],
         smem_first=True,
     )
     sums_a = lax.psum_scatter(grads_a, "dp", scatter_dimension=0)
-    sums_a = lax.psum(sums_a, "context")
-    full_a = lax.all_gather(sums_a, "dp")
     parts_other = swap(parts)
     recv_both = exchange(send, "context")
     (both_send,) = call(
         attend_both_body,
         [((8, 2, 256, BLK), BF)],
-        (recv_both, start),
+        (recv_both, start, After(parts_other)),
         "attend_both",
         scratch=[pltpu.VMEM((HEAD, 1024), F32), pltpu.VMEM((HEAD, 1024), F32)],
     )
@@ -652,8 +700,8 @@
         [
             ((rows, width), F32),
             ((rows, width), F32),
-            ((8, HEAD, BLK), BF),
-            ((8, 768, 256), BF),
+            ((8, 192, BLK), BF),
+            ((8, 832, 256), BF),
             ((rows, width), BF),
             ((1, 1024), F32),
             ((3, 256), F32),
@@ -663,7 +711,7 @@
         (
             at, stream, parts, parts_other, recv_grad, Layer(w_out, 1), Layer(wq, 1), Layer(others, 1),
             out_bias, ln_gain, ln_bias, cot, cs, x, act, slope, Layer(w_up, 0), Layer(w_down, 0),
-            Layer(w_out, 0),
+            Layer(w_out, 0), recv_ctx, sums_a,
         ),
         "turn_point",
         smem_first=True,
@@ -673,27 +721,34 @@
     recv_d = exchange(send, "context")
     (back_send,) = call(
         attend_back_body,
-        [((8, 2, 192, BLK), BF)],
-        (recv, recv_d, start, lse, ctx),
+        [((8, 2, 320, BLK), BF)],
+        (recv, recv_d, start, lse, ctx, After(part_g_other)),
         "attend_back",
         scratch=[pltpu.VMEM((HEAD, 1024), F32), pltpu.VMEM((HEAD, 1024), F32)],
     )
     recv_grad0 = both(back_send)
-    in_grad, grads_c, _, _ = call(
+    in_grad, grads_c, sums_a, _, _ = call(
         last_body,
-        [((rows, width), F32), ((8, 272, 256), BF), ((3, 256), F32), ((4, width), F32)],
+        [
+            ((rows, width), F32),
+            ((8, 208, 256), BF),
+            ((512, 256), BF),
+            ((3, 256), F32),
+            ((4, width), F32),
+        ],
         (
-            at, x, g, part_g, part_g_other, recv_grad0, recv_ctx, Layer(wq, 0), Layer(others, 0), cs,
+            at, x, g, part_g, part_g_other, recv_grad0, Layer(wq, 0), Layer(others, 0), cs,
             ln_gain, ln_bias, d_b_up0, d_b_up1, d_b_qkv1, d_norm1, d_sum0, d_sum1,
         ),
         "last",
         smem_first=True,
     )
+    full_a = lax.all_gather(sums_a, "dp")
     (mixed,) = call(mix_body, [((8, 144, 256), BF)], (exchange(grads_c, "dp"), sums_b), "mix")
     (summed,) = call(sum_body, [((144, 256), BF)], (exchange(mixed, "context"),), "sum")
     summed = exchange(jnp.broadcast_to(summed[None], (8, 144, 256)), "context")
     full_bc = lax.all_gather(summed, "dp")
-    g_qkv, g_out, g_up, g_down, g_b_up, g_b_qkv, g_sum, g_gain, g_bias = unpack(full_a, full_bc)
+    g_up, g_down, g_qkv, g_out, g_b_up, g_b_qkv, g_sum, g_gain, g_bias = unpack(full_a, full_bc)
     return (
         block_out.reshape(tokens_in.shape),
         in_grad.reshape(tokens_in.shape),

time: 320 us -> 263 us (0.82)
  waiting for transfers between devices: 131 us -> 51.3 us
  blocking collectives: 77.8 us -> 108 us
  starting transfers between devices: 33.1 us -> 23.4 us
    psum x1 -> x0, waiting for transfers between devices: 49.3 us -> none  [shards(): sums_a = lax.psum(sums_a, 'context')]
    all_to_all x5 -> x6, blocking collectives: 77.8 us -> 108 us  [exchange(): return lax.all_to_all(value, axes, 0, 0)]
    ppermute x4, waiting for transfers between devices: 28.6 us -> 15.3 us  [swap(): return lax.ppermute(value, 'tensor', [(0, 1), (1, 0)])]
    reduce_scatter x1, waiting for transfers between devices: 8.5 us -> 0.01 us  [shards(): sums_a = lax.psum_scatter(grads_a, 'dp', scatter_dimension=0)]
    all_gather x1, waiting for transfers between devices: 34 us -> 27.3 us  [shards(): full_bc = lax.all_gather(summed, 'dp')]
    all_to_all x4 -> x3, starting transfers between devices: 19.2 us -> 14 us  [exchange(): return lax.all_to_all(value, axes, 0, 0)]
    pallas_call x1 -> x2, Pallas kernels: 9.08 us -> 13.5 us  [the longest x1 7.57 us: unpack(): pl.pallas_call(unpack_rest_body, grid=(8,), out_shape=[jax.ShapeDtypeStru...]
    ppermute x4, starting transfers between devices: 13.5 us -> 9.19 us  [swap(): return lax.ppermute(value, 'tensor', [(0, 1), (1, 0)])]
  transfers between devices with their start and end apart: 14 -> 12, of which waited for: 8 -> 7; matrix products, arithmetic and copies ran while one was open for 0% -> 0% of each run, Pallas kernels for 12% -> 14%
where the time goes in v3:
time: 263 us; the launch traced here: 262 us
  blocking collectives  108 us (41%)
  Pallas kernels  58.8 us (22%)
  waiting for transfers between devices  51.3 us (20%)
  starting transfers between devices  23.4 us (9%)
  between operations  13.9 us (5%)
  local copies, waits for them, and re-layouts  5.71 us (2%)
    all_to_all x6, blocking collectives, exchange(): return lax.all_to_all(value, axes, 0, 0)  108 us
    pallas_call x9, Pallas kernels, call(): pl.pallas_call(body, grid=(1,), out_shape=[jax.ShapeDtypeStruct(s, d) for...  45.2 us
    all_gather x1, waiting for transfers between devices, shards(): full_bc = lax.all_gather(summed, 'dp')  27.3 us
    ppermute x4, waiting for transfers between devices, swap(): return lax.ppermute(value, 'tensor', [(0, 1), (1, 0)])  15.3 us
    all_to_all x3, starting transfers between devices, exchange(): return lax.all_to_all(value, axes, 0, 0)  14 us
    ppermute x4, starting transfers between devices, swap(): return lax.ppermute(value, 'tensor', [(0, 1), (1, 0)])  9.19 us
    all_to_all x3, waiting for transfers between devices, exchange(): return lax.all_to_all(value, axes, 0, 0)  8.7 us
    pallas_call x1, Pallas kernels, unpack(): pl.pallas_call(unpack_rest_body, grid=(8,), out_shape=[jax.ShapeDtypeStru...  7.57 us
  transfers between devices with their start and end apart: 12, of which 7 were waited for; matrix products, arithmetic and copies ran while one was open for 0% of the time, Pallas kernels for 14%

profile of v3, /device:TPU:1, one launch (start us, length us, event | category | flops | bytes accessed | tf_op | source)
XLA Modules:
  0.0 261.9 jit_solution(8883101660974854120)
XLA Ops:
  7.8 5.2 %norm_qkv_feed.1 = (bf16[8,208,128]{2,1,0:T(8,128)(2,1)}, bf16[512,512]{1,0:T(8,128)(2,1)}, bf16[256,1024]{1,0:T(8,128)(2,1)}, f32[256,1024]{1,0:T(8,128)}, f32[...) custom-call(s32[3]{0:T(128)} %pad_add_fusion.at, s32[2,128]{1,0:T(2,128)} %pos.1, f32[8,1]{1,0:T(8,128)} %constant.18.freqs, ...), custom_call_target="tpu_custom_call" | custom-call | tf_op jit(solution)/shard_map/norm_qkv_feed/pallas_call | solution.py:57
  13.0 4.4 %collective-permute-start.2 = (bf16[2,4,64,256]{3,2,1,0:T(8,128)(2,1)}, bf16[2,4,64,256]{3,2,1,0:T(8,128)(2,1)S(1)}, u32[]{:S(2)}, u32[]{:S(2)}) collective-permute-start(bf16[2,4,64,256]{3,2,1,0:T(8,128)(2,1)} %get-tuple-element.58), channel_id=1, source_target_pairs={{0,1},{1,0},{2,3},{3,2},{4,5},{5,4},{6,7},{7,6},{8,9},{9,8},{10,11... | collective-permute-start | bytes 786440 | tf_op jit(solution)/shard_map/ppermute | solution.py:618
  17.5 6.3 %collective-permute-done.2 = bf16[2,4,64,256]{3,2,1,0:T(8,128)(2,1)S(1)} collective-permute-done((bf16[2,4,64,256]{3,2,1,0:T(8,128)(2,1)}, bf16[2,4,64,256]{3,2,1,0:T(8,128)(2,1)S(1)}, u32[]{:S(2)}, u32[]{:S(2)}) %collective-permute-start.2) | collective-permute-done | bytes 262176 | tf_op jit(solution)/shard_map/ppermute | solution.py:618
  24.4 4.6 %all-to-all-start = ((bf16[8,208,128]{2,1,0:T(8,128)(2,1)}), bf16[8,208,128]{2,1,0:T(8,128)(2,1)S(1)}, u32[]{:S(2)}, u32[]{:S(2)}) async-start(bf16[8,208,128]{2,1,0:T(8,128)(2,1)} %get-tuple-element.51), calls=%async_computation | async-start | bytes 851968 | tf_op jit(solution)/shard_map/all_to_all | solution.py:622
  29.0 3.3 %collective-permute-start = (bf16[512,512]{1,0:T(8,128)(2,1)}, bf16[512,512]{1,0:T(8,128)(2,1)S(1)}, u32[]{:S(2)}, u32[]{:S(2)}) collective-permute-start(bf16[512,512]{1,0:T(8,128)(2,1)} %get-tuple-element.50.pair), channel_id=1, source_target_pairs={{0,1},{1,0},{2,3},{3,2},{4,5},{5,4},{6,7},{7,6},{8,9},{9,8},{10,11... | collective-permute-start | bytes 1572872 | tf_op jit(solution)/shard_map/ppermute | solution.py:618
  36.3 3.8 %attend.1 = (bf16[8,2,64,128]{3,2,1,0:T(8,128)(2,1)}, f32[1,1024]{1,0:T(1,128)}, f32[64,1024]{1,0:T(8,128)}, s32[1,1024]{1,0:T(1,128)}) custom-call(bf16[8,208,128]{2,1,0:T(8,128)(2,1)} %copy-done), custom_call_target="tpu_custom_call" | custom-call | tf_op jit(solution)/shard_map/attend/pallas_call | solution.py:57
  40.1 5.9 %all-to-all-start.1 = ((bf16[16,64,128]{2,1,0:T(8,128)(2,1)}), bf16[16,64,128]{2,1,0:T(8,128)(2,1)S(1)}, u32[]{:S(2)}, u32[]{:S(2)}) async-start(bf16[16,64,128]{2,1,0:T(8,128)(2,1)} %bitcast.41), calls=%async_computation.1 | async-start | bytes 524288 | tf_op jit(solution)/shard_map/all_to_all | solution.py:622
  48.1 5.5 %all-to-all-done.1 = bf16[16,64,128]{2,1,0:T(8,128)(2,1)S(1)} async-done(((bf16[16,64,128]{2,1,0:T(8,128)(2,1)}), bf16[16,64,128]{2,1,0:T(8,128)(2,1)S(1)}, u32[]{:S(2)}, u32[]{:S(2)}) %all-to-all-start.1) | async-done | bytes 262176 | tf_op jit(solution)/shard_map/all_to_all | solution.py:622
  54.3 7.6 %middle.1 = (f32[256,512]{1,0:T(8,128)}, bf16[8,256,128]{2,1,0:T(8,128)(2,1)}, bf16[8,512,256]{2,1,0:T(8,128)(2,1)}, bf16[512,512]{1,0:T(8,128)(2,1)}, f32[1,1024]{1,0:T(1,128)}, /*index=5*/f32[1,512]{1,0:T(1,128)}) custom-call(s32[3]{0:T(128)} %pad_add_fusion.at, f32[256,512]{1,0:T(8,128)} %bitcast.26, bf16[512,512]{1,0:T(8,128)(2,1)} %get-tuple-element.50.pair, ...), custom_call_target="tpu_custom_call" | custom-call | tf_op jit(solution)/shard_map/middle/pallas_call | solution.py:57
  63.4 11.7 %all_to_all.45.recv = bf16[8,256,128]{2,1,0:T(8,128)(2,1)} all-to-all(bf16[8,256,128]{2,1,0:T(8,128)(2,1)S(1)} %copy-done.7), channel_id=1, replica_groups=mesh['dp'=8,'context'=8,'tensor'=2] {'context'}, dimensions={0} | all-to-all | bytes 1048576 | tf_op jit(solution)/shard_map/all_to_all | solution.py:622
  76.0 6.2 %attend_both.1 = bf16[8,2,256,128]{3,2,1,0:T(8,128)(2,1)} custom-call(bf16[8,256,128]{2,1,0:T(8,128)(2,1)} %all_to_all.45.recv, s32[1,1024]{1,0:T(1,128)} %get-tuple-element.57.start, bf16[512,512]{1,0:T(8,128)(2,1)} %copy-done.2), custom_call_target="tpu_custom_call" | custom-call | tf_op jit(solution)/shard_map/attend_both/pallas_call | solution.py:57
  82.2 16.5 %all_to_all.46 = bf16[16,256,128]{2,1,0:T(8,128)(2,1)} all-to-all(bf16[16,256,128]{2,1,0:T(8,128)(2,1)} %bitcast.32), channel_id=1, replica_groups=mesh['dp'=8,'context'=8,'tensor'=2] {'context','tensor'}, dimensions={0} | all-to-all | bytes 2097152 | tf_op jit(solution)/shard_map/all_to_all | solution.py:622
  98.7 9.2 %turn_point.1 = (f32[256,512]{1,0:T(8,128)}, f32[256,512]{1,0:T(8,128)}, bf16[8,192,128]{2,1,0:T(8,128)(2,1)}, bf16[8,832,256]{2,1,0:T(8,128)(2,1)}, bf16[256,51...) custom-call(s32[3]{0:T(128)} %pad_add_fusion.at, ...), custom_call_target="tpu_custom_call" | custom-call | tf_op jit(solution)/shard_map/turn_point/pallas_call | solution.py:57
  107.9 3.6 %all-to-all-start.4 = ((bf16[8,192,128]{2,1,0:T(8,128)(2,1)}), bf16[8,192,128]{2,1,0:T(8,128)(2,1)S(1)}, u32[]{:S(2)}, u32[]{:S(2)}) async-start(bf16[8,192,128]{2,1,0:T(8,128)(2,1)} %get-tuple-element.65), calls=%async_computation.5 | async-start | bytes 786432 | tf_op jit(solution)/shard_map/all_to_all | solution.py:622
  112.6 6.8 %collective-permute-done.3._.part_other = bf16[256,512]{1,0:T(8,128)(2,1)S(1)} collective-permute-done((bf16[256,512]{1,0:T(8,128)(2,1)S(1)}, bf16[256,512]{1,0:T(8,128)(2,1)S(1)}, u32[]{:S(2)}, u32[]{:S(2)}) %collective-permute-start.3) | collective-permute-done | bytes 262176 | tf_op jit(solution)/shard_map/ppermute | solution.py:618
  120.3 4.5 %attend_back.1 = bf16[8,2,320,128]{3,2,1,0:T(8,128)(2,1)} custom-call(bf16[8,208,128]{2,1,0:T(8,128)(2,1)} %copy-done, bf16[8,192,128]{2,1,0:T(8,128)(2,1)} %copy-done.3, s32[1,1024]{1,0:T(1,128)} %get-tuple-element.57.start, f32[1,1024]{1,0:T(1,128)} %get-tuple-element.66.lse, f32[64,1024]{1,0:T(8,128)} %get-tuple-element.67.ctx, bf16[256,512]{1,0:T(8,128)(2,1)} %copy-done.4), custom_call_target="tpu_custom_call" | custom-call | tf_op jit(solution)/shard_map/attend_back/pallas_call | solution.py:57
  124.8 19.1 %all_to_all.47 = bf16[16,320,128]{2,1,0:T(8,128)(2,1)} all-to-all(bf16[16,320,128]{2,1,0:T(8,128)(2,1)} %bitcast.29), channel_id=1, replica_groups=mesh['dp'=8,'context'=8,'tensor'=2] {'context','tensor'}, dimensions={0} | all-to-all | bytes 2621440 | tf_op jit(solution)/shard_map/all_to_all | solution.py:622
  143.9 4.7 %last.1 = (f32[256,512]{1,0:T(8,128)}, bf16[8,208,256]{2,1,0:T(8,128)(2,1)}, bf16[512,256]{1,0:T(8,128)(2,1)}, f32[3,256]{1,0:T(4,128)}, f32[4,512]{1,0:T(4,128)}) custom-call(s32[3]{0:T(128)} %pad_add_fusion.at, f32[256,512]{1,0:T(8,128)} %bitcast.28, f32[256,512]{1,0:T(8,128)} %get-tuple-element.63.g, bf16[256,512]{1,0:T(8,128)(2,1)} %get-tuple-element.64.part, ...), custom_call_target="tpu_custom_call" | custom-call | tf_op jit(solution)/shard_map/last/pallas_call | solution.py:57
  148.7 35.9 %all_to_all.48.got = bf16[8,208,256]{2,1,0:T(8,128)(2,1)} all-to-all(bf16[8,208,256]{2,1,0:T(8,128)(2,1)} %get-tuple-element.75), channel_id=1, replica_groups=mesh['dp'=8,'context'=8,'tensor'=2] {'dp'}, dimensions={0} | all-to-all | bytes 1703936 | tf_op jit(solution)/shard_map/all_to_all | solution.py:622
  186.8 13.6 %all_to_all.49.got = bf16[8,144,256]{2,1,0:T(8,128)(2,1)} all-to-all(bf16[8,144,256]{2,1,0:T(8,128)(2,1)} %mix.1), channel_id=1, replica_groups=mesh['dp'=8,'context'=8,'tensor'=2] {'context'}, dimensions={0} | all-to-all | bytes 1179648 | tf_op jit(solution)/shard_map/all_to_all | solution.py:622
  203.1 11.3 %all_to_all.50 = bf16[8,144,256]{2,1,0:T(8,128)(2,1)} all-to-all(bf16[8,144,256]{2,1,0:T(8,128)(2,1)S(1)} %broadcast_in_dim.2), channel_id=1, replica_groups=mesh['dp'=8,'context'=8,'tensor'=2] {'context'}, dimensions={0} | all-to-all | bytes 1179648 | tf_op jit(solution)/shard_map/all_to_all | solution.py:622
  214.5 6.0 %unpack_first.1 = (f32[2,512,1024]{2,1,0:T(8,128)}, f32[2,1024,512]{2,1,0:T(8,128)}) custom-call(bf16[8,512,256]{2,1,0:T(8,128)(2,1)} %bitcast.38), custom_call_target="tpu_custom_call" | custom-call | tf_op jit(solution)/shard_map/unpack_first/pallas_call | solution.py:583
  220.5 27.3 %all-gather.8.cloned.1.call-done = bf16[64,144,256]{2,1,0:T(8,128)(2,1)} async-done(((bf16[8,144,256]{2,1,0:T(8,128)(2,1)}), bf16[64,144,256]{2,1,0:T(8,128)(2,1)}) %all-gather.8.cloned.1.call-update) | async-done | bytes 4718608 | tf_op jit(solution)/shard_map/all_gather | solution.py:750
  247.8 7.6 %unpack_rest.1 = (f32[2,512,1024]{2,1,0:T(8,128)}, f32[2,1024,512]{2,1,0:T(8,128)}, f32[2,3,512,256]{3,2,1,0:T(8,128)}, f32[2,256,512]{2,1,0:T(8,128)}, f32[2,10...) custom-call(bf16[8,8,144,256]{3,2,1,0:T(8,128)(2,1)} %bitcast.31, ...), custom_call_target="tpu_custom_call", output_to_operand_aliasing={{0}: (1, {}), {1}: (2, {})} | custom-call | tf_op jit(solution)/shard_map/unpack_rest/pallas_call | solution.py:601
  (44 shorter events, 17.4 us)
Async XLA Ops:
  7.2 91.5 %all-gather.6.cloned.1.call-start = ((), (), s32[]{:S(2)}) async-start(), calls=%async_computation.11 | async-start | bytes 2359296 | tf_op jit(solution)/shard_map/all_gather | solution.py:660
  13.0 10.7 %collective-permute-start.2 = (bf16[2,4,64,256]{3,2,1,0:T(8,128)(2,1)}, bf16[2,4,64,256]{3,2,1,0:T(8,128)(2,1)S(1)}, u32[]{:S(2)}, u32[]{:S(2)}) collective-permute-start(bf16[2,4,64,256]{3,2,1,0:T(8,128)(2,1)} %get-tuple-element.58), channel_id=1, source_target_pairs={{0,1},{1,0},{2,3},{3,2},{4,5},{5,4},{6,7},{7,6},{8,9},{9,8},{10,11... | collective-permute-start | bytes 786440 | tf_op jit(solution)/shard_map/ppermute | solution.py:618
  23.7 0.7 copy-start.8
  24.4 11.1 %all-to-all-start = ((bf16[8,208,128]{2,1,0:T(8,128)(2,1)}), bf16[8,208,128]{2,1,0:T(8,128)(2,1)S(1)}, u32[]{:S(2)}, u32[]{:S(2)}) async-start(bf16[8,208,128]{2,1,0:T(8,128)(2,1)} %get-tuple-element.51), calls=%async_computation | async-start | bytes 851968 | tf_op jit(solution)/shard_map/all_to_all | solution.py:622
  29.0 19.1 %collective-permute-start = (bf16[512,512]{1,0:T(8,128)(2,1)}, bf16[512,512]{1,0:T(8,128)(2,1)S(1)}, u32[]{:S(2)}, u32[]{:S(2)}) collective-permute-start(bf16[512,512]{1,0:T(8,128)(2,1)} %get-tuple-element.50.pair), channel_id=1, source_target_pairs={{0,1},{1,0},{2,3},{3,2},{4,5},{5,4},{6,7},{7,6},{8,9},{9,8},{10,11... | collective-permute-start | bytes 1572872 | tf_op jit(solution)/shard_map/ppermute | solution.py:618
  35.5 0.8 copy-start
  40.1 13.5 %all-to-all-start.1 = ((bf16[16,64,128]{2,1,0:T(8,128)(2,1)}), bf16[16,64,128]{2,1,0:T(8,128)(2,1)S(1)}, u32[]{:S(2)}, u32[]{:S(2)}) async-start(bf16[16,64,128]{2,1,0:T(8,128)(2,1)} %bitcast.41), calls=%async_computation.1 | async-start | bytes 524288 | tf_op jit(solution)/shard_map/all_to_all | solution.py:622
  46.0 52.7 %reduce-scatter.3.cloned.1.call-start = ((), (), s32[]{:S(2)}) async-start(), calls=%async_computation.12 | async-start | bytes 2359296 | tf_op jit(solution)/shard_map/reduce_scatter | solution.py:687
  48.1 5.5 %copy-start.6 = (bf16[512,512]{1,0:T(8,128)(2,1)}, bf16[512,512]{1,0:T(8,128)(2,1)S(1)}, u32[]{:S(2)}) copy-start(bf16[512,512]{1,0:T(8,128)(2,1)S(1)} %collective-permute-done.pair_other) | copy-start | bytes 1572868
  53.6 0.7 copy-start.1
  61.9 1.0 copy-start.5
  61.9 1.5 copy-start.7
  62.0 122.7 %reduce-scatter.5.cloned.1.call-start = ((), (), s32[]{:S(2)}) async-start(), calls=%async_computation.13 | async-start | bytes 3833856 | tf_op jit(solution)/shard_map/reduce_scatter | solution.py:719
  63.0 12.3 %collective-permute-start.1 = (bf16[512,512]{1,0:T(8,128)(2,1)S(1)}, bf16[512,512]{1,0:T(8,128)(2,1)S(1)}, u32[]{:S(2)}, u32[]{:S(2)}) collective-permute-start(bf16[512,512]{1,0:T(8,128)(2,1)S(1)} %copy-done.5), channel_id=1, source_target_pairs={{0,1},{1,0},{2,3},{3,2},{4,5},{5,4},{6,7},{7,6},{8,9},{9,8},{10,11... | collective-permute-start | bytes 1572872 | tf_op jit(solution)/shard_map/ppermute | solution.py:618
  75.2 0.8 copy-start.2
  107.9 3.7 %copy-start.9 = (bf16[256,512]{1,0:T(8,128)(2,1)S(1)}, bf16[256,512]{1,0:T(8,128)(2,1)}, u32[]{:S(2)}) copy-start(bf16[256,512]{1,0:T(8,128)(2,1)} %get-tuple-element.64.part) | copy-start | bytes 786436
  107.9 11.5 %all-to-all-start.4 = ((bf16[8,192,128]{2,1,0:T(8,128)(2,1)}), bf16[8,192,128]{2,1,0:T(8,128)(2,1)S(1)}, u32[]{:S(2)}, u32[]{:S(2)}) async-start(bf16[8,192,128]{2,1,0:T(8,128)(2,1)} %get-tuple-element.65), calls=%async_computation.5 | async-start | bytes 786432 | tf_op jit(solution)/shard_map/all_to_all | solution.py:622
  111.5 103.0 %all-gather.10.cloned.1.call-start = ((), (), s32[]{:S(2)}) async-start(), calls=%async_computation.15 | async-start | bytes 2359296 | tf_op jit(solution)/shard_map/all_gather | solution.py:746
  111.6 7.9 %collective-permute-start.3 = (bf16[256,512]{1,0:T(8,128)(2,1)S(1)}, bf16[256,512]{1,0:T(8,128)(2,1)S(1)}, u32[]{:S(2)}, u32[]{:S(2)}) collective-permute-start(bf16[256,512]{1,0:T(8,128)(2,1)S(1)} %copy-done.9), channel_id=1, source_target_pairs={{0,1},{1,0},{2,3},{3,2},{4,5},{5,4},{6,7},{7,6},{8,9},{9,8},{10,11... | collective-permute-start | bytes 786440 | tf_op jit(solution)/shard_map/ppermute | solution.py:618
  119.4 0.7 copy-start.4
  119.4 0.8 copy-start.3
  148.6 99.1 %all-gather.8.cloned.1.call-start = ((), (), s32[]{:S(2)}) async-start(), calls=%async_computation.14 | async-start | bytes 5308416 | tf_op jit(solution)/shard_map/all_gather | solution.py:750
Sparse Core Ops, SparseCore 0:
  24.6 27.8 all-gather.5
  62.1 32.8 reduce-scatter.2
  108.0 39.6 reduce-scatter.4
  149.9 38.0 all-gather.9
  214.6 33.0 all-gather.7

commit v4 on v3

--- a/solution.py
+++ b/solution.py
@@ -33,6 +33,16 @@
         return pl.BlockSpec(memory_space=pl.ANY)
 
 
+class Rows:
+    def __init__(self, array, rows, at=0):
+        self.array, self.rows, self.at = array, rows, at
+
+    def spec(self):
+        shape = self.array.shape
+        place = (0,) * (len(shape) - 2) + (self.at, 0)
+        return pl.BlockSpec(shape[:-2] + (self.rows, shape[-1]), lambda i: place)
+
+
 class Layer:
     def __init__(self, array, index):
         self.array, self.index = array, index
@@ -49,9 +59,9 @@
 
 def call(body, out_shape, args, name, scratch=(), smem_first=False):
     specs = [
-        a.spec() if isinstance(a, (Layer, After)) else whole(a.shape) for a in args
+        a.spec() if isinstance(a, (Layer, Rows, After)) else whole(a.shape) for a in args
     ]
-    args = [a.array if isinstance(a, (Layer, After)) else a for a in args]
+    args = [a.array if isinstance(a, (Layer, Rows, After)) else a for a in args]
     if smem_first:
         specs[0] = pl.BlockSpec(memory_space=pltpu.SMEM)
     return pl.pallas_call(
@@ -173,10 +183,9 @@
 
 def first_body(
     at, pos, freqs, x, gain, bias, w_qkv, b_qkv, w_up, b_up, w_down, w_out,
-    send, pair, act, slope, cs, chunk,
+    send, pair, act, slope, cs,
 ):
-    chunk_of(at, w_qkv, w_out, chunk)
-    pair[256:512] = w_out[0]
+    pair[256:512] = w_out[...]
     for s in range(2):
         p = pos[s : s + 1, :].astype(F32)
         angle = freqs[...] * p
@@ -185,7 +194,7 @@
     normed, _ = norm_rows(x[...])
     attn_in = (normed * gain[0, 0:1] + bias[0, 0:1]).astype(BF)
     mlp_in = (normed * gain[0, 1:2] + bias[0, 1:2]).astype(BF)
-    send_qkv(send, attn_in, w_qkv.at[0], b_qkv, 0, cs)
+    send_qkv(send, attn_in, w_qkv, b_qkv, 0, cs)
     row = lax.broadcasted_iota(jnp.int32, (16, BLK), 0)
     token = at[0] * BLK + lax.broadcasted_iota(jnp.int32, (1, BLK), 1)
     for s in range(2):
@@ -213,7 +222,14 @@
     return (key <= query) & (key >= start[:, c * CHUNK : (c + 1) * CHUNK])
 
 
-def attend_body(recv, send, lse, ctx, start_out):
+def attend_body(at, recv, w_qkv, w_out, send, lse, ctx, start_out):
+    for layer in range(2):
+        piece = jnp.where(at[2] // 2 == 3, w_out[layer], w_qkv[layer, 0])
+        for b in range(8):
+            for t in range(2):
+                for half in range(2):
+                    row = 64 + 64 * layer + 32 * half
+                    send[b, t, row : row + 32] = piece[:, BLK * half : BLK * (half + 1)]
     q = load_rows(recv, 0, HEAD)
     k_t = load_rows(recv, HEAD, 2 * HEAD)
     v_t = load_rows(recv, 2 * HEAD, 3 * HEAD)
@@ -234,10 +250,12 @@
         for i in range(CHUNK // BLK):
             block = out[:, i * BLK : (i + 1) * BLK].astype(BF)
             for t in range(2):
-                send[c * (CHUNK // BLK) + i, t] = block
-
-
-def attend_both_body(recv, start, _, send, dk, dv):
+                send[c * (CHUNK // BLK) + i, t, 0:HEAD] = block
+
+
+def attend_both_body(at, recv, start, pieces, _, send, piece, dk, dv):
+    for b in range(8):
+        piece[b] = jnp.where(at[1] == 0, pieces[b, 1], pieces[b, 0])
     q = load_rows(recv, 0, HEAD)
     k_t = load_rows(recv, HEAD, 2 * HEAD)
     v_t = load_rows(recv, 2 * HEAD, 3 * HEAD)
@@ -320,12 +338,17 @@
     return jnp.where(t == 0, own, other), jnp.where(t == 0, other, own)
 
 
+def other_matrix(others, m):
+    rows = []
+    for d in (2 * m, 2 * m + 1):
+        for c in range(8):
+            rows.append(jnp.concatenate([others[d, c, 0:32, :], others[d, c, 32:64, :]], 1))
+    return jnp.concatenate(rows, 0)
+
+
 def out_other(others):
-    halves = [
-        jnp.concatenate([others[3, 64 * p + 32 * c : 64 * p + 32 * (c + 1), :] for p in range(8)], 0)
-        for c in range(2)
-    ]
-    return jnp.concatenate(halves, 1)
+    stacked = other_matrix(others, 3)
+    return jnp.concatenate([stacked[0:256], stacked[256:512]], 1)
 
 
 def branch_of(t, recv, w_own, w_other):
@@ -385,7 +408,7 @@
                     pieces.append(u)
                 blocks.append(jnp.concatenate(pieces, 1))
             halves.append(jnp.concatenate(blocks, 0))
-        first, second = ordered(t, w_own[e], others[e])
+        first, second = ordered(t, w_own[e], other_matrix(others, e))
         term = mm(first, halves[0]) + mm(second, halves[1])
         d_attn_t = term if d_attn_t is None else d_attn_t + term
         own = jnp.where(t == 0, halves[0], halves[1])
@@ -443,7 +466,7 @@
 
 def last_body(
     at, x, g, part, part_other, recv, w_qkv, others, cs, gain, bias,
-    d_b_up0, d_b_up1, d_b_qkv1, d_norm1, d_sum0, d_sum1,
+    d_b_up0, d_b_up1, d_b_qkv1, d_norm1, d_sum0, d_sum1, sums_b,
     in_grad, grads, sums_a, d_b_qkv0, d_norm0,
 ):
     d_mlp_in = part[...].astype(F32) + part_other[...].astype(F32)
@@ -474,32 +497,28 @@
         have = rows[p] if p < len(rows) else []
         fill = [jnp.zeros((16 - len(have), 256), F32)]
         grads[p, 192:208, :] = jnp.concatenate(have + fill, 0).astype(BF)
-
-
-def chunk_of(at, w_qkv, w_out, out):
-    for layer in range(2):
-        for e in range(3):
-            out[layer, e] = w_qkv[layer, e, pl.ds(pl.multiple_of(at[2] * 64, 64), 64), :]
-        rows = w_out[layer, pl.ds(pl.multiple_of(at[2] * 32, 32), 32), :]
-        out[layer, 3, 0:32] = rows[:, 0:256]
-        out[layer, 3, 32:64] = rows[:, 256:512]
-
-
-def mix_body(got, early, out):
+        rows_b = sums_b[104 * p : 104 * (p + 1)].astype(F32)
+        grads[p, 208:320, :] = jnp.concatenate([rows_b, jnp.zeros((8, 256), F32)], 0).astype(BF)
+
+
+def sum_of(got):
     total = got[0].astype(F32)
     for i in range(1, 8):
         total = total + got[i].astype(F32)
+    return total.astype(BF)
+
+
+def sum_both_body(got, late, early):
+    total = sum_of(got)
     for q in range(8):
-        mine = [early[104 * q : 104 * (q + 1)].astype(F32), total[24 * q : 24 * (q + 1)]]
-        out[q, 0:128] = jnp.concatenate(mine, 0).astype(BF)
-        out[q, 128:144] = total[192:208].astype(BF) if q == 0 else jnp.zeros((16, 256), BF)
-
-
-def sum_body(got, out):
-    total = got[0].astype(F32)
-    for i in range(1, 8):
-        total = total + got[i].astype(F32)
-    out[...] = total.astype(BF)
+        late[q] = total[0:208]
+        early[q] = total[208:320]
+
+
+def sum_body(got, late):
+    total = sum_of(got)
+    for q in range(8):
+        late[q] = total
 
 
 def unpack_first_body(first, g_up, g_down):
@@ -510,30 +529,30 @@
         g_down[0, :, 256 * c : 256 * (c + 1)] = rows.astype(F32)
 
 
-def unpack_rest_body(rest, _, __, g_up, g_down, g_qkv, g_out, g_b_up, g_b_qkv, g_sum, g_gain, g_bias):
+def unpack_rest_body(
+    rest, last, _, __, g_up, g_down, g_qkv, g_out, g_b_up, g_b_qkv, g_sum, g_gain, g_bias
+):
     p = pl.program_id(0)
-
-    def early(row):
-        return rest[row // 104, row % 104 : row % 104 + 8].astype(F32)
-
-    def late(row):
-        return rest[row // 24, 104 + row % 24 : 104 + row % 24 + 8].astype(F32)
-
-    for k in range(0, 64, 8):
-        for e in range(3):
-            g_qkv[0, e, k : k + 8] = late(64 * e + k)
-            g_qkv[1, e, k : k + 8] = early(64 * e + k)
-        for c in range(4):
-            g_up[0, k : k + 8, 256 * c : 256 * (c + 1)] = early(192 + 64 * c + k)
-    for k in range(0, 32, 8):
-        for c in range(2):
-            g_out[0, k : k + 8, 256 * c : 256 * (c + 1)] = early(768 + 32 * c + k)
-            g_out[1, k : k + 8, 256 * c : 256 * (c + 1)] = early(704 + 32 * c + k)
-    for k in range(0, 128, 8):
-        for c in range(2):
-            g_down[0, k : k + 8, 256 * c : 256 * (c + 1)] = early(448 + 128 * c + k)
-
-    tiny = rest[0, 128:144].astype(F32)
+    for e in range(3):
+        g_qkv[0, e] = last[64 * e : 64 * (e + 1)].astype(F32)
+    for q in range(8):
+        block = rest[q, 0:104].astype(F32)
+        for i in range(13):
+            row = 104 * q + 8 * i
+            value = block[8 * i : 8 * (i + 1)]
+            if row < 192:
+                g_qkv[1, row // 64, row % 64 : row % 64 + 8] = value
+            elif row < 448:
+                c, r = divmod(row - 192, 64)
+                g_up[0, r : r + 8, 256 * c : 256 * (c + 1)] = value
+            elif row < 704:
+                c, r = divmod(row - 448, 128)
+                g_down[0, r : r + 8, 256 * c : 256 * (c + 1)] = value
+            else:
+                c, r = divmod((row - 704) % 64, 32)
+                g_out[1 - (row - 704) // 64, r : r + 8, 256 * c : 256 * (c + 1)] = value
+
+    tiny = last[192:208].astype(F32)
 
     @pl.when(p == 0)
     def _():
@@ -572,7 +591,7 @@
 DOWN = (2, 1024, 512)
 
 
-def unpack(first, rest):
+def unpack(first, rest, last):
     def place(layer):
         return [
             pl.BlockSpec((1, 64, 1024), lambda p: (layer, p, 0)),
@@ -603,15 +622,16 @@
         grid=(8,),
         out_shape=[jax.ShapeDtypeStruct(shape, F32) for shape in [UP, DOWN] + [o[0] for o in outs]],
         in_specs=[
-            pl.BlockSpec((None, 8, 144, 256), lambda p: (p, 0, 0, 0)),
+            pl.BlockSpec((None, 8, 112, 256), lambda p: (p, 0, 0, 0)),
+            pl.BlockSpec((None, 208, 256), lambda p: (p, 0, 0)),
             pl.BlockSpec(memory_space=pl.ANY),
             pl.BlockSpec(memory_space=pl.ANY),
         ],
         out_specs=place(0) + [spec for _, spec in outs],
-        input_output_aliases={1: 0, 2: 1},
+        input_output_aliases={2: 0, 3: 1},
         compiler_params=params,
         name="unpack_rest",
-    )(rest, g_up, g_down)
+    )(rest, last, g_up, g_down)
 
 
 def swap(value):
@@ -625,6 +645,33 @@
 def both(value):
     flat = value.reshape((16,) + value.shape[2:])
     return exchange(flat, ("context", "tensor")).reshape(value.shape)
+
+
+def attend(at, recv, wq, w_out):
+    outs = [((8, 2, 192, BLK), BF), ((1, 1024), F32), ((HEAD, 1024), F32), ((1, 1024), jnp.int32)]
+
+    def all_of(shape):
+        return pl.BlockSpec(shape, lambda i, at: (0,) * len(shape))
+
+    return pl.pallas_call(
+        attend_body,
+        out_shape=[jax.ShapeDtypeStruct(s, d) for s, d in outs],
+        grid_spec=pltpu.PrefetchScalarGridSpec(
+            num_scalar_prefetch=1,
+            grid=(1,),
+            in_specs=[
+                all_of(recv.shape),
+                pl.BlockSpec(
+                    (2, 1, 32, 256),
+                    lambda i, at: (0, jnp.minimum(at[2] // 2, 2), (at[2] % 2) * 8 + at[0], 0),
+                ),
+                pl.BlockSpec((2, 32, 256), lambda i, at: (0, at[0], at[2] % 2)),
+            ],
+            out_specs=[all_of(s) for s, _ in outs],
+        ),
+        compiler_params=pltpu.CompilerParams(vmem_limit_bytes=56 * 1024 * 1024),
+        name="attend",
+    )(at, recv, wq, w_out)
 
 
 def shards(
@@ -639,7 +686,7 @@
         [lax.axis_index("context"), lax.axis_index("tensor"), lax.axis_index("dp")]
     ).astype(jnp.int32)
     freqs = jnp.asarray(FREQS).reshape(HALF, 1)
-    send, pair, act, slope, cs, chunk = call(
+    send, pair, act, slope, cs = call(
         first_body,
         [
             ((8, 208, BLK), BF),
@@ -647,25 +694,20 @@
             ((rows, 1024), BF),
             ((rows, 1024), F32),
             ((2, 2, HALF, BLK), F32),
-            ((2, 4, 64, 256), BF),
         ],
         (
-            at, positions, freqs, x, ln_gain, ln_bias, wq, bq, Layer(w_up, 0), b_up,
-            Layer(w_down, 0), w_out,
+            at, positions, freqs, x, ln_gain, ln_bias, Layer(wq, 0), bq, Layer(w_up, 0), b_up,
+            Layer(w_down, 0), Layer(w_out, 0),
         ),
         "norm_qkv_feed",
         smem_first=True,
     )
     pair_other = swap(pair)
-    others = lax.all_gather(swap(chunk), "dp", axis=2, tiled=True)
     recv = exchange(send, "context")
-    ctx_send, lse, ctx, start = call(
-        attend_body,
-        [((8, 2, HEAD, BLK), BF), ((1, 1024), F32), ((HEAD, 1024), F32), ((1, 1024), jnp.int32)],
-        (recv,),
-        "attend",
-    )
+    ctx_send, lse, ctx, start = attend(at, recv, wq, w_out)
     recv_ctx = both(ctx_send)
+    piece = lax.dynamic_index_in_dim(recv_ctx, 1 - at[1], 1, keepdims=False)[:, 128:192]
+    others1 = lax.all_gather(piece, "dp")
     stream, send, grads_a, parts, d_b_up1, d_sum1 = call(
         middle_body,
         [
@@ -677,7 +719,7 @@
             ((1, width), F32),
         ],
         (
-            at, x, pair, pair_other, recv_ctx, Layer(w_out, 0), out_bias, ln_gain, ln_bias,
+            at, x, pair, pair_other, Rows(recv_ctx, HEAD), Layer(w_out, 0), out_bias, ln_gain, ln_bias,
             Layer(wq, 1), bq, Layer(w_up, 1), b_up, Layer(w_down, 1), Layer(w_out, 1), cot, cs,
         ),
         "middle",
@@ -687,13 +729,15 @@
     sums_a = lax.psum_scatter(grads_a, "dp", scatter_dimension=0)
     parts_other = swap(parts)
     recv_both = exchange(send, "context")
-    (both_send,) = call(
+    both_send, piece = call(
         attend_both_body,
-        [((8, 2, 256, BLK), BF)],
-        (recv_both, start, After(parts_other)),
+        [((8, 2, 256, BLK), BF), ((8, HEAD, BLK), BF)],
+        (at, recv_both, start, Rows(recv_ctx, HEAD, 1), After(parts_other)),
         "attend_both",
         scratch=[pltpu.VMEM((HEAD, 1024), F32), pltpu.VMEM((HEAD, 1024), F32)],
-    )
+        smem_first=True,
+    )
+    others0 = lax.all_gather(piece, "dp")
     recv_grad = both(both_send)
     block_out, g, send, grads_b, part_g, d_b_up0, d_b_qkv1, d_norm1, d_sum0 = call(
         turn_point_body,
@@ -709,9 +753,9 @@
             ((1, width), F32),
         ],
         (
-            at, stream, parts, parts_other, recv_grad, Layer(w_out, 1), Layer(wq, 1), Layer(others, 1),
+            at, stream, parts, parts_other, recv_grad, Layer(w_out, 1), Layer(wq, 1), others1,
             out_bias, ln_gain, ln_bias, cot, cs, x, act, slope, Layer(w_up, 0), Layer(w_down, 0),
-            Layer(w_out, 0), recv_ctx, sums_a,
+            Layer(w_out, 0), Rows(recv_ctx, HEAD), sums_a,
         ),
         "turn_point",
         smem_first=True,
@@ -731,24 +775,29 @@
         last_body,
         [
             ((rows, width), F32),
-            ((8, 208, 256), BF),
+            ((8, 320, 256), BF),
             ((512, 256), BF),
             ((3, 256), F32),
             ((4, width), F32),
         ],
         (
-            at, x, g, part_g, part_g_other, recv_grad0, Layer(wq, 0), Layer(others, 0), cs,
-            ln_gain, ln_bias, d_b_up0, d_b_up1, d_b_qkv1, d_norm1, d_sum0, d_sum1,
+            at, x, g, part_g, part_g_other, recv_grad0, Layer(wq, 0), others0, cs,
+            ln_gain, ln_bias, d_b_up0, d_b_up1, d_b_qkv1, d_norm1, d_sum0, d_sum1, sums_b,
         ),
         "last",
         smem_first=True,
     )
     full_a = lax.all_gather(sums_a, "dp")
-    (mixed,) = call(mix_body, [((8, 144, 256), BF)], (exchange(grads_c, "dp"), sums_b), "mix")
-    (summed,) = call(sum_body, [((144, 256), BF)], (exchange(mixed, "context"),), "sum")
-    summed = exchange(jnp.broadcast_to(summed[None], (8, 144, 256)), "context")
-    full_bc = lax.all_gather(summed, "dp")
-    g_up, g_down, g_qkv, g_out, g_b_up, g_b_qkv, g_sum, g_gain, g_bias = unpack(full_a, full_bc)
+    late, early = call(
+        sum_both_body,
+        [((8, 208, 256), BF), ((8, 112, 256), BF)],
+        (exchange(grads_c, "context"),),
+        "sum_both",
+    )
+    full_b = lax.all_gather(exchange(early, "context"), "dp")
+    (late,) = call(sum_body, [((8, 208, 256), BF)], (exchange(late, "dp"),), "sum")
+    full_c = exchange(late, "context")
+    g_up, g_down, g_qkv, g_out, g_b_up, g_b_qkv, g_sum, g_gain, g_bias = unpack(full_a, full_b, full_c)
     return (
         block_out.reshape(tokens_in.shape),
         in_grad.reshape(tokens_in.shape),

time: 263 us -> 274 us (1.042)
  waiting for transfers between devices: 51.3 us -> 59.7 us
  blocking collectives: 108 us -> 112 us
  starting transfers between devices: 23.4 us -> 20.5 us
    all_gather x2 -> x3, waiting for transfers between devices: 27.3 us -> 0.02 us  [the longest x1 0.02 us: shards(): others0 = lax.all_gather(piece, 'dp')]
    all_to_all x3 -> x4, waiting for transfers between devices: 8.7 us -> 31.8 us  [exchange(): return lax.all_to_all(value, axes, 0, 0)]
    reduce_scatter x1, waiting for transfers between devices: 0.01 us -> 10.2 us  [shards(): sums_b = lax.psum_scatter(grads_b, 'dp', scatter_dimension=0)]
    ppermute x4 -> x3, starting transfers between devices: 9.19 us -> 1.42 us  [swap(): return lax.ppermute(value, 'tensor', [(0, 1), (1, 0)])]
    pallas_call x0 -> x1, Pallas kernels: none -> 4.79 us  [attend(): pl.pallas_call(attend_body, out_shape=[jax.ShapeDtypeStruct(s, d) for s,...]
    all_to_all x3 -> x4, starting transfers between devices: 14 us -> 18.8 us  [exchange(): return lax.all_to_all(value, axes, 0, 0)]
    all_to_all x6, blocking collectives: 108 us -> 112 us  [exchange(): return lax.all_to_all(value, axes, 0, 0)]
    pallas_call x9 -> x8, Pallas kernels: 45.2 us -> 42.1 us  [call(): pl.pallas_call(body, grid=(1,), out_shape=[jax.ShapeDtypeStruct(s, d) for...]
  transfers between devices with their start and end apart: 12 -> 13, of which waited for: 7 -> 6; matrix products, arithmetic and copies ran while one was open for 0% -> 0% of each run, Pallas kernels for 14% -> 14%
where the time goes in v4:
time: 274 us; the launch traced here: 272 us
  blocking collectives  112 us (41%)
  Pallas kernels  60.3 us (22%)
  waiting for transfers between devices  59.7 us (22%)
  starting transfers between devices  20.5 us (7%)
  between operations  14.3 us (5%)
  local copies, waits for them, and re-layouts  5.22 us (2%)
    all_to_all x6, blocking collectives, exchange(): return lax.all_to_all(value, axes, 0, 0)  112 us
    pallas_call x8, Pallas kernels, call(): pl.pallas_call(body, grid=(1,), out_shape=[jax.ShapeDtypeStruct(s, d) for...  42.1 us
    all_to_all x4, waiting for transfers between devices, exchange(): return lax.all_to_all(value, axes, 0, 0)  31.8 us
    all_to_all x4, starting transfers between devices, exchange(): return lax.all_to_all(value, axes, 0, 0)  18.8 us
    ppermute x3, waiting for transfers between devices, swap(): return lax.ppermute(value, 'tensor', [(0, 1), (1, 0)])  17.6 us
    reduce_scatter x1, waiting for transfers between devices, shards(): sums_b = lax.psum_scatter(grads_b, 'dp', scatter_dimension=0)  10.2 us
    pallas_call x1, Pallas kernels, unpack(): pl.pallas_call(unpack_rest_body, grid=(8,), out_shape=[jax.ShapeDtypeStru...  7.41 us
    pallas_call x1, Pallas kernels, unpack(): pl.pallas_call(unpack_first_body, grid=(8,), out_shape=[jax.ShapeDtypeStr...  5.96 us
  transfers between devices with their start and end apart: 13, of which 6 were waited for; matrix products, arithmetic and copies ran while one was open for 0% of the time, Pallas kernels for 14%

profile of v4, /device:TPU:1, one launch (start us, length us, event | category | flops | bytes accessed | tf_op | source)
XLA Modules:
  0.0 272.2 jit_solution(16987725133212445765)
XLA Ops:
  7.8 4.8 %norm_qkv_feed.1 = (bf16[8,208,128]{2,1,0:T(8,128)(2,1)}, bf16[512,512]{1,0:T(8,128)(2,1)}, bf16[256,1024]{1,0:T(8,128)(2,1)}, f32[256,1024]{1,0:T(8,128)}, f32[2,2,8,128]{3,2,1,0:T(8,128)}) custom-call(s32[3]{0:T(128)} %pad_add_fusion.at, s32[2,128]{1,0:T(2,128)} %pos.1, f32[8,1]{1,0:T(8,128)} %constant.27.freqs, f32[256,512]{1,0:T(8,128)} %bitcast.34, ...), custom_call_target="tpu_custom_call" | custom-call | tf_op jit(solution)/shard_map/norm_qkv_feed/pallas_call | solution.py:67
  12.6 14.0 %all_to_all.50.recv = bf16[8,208,128]{2,1,0:T(8,128)(2,1)} all-to-all(bf16[8,208,128]{2,1,0:T(8,128)(2,1)} %get-tuple-element.54), channel_id=1, replica_groups=mesh['dp'=8,'context'=8,'tensor'=2] {'context'}, dimensions={0} | all-to-all | bytes 851968 | tf_op jit(solution)/shard_map/all_to_all | solution.py:642
  26.5 4.8 %attend.1 = (bf16[8,2,192,128]{3,2,1,0:T(8,128)(2,1)}, f32[1,1024]{1,0:T(1,128)}, f32[64,1024]{1,0:T(8,128)}, s32[1,1024]{1,0:T(1,128)}) custom-call(s32[3]{0:T(128)} %pad_add_fusion.at, bf16[8,208,128]{2,1,0:T(8,128)(2,1)} %all_to_all.50.recv, bf16[2,3,512,256]{3,2,1,0:T(8,128)(2,1)} %bitcast.26, bf16[2,256,512]{2,1,0:T(8,128)(2,1)} %w_out_first.1), custom_call_target="tpu_custom_call" | custom-call | tf_op jit(solution)/shard_map/attend/pallas_call | solution.py:656
  31.3 5.8 %all-to-all-start.1 = ((bf16[16,192,128]{2,1,0:T(8,128)(2,1)}), bf16[16,192,128]{2,1,0:T(8,128)(2,1)S(1)}, u32[]{:S(2)}, u32[]{:S(2)}) async-start(bf16[16,192,128]{2,1,0:T(8,128)(2,1)} %bitcast.48), calls=%async_computation.1 | async-start | bytes 1572864 | tf_op jit(solution)/shard_map/all_to_all | solution.py:642
  37.2 11.2 %all-to-all-done.1 = bf16[16,192,128]{2,1,0:T(8,128)(2,1)S(1)} async-done(((bf16[16,192,128]{2,1,0:T(8,128)(2,1)}), bf16[16,192,128]{2,1,0:T(8,128)(2,1)S(1)}, u32[]{:S(2)}, u32[]{:S(2)}) %all-to-all-start.1) | async-done | bytes 786464 | tf_op jit(solution)/shard_map/all_to_all | solution.py:642
  49.6 10.8 %collective-permute-done.pair_other = bf16[512,512]{1,0:T(8,128)(2,1)S(1)} collective-permute-done((bf16[512,512]{1,0:T(8,128)(2,1)S(1)}, bf16[512,512]{1,0:T(8,128)(2,1)S(1)}, u32[]{:S(2)}, u32[]{:S(2)}) %collective-permute-start) | collective-permute-done | bytes 524320 | tf_op jit(solution)/shard_map/ppermute | solution.py:638
  61.2 7.6 %middle.1 = (f32[256,512]{1,0:T(8,128)}, bf16[8,256,128]{2,1,0:T(8,128)(2,1)}, bf16[8,512,256]{2,1,0:T(8,128)(2,1)}, bf16[512,512]{1,0:T(8,128)(2,1)}, f32[1,1024]{1,0:T(1,128)}, /*index=5*/f32[1,512]{1,0:T(1,128)}) custom-call(s32[3]{0:T(128)} %pad_add_fusion.at, f32[256,512]{1,0:T(8,128)} %bitcast.35, bf16[512,512]{1,0:T(8,128)(2,1)} %get-tuple-element.53.pair, ...), custom_call_target="tpu_custom_call" | custom-call | tf_op jit(solution)/shard_map/middle/pallas_call | solution.py:67
  70.0 15.0 %all_to_all.51.recv = bf16[8,256,128]{2,1,0:T(8,128)(2,1)} all-to-all(bf16[8,256,128]{2,1,0:T(8,128)(2,1)S(1)} %copy-done.8), channel_id=1, replica_groups=mesh['dp'=8,'context'=8,'tensor'=2] {'context'}, dimensions={0} | all-to-all | bytes 1048576 | tf_op jit(solution)/shard_map/all_to_all | solution.py:642
  85.9 6.3 %attend_both.1 = (bf16[8,2,256,128]{3,2,1,0:T(8,128)(2,1)}, bf16[8,64,128]{2,1,0:T(8,128)(2,1)}) custom-call(s32[3]{0:T(128)} %pad_add_fusion.at, bf16[8,256,128]{2,1,0:T(8,128)(2,1)} %all_to_all.51.recv, s32[1,1024]{1,0:T(1,128)} %get-tuple-element.60.start, bf16[8,2,192,128]{3,2,1,0:T(8,128)(2,1)} %bitcast.32, bf16[512,512]{1,0:T(8,128)(2,1)} %copy-done.3), custom_call_target="tpu_custom_call" | custom-call | tf_op jit(solution)/shard_map/attend_both/pallas_call | solution.py:67
  92.3 22.1 %all_to_all.52 = bf16[16,256,128]{2,1,0:T(8,128)(2,1)} all-to-all(bf16[16,256,128]{2,1,0:T(8,128)(2,1)} %bitcast.45), channel_id=1, replica_groups=mesh['dp'=8,'context'=8,'tensor'=2] {'context','tensor'}, dimensions={0} | all-to-all | bytes 2097152 | tf_op jit(solution)/shard_map/all_to_all | solution.py:642
  114.4 9.2 %turn_point.1 = (f32[256,512]{1,0:T(8,128)}, f32[256,512]{1,0:T(8,128)}, bf16[8,192,128]{2,1,0:T(8,128)(2,1)}, bf16[8,832,256]{2,1,0:T(8,128)(2,1)}, bf16[256,51...) custom-call(s32[3]{0:T(128)} %pad_add_fusion.at, ...), custom_call_target="tpu_custom_call" | custom-call | tf_op jit(solution)/shard_map/turn_point/pallas_call | solution.py:67
  123.6 3.6 %all-to-all-start.4 = ((bf16[8,192,128]{2,1,0:T(8,128)(2,1)}), bf16[8,192,128]{2,1,0:T(8,128)(2,1)S(1)}, u32[]{:S(2)}, u32[]{:S(2)}) async-start(bf16[8,192,128]{2,1,0:T(8,128)(2,1)} %get-tuple-element.68), calls=%async_computation.5 | async-start | bytes 786432 | tf_op jit(solution)/shard_map/all_to_all | solution.py:642
  128.3 6.8 %collective-permute-done.2._.part_other = bf16[256,512]{1,0:T(8,128)(2,1)S(1)} collective-permute-done((bf16[256,512]{1,0:T(8,128)(2,1)S(1)}, bf16[256,512]{1,0:T(8,128)(2,1)S(1)}, u32[]{:S(2)}, u32[]{:S(2)}) %collective-permute-start.2) | collective-permute-done | bytes 262176 | tf_op jit(solution)/shard_map/ppermute | solution.py:638
  135.9 4.5 %attend_back.1 = bf16[8,2,320,128]{3,2,1,0:T(8,128)(2,1)} custom-call(bf16[8,208,128]{2,1,0:T(8,128)(2,1)} %all_to_all.50.recv, bf16[8,192,128]{2,1,0:T(8,128)(2,1)} %copy-done.4, s32[1,1024]{1,0:T(1,128)} %get-tuple-element.60.start, f32[1,1024]{1,0:T(1,128)} %get-tuple-element.69.lse, f32[64,1024]{1,0:T(8,128)} %get-tuple-element.70.ctx, ...), custom_call_target="tpu_custom_call" | custom-call | tf_op jit(solution)/shard_map/attend_back/pallas_call | solution.py:67
  140.4 5.9 %all-to-all-start.5 = ((bf16[16,320,128]{2,1,0:T(8,128)(2,1)}), bf16[16,320,128]{2,1,0:T(8,128)(2,1)S(1)}, u32[]{:S(2)}, u32[]{:S(2)}) async-start(bf16[16,320,128]{2,1,0:T(8,128)(2,1)} %bitcast.38), calls=%async_computation.6 | async-start | bytes 2621440 | tf_op jit(solution)/shard_map/all_to_all | solution.py:642
  146.4 14.1 %all-to-all-done.5 = bf16[16,320,128]{2,1,0:T(8,128)(2,1)S(1)} async-done(((bf16[16,320,128]{2,1,0:T(8,128)(2,1)}), bf16[16,320,128]{2,1,0:T(8,128)(2,1)S(1)}, u32[]{:S(2)}, u32[]{:S(2)}) %all-to-all-start.5) | async-done | bytes 1310752 | tf_op jit(solution)/shard_map/all_to_all | solution.py:642
  160.5 10.2 %reduce-scatter.5.cloned.1.call-done = bf16[1,832,256]{2,1,0:T(8,128)(2,1)} async-done(((bf16[8,832,256]{2,1,0:T(8,128)(2,1)}), bf16[1,832,256]{2,1,0:T(8,128)(2,1)}) %reduce-scatter.5.cloned.1.call-update) | async-done | bytes 426000 | tf_op jit(solution)/shard_map/reduce_scatter | solution.py:763
  170.7 5.0 %last.1 = (f32[256,512]{1,0:T(8,128)}, bf16[8,320,256]{2,1,0:T(8,128)(2,1)}, bf16[512,256]{1,0:T(8,128)(2,1)}, f32[3,256]{1,0:T(4,128)}, f32[4,512]{1,0:T(4,128)}) custom-call(s32[3]{0:T(128)} %pad_add_fusion.at, f32[256,512]{1,0:T(8,128)} %bitcast.37, f32[256,512]{1,0:T(8,128)} %get-tuple-element.66.g, bf16[256,512]{1,0:T(8,128)(2,1)} %get-tuple-element.67.part, ...), custom_call_target="tpu_custom_call" | custom-call | tf_op jit(solution)/shard_map/last/pallas_call | solution.py:67
  175.8 19.3 %all_to_all.53.got = bf16[8,320,256]{2,1,0:T(8,128)(2,1)} all-to-all(bf16[8,320,256]{2,1,0:T(8,128)(2,1)} %get-tuple-element.80), channel_id=1, replica_groups=mesh['dp'=8,'context'=8,'tensor'=2] {'context'}, dimensions={0} | all-to-all | bytes 2621440 | tf_op jit(solution)/shard_map/all_to_all | solution.py:642
  197.6 11.0 %all_to_all.54 = bf16[8,112,256]{2,1,0:T(8,128)(2,1)} all-to-all(bf16[8,112,256]{2,1,0:T(8,128)(2,1)} %get-tuple-element.81), channel_id=1, replica_groups=mesh['dp'=8,'context'=8,'tensor'=2] {'context'}, dimensions={0} | all-to-all | bytes 917504 | tf_op jit(solution)/shard_map/all_to_all | solution.py:642
  208.6 30.2 %all_to_all.55.got = bf16[8,208,256]{2,1,0:T(8,128)(2,1)} all-to-all(bf16[8,208,256]{2,1,0:T(8,128)(2,1)} %get-tuple-element.82), channel_id=1, replica_groups=mesh['dp'=8,'context'=8,'tensor'=2] {'dp'}, dimensions={0} | all-to-all | bytes 1703936 | tf_op jit(solution)/shard_map/all_to_all | solution.py:642
  244.6 6.0 %unpack_first.1 = (f32[2,512,1024]{2,1,0:T(8,128)}, f32[2,1024,512]{2,1,0:T(8,128)}) custom-call(bf16[8,512,256]{2,1,0:T(8,128)(2,1)} %bitcast.42), custom_call_target="tpu_custom_call" | custom-call | tf_op jit(solution)/shard_map/unpack_first/pallas_call | solution.py:602
  250.6 6.4 %all-to-all-done.9.last = bf16[8,208,256]{2,1,0:T(8,128)(2,1)S(1)} async-done(((bf16[8,208,256]{2,1,0:T(8,128)(2,1)}), bf16[8,208,256]{2,1,0:T(8,128)(2,1)S(1)}, u32[]{:S(2)}, u32[]{:S(2)}) %all-to-all-start.9) | async-done | bytes 852000 | tf_op jit(solution)/shard_map/all_to_all | solution.py:642
  258.0 7.4 %unpack_rest.1 = (f32[2,512,1024]{2,1,0:T(8,128)}, f32[2,1024,512]{2,1,0:T(8,128)}, f32[2,3,512,256]{3,2,1,0:T(8,128)}, f32[2,256,512]{2,1,0:T(8,128)}, f32[2,10...) custom-call(bf16[8,8,112,256]{3,2,1,0:T(8,128)(2,1)} %bitcast.41, ...), custom_call_target="tpu_custom_call", output_to_operand_aliasing={{0}: (2, {}), {1}: (3, {})} | custom-call | tf_op jit(solution)/shard_map/unpack_rest/pallas_call | solution.py:620
  (50 shorter events, 15.9 us)
Async XLA Ops:
  26.5 22.7 %copy-start.6 = (bf16[512,512]{1,0:T(8,128)(2,1)S(1)}, bf16[512,512]{1,0:T(8,128)(2,1)}, u32[]{:S(2)}) copy-start(bf16[512,512]{1,0:T(8,128)(2,1)} %get-tuple-element.53.pair) | copy-start | bytes 1572868
  31.3 17.1 %all-to-all-start.1 = ((bf16[16,192,128]{2,1,0:T(8,128)(2,1)}), bf16[16,192,128]{2,1,0:T(8,128)(2,1)S(1)}, u32[]{:S(2)}, u32[]{:S(2)}) async-start(bf16[16,192,128]{2,1,0:T(8,128)(2,1)} %bitcast.48), calls=%async_computation.1 | async-start | bytes 1572864 | tf_op jit(solution)/shard_map/all_to_all | solution.py:642
  37.1 77.3 %all-gather.9.cloned.1.call-start = ((), (), s32[]{:S(2)}) async-start(), calls=%async_computation.14 | async-start | bytes 1179648 | tf_op jit(solution)/shard_map/all_gather | solution.py:710
  48.4 12.0 %copy-start = (bf16[16,192,128]{2,1,0:T(8,128)(2,1)}, bf16[16,192,128]{2,1,0:T(8,128)(2,1)S(1)}, u32[]{:S(2)}) copy-start(bf16[16,192,128]{2,1,0:T(8,128)(2,1)S(1)} %all-to-all-done.1) | copy-start | bytes 2359300
  49.2 65.2 %reduce-scatter.3.cloned.1.call-start = ((), (), s32[]{:S(2)}) async-start(), calls=%async_computation.12 | async-start | bytes 2359296 | tf_op jit(solution)/shard_map/reduce_scatter | solution.py:729
  49.3 11.2 %collective-permute-start = (bf16[512,512]{1,0:T(8,128)(2,1)S(1)}, bf16[512,512]{1,0:T(8,128)(2,1)S(1)}, u32[]{:S(2)}, u32[]{:S(2)}) collective-permute-start(bf16[512,512]{1,0:T(8,128)(2,1)S(1)} %copy-done.6), channel_id=1, source_target_pairs={{0,1},{1,0},{2,3},{3,2},{4,5},{5,4},{6,7},{7,6},{8,9},{9,8},{10,11... | collective-permute-start | bytes 1572872 | tf_op jit(solution)/shard_map/ppermute | solution.py:638
  60.4 0.8 copy-start.7
  68.8 1.0 copy-start.9
  68.8 1.2 copy-start.8
  68.9 77.5 %all-gather.11.cloned.1.call-start = ((), (), s32[]{:S(2)}) async-start(), calls=%async_computation.15 | async-start | bytes 1179648 | tf_op jit(solution)/shard_map/all_gather | solution.py:740
  69.9 15.2 %collective-permute-start.1 = (bf16[512,512]{1,0:T(8,128)(2,1)S(1)}, bf16[512,512]{1,0:T(8,128)(2,1)S(1)}, u32[]{:S(2)}, u32[]{:S(2)}) collective-permute-start(bf16[512,512]{1,0:T(8,128)(2,1)S(1)} %copy-done.9), channel_id=1, source_target_pairs={{0,1},{1,0},{2,3},{3,2},{4,5},{5,4},{6,7},{7,6},{8,9},{9,8},{10,11... | collective-permute-start | bytes 1572872 | tf_op jit(solution)/shard_map/ppermute | solution.py:638
  85.1 0.8 copy-start.3
  92.2 78.5 %reduce-scatter.5.cloned.1.call-start = ((), (), s32[]{:S(2)}) async-start(), calls=%async_computation.13 | async-start | bytes 3833856 | tf_op jit(solution)/shard_map/reduce_scatter | solution.py:763
  123.6 3.6 %copy-start.10 = (bf16[256,512]{1,0:T(8,128)(2,1)S(1)}, bf16[256,512]{1,0:T(8,128)(2,1)}, u32[]{:S(2)}) copy-start(bf16[256,512]{1,0:T(8,128)(2,1)} %get-tuple-element.67.part) | copy-start | bytes 786436
  123.6 11.5 %all-to-all-start.4 = ((bf16[8,192,128]{2,1,0:T(8,128)(2,1)}), bf16[8,192,128]{2,1,0:T(8,128)(2,1)S(1)}, u32[]{:S(2)}, u32[]{:S(2)}) async-start(bf16[8,192,128]{2,1,0:T(8,128)(2,1)} %get-tuple-element.68), calls=%async_computation.5 | async-start | bytes 786432 | tf_op jit(solution)/shard_map/all_to_all | solution.py:642
  127.2 7.9 %collective-permute-start.2 = (bf16[256,512]{1,0:T(8,128)(2,1)S(1)}, bf16[256,512]{1,0:T(8,128)(2,1)S(1)}, u32[]{:S(2)}, u32[]{:S(2)}) collective-permute-start(bf16[256,512]{1,0:T(8,128)(2,1)S(1)} %copy-done.10), channel_id=1, source_target_pairs={{0,1},{1,0},{2,3},{3,2},{4,5},{5,4},{6,7},{7,6},{8,9},{9,8},{10,11... | collective-permute-start | bytes 786440 | tf_op jit(solution)/shard_map/ppermute | solution.py:638
  135.1 0.7 copy-start.5
  135.1 0.8 copy-start.4
  140.4 20.1 %all-to-all-start.5 = ((bf16[16,320,128]{2,1,0:T(8,128)(2,1)}), bf16[16,320,128]{2,1,0:T(8,128)(2,1)S(1)}, u32[]{:S(2)}, u32[]{:S(2)}) async-start(bf16[16,320,128]{2,1,0:T(8,128)(2,1)} %bitcast.38), calls=%async_computation.6 | async-start | bytes 2621440 | tf_op jit(solution)/shard_map/all_to_all | solution.py:642
  146.3 98.3 %all-gather.15.cloned.1.call-start = ((), (), s32[]{:S(2)}) async-start(), calls=%async_computation.17 | async-start | bytes 2359296 | tf_op jit(solution)/shard_map/all_gather | solution.py:790
  160.5 10.2 %copy-start.1 = (bf16[16,320,128]{2,1,0:T(8,128)(2,1)}, bf16[16,320,128]{2,1,0:T(8,128)(2,1)S(1)}, u32[]{:S(2)}) copy-start(bf16[16,320,128]{2,1,0:T(8,128)(2,1)S(1)} %all-to-all-done.5) | copy-start | bytes 3932164
  175.7 81.3 %all-gather.13.cloned.1.call-start = ((), (), s32[]{:S(2)}) async-start(), calls=%async_computation.16 | async-start | bytes 4128768 | tf_op jit(solution)/shard_map/all_gather | solution.py:797
  241.1 16.0 %all-to-all-start.9 = ((bf16[8,208,256]{2,1,0:T(8,128)(2,1)}), bf16[8,208,256]{2,1,0:T(8,128)(2,1)S(1)}, u32[]{:S(2)}, u32[]{:S(2)}) async-start(bf16[8,208,256]{2,1,0:T(8,128)(2,1)} %sum.1), calls=%async_computation.11 | async-start | bytes 1703936 | tf_op jit(solution)/shard_map/all_to_all | solution.py:642
  257.0 0.9 copy-start.2
Sparse Core Ops, SparseCore 0:
  49.3 25.1 all-gather.8
  77.5 30.3 reduce-scatter.2
  109.7 25.2 all-gather.10
  137.9 32.7 reduce-scatter.4
  175.8 27.4 all-gather.14
  208.7 41.6 all-gather.12

commit v5 on v4

--- a/solution.py
+++ b/solution.py
@@ -43,6 +43,16 @@
         return pl.BlockSpec(shape[:-2] + (self.rows, shape[-1]), lambda i: place)
 
 
+class Lead:
+    def __init__(self, array, count, at):
+        self.array, self.count, self.at = array, count, at
+
+    def spec(self):
+        rest = self.array.shape[1:]
+        place = (self.at,) + (0,) * len(rest)
+        return pl.BlockSpec((self.count,) + rest, lambda i: place)
+
+
 class Layer:
     def __init__(self, array, index):
         self.array, self.index = array, index
@@ -59,9 +69,9 @@
 
 def call(body, out_shape, args, name, scratch=(), smem_first=False):
     specs = [
-        a.spec() if isinstance(a, (Layer, Rows, After)) else whole(a.shape) for a in args
+        a.spec() if isinstance(a, (Layer, Lead, Rows, After)) else whole(a.shape) for a in args
     ]
-    args = [a.array if isinstance(a, (Layer, Rows, After)) else a for a in args]
+    args = [a.array if isinstance(a, (Layer, Lead, Rows, After)) else a for a in args]
     if smem_first:
         specs[0] = pl.BlockSpec(memory_space=pltpu.SMEM)
     return pl.pallas_call(
@@ -159,8 +169,10 @@
     return put
 
 
-def pack_qkv(out, row):
-    def put(e, value):
+def pack_qkv(out, row, d_b_qkv):
+    def put(e, attn_t, own):
+        d_b_qkv[e : e + 1] = mm(jnp.ones((8, own.shape[1]), BF), own, 1, 1)[0:1]
+        value = mm(attn_t, own, 1, 1)
         for p in range(8):
             out[p, row + 64 * e : row + 64 * (e + 1), :] = value[64 * p : 64 * (p + 1)].astype(BF)
 
@@ -222,7 +234,7 @@
     return (key <= query) & (key >= start[:, c * CHUNK : (c + 1) * CHUNK])
 
 
-def attend_body(at, recv, w_qkv, w_out, send, lse, ctx, start_out):
+def attend_body(at, recv, w_qkv, w_out, _, send, lse, ctx, start_out):
     for layer in range(2):
         piece = jnp.where(at[2] // 2 == 3, w_out[layer], w_qkv[layer, 0])
         for b in range(8):
@@ -300,7 +312,7 @@
             send[b, t, row + HEAD : row + 2 * HEAD] = dv[:, b * BLK : (b + 1) * BLK].astype(BF)
 
 
-def attend_back_body(recv, recv_d, start, lse, ctx, _, send, dk, dv):
+def attend_back_body(recv, recv_d, start, lse, ctx, send, dk, dv):
     ride = recv_d[0, 64:192].astype(F32)
     for i in range(1, 8):
         ride = ride + recv_d[i, 64:192].astype(F32)
@@ -347,7 +359,7 @@
 
 
 def out_other(others):
-    stacked = other_matrix(others, 3)
+    stacked = other_matrix(others, 0)
     return jnp.concatenate([stacked[0:256], stacked[256:512]], 1)
 
 
@@ -388,7 +400,7 @@
 
 
 def norm_back(
-    t, x, g, d_mlp_in, recv, row, w_own, others, cs, gain, bias, layer, d_qkv, d_b_qkv, d_norm
+    t, x, g, d_mlp_in, recv, row, w_own, others, cs, gain, bias, layer, d_qkv, d_norm
 ):
     normed, inv = norm_rows(x)
     attn_in = (normed * gain[layer, 0:1] + bias[layer, 0:1]).astype(BF)
@@ -411,9 +423,7 @@
         first, second = ordered(t, w_own[e], other_matrix(others, e))
         term = mm(first, halves[0]) + mm(second, halves[1])
         d_attn_t = term if d_attn_t is None else d_attn_t + term
-        own = jnp.where(t == 0, halves[0], halves[1])
-        d_qkv(e, mm(attn_t, own, 1, 1))
-        d_b_qkv[e : e + 1] = mm(jnp.ones((8, own.shape[1]), BF), own, 1, 1)[0:1]
+        d_qkv(e, attn_t, jnp.where(t == 0, halves[0], halves[1]))
     d_attn_in = d_attn_t.T
     d_norm[0:1] = jnp.sum(d_attn_in * normed, 0, keepdims=True)
     d_norm[1:2] = jnp.sum(d_mlp_in * normed, 0, keepdims=True)
@@ -428,23 +438,20 @@
 
 
 def turn_point_body(
-    at, stream, parts, parts_other, recv, w_out, w_qkv, others, out_bias,
-    gain, bias, cot, cs, x, act, slope, w_up, w_down, w_out_first, recv_first, sums_a,
-    block_out, g_out, send, grads, part, d_b_up, d_b_qkv, d_norm, d_sum,
+    at, stream, parts, parts_other, recv, w_qkv, others, gain, bias, cot, cs, w_out_first, sums_a,
+    g_out, send, d_qkv, d_norm, d_sum,
 ):
-    t = at[1]
-    branch = parts[0:256].astype(F32) + parts_other[0:256].astype(F32)
-    branch = branch + branch_of(t, recv, w_out[...], out_other(others))
-    block_out[...] = stream[...] + branch + out_bias[1, 0:1] + out_bias[1, 1:2]
-    d_mlp_in = parts[256:512].astype(F32) + parts_other[256:512].astype(F32)
+    def keep(e, _, own):
+        d_qkv[e] = own
+
+    d_mlp_in = parts[...].astype(F32) + parts_other[...].astype(F32)
     g = norm_back(
-        t, stream[...], cot[...], d_mlp_in, recv, HEAD, w_qkv, others, cs, gain, bias, 1,
-        pack_qkv(grads, 0), d_b_qkv, d_norm,
+        at[1], stream[...], cot[...], d_mlp_in, recv, HEAD, w_qkv, others, cs, gain, bias, 1,
+        keep, d_norm,
     )
     g_out[...] = g
-    g_b = g.astype(BF)
     d_sum[...] = jnp.sum(g, 0, keepdims=True)
-    d_ctx = mm(w_out_first[...], g_b, 1, 1)
+    d_ctx = mm(w_out_first[...], g.astype(BF), 1, 1)
     for s in range(2):
         for h in range(4):
             send[s * 4 + h, 0:HEAD] = d_ctx[
@@ -455,24 +462,41 @@
             send[q, 64 + 64 * c : 128 + 64 * c] = sums_a[
                 64 * q : 64 * (q + 1), BLK * c : BLK * (c + 1)
             ]
-    pack_out(grads, 704, own_ctx(t, recv), cot[...].astype(BF))
-    pack_out(grads, 768, own_ctx(t, recv_first), g_b)
+
+
+def weights_body(
+    at, stream, parts, parts_other, recv, w_out, others, out_bias, gain, bias, cot, x, g, d_qkv,
+    act, slope, w_up, w_down, recv_first,
+    block_out, grads, part, d_b_up, d_b_qkv,
+):
+    t = at[1]
+    g_b = g[...].astype(BF)
     normed, _ = norm_rows(x[...])
     mlp_in = (normed * gain[0, 1:2] + bias[0, 1:2]).astype(BF)
     part[...] = feed_back(
         g_b, act, slope, mlp_in, w_up, w_down, pack_up(grads, 192), pack_down(grads, 448), d_b_up
     ).astype(BF)
+    branch = parts[...].astype(F32) + parts_other[...].astype(F32)
+    branch = branch + branch_of(t, recv, w_out[...], out_other(others))
+    block_out[...] = stream[...] + branch + out_bias[1, 0:1] + out_bias[1, 1:2]
+    normed, _ = norm_rows(stream[...])
+    attn_t = (normed * gain[1, 0:1] + bias[1, 0:1]).T.astype(BF)
+    put = pack_qkv(grads, 0, d_b_qkv)
+    for e in range(3):
+        put(e, attn_t, d_qkv[e])
+    pack_out(grads, 704, own_ctx(t, recv), cot[...].astype(BF))
+    pack_out(grads, 768, own_ctx(t, recv_first), g_b)
 
 
 def last_body(
     at, x, g, part, part_other, recv, w_qkv, others, cs, gain, bias,
-    d_b_up0, d_b_up1, d_b_qkv1, d_norm1, d_sum0, d_sum1, sums_b,
+    d_b_up0, d_b_up1, d_b_qkv1, d_norm1, d_sum0, d_sum1,
     in_grad, grads, sums_a, d_b_qkv0, d_norm0,
 ):
     d_mlp_in = part[...].astype(F32) + part_other[...].astype(F32)
     in_grad[...] = norm_back(
         at[1], x[...], g[...], d_mlp_in, recv, 0, w_qkv, others, cs, gain, bias, 0,
-        pack_qkv(grads, 0), d_b_qkv0, d_norm0,
+        pack_qkv(grads, 0, d_b_qkv0), d_norm0,
     )
     for q in range(8):
         both_planes = recv[q, :, 192:320]
@@ -497,8 +521,6 @@
         have = rows[p] if p < len(rows) else []
         fill = [jnp.zeros((16 - len(have), 256), F32)]
         grads[p, 192:208, :] = jnp.concatenate(have + fill, 0).astype(BF)
-        rows_b = sums_b[104 * p : 104 * (p + 1)].astype(F32)
-        grads[p, 208:320, :] = jnp.concatenate([rows_b, jnp.zeros((8, 256), F32)], 0).astype(BF)
 
 
 def sum_of(got):
@@ -508,17 +530,19 @@
     return total.astype(BF)
 
 
-def sum_both_body(got, late, early):
+def mix_body(got, early, first, out, first_out):
+    total = sum_of(got).astype(F32)
+    for q in range(8):
+        mine = [early[104 * q : 104 * (q + 1)].astype(F32), total[24 * q : 24 * (q + 1)]]
+        out[q, 0:128] = jnp.concatenate(mine, 0).astype(BF)
+        out[q, 128:144] = total[192:208].astype(BF) if q == 0 else jnp.zeros((16, 256), BF)
+    first_out[...] = first[...]
+
+
+def sum_body(got, out):
     total = sum_of(got)
     for q in range(8):
-        late[q] = total[0:208]
-        early[q] = total[208:320]
-
-
-def sum_body(got, late):
-    total = sum_of(got)
-    for q in range(8):
-        late[q] = total
+        out[q] = total
 
 
 def unpack_first_body(first, g_up, g_down):
@@ -530,13 +554,14 @@
 
 
 def unpack_rest_body(
-    rest, last, _, __, g_up, g_down, g_qkv, g_out, g_b_up, g_b_qkv, g_sum, g_gain, g_bias
+    rest, _, __, g_up, g_down, g_qkv, g_out, g_b_up, g_b_qkv, g_sum, g_gain, g_bias
 ):
     p = pl.program_id(0)
-    for e in range(3):
-        g_qkv[0, e] = last[64 * e : 64 * (e + 1)].astype(F32)
     for q in range(8):
-        block = rest[q, 0:104].astype(F32)
+        block = rest[q, 0:128].astype(F32)
+        for i in range(3):
+            row = 24 * q + 8 * i
+            g_qkv[0, row // 64, row % 64 : row % 64 + 8] = block[104 + 8 * i : 112 + 8 * i]
         for i in range(13):
             row = 104 * q + 8 * i
             value = block[8 * i : 8 * (i + 1)]
@@ -552,7 +577,7 @@
                 c, r = divmod((row - 704) % 64, 32)
                 g_out[1 - (row - 704) // 64, r : r + 8, 256 * c : 256 * (c + 1)] = value
 
-    tiny = last[192:208].astype(F32)
+    tiny = rest[0, 128:144].astype(F32)
 
     @pl.when(p == 0)
     def _():
@@ -591,7 +616,7 @@
 DOWN = (2, 1024, 512)
 
 
-def unpack(first, rest, last):
+def unpack(first, rest):
     def place(layer):
         return [
             pl.BlockSpec((1, 64, 1024), lambda p: (layer, p, 0)),
@@ -622,16 +647,15 @@
         grid=(8,),
         out_shape=[jax.ShapeDtypeStruct(shape, F32) for shape in [UP, DOWN] + [o[0] for o in outs]],
         in_specs=[
-            pl.BlockSpec((None, 8, 112, 256), lambda p: (p, 0, 0, 0)),
-            pl.BlockSpec((None, 208, 256), lambda p: (p, 0, 0)),
+            pl.BlockSpec((None, 8, 144, 256), lambda p: (p, 0, 0, 0)),
             pl.BlockSpec(memory_space=pl.ANY),
             pl.BlockSpec(memory_space=pl.ANY),
         ],
         out_specs=place(0) + [spec for _, spec in outs],
-        input_output_aliases={2: 0, 3: 1},
+        input_output_aliases={1: 0, 2: 1},
         compiler_params=params,
         name="unpack_rest",
-    )(rest, last, g_up, g_down)
+    )(rest, g_up, g_down)
 
 
 def swap(value):
@@ -647,7 +671,7 @@
     return exchange(flat, ("context", "tensor")).reshape(value.shape)
 
 
-def attend(at, recv, wq, w_out):
+def attend(at, recv, wq, w_out, after):
     outs = [((8, 2, 192, BLK), BF), ((1, 1024), F32), ((HEAD, 1024), F32), ((1, 1024), jnp.int32)]
 
     def all_of(shape):
@@ -666,12 +690,13 @@
                     lambda i, at: (0, jnp.minimum(at[2] // 2, 2), (at[2] % 2) * 8 + at[0], 0),
                 ),
                 pl.BlockSpec((2, 32, 256), lambda i, at: (0, at[0], at[2] % 2)),
+                pl.BlockSpec(memory_space=pl.ANY),
             ],
             out_specs=[all_of(s) for s, _ in outs],
         ),
         compiler_params=pltpu.CompilerParams(vmem_limit_bytes=56 * 1024 * 1024),
         name="attend",
-    )(at, recv, wq, w_out)
+    )(at, recv, wq, w_out, after)
 
 
 def shards(
@@ -704,7 +729,7 @@
     )
     pair_other = swap(pair)
     recv = exchange(send, "context")
-    ctx_send, lse, ctx, start = attend(at, recv, wq, w_out)
+    ctx_send, lse, ctx, start = attend(at, recv, wq, w_out, pair_other)
     recv_ctx = both(ctx_send)
     piece = lax.dynamic_index_in_dim(recv_ctx, 1 - at[1], 1, keepdims=False)[:, 128:192]
     others1 = lax.all_gather(piece, "dp")
@@ -739,34 +764,46 @@
     )
     others0 = lax.all_gather(piece, "dp")
     recv_grad = both(both_send)
-    block_out, g, send, grads_b, part_g, d_b_up0, d_b_qkv1, d_norm1, d_sum0 = call(
+    g, send, d_qkv, d_norm1, d_sum0 = call(
         turn_point_body,
         [
             ((rows, width), F32),
+            ((8, 192, BLK), BF),
+            ((3, 256, rows), BF),
+            ((4, width), F32),
+            ((1, width), F32),
+        ],
+        (
+            at, stream, Rows(parts, rows, 1), Rows(parts_other, rows, 1), recv_grad, Layer(wq, 1),
+            others1, ln_gain, ln_bias, cot, cs, Layer(w_out, 0), sums_a,
+        ),
+        "turn_point",
+        smem_first=True,
+    )
+    recv_d = exchange(send, "context")
+    block_out, grads_b, part_g, d_b_up0, d_b_qkv1 = call(
+        weights_body,
+        [
             ((rows, width), F32),
-            ((8, 192, BLK), BF),
             ((8, 832, 256), BF),
             ((rows, width), BF),
             ((1, 1024), F32),
             ((3, 256), F32),
-            ((4, width), F32),
-            ((1, width), F32),
         ],
         (
-            at, stream, parts, parts_other, recv_grad, Layer(w_out, 1), Layer(wq, 1), others1,
-            out_bias, ln_gain, ln_bias, cot, cs, x, act, slope, Layer(w_up, 0), Layer(w_down, 0),
-            Layer(w_out, 0), Rows(recv_ctx, HEAD), sums_a,
+            at, stream, Rows(parts, rows), Rows(parts_other, rows), Rows(recv_grad, HEAD),
+            Layer(w_out, 1), Lead(others1, 2, 3), out_bias, ln_gain, ln_bias, cot, x, g, d_qkv, act,
+            slope, Layer(w_up, 0), Layer(w_down, 0), Rows(recv_ctx, HEAD),
         ),
-        "turn_point",
+        "weights",
         smem_first=True,
     )
     sums_b = lax.psum_scatter(grads_b, "dp", scatter_dimension=0)
     part_g_other = swap(part_g)
-    recv_d = exchange(send, "context")
     (back_send,) = call(
         attend_back_body,
         [((8, 2, 320, BLK), BF)],
-        (recv, recv_d, start, lse, ctx, After(part_g_other)),
+        (recv, recv_d, start, lse, ctx),
         "attend_back",
         scratch=[pltpu.VMEM((HEAD, 1024), F32), pltpu.VMEM((HEAD, 1024), F32)],
     )
@@ -775,29 +812,28 @@
         last_body,
         [
             ((rows, width), F32),
-            ((8, 320, 256), BF),
+            ((8, 208, 256), BF),
             ((512, 256), BF),
             ((3, 256), F32),
             ((4, width), F32),
         ],
         (
             at, x, g, part_g, part_g_other, recv_grad0, Layer(wq, 0), others0, cs,
-            ln_gain, ln_bias, d_b_up0, d_b_up1, d_b_qkv1, d_norm1, d_sum0, d_sum1, sums_b,
+            ln_gain, ln_bias, d_b_up0, d_b_up1, d_b_qkv1, d_norm1, d_sum0, d_sum1,
         ),
         "last",
         smem_first=True,
     )
+    mixed, sums_a = call(
+        mix_body,
+        [((8, 144, 256), BF), ((512, 256), BF)],
+        (exchange(grads_c, "dp"), sums_b, sums_a),
+        "mix",
+    )
     full_a = lax.all_gather(sums_a, "dp")
-    late, early = call(
-        sum_both_body,
-        [((8, 208, 256), BF), ((8, 112, 256), BF)],
-        (exchange(grads_c, "context"),),
-        "sum_both",
-    )
-    full_b = lax.all_gather(exchange(early, "context"), "dp")
-    (late,) = call(sum_body, [((8, 208, 256), BF)], (exchange(late, "dp"),), "sum")
-    full_c = exchange(late, "context")
-    g_up, g_down, g_qkv, g_out, g_b_up, g_b_qkv, g_sum, g_gain, g_bias = unpack(full_a, full_b, full_c)
+    (summed,) = call(sum_body, [((8, 144, 256), BF)], (exchange(mixed, "context"),), "sum")
+    full_b = lax.all_gather(exchange(summed, "context"), "dp")
+    g_up, g_down, g_qkv, g_out, g_b_up, g_b_qkv, g_sum, g_gain, g_bias = unpack(full_a, full_b)
     return (
         block_out.reshape(tokens_in.shape),
         in_grad.reshape(tokens_in.shape),

time: 274 us -> 284 us (1.036)
  waiting for transfers between devices: 59.7 us -> 66.4 us
  blocking collectives: 112 us -> 116 us
    all_gather x1, waiting for transfers between devices: 0.01 us -> 28.7 us  [shards(): full_b = lax.all_gather(exchange(summed, 'context'), 'dp')]
    all_to_all x4 -> x2, waiting for transfers between devices: 31.8 us -> 11.2 us  [exchange(): return lax.all_to_all(value, axes, 0, 0)]
    reduce_scatter x1, waiting for transfers between devices: 10.2 us -> 0.01 us  [shards(): sums_b = lax.psum_scatter(grads_b, 'dp', scatter_dimension=0)]
    all_to_all x4 -> x2, starting transfers between devices: 18.8 us -> 10.8 us  [exchange(): return lax.all_to_all(value, axes, 0, 0)]
    ppermute x3, starting transfers between devices: 1.42 us -> 7.74 us  [swap(): return lax.ppermute(value, 'tensor', [(0, 1), (1, 0)])]
    reduce_scatter x1, waiting for transfers between devices: 0.01 us -> 5.85 us  [shards(): sums_a = lax.psum_scatter(grads_a, 'dp', scatter_dimension=0)]
    all_to_all x6 -> x7, blocking collectives: 112 us -> 116 us  [exchange(): return lax.all_to_all(value, axes, 0, 0)]
    ppermute x3, waiting for transfers between devices: 17.6 us -> 20.5 us  [swap(): return lax.ppermute(value, 'tensor', [(0, 1), (1, 0)])]
  transfers between devices with their start and end apart: 13 -> 11, of which waited for: 6 -> 4; matrix products, arithmetic and copies ran while one was open for 0% -> 0% of each run, Pallas kernels for 14% -> 15%
where the time goes in v5:
time: 284 us; the launch traced here: 283 us
  blocking collectives  116 us (41%)
  waiting for transfers between devices  66.4 us (23%)
  Pallas kernels  62.5 us (22%)
  starting transfers between devices  18.8 us (7%)
  between operations  14.2 us (5%)
  local copies, waits for them, and re-layouts  4.54 us (2%)
    all_to_all x7, blocking collectives, exchange(): return lax.all_to_all(value, axes, 0, 0)  116 us
    pallas_call x9, Pallas kernels, call(): pl.pallas_call(body, grid=(1,), out_shape=[jax.ShapeDtypeStruct(s, d) for...  44.3 us
    all_gather x1, waiting for transfers between devices, shards(): full_b = lax.all_gather(exchange(summed, 'context'), 'dp')  28.7 us
    ppermute x3, waiting for transfers between devices, swap(): return lax.ppermute(value, 'tensor', [(0, 1), (1, 0)])  20.5 us
    all_to_all x2, waiting for transfers between devices, exchange(): return lax.all_to_all(value, axes, 0, 0)  11.2 us
    all_to_all x2, starting transfers between devices, exchange(): return lax.all_to_all(value, axes, 0, 0)  10.8 us
    ppermute x3, starting transfers between devices, swap(): return lax.ppermute(value, 'tensor', [(0, 1), (1, 0)])  7.74 us
    pallas_call x1, Pallas kernels, unpack(): pl.pallas_call(unpack_rest_body, grid=(8,), out_shape=[jax.ShapeDtypeStru...  7.57 us
  transfers between devices with their start and end apart: 11, of which 4 were waited for; matrix products, arithmetic and copies ran while one was open for 0% of the time, Pallas kernels for 15%

profile of v5, /device:TPU:1, one launch (start us, length us, event | category | flops | bytes accessed | tf_op | source)
XLA Modules:
  0.0 282.7 jit_solution(13100702994674420959)
XLA Ops:
  7.8 4.8 %norm_qkv_feed.1 = (bf16[8,208,128]{2,1,0:T(8,128)(2,1)}, bf16[512,512]{1,0:T(8,128)(2,1)}, bf16[256,1024]{1,0:T(8,128)(2,1)}, f32[256,1024]{1,0:T(8,128)}, f32[2,2,8,128]{3,2,1,0:T(8,128)}) custom-call(s32[3]{0:T(128)} %pad_add_fusion.at, s32[2,128]{1,0:T(2,128)} %pos.1, f32[8,1]{1,0:T(8,128)} %constant.27.freqs, f32[256,512]{1,0:T(8,128)} %bitcast.36, ...), custom_call_target="tpu_custom_call" | custom-call | tf_op jit(solution)/shard_map/norm_qkv_feed/pallas_call | solution.py:77
  12.6 4.4 %collective-permute-start = (bf16[512,512]{1,0:T(8,128)(2,1)}, bf16[512,512]{1,0:T(8,128)(2,1)S(1)}, u32[]{:S(2)}, u32[]{:S(2)}) collective-permute-start(bf16[512,512]{1,0:T(8,128)(2,1)} %get-tuple-element.54.pair), channel_id=1, source_target_pairs={{0,1},{1,0},{2,3},{3,2},{4,5},{5,4},{6,7},{7,6},{8,9},{9,8},{10,11... | collective-permute-start | bytes 1572872 | tf_op jit(solution)/shard_map/ppermute | solution.py:662
  17.0 16.7 %all_to_all.45.recv = bf16[8,208,128]{2,1,0:T(8,128)(2,1)} all-to-all(bf16[8,208,128]{2,1,0:T(8,128)(2,1)} %get-tuple-element.55), channel_id=1, replica_groups=mesh['dp'=8,'context'=8,'tensor'=2] {'context'}, dimensions={0} | all-to-all | bytes 851968 | tf_op jit(solution)/shard_map/all_to_all | solution.py:666
  34.5 4.7 %attend.1 = (bf16[8,2,192,128]{3,2,1,0:T(8,128)(2,1)}, f32[1,1024]{1,0:T(1,128)}, f32[64,1024]{1,0:T(8,128)}, s32[1,1024]{1,0:T(1,128)}) custom-call(s32[3]{0:T(128)} %pad_add_fusion.at, bf16[8,208,128]{2,1,0:T(8,128)(2,1)} %all_to_all.45.recv, bf16[2,3,512,256]{3,2,1,0:T(8,128)(2,1)} %bitcast.26, bf16[2,256,512]{2,1,0:T(8,128)(2,1)} %w_out.7, ...), custom_call_target="tpu_custom_call" | custom-call | tf_op jit(solution)/shard_map/attend/pallas_call | solution.py:680
  39.2 5.4 %all-to-all-start.1 = ((bf16[16,192,128]{2,1,0:T(8,128)(2,1)}), bf16[16,192,128]{2,1,0:T(8,128)(2,1)S(1)}, u32[]{:S(2)}, u32[]{:S(2)}) async-start(bf16[16,192,128]{2,1,0:T(8,128)(2,1)} %bitcast.51), calls=%async_computation.1 | async-start | bytes 1572864 | tf_op jit(solution)/shard_map/all_to_all | solution.py:666
  44.7 11.2 %all-to-all-done.1 = bf16[16,192,128]{2,1,0:T(8,128)(2,1)S(1)} async-done(((bf16[16,192,128]{2,1,0:T(8,128)(2,1)}), bf16[16,192,128]{2,1,0:T(8,128)(2,1)S(1)}, u32[]{:S(2)}, u32[]{:S(2)}) %all-to-all-start.1) | async-done | bytes 786464 | tf_op jit(solution)/shard_map/all_to_all | solution.py:666
  56.8 7.6 %middle.1 = (f32[256,512]{1,0:T(8,128)}, bf16[8,256,128]{2,1,0:T(8,128)(2,1)}, bf16[8,512,256]{2,1,0:T(8,128)(2,1)}, bf16[512,512]{1,0:T(8,128)(2,1)}, f32[1,1024]{1,0:T(1,128)}, /*index=5*/f32[1,512]{1,0:T(1,128)}) custom-call(s32[3]{0:T(128)} %pad_add_fusion.at, f32[256,512]{1,0:T(8,128)} %bitcast.37, bf16[512,512]{1,0:T(8,128)(2,1)} %get-tuple-element.54.pair, ...), custom_call_target="tpu_custom_call" | custom-call | tf_op jit(solution)/shard_map/middle/pallas_call | solution.py:77
  64.8 13.1 %all_to_all.46.recv = bf16[8,256,128]{2,1,0:T(8,128)(2,1)} all-to-all(bf16[8,256,128]{2,1,0:T(8,128)(2,1)} %get-tuple-element.60), channel_id=1, replica_groups=mesh['dp'=8,'context'=8,'tensor'=2] {'context'}, dimensions={0} | all-to-all | bytes 1048576 | tf_op jit(solution)/shard_map/all_to_all | solution.py:666
  78.8 6.3 %attend_both.1 = (bf16[8,2,256,128]{3,2,1,0:T(8,128)(2,1)}, bf16[8,64,128]{2,1,0:T(8,128)(2,1)}) custom-call(s32[3]{0:T(128)} %pad_add_fusion.at, bf16[8,256,128]{2,1,0:T(8,128)(2,1)} %all_to_all.46.recv, s32[1,1024]{1,0:T(1,128)} %get-tuple-element.61.start, bf16[8,2,192,128]{3,2,1,0:T(8,128)(2,1)} %bitcast.32, bf16[512,512]{1,0:T(8,128)(2,1)} %copy-done.2), custom_call_target="tpu_custom_call" | custom-call | tf_op jit(solution)/shard_map/attend_both/pallas_call | solution.py:77
  85.2 24.4 %all_to_all.47 = bf16[16,256,128]{2,1,0:T(8,128)(2,1)} all-to-all(bf16[16,256,128]{2,1,0:T(8,128)(2,1)} %bitcast.49), channel_id=1, replica_groups=mesh['dp'=8,'context'=8,'tensor'=2] {'context','tensor'}, dimensions={0} | all-to-all | bytes 2097152 | tf_op jit(solution)/shard_map/all_to_all | solution.py:666
  109.5 5.8 %reduce-scatter.3.cloned.1.call-done = bf16[1,512,256]{2,1,0:T(8,128)(2,1)} async-done(((bf16[8,512,256]{2,1,0:T(8,128)(2,1)}), bf16[1,512,256]{2,1,0:T(8,128)(2,1)}) %reduce-scatter.3.cloned.1.call-update) | async-done | bytes 262160 | tf_op jit(solution)/shard_map/reduce_scatter | solution.py:754
  115.4 4.5 %turn_point.1 = (f32[256,512]{1,0:T(8,128)}, bf16[8,192,128]{2,1,0:T(8,128)(2,1)}, bf16[3,256,256]{2,1,0:T(8,128)(2,1)}, f32[4,512]{1,0:T(4,128)}, f32[1,512]{1,0:T(1,128)}) custom-call(s32[3]{0:T(128)} %pad_add_fusion.at, f32[256,512]{1,0:T(8,128)} %get-tuple-element.58.stream, bf16[512,512]{1,0:T(8,128)(2,1)} %get-tuple-element.59.parts, ...), custom_call_target="tpu_custom_call" | custom-call | tf_op jit(solution)/shard_map/turn_point/pallas_call | solution.py:77
  119.9 7.5 %weights.1 = (f32[256,512]{1,0:T(8,128)}, bf16[8,832,256]{2,1,0:T(8,128)(2,1)}, bf16[256,512]{1,0:T(8,128)(2,1)}, f32[1,1024]{1,0:T(1,128)}, f32[3,256]{1,0:T(4,128)}) custom-call(s32[3]{0:T(128)} %pad_add_fusion.at, f32[256,512]{1,0:T(8,128)} %get-tuple-element.58.stream, bf16[512,512]{1,0:T(8,128)(2,1)} %get-tuple-element.59.parts, ...), custom_call_target="tpu_custom_call" | custom-call | tf_op jit(solution)/shard_map/weights/pallas_call | solution.py:77
  128.4 11.7 %all_to_all.48.recv_d = bf16[8,192,128]{2,1,0:T(8,128)(2,1)} all-to-all(bf16[8,192,128]{2,1,0:T(8,128)(2,1)S(1)} %copy-done.4), channel_id=1, replica_groups=mesh['dp'=8,'context'=8,'tensor'=2] {'context'}, dimensions={0} | all-to-all | bytes 786432 | tf_op jit(solution)/shard_map/all_to_all | solution.py:666
  140.1 4.5 %attend_back.1 = bf16[8,2,320,128]{3,2,1,0:T(8,128)(2,1)} custom-call(bf16[8,208,128]{2,1,0:T(8,128)(2,1)} %all_to_all.45.recv, bf16[8,192,128]{2,1,0:T(8,128)(2,1)} %all_to_all.48.recv_d, s32[1,1024]{1,0:T(1,128)} %get-tuple-element.61.start, f32[1,1024]{1,0:T(1,128)} %get-tuple-element.71.lse, f32[64,1024]{1,0:T(8,128)} %get-tuple-element.72.ctx), custom_call_target="tpu_custom_call" | custom-call | tf_op jit(solution)/shard_map/attend_back/pallas_call | solution.py:77
  144.6 5.4 %all-to-all-start.5 = ((bf16[16,320,128]{2,1,0:T(8,128)(2,1)}), bf16[16,320,128]{2,1,0:T(8,128)(2,1)S(1)}, u32[]{:S(2)}, u32[]{:S(2)}) async-start(bf16[16,320,128]{2,1,0:T(8,128)(2,1)} %bitcast.40), calls=%async_computation.6 | async-start | bytes 2621440 | tf_op jit(solution)/shard_map/all_to_all | solution.py:666
  153.0 20.5 %collective-permute-done.2.part_other = bf16[256,512]{1,0:T(8,128)(2,1)S(1)} collective-permute-done((bf16[256,512]{1,0:T(8,128)(2,1)S(1)}, bf16[256,512]{1,0:T(8,128)(2,1)S(1)}, u32[]{:S(2)}, u32[]{:S(2)}) %collective-permute-start.2) | collective-permute-done | bytes 262176 | tf_op jit(solution)/shard_map/ppermute | solution.py:662
  174.7 4.8 %last.1 = (f32[256,512]{1,0:T(8,128)}, bf16[8,208,256]{2,1,0:T(8,128)(2,1)}, bf16[512,256]{1,0:T(8,128)(2,1)}, f32[3,256]{1,0:T(4,128)}, f32[4,512]{1,0:T(4,128)}) custom-call(s32[3]{0:T(128)} %pad_add_fusion.at, f32[256,512]{1,0:T(8,128)} %bitcast.39, f32[256,512]{1,0:T(8,128)} %get-tuple-element.64.g, bf16[256,512]{1,0:T(8,128)(2,1)} %get-tuple-element.69.part, ...), custom_call_target="tpu_custom_call" | custom-call | tf_op jit(solution)/shard_map/last/pallas_call | solution.py:77
  179.5 23.7 %all_to_all.49.got = bf16[8,208,256]{2,1,0:T(8,128)(2,1)} all-to-all(bf16[8,208,256]{2,1,0:T(8,128)(2,1)} %get-tuple-element.81), channel_id=1, replica_groups=mesh['dp'=8,'context'=8,'tensor'=2] {'dp'}, dimensions={0} | all-to-all | bytes 1703936 | tf_op jit(solution)/shard_map/all_to_all | solution.py:666
  205.6 13.8 %all_to_all.50.got = bf16[8,144,256]{2,1,0:T(8,128)(2,1)} all-to-all(bf16[8,144,256]{2,1,0:T(8,128)(2,1)} %get-tuple-element.84), channel_id=1, replica_groups=mesh['dp'=8,'context'=8,'tensor'=2] {'context'}, dimensions={0} | all-to-all | bytes 1179648 | tf_op jit(solution)/shard_map/all_to_all | solution.py:666
  221.4 12.1 %all_to_all.51 = bf16[8,144,256]{2,1,0:T(8,128)(2,1)} all-to-all(bf16[8,144,256]{2,1,0:T(8,128)(2,1)} %sum.1), channel_id=1, replica_groups=mesh['dp'=8,'context'=8,'tensor'=2] {'context'}, dimensions={0} | all-to-all | bytes 1179648 | tf_op jit(solution)/shard_map/all_to_all | solution.py:666
  233.6 6.0 %unpack_first.1 = (f32[2,512,1024]{2,1,0:T(8,128)}, f32[2,1024,512]{2,1,0:T(8,128)}) custom-call(bf16[8,512,256]{2,1,0:T(8,128)(2,1)} %bitcast.48), custom_call_target="tpu_custom_call" | custom-call | tf_op jit(solution)/shard_map/unpack_first/pallas_call | solution.py:627
  239.5 28.7 %all-gather.13.cloned.1.call-done = bf16[64,144,256]{2,1,0:T(8,128)(2,1)} async-done(((bf16[8,144,256]{2,1,0:T(8,128)(2,1)}), bf16[64,144,256]{2,1,0:T(8,128)(2,1)}) %all-gather.13.cloned.1.call-update) | async-done | bytes 4718608 | tf_op jit(solution)/shard_map/all_gather | solution.py:835
  268.2 7.6 %unpack_rest.1 = (f32[2,512,1024]{2,1,0:T(8,128)}, f32[2,1024,512]{2,1,0:T(8,128)}, f32[2,3,512,256]{3,2,1,0:T(8,128)}, f32[2,256,512]{2,1,0:T(8,128)}, f32[2,10...) custom-call(bf16[8,8,144,256]{3,2,1,0:T(8,128)(2,1)} %bitcast.42, ...), custom_call_target="tpu_custom_call", output_to_operand_aliasing={{0}: (1, {}), {1}: (2, {})} | custom-call | tf_op jit(solution)/shard_map/unpack_rest/pallas_call | solution.py:645
  (40 shorter events, 13.2 us)
Async XLA Ops:
  12.6 21.1 %collective-permute-start = (bf16[512,512]{1,0:T(8,128)(2,1)}, bf16[512,512]{1,0:T(8,128)(2,1)S(1)}, u32[]{:S(2)}, u32[]{:S(2)}) collective-permute-start(bf16[512,512]{1,0:T(8,128)(2,1)} %get-tuple-element.54.pair), channel_id=1, source_target_pairs={{0,1},{1,0},{2,3},{3,2},{4,5},{5,4},{6,7},{7,6},{8,9},{9,8},{10,11... | collective-permute-start | bytes 1572872 | tf_op jit(solution)/shard_map/ppermute | solution.py:662
  33.7 0.8 copy-start.3
  39.2 16.7 %all-to-all-start.1 = ((bf16[16,192,128]{2,1,0:T(8,128)(2,1)}), bf16[16,192,128]{2,1,0:T(8,128)(2,1)S(1)}, u32[]{:S(2)}, u32[]{:S(2)}) async-start(bf16[16,192,128]{2,1,0:T(8,128)(2,1)} %bitcast.51), calls=%async_computation.1 | async-start | bytes 1572864 | tf_op jit(solution)/shard_map/all_to_all | solution.py:666
  44.6 64.9 %all-gather.9.cloned.1.call-start = ((), (), s32[]{:S(2)}) async-start(), calls=%async_computation.13 | async-start | bytes 1179648 | tf_op jit(solution)/shard_map/all_gather | solution.py:735
  55.9 0.9 copy-start
  56.6 58.7 %reduce-scatter.3.cloned.1.call-start = ((), (), s32[]{:S(2)}) async-start(), calls=%async_computation.11 | async-start | bytes 2359296 | tf_op jit(solution)/shard_map/reduce_scatter | solution.py:754
  64.4 88.6 %all-gather.11.cloned.1.call-start = ((), (), s32[]{:S(2)}) async-start(), calls=%async_computation.14 | async-start | bytes 1179648 | tf_op jit(solution)/shard_map/all_gather | solution.py:765
  64.5 13.5 %collective-permute-start.1 = (bf16[512,512]{1,0:T(8,128)(2,1)}, bf16[512,512]{1,0:T(8,128)(2,1)S(1)}, u32[]{:S(2)}, u32[]{:S(2)}) collective-permute-start(bf16[512,512]{1,0:T(8,128)(2,1)} %get-tuple-element.59.parts), channel_id=1, source_target_pairs={{0,1},{1,0},{2,3},{3,2},{4,5},{5,4},{6,7},{7,6},{8,9},{9,8},{10,11... | collective-permute-start | bytes 1572872 | tf_op jit(solution)/shard_map/ppermute | solution.py:662
  78.0 0.8 copy-start.2
  85.1 118.1 %reduce-scatter.5.cloned.1.call-start = ((), (), s32[]{:S(2)}) async-start(), calls=%async_computation.12 | async-start | bytes 3833856 | tf_op jit(solution)/shard_map/reduce_scatter | solution.py:801
  127.4 1.0 copy-start.4
  127.4 22.7 %copy-start.5 = (bf16[256,512]{1,0:T(8,128)(2,1)S(1)}, bf16[256,512]{1,0:T(8,128)(2,1)}, u32[]{:S(2)}) copy-start(bf16[256,512]{1,0:T(8,128)(2,1)} %get-tuple-element.69.part) | copy-start | bytes 786436
  144.6 28.9 %all-to-all-start.5 = ((bf16[16,320,128]{2,1,0:T(8,128)(2,1)}), bf16[16,320,128]{2,1,0:T(8,128)(2,1)S(1)}, u32[]{:S(2)}, u32[]{:S(2)}) async-start(bf16[16,320,128]{2,1,0:T(8,128)(2,1)} %bitcast.40), calls=%async_computation.6 | async-start | bytes 2621440 | tf_op jit(solution)/shard_map/all_to_all | solution.py:666
  150.0 83.5 %all-gather.15.cloned.1.call-start = ((), (), s32[]{:S(2)}) async-start(), calls=%async_computation.16 | async-start | bytes 2359296 | tf_op jit(solution)/shard_map/all_gather | solution.py:833
  150.1 23.5 %collective-permute-start.2 = (bf16[256,512]{1,0:T(8,128)(2,1)S(1)}, bf16[256,512]{1,0:T(8,128)(2,1)S(1)}, u32[]{:S(2)}, u32[]{:S(2)}) collective-permute-start(bf16[256,512]{1,0:T(8,128)(2,1)S(1)} %copy-done.5), channel_id=1, source_target_pairs={{0,1},{1,0},{2,3},{3,2},{4,5},{5,4},{6,7},{7,6},{8,9},{9,8},{10,11... | collective-permute-start | bytes 786440 | tf_op jit(solution)/shard_map/ppermute | solution.py:662
  173.6 0.7 copy-start.6
  173.6 1.1 copy-start.1
  205.6 62.7 %all-gather.13.cloned.1.call-start = ((), (), s32[]{:S(2)}) async-start(), calls=%async_computation.15 | async-start | bytes 5308416 | tf_op jit(solution)/shard_map/all_gather | solution.py:835
Sparse Core Ops, SparseCore 0:
  56.8 25.1 all-gather.8
  85.0 30.3 reduce-scatter.2
  117.1 25.5 all-gather.10
  145.6 32.9 reduce-scatter.4
  205.7 23.3 all-gather.14
  233.7 34.5 all-gather.12

commit v6 on v3

--- a/solution.py
+++ b/solution.py
@@ -61,7 +61,7 @@
         in_specs=specs,
         out_specs=[whole(s) for s, _ in out_shape],
         scratch_shapes=list(scratch),
-        compiler_params=pltpu.CompilerParams(vmem_limit_bytes=56 * 1024 * 1024),
+        compiler_params=pltpu.CompilerParams(vmem_limit_bytes=63 * 1024 * 1024),
         name=name,
     )(*args)
 
@@ -173,10 +173,9 @@
 
 def first_body(
     at, pos, freqs, x, gain, bias, w_qkv, b_qkv, w_up, b_up, w_down, w_out,
-    send, pair, act, slope, cs, chunk,
+    send, pair, act, slope, cs,
 ):
-    chunk_of(at, w_qkv, w_out, chunk)
-    pair[256:512] = w_out[0]
+    pair[256:512] = w_out[...]
     for s in range(2):
         p = pos[s : s + 1, :].astype(F32)
         angle = freqs[...] * p
@@ -185,7 +184,7 @@
     normed, _ = norm_rows(x[...])
     attn_in = (normed * gain[0, 0:1] + bias[0, 0:1]).astype(BF)
     mlp_in = (normed * gain[0, 1:2] + bias[0, 1:2]).astype(BF)
-    send_qkv(send, attn_in, w_qkv.at[0], b_qkv, 0, cs)
+    send_qkv(send, attn_in, w_qkv, b_qkv, 0, cs)
     row = lax.broadcasted_iota(jnp.int32, (16, BLK), 0)
     token = at[0] * BLK + lax.broadcasted_iota(jnp.int32, (1, BLK), 1)
     for s in range(2):
@@ -476,16 +475,37 @@
         grads[p, 192:208, :] = jnp.concatenate(have + fill, 0).astype(BF)
 
 
-def chunk_of(at, w_qkv, w_out, out):
+def chunk_body(at, w_qkv, w_out, out):
     for layer in range(2):
         for e in range(3):
-            out[layer, e] = w_qkv[layer, e, pl.ds(pl.multiple_of(at[2] * 64, 64), 64), :]
-        rows = w_out[layer, pl.ds(pl.multiple_of(at[2] * 32, 32), 32), :]
-        out[layer, 3, 0:32] = rows[:, 0:256]
-        out[layer, 3, 32:64] = rows[:, 256:512]
-
-
-def mix_body(got, early, out):
+            out[layer, e] = w_qkv[layer, e]
+        out[layer, 3, 0:32] = w_out[layer, :, 0:256]
+        out[layer, 3, 32:64] = w_out[layer, :, 256:512]
+
+
+def chunk_of(at, wq, w_out):
+    return pl.pallas_call(
+        chunk_body,
+        out_shape=jax.ShapeDtypeStruct((2, 4, 64, 256), BF),
+        grid_spec=pltpu.PrefetchScalarGridSpec(
+            num_scalar_prefetch=1,
+            grid=(1,),
+            in_specs=[
+                pl.BlockSpec((2, 3, 64, 256), lambda i, at: (0, 0, at[2], 0)),
+                pl.BlockSpec((2, 32, 512), lambda i, at: (0, at[2], 0)),
+            ],
+            out_specs=pl.BlockSpec((2, 4, 64, 256), lambda i, at: (0, 0, 0, 0)),
+        ),
+        compiler_params=pltpu.CompilerParams(vmem_limit_bytes=63 * 1024 * 1024),
+        name="chunk",
+    )(at, wq, w_out)
+
+
+def hand_on_body(value, _, out):
+    out[...] = value[...]
+
+
+def mix_body(got, early, first, out, first_out):
     total = got[0].astype(F32)
     for i in range(1, 8):
         total = total + got[i].astype(F32)
@@ -493,79 +513,89 @@
         mine = [early[104 * q : 104 * (q + 1)].astype(F32), total[24 * q : 24 * (q + 1)]]
         out[q, 0:128] = jnp.concatenate(mine, 0).astype(BF)
         out[q, 128:144] = total[192:208].astype(BF) if q == 0 else jnp.zeros((16, 256), BF)
+    first_out[...] = first[...]
 
 
 def sum_body(got, out):
     total = got[0].astype(F32)
     for i in range(1, 8):
         total = total + got[i].astype(F32)
-    out[...] = total.astype(BF)
+    for q in range(8):
+        out[q] = total.astype(BF)
 
 
 def unpack_first_body(first, g_up, g_down):
-    for c in range(4):
-        g_up[0, :, 256 * c : 256 * (c + 1)] = first[64 * c : 64 * (c + 1)].astype(F32)
-    for c in range(2):
-        rows = first[256 + 128 * c : 256 + 128 * (c + 1)]
-        g_down[0, :, 256 * c : 256 * (c + 1)] = rows.astype(F32)
+    for k in range(2):
+        for c in range(4):
+            cols = slice(256 * c, 256 * (c + 1))
+            g_up[0, 64 * k : 64 * (k + 1), cols] = first[k, 64 * c : 64 * (c + 1)].astype(F32)
+        for c in range(2):
+            rows = first[k, 256 + 128 * c : 256 + 128 * (c + 1)]
+            cols = slice(256 * c, 256 * (c + 1))
+            g_down[0, 128 * k : 128 * (k + 1), cols] = rows.astype(F32)
 
 
 def unpack_rest_body(rest, _, __, g_up, g_down, g_qkv, g_out, g_b_up, g_b_qkv, g_sum, g_gain, g_bias):
     p = pl.program_id(0)
-
-    def early(row):
-        return rest[row // 104, row % 104 : row % 104 + 8].astype(F32)
-
-    def late(row):
-        return rest[row // 24, 104 + row % 24 : 104 + row % 24 + 8].astype(F32)
-
-    for k in range(0, 64, 8):
-        for e in range(3):
-            g_qkv[0, e, k : k + 8] = late(64 * e + k)
-            g_qkv[1, e, k : k + 8] = early(64 * e + k)
-        for c in range(4):
-            g_up[0, k : k + 8, 256 * c : 256 * (c + 1)] = early(192 + 64 * c + k)
-    for k in range(0, 32, 8):
-        for c in range(2):
-            g_out[0, k : k + 8, 256 * c : 256 * (c + 1)] = early(768 + 32 * c + k)
-            g_out[1, k : k + 8, 256 * c : 256 * (c + 1)] = early(704 + 32 * c + k)
-    for k in range(0, 128, 8):
-        for c in range(2):
-            g_down[0, k : k + 8, 256 * c : 256 * (c + 1)] = early(448 + 128 * c + k)
-
-    tiny = rest[0, 128:144].astype(F32)
+    for k in range(2):
+        for q in range(8):
+            block = rest[k, q, 0:128].astype(F32)
+            for i in range(16):
+                value = block[8 * i : 8 * (i + 1)]
+                row = 104 * q + 8 * i
+                if i >= 13:
+                    row = 24 * q + 8 * (i - 13)
+                    r = 64 * k + row % 64
+                    g_qkv[0, row // 64, r : r + 8] = value
+                elif row < 192:
+                    r = 64 * k + row % 64
+                    g_qkv[1, row // 64, r : r + 8] = value
+                elif row < 448:
+                    c, r = divmod(row - 192, 64)
+                    r += 64 * k
+                    g_up[0, r : r + 8, 256 * c : 256 * (c + 1)] = value
+                elif row < 704:
+                    c, r = divmod(row - 448, 128)
+                    r += 128 * k
+                    g_down[0, r : r + 8, 256 * c : 256 * (c + 1)] = value
+                else:
+                    c, r = divmod((row - 704) % 64, 32)
+                    r += 32 * k
+                    g_out[1 - (row - 704) // 64, r : r + 8, 256 * c : 256 * (c + 1)] = value
+
+    tiny = [rest[k, 0, 128:144].astype(F32) for k in range(2)]
 
     @pl.when(p == 0)
     def _():
         for layer in range(2):
             for c in range(4):
                 r = 4 * layer + c
-                g_b_up[layer : layer + 1, 256 * c : 256 * (c + 1)] = tiny[r : r + 1]
+                g_b_up[layer : layer + 1, 256 * c : 256 * (c + 1)] = tiny[0][r : r + 1]
         for e in range(3):
             for layer in range(2):
                 r = 8 + 2 * e + layer
-                g_b_qkv[e, layer : layer + 1, :] = tiny[r : r + 1]
-
-    def norms(layer, base):
+                g_b_qkv[e, layer : layer + 1, :] = tiny[0][r : r + 1]
+        for layer in range(2):
+            for c in range(2):
+                r = 2 * layer + c
+                for which in range(2):
+                    g_sum[layer, which : which + 1, 256 * c : 256 * (c + 1)] = tiny[1][r : r + 1]
+
+    def norms(layer, rows, base):
         for which in range(2):
             for c in range(2):
                 cols = slice(256 * c, 256 * (c + 1))
                 r = base + 2 * which + c
-                g_gain[layer, which : which + 1, cols] = tiny[r : r + 1]
-                g_bias[layer, which : which + 1, cols] = tiny[r + 4 : r + 5]
+                g_gain[layer, which : which + 1, cols] = rows[r : r + 1]
+                g_bias[layer, which : which + 1, cols] = rows[r + 4 : r + 5]
+
+    @pl.when(p == 0)
+    def _():
+        norms(0, tiny[1], 4)
 
     @pl.when(p == 1)
     def _():
-        for layer in range(2):
-            for c in range(2):
-                r = 2 * layer + c
-                for which in range(2):
-                    g_sum[layer, which : which + 1, 256 * c : 256 * (c + 1)] = tiny[r : r + 1]
-        norms(0, 4)
-
-    @pl.when(p == 2)
-    def _():
-        norms(1, 0)
+        norms(1, tiny[0], 0)
 
 
 UP = (2, 512, 1024)
@@ -575,23 +605,23 @@
 def unpack(first, rest):
     def place(layer):
         return [
-            pl.BlockSpec((1, 64, 1024), lambda p: (layer, p, 0)),
-            pl.BlockSpec((1, 128, 512), lambda p: (layer, p, 0)),
+            pl.BlockSpec((1, 128, 1024), lambda p: (layer, p, 0)),
+            pl.BlockSpec((1, 256, 512), lambda p: (layer, p, 0)),
         ]
 
-    params = pltpu.CompilerParams(vmem_limit_bytes=56 * 1024 * 1024)
+    params = pltpu.CompilerParams(vmem_limit_bytes=63 * 1024 * 1024)
     g_up, g_down = pl.pallas_call(
         unpack_first_body,
-        grid=(8,),
+        grid=(4,),
         out_shape=[jax.ShapeDtypeStruct(UP, F32), jax.ShapeDtypeStruct(DOWN, F32)],
-        in_specs=[pl.BlockSpec((None, 512, 256), lambda p: (p, 0, 0))],
+        in_specs=[pl.BlockSpec((2, 512, 256), lambda p: (p, 0, 0))],
         out_specs=place(1),
         compiler_params=params,
         name="unpack_first",
     )(first)
     outs = [
-        ((2, 3, 512, 256), pl.BlockSpec((2, 3, 64, 256), lambda p: (0, 0, p, 0))),
-        ((2, 256, 512), pl.BlockSpec((2, 32, 512), lambda p: (0, p, 0))),
+        ((2, 3, 512, 256), pl.BlockSpec((2, 3, 128, 256), lambda p: (0, 0, p, 0))),
+        ((2, 256, 512), pl.BlockSpec((2, 64, 512), lambda p: (0, p, 0))),
         ((2, 1024), whole((2, 1024))),
         ((3, 2, 256), whole((3, 2, 256))),
         ((2, 2, 512), whole((2, 2, 512))),
@@ -600,10 +630,10 @@
     ]
     return pl.pallas_call(
         unpack_rest_body,
-        grid=(8,),
+        grid=(4,),
         out_shape=[jax.ShapeDtypeStruct(shape, F32) for shape in [UP, DOWN] + [o[0] for o in outs]],
         in_specs=[
-            pl.BlockSpec((None, 8, 144, 256), lambda p: (p, 0, 0, 0)),
+            pl.BlockSpec((2, 8, 144, 256), lambda p: (p, 0, 0, 0)),
             pl.BlockSpec(memory_space=pl.ANY),
             pl.BlockSpec(memory_space=pl.ANY),
         ],
@@ -639,7 +669,8 @@
         [lax.axis_index("context"), lax.axis_index("tensor"), lax.axis_index("dp")]
     ).astype(jnp.int32)
     freqs = jnp.asarray(FREQS).reshape(HALF, 1)
-    send, pair, act, slope, cs, chunk = call(
+    chunk = swap(chunk_of(at, wq, w_out))
+    send, pair, act, slope, cs = call(
         first_body,
         [
             ((8, 208, BLK), BF),
@@ -647,17 +678,17 @@
             ((rows, 1024), BF),
             ((rows, 1024), F32),
             ((2, 2, HALF, BLK), F32),
-            ((2, 4, 64, 256), BF),
         ],
         (
-            at, positions, freqs, x, ln_gain, ln_bias, wq, bq, Layer(w_up, 0), b_up,
-            Layer(w_down, 0), w_out,
+            at, positions, freqs, x, ln_gain, ln_bias, Layer(wq, 0), bq, Layer(w_up, 0), b_up,
+            Layer(w_down, 0), Layer(w_out, 0),
         ),
         "norm_qkv_feed",
         smem_first=True,
     )
     pair_other = swap(pair)
-    others = lax.all_gather(swap(chunk), "dp", axis=2, tiled=True)
+    (chunk,) = call(hand_on_body, [(chunk.shape, BF)], (chunk, After(send)), "hand_on")
+    others = lax.all_gather(chunk, "dp", axis=2, tiled=True)
     recv = exchange(send, "context")
     ctx_send, lse, ctx, start = call(
         attend_body,
@@ -743,11 +774,15 @@
         "last",
         smem_first=True,
     )
+    mixed, sums_a = call(
+        mix_body,
+        [((8, 144, 256), BF), ((512, 256), BF)],
+        (exchange(grads_c, "dp"), sums_b, sums_a),
+        "mix",
+    )
     full_a = lax.all_gather(sums_a, "dp")
-    (mixed,) = call(mix_body, [((8, 144, 256), BF)], (exchange(grads_c, "dp"), sums_b), "mix")
-    (summed,) = call(sum_body, [((144, 256), BF)], (exchange(mixed, "context"),), "sum")
-    summed = exchange(jnp.broadcast_to(summed[None], (8, 144, 256)), "context")
-    full_bc = lax.all_gather(summed, "dp")
+    (summed,) = call(sum_body, [((8, 144, 256), BF)], (exchange(mixed, "context"),), "sum")
+    full_bc = lax.all_gather(exchange(summed, "context"), "dp")
     g_up, g_down, g_qkv, g_out, g_b_up, g_b_qkv, g_sum, g_gain, g_bias = unpack(full_a, full_bc)
     return (
         block_out.reshape(tokens_in.shape),

time: 263 us -> 255 us (0.970)
  blocking collectives: 108 us -> 103 us
  waiting for transfers between devices: 51.3 us -> 47.9 us
    all_to_all x6, blocking collectives: 108 us -> 103 us  [exchange(): return lax.all_to_all(value, axes, 0, 0)]
    ppermute x4, waiting for transfers between devices: 15.3 us -> 10.5 us  [swap(): return lax.ppermute(value, 'tensor', [(0, 1), (1, 0)])]
    pallas_call x9 -> x10, Pallas kernels: 45.2 us -> 46.8 us  [call(): pl.pallas_call(body, grid=(1,), out_shape=[jax.ShapeDtypeStruct(s, d) for...]
    pallas_call x2 -> x3, Pallas kernels: 13.5 us -> 12.6 us  [the longest x1 6.11 us: unpack(): pl.pallas_call(unpack_rest_body, grid=(4,), out_shape=[jax.ShapeDtypeStru...]
  transfers between devices with their start and end apart: 12 -> 12, of which waited for: 7 -> 7; matrix products, arithmetic and copies ran while one was open for 0% -> 0% of each run, Pallas kernels for 14% -> 15%
where the time goes in v6:
time: 255 us; the launch traced here: 253 us
  blocking collectives  103 us (40%)
  Pallas kernels  59.4 us (23%)
  waiting for transfers between devices  47.9 us (19%)
  starting transfers between devices  23.4 us (9%)
  between operations  13.9 us (5%)
  local copies, waits for them, and re-layouts  4.77 us (2%)
    all_to_all x6, blocking collectives, exchange(): return lax.all_to_all(value, axes, 0, 0)  103 us
    pallas_call x10, Pallas kernels, call(): pl.pallas_call(body, grid=(1,), out_shape=[jax.ShapeDtypeStruct(s, d) for...  46.8 us
    all_gather x1, waiting for transfers between devices, shards(): full_bc = lax.all_gather(exchange(summed, 'context'), 'dp')  28.6 us
    all_to_all x3, starting transfers between devices, exchange(): return lax.all_to_all(value, axes, 0, 0)  14.1 us
    ppermute x4, waiting for transfers between devices, swap(): return lax.ppermute(value, 'tensor', [(0, 1), (1, 0)])  10.5 us
    ppermute x4, starting transfers between devices, swap(): return lax.ppermute(value, 'tensor', [(0, 1), (1, 0)])  9.17 us
    all_to_all x3, waiting for transfers between devices, exchange(): return lax.all_to_all(value, axes, 0, 0)  8.7 us
    pallas_call x1, Pallas kernels, unpack(): pl.pallas_call(unpack_rest_body, grid=(4,), out_shape=[jax.ShapeDtypeStru...  6.11 us
  transfers between devices with their start and end apart: 12, of which 7 were waited for; matrix products, arithmetic and copies ran while one was open for 0% of the time, Pallas kernels for 15%

profile of v6, /device:TPU:1, one launch (start us, length us, event | category | flops | bytes accessed | tf_op | source)
XLA Modules:
  0.0 253.3 jit_solution(889773562650669907)
XLA Ops:
  10.1 4.4 %collective-permute-start.2 = (bf16[2,4,64,256]{3,2,1,0:T(8,128)(2,1)}, bf16[2,4,64,256]{3,2,1,0:T(8,128)(2,1)S(1)}, u32[]{:S(2)}, u32[]{:S(2)}) collective-permute-start(bf16[2,4,64,256]{3,2,1,0:T(8,128)(2,1)} %chunk.1), channel_id=1, source_target_pairs={{0,1},{1,0},{2,3},{3,2},{4,5},{5,4},{6,7},{7,6},{8,9},{9,8},{10,11... | collective-permute-start | bytes 786440 | tf_op jit(solution)/shard_map/ppermute | solution.py:648
  14.6 4.8 %norm_qkv_feed.1 = (bf16[8,208,128]{2,1,0:T(8,128)(2,1)}, bf16[512,512]{1,0:T(8,128)(2,1)}, bf16[256,1024]{1,0:T(8,128)(2,1)}, f32[256,1024]{1,0:T(8,128)}, f32[2,2,8,128]{3,2,1,0:T(8,128)}) custom-call(s32[3]{0:T(128)} %pad_add_fusion.at, s32[2,128]{1,0:T(2,128)} %pos.1, f32[8,1]{1,0:T(8,128)} %constant.18.freqs, f32[256,512]{1,0:T(8,128)} %bitcast.26, ...), custom_call_target="tpu_custom_call" | custom-call | tf_op jit(solution)/shard_map/norm_qkv_feed/pallas_call | solution.py:57
  23.2 4.6 %all-to-all-start = ((bf16[8,208,128]{2,1,0:T(8,128)(2,1)}), bf16[8,208,128]{2,1,0:T(8,128)(2,1)S(1)}, u32[]{:S(2)}, u32[]{:S(2)}) async-start(bf16[8,208,128]{2,1,0:T(8,128)(2,1)} %get-tuple-element.52._), calls=%async_computation | async-start | bytes 851968 | tf_op jit(solution)/shard_map/all_to_all | solution.py:652
  27.8 3.3 %collective-permute-start = (bf16[512,512]{1,0:T(8,128)(2,1)}, bf16[512,512]{1,0:T(8,128)(2,1)S(1)}, u32[]{:S(2)}, u32[]{:S(2)}) collective-permute-start(bf16[512,512]{1,0:T(8,128)(2,1)} %get-tuple-element.51.pair), channel_id=1, source_target_pairs={{0,1},{1,0},{2,3},{3,2},{4,5},{5,4},{6,7},{7,6},{8,9},{9,8},{10,11... | collective-permute-start | bytes 1572872 | tf_op jit(solution)/shard_map/ppermute | solution.py:648
  31.1 3.2 %all-to-all-done.recv = bf16[8,208,128]{2,1,0:T(8,128)(2,1)S(1)} async-done(((bf16[8,208,128]{2,1,0:T(8,128)(2,1)}), bf16[8,208,128]{2,1,0:T(8,128)(2,1)S(1)}, u32[]{:S(2)}, u32[]{:S(2)}) %all-to-all-start) | async-done | bytes 426016 | tf_op jit(solution)/shard_map/all_to_all | solution.py:652
  35.1 3.8 %attend.1 = (bf16[8,2,64,128]{3,2,1,0:T(8,128)(2,1)}, f32[1,1024]{1,0:T(1,128)}, f32[64,1024]{1,0:T(8,128)}, s32[1,1024]{1,0:T(1,128)}) custom-call(bf16[8,208,128]{2,1,0:T(8,128)(2,1)} %copy-done), custom_call_target="tpu_custom_call" | custom-call | tf_op jit(solution)/shard_map/attend/pallas_call | solution.py:57
  38.9 5.8 %all-to-all-start.1 = ((bf16[16,64,128]{2,1,0:T(8,128)(2,1)}), bf16[16,64,128]{2,1,0:T(8,128)(2,1)S(1)}, u32[]{:S(2)}, u32[]{:S(2)}) async-start(bf16[16,64,128]{2,1,0:T(8,128)(2,1)} %bitcast.42), calls=%async_computation.1 | async-start | bytes 524288 | tf_op jit(solution)/shard_map/all_to_all | solution.py:652
  46.9 5.5 %all-to-all-done.1 = bf16[16,64,128]{2,1,0:T(8,128)(2,1)S(1)} async-done(((bf16[16,64,128]{2,1,0:T(8,128)(2,1)}), bf16[16,64,128]{2,1,0:T(8,128)(2,1)S(1)}, u32[]{:S(2)}, u32[]{:S(2)}) %all-to-all-start.1) | async-done | bytes 262176 | tf_op jit(solution)/shard_map/all_to_all | solution.py:652
  53.1 7.6 %middle.1 = (f32[256,512]{1,0:T(8,128)}, bf16[8,256,128]{2,1,0:T(8,128)(2,1)}, bf16[8,512,256]{2,1,0:T(8,128)(2,1)}, bf16[512,512]{1,0:T(8,128)(2,1)}, f32[1,1024]{1,0:T(1,128)}, /*index=5*/f32[1,512]{1,0:T(1,128)}) custom-call(s32[3]{0:T(128)} %pad_add_fusion.at, f32[256,512]{1,0:T(8,128)} %bitcast.27, bf16[512,512]{1,0:T(8,128)(2,1)} %get-tuple-element.51.pair, ...), custom_call_target="tpu_custom_call" | custom-call | tf_op jit(solution)/shard_map/middle/pallas_call | solution.py:57
  62.1 11.7 %all_to_all.45.recv = bf16[8,256,128]{2,1,0:T(8,128)(2,1)} all-to-all(bf16[8,256,128]{2,1,0:T(8,128)(2,1)S(1)} %copy-done.7), channel_id=1, replica_groups=mesh['dp'=8,'context'=8,'tensor'=2] {'context'}, dimensions={0} | all-to-all | bytes 1048576 | tf_op jit(solution)/shard_map/all_to_all | solution.py:652
  74.8 6.2 %attend_both.1 = bf16[8,2,256,128]{3,2,1,0:T(8,128)(2,1)} custom-call(bf16[8,256,128]{2,1,0:T(8,128)(2,1)} %all_to_all.45.recv, s32[1,1024]{1,0:T(1,128)} %get-tuple-element.58.start, bf16[512,512]{1,0:T(8,128)(2,1)} %copy-done.2), custom_call_target="tpu_custom_call" | custom-call | tf_op jit(solution)/shard_map/attend_both/pallas_call | solution.py:57
  81.0 16.5 %all_to_all.46 = bf16[16,256,128]{2,1,0:T(8,128)(2,1)} all-to-all(bf16[16,256,128]{2,1,0:T(8,128)(2,1)} %bitcast.33), channel_id=1, replica_groups=mesh['dp'=8,'context'=8,'tensor'=2] {'context','tensor'}, dimensions={0} | all-to-all | bytes 2097152 | tf_op jit(solution)/shard_map/all_to_all | solution.py:652
  97.5 9.2 %turn_point.1 = (f32[256,512]{1,0:T(8,128)}, f32[256,512]{1,0:T(8,128)}, bf16[8,192,128]{2,1,0:T(8,128)(2,1)}, bf16[8,832,256]{2,1,0:T(8,128)(2,1)}, bf16[256,51...) custom-call(s32[3]{0:T(128)} %pad_add_fusion.at, ...), custom_call_target="tpu_custom_call" | custom-call | tf_op jit(solution)/shard_map/turn_point/pallas_call | solution.py:57
  106.7 3.6 %all-to-all-start.4 = ((bf16[8,192,128]{2,1,0:T(8,128)(2,1)}), bf16[8,192,128]{2,1,0:T(8,128)(2,1)S(1)}, u32[]{:S(2)}, u32[]{:S(2)}) async-start(bf16[8,192,128]{2,1,0:T(8,128)(2,1)} %get-tuple-element.65), calls=%async_computation.5 | async-start | bytes 786432 | tf_op jit(solution)/shard_map/all_to_all | solution.py:652
  111.4 6.8 %collective-permute-done.3._.part_other = bf16[256,512]{1,0:T(8,128)(2,1)S(1)} collective-permute-done((bf16[256,512]{1,0:T(8,128)(2,1)S(1)}, bf16[256,512]{1,0:T(8,128)(2,1)S(1)}, u32[]{:S(2)}, u32[]{:S(2)}) %collective-permute-start.3) | collective-permute-done | bytes 262176 | tf_op jit(solution)/shard_map/ppermute | solution.py:648
  119.0 4.5 %attend_back.1 = bf16[8,2,320,128]{3,2,1,0:T(8,128)(2,1)} custom-call(bf16[8,208,128]{2,1,0:T(8,128)(2,1)} %copy-done, bf16[8,192,128]{2,1,0:T(8,128)(2,1)} %copy-done.3, s32[1,1024]{1,0:T(1,128)} %get-tuple-element.58.start, f32[1,1024]{1,0:T(1,128)} %get-tuple-element.66.lse, f32[64,1024]{1,0:T(8,128)} %get-tuple-element.67.ctx, bf16[256,512]{1,0:T(8,128)(2,1)} %copy-done.4), custom_call_target="tpu_custom_call" | custom-call | tf_op jit(solution)/shard_map/attend_back/pallas_call | solution.py:57
  123.6 19.1 %all_to_all.47 = bf16[16,320,128]{2,1,0:T(8,128)(2,1)} all-to-all(bf16[16,320,128]{2,1,0:T(8,128)(2,1)} %bitcast.30), channel_id=1, replica_groups=mesh['dp'=8,'context'=8,'tensor'=2] {'context','tensor'}, dimensions={0} | all-to-all | bytes 2621440 | tf_op jit(solution)/shard_map/all_to_all | solution.py:652
  142.6 4.8 %last.1 = (f32[256,512]{1,0:T(8,128)}, bf16[8,208,256]{2,1,0:T(8,128)(2,1)}, bf16[512,256]{1,0:T(8,128)(2,1)}, f32[3,256]{1,0:T(4,128)}, f32[4,512]{1,0:T(4,128)}) custom-call(s32[3]{0:T(128)} %pad_add_fusion.at, f32[256,512]{1,0:T(8,128)} %bitcast.29, f32[256,512]{1,0:T(8,128)} %get-tuple-element.63.g, bf16[256,512]{1,0:T(8,128)(2,1)} %get-tuple-element.64.part, ...), custom_call_target="tpu_custom_call" | custom-call | tf_op jit(solution)/shard_map/last/pallas_call | solution.py:57
  147.4 29.3 %all_to_all.48.got = bf16[8,208,256]{2,1,0:T(8,128)(2,1)} all-to-all(bf16[8,208,256]{2,1,0:T(8,128)(2,1)} %get-tuple-element.75), channel_id=1, replica_groups=mesh['dp'=8,'context'=8,'tensor'=2] {'dp'}, dimensions={0} | all-to-all | bytes 1703936 | tf_op jit(solution)/shard_map/all_to_all | solution.py:652
  179.1 14.1 %all_to_all.49.got = bf16[8,144,256]{2,1,0:T(8,128)(2,1)} all-to-all(bf16[8,144,256]{2,1,0:T(8,128)(2,1)} %get-tuple-element.78), channel_id=1, replica_groups=mesh['dp'=8,'context'=8,'tensor'=2] {'context'}, dimensions={0} | all-to-all | bytes 1179648 | tf_op jit(solution)/shard_map/all_to_all | solution.py:652
  195.1 12.6 %all_to_all.50 = bf16[8,144,256]{2,1,0:T(8,128)(2,1)} all-to-all(bf16[8,144,256]{2,1,0:T(8,128)(2,1)} %sum.1), channel_id=1, replica_groups=mesh['dp'=8,'context'=8,'tensor'=2] {'context'}, dimensions={0} | all-to-all | bytes 1179648 | tf_op jit(solution)/shard_map/all_to_all | solution.py:652
  207.8 4.2 %unpack_first.1 = (f32[2,512,1024]{2,1,0:T(8,128)}, f32[2,1024,512]{2,1,0:T(8,128)}) custom-call(bf16[8,512,256]{2,1,0:T(8,128)(2,1)} %bitcast.39), custom_call_target="tpu_custom_call" | custom-call | tf_op jit(solution)/shard_map/unpack_first/pallas_call | solution.py:613
  212.0 28.6 %all-gather.8.cloned.1.call-done = bf16[64,144,256]{2,1,0:T(8,128)(2,1)} async-done(((bf16[8,144,256]{2,1,0:T(8,128)(2,1)}), bf16[64,144,256]{2,1,0:T(8,128)(2,1)}) %all-gather.8.cloned.1.call-update) | async-done | bytes 4718608 | tf_op jit(solution)/shard_map/all_gather | solution.py:785
  240.6 6.1 %unpack_rest.1 = (f32[2,512,1024]{2,1,0:T(8,128)}, f32[2,1024,512]{2,1,0:T(8,128)}, f32[2,3,512,256]{3,2,1,0:T(8,128)}, f32[2,256,512]{2,1,0:T(8,128)}, f32[2,10...) custom-call(bf16[8,8,144,256]{3,2,1,0:T(8,128)(2,1)} %bitcast.32, ...), custom_call_target="tpu_custom_call", output_to_operand_aliasing={{0}: (1, {}), {1}: (2, {})} | custom-call | tf_op jit(solution)/shard_map/unpack_rest/pallas_call | solution.py:631
  (45 shorter events, 19.0 us)
Async XLA Ops:
  7.2 90.3 %all-gather.6.cloned.1.call-start = ((), (), s32[]{:S(2)}) async-start(), calls=%async_computation.11 | async-start | bytes 2359296 | tf_op jit(solution)/shard_map/all_gather | solution.py:691
  10.1 10.7 %collective-permute-start.2 = (bf16[2,4,64,256]{3,2,1,0:T(8,128)(2,1)}, bf16[2,4,64,256]{3,2,1,0:T(8,128)(2,1)S(1)}, u32[]{:S(2)}, u32[]{:S(2)}) collective-permute-start(bf16[2,4,64,256]{3,2,1,0:T(8,128)(2,1)} %chunk.1), channel_id=1, source_target_pairs={{0,1},{1,0},{2,3},{3,2},{4,5},{5,4},{6,7},{7,6},{8,9},{9,8},{10,11... | collective-permute-start | bytes 786440 | tf_op jit(solution)/shard_map/ppermute | solution.py:648
  20.8 0.7 copy-start.8
  23.2 11.1 %all-to-all-start = ((bf16[8,208,128]{2,1,0:T(8,128)(2,1)}), bf16[8,208,128]{2,1,0:T(8,128)(2,1)S(1)}, u32[]{:S(2)}, u32[]{:S(2)}) async-start(bf16[8,208,128]{2,1,0:T(8,128)(2,1)} %get-tuple-element.52._), calls=%async_computation | async-start | bytes 851968 | tf_op jit(solution)/shard_map/all_to_all | solution.py:652
  27.8 19.1 %collective-permute-start = (bf16[512,512]{1,0:T(8,128)(2,1)}, bf16[512,512]{1,0:T(8,128)(2,1)S(1)}, u32[]{:S(2)}, u32[]{:S(2)}) collective-permute-start(bf16[512,512]{1,0:T(8,128)(2,1)} %get-tuple-element.51.pair), channel_id=1, source_target_pairs={{0,1},{1,0},{2,3},{3,2},{4,5},{5,4},{6,7},{7,6},{8,9},{9,8},{10,11... | collective-permute-start | bytes 1572872 | tf_op jit(solution)/shard_map/ppermute | solution.py:648
  34.3 0.8 copy-start
  38.9 13.5 %all-to-all-start.1 = ((bf16[16,64,128]{2,1,0:T(8,128)(2,1)}), bf16[16,64,128]{2,1,0:T(8,128)(2,1)S(1)}, u32[]{:S(2)}, u32[]{:S(2)}) async-start(bf16[16,64,128]{2,1,0:T(8,128)(2,1)} %bitcast.42), calls=%async_computation.1 | async-start | bytes 524288 | tf_op jit(solution)/shard_map/all_to_all | solution.py:652
  44.7 52.7 %reduce-scatter.3.cloned.1.call-start = ((), (), s32[]{:S(2)}) async-start(), calls=%async_computation.12 | async-start | bytes 2359296 | tf_op jit(solution)/shard_map/reduce_scatter | solution.py:718
  46.9 5.5 %copy-start.6 = (bf16[512,512]{1,0:T(8,128)(2,1)}, bf16[512,512]{1,0:T(8,128)(2,1)S(1)}, u32[]{:S(2)}) copy-start(bf16[512,512]{1,0:T(8,128)(2,1)S(1)} %collective-permute-done.pair_other) | copy-start | bytes 1572868
  52.4 0.7 copy-start.1
  60.7 1.0 copy-start.5
  60.7 1.5 copy-start.7
  60.7 116.0 %reduce-scatter.5.cloned.1.call-start = ((), (), s32[]{:S(2)}) async-start(), calls=%async_computation.13 | async-start | bytes 3833856 | tf_op jit(solution)/shard_map/reduce_scatter | solution.py:750
  61.7 12.3 %collective-permute-start.1 = (bf16[512,512]{1,0:T(8,128)(2,1)S(1)}, bf16[512,512]{1,0:T(8,128)(2,1)S(1)}, u32[]{:S(2)}, u32[]{:S(2)}) collective-permute-start(bf16[512,512]{1,0:T(8,128)(2,1)S(1)} %copy-done.5), channel_id=1, source_target_pairs={{0,1},{1,0},{2,3},{3,2},{4,5},{5,4},{6,7},{7,6},{8,9},{9,8},{10,11... | collective-permute-start | bytes 1572872 | tf_op jit(solution)/shard_map/ppermute | solution.py:648
  74.0 0.8 copy-start.2
  106.6 3.7 %copy-start.9 = (bf16[256,512]{1,0:T(8,128)(2,1)S(1)}, bf16[256,512]{1,0:T(8,128)(2,1)}, u32[]{:S(2)}) copy-start(bf16[256,512]{1,0:T(8,128)(2,1)} %get-tuple-element.64.part) | copy-start | bytes 786436
  106.7 11.5 %all-to-all-start.4 = ((bf16[8,192,128]{2,1,0:T(8,128)(2,1)}), bf16[8,192,128]{2,1,0:T(8,128)(2,1)S(1)}, u32[]{:S(2)}, u32[]{:S(2)}) async-start(bf16[8,192,128]{2,1,0:T(8,128)(2,1)} %get-tuple-element.65), calls=%async_computation.5 | async-start | bytes 786432 | tf_op jit(solution)/shard_map/all_to_all | solution.py:652
  110.3 97.5 %all-gather.10.cloned.1.call-start = ((), (), s32[]{:S(2)}) async-start(), calls=%async_computation.15 | async-start | bytes 2359296 | tf_op jit(solution)/shard_map/all_gather | solution.py:783
  110.3 7.9 %collective-permute-start.3 = (bf16[256,512]{1,0:T(8,128)(2,1)S(1)}, bf16[256,512]{1,0:T(8,128)(2,1)S(1)}, u32[]{:S(2)}, u32[]{:S(2)}) collective-permute-start(bf16[256,512]{1,0:T(8,128)(2,1)S(1)} %copy-done.9), channel_id=1, source_target_pairs={{0,1},{1,0},{2,3},{3,2},{4,5},{5,4},{6,7},{7,6},{8,9},{9,8},{10,11... | collective-permute-start | bytes 786440 | tf_op jit(solution)/shard_map/ppermute | solution.py:648
  118.2 0.7 copy-start.4
  118.2 0.8 copy-start.3
  179.0 61.6 %all-gather.8.cloned.1.call-start = ((), (), s32[]{:S(2)}) async-start(), calls=%async_computation.14 | async-start | bytes 5308416 | tf_op jit(solution)/shard_map/all_gather | solution.py:785
Sparse Core Ops, SparseCore 0:
  23.3 27.8 all-gather.5
  60.8 32.8 reduce-scatter.2
  106.8 39.6 reduce-scatter.4
  179.1 21.4 all-gather.9
  207.9 32.6 all-gather.7

commit v7 on v6

--- a/solution.py
+++ b/solution.py
@@ -47,23 +47,123 @@
     return pl.BlockSpec(shape, lambda i: (0,) * len(shape))
 
 
+class Fetch:
+    def __init__(self, array, layer=None, rows=None, at=0):
+        self.array, self.layer, self.rows, self.at = array, layer, rows, at
+        shape = array.shape if layer is None else array.shape[1:]
+        self.shape = shape if rows is None else shape[:-2] + (rows, shape[-1])
+
+    def spec(self):
+        return pl.BlockSpec(memory_space=pl.ANY)
+
+    def source(self, ref):
+        if self.layer is not None:
+            ref = ref.at[self.layer]
+        if self.rows is not None:
+            place = (slice(None),) * (len(self.shape) - 2) + (pl.ds(self.at * self.rows, self.rows),)
+            ref = ref.at[place]
+        return ref
+
+
+class Lazy:
+    def __init__(self, ref, copy):
+        self.ref, self.copy, self.shape = ref, copy, ref.shape
+
+    def __getitem__(self, index):
+        if self.copy is not None:
+            self.copy.wait()
+            self.copy = None
+        return self.ref[index]
+
+
+class Store:
+    def __init__(self, shape, dtype):
+        self.shape, self.dtype = shape, dtype
+
+
+class Out:
+    def __init__(self, ref, target, sems, copies):
+        self.ref, self.target, self.sems, self.copies, self.done = ref, target, sems, copies, False
+
+    def __setitem__(self, index, value):
+        self.ref[index] = value
+
+    def __getitem__(self, index):
+        return self.ref[index]
+
+    def flush(self, *place):
+        source, target = self.ref, self.target
+        if place:
+            source, target = source.at[place], target.at[place]
+        copy = pltpu.make_async_copy(source, target, self.sems.at[len(self.copies)])
+        copy.start()
+        self.copies.append(copy)
+        self.done = True
+
+
+FLUSHES = 40
+
+
+def flush(ref, *place):
+    if isinstance(ref, Out):
+        ref.flush(*place)
+
+
 def call(body, out_shape, args, name, scratch=(), smem_first=False):
-    specs = [
-        a.spec() if isinstance(a, (Layer, After)) else whole(a.shape) for a in args
-    ]
-    args = [a.array if isinstance(a, (Layer, After)) else a for a in args]
+    own = (Layer, After, Fetch)
+    specs = [a.spec() if isinstance(a, own) else whole(a.shape) for a in args]
+    fetched = [i for i, a in enumerate(args) if isinstance(a, Fetch)]
+    stored = [i for i, o in enumerate(out_shape) if isinstance(o, Store)]
+    plans = list(args)
+    arrays = [a.array if isinstance(a, own) else a for a in args]
+    shapes = [(o.shape, o.dtype) if isinstance(o, Store) else o for o in out_shape]
     if smem_first:
         specs[0] = pl.BlockSpec(memory_space=pltpu.SMEM)
+    buffers = [pltpu.VMEM(plans[i].shape, arrays[i].dtype) for i in fetched]
+    buffers += [pltpu.VMEM(*shapes[i]) for i in stored]
+    sems = []
+    if fetched:
+        sems.append(pltpu.SemaphoreType.DMA((len(fetched),)))
+    if stored:
+        sems.append(pltpu.SemaphoreType.DMA((FLUSHES,)))
+    n_in, n_out, n_scratch = len(args), len(out_shape), len(scratch)
+
+    def run(*refs):
+        ins, outs = list(refs[:n_in]), list(refs[n_in : n_in + n_out])
+        rest = list(refs[n_in + n_out :])
+        mine, rest = rest[:n_scratch], rest[n_scratch:]
+        for k, i in enumerate(fetched):
+            copy = pltpu.make_async_copy(
+                plans[i].source(ins[i]), rest[k], rest[len(buffers)].at[k]
+            )
+            copy.start()
+            ins[i] = Lazy(rest[k], copy)
+        copies = []
+        for k, i in enumerate(stored):
+            outs[i] = Out(rest[len(fetched) + k], outs[i], rest[-1], copies)
+        body(*ins, *outs, *mine)
+        for i in fetched:
+            if ins[i].copy is not None:
+                ins[i].copy.wait()
+        for i in stored:
+            if not outs[i].done:
+                outs[i].flush()
+        for copy in copies:
+            copy.wait()
+
     return pl.pallas_call(
-        body,
+        run,
         grid=(1,),
-        out_shape=[jax.ShapeDtypeStruct(s, d) for s, d in out_shape],
+        out_shape=[jax.ShapeDtypeStruct(s, d) for s, d in shapes],
         in_specs=specs,
-        out_specs=[whole(s) for s, _ in out_shape],
-        scratch_shapes=list(scratch),
+        out_specs=[
+            pl.BlockSpec(memory_space=pl.ANY) if isinstance(o, Store) else whole(o[0])
+            for o in out_shape
+        ],
+        scratch_shapes=list(scratch) + buffers + sems,
         compiler_params=pltpu.CompilerParams(vmem_limit_bytes=63 * 1024 * 1024),
         name=name,
-    )(*args)
+    )(*arrays)
 
 
 def norm_rows(x):
@@ -107,7 +207,10 @@
         cdf = 0.5 + 0.5 * lax.erf(pre * np.float32(0.7071067811865476))
         a = (pre * cdf).astype(BF)
         act[:, cols] = a
-        slope[:, cols] = cdf + pre * (jnp.exp(-0.5 * pre * pre) * np.float32(0.3989422804014327))
+        tail = pre * (jnp.exp(-0.5 * pre * pre) * np.float32(0.3989422804014327))
+        slope[:, cols] = (cdf + tail).astype(BF)
+        flush(act, slice(None), cols)
+        flush(slope, slice(None), cols)
         term = mm(a, w_down[cols, :])
         total = term if total is None else total + term
     return total
@@ -120,7 +223,7 @@
     for c in range(0, width, 256):
         cols = slice(c, c + 256)
         d_act = mm(g_b, w_down[cols, :], 1, 1)
-        d_pre = d_act * slope[:, cols]
+        d_pre = d_act * slope[:, cols].astype(F32)
         d_pre_b = d_pre.astype(BF)
         d_b_up[:, cols] = jnp.sum(d_pre_b.astype(F32), 0, keepdims=True)
         d_up(c // 256, mm(mlp_t, d_pre_b))
@@ -134,6 +237,7 @@
     def put(c, value):
         for p in range(8):
             out[p, row + 64 * c : row + 64 * (c + 1), :] = value[64 * p : 64 * (p + 1)].astype(BF)
+        flush(out, slice(None), slice(row + 64 * c, row + 64 * (c + 1)))
 
     return put
 
@@ -145,6 +249,7 @@
                 out[c // 128 + k, row + 128 * half : row + 128 * (half + 1), :] = value[
                     128 * k : 128 * (k + 1), 256 * half : 256 * (half + 1)
                 ].astype(BF)
+        flush(out, slice(c // 128, c // 128 + 2), slice(row, row + 256))
 
     return put
 
@@ -153,6 +258,7 @@
     def put(e, value):
         for p in range(8):
             out[p, row + 64 * e : row + 64 * (e + 1), :] = value[64 * p : 64 * (p + 1)].astype(BF)
+        flush(out, slice(None), slice(row + 64 * e, row + 64 * (e + 1)))
 
     return put
 
@@ -169,13 +275,14 @@
             out[p, row + 32 * half : row + 32 * (half + 1), :] = value[
                 32 * p : 32 * (p + 1), 256 * half : 256 * (half + 1)
             ].astype(BF)
+    flush(out, slice(None), slice(row, row + 64))
 
 
 def first_body(
     at, pos, freqs, x, gain, bias, w_qkv, b_qkv, w_up, b_up, w_down, w_out,
     send, pair, act, slope, cs,
 ):
-    pair[256:512] = w_out[...]
+
     for s in range(2):
         p = pos[s : s + 1, :].astype(F32)
         angle = freqs[...] * p
@@ -194,6 +301,8 @@
         block = jnp.where(row == 0, high, jnp.where(row == 1, low, 0.0)).astype(BF)
         for h in range(4):
             send[s * 4 + h, 3 * HEAD : 3 * HEAD + 16, :] = block
+    flush(send)
+    pair[256:512] = w_out[...]
     pair[0:256] = feed_forward(mlp_in, w_up, b_up, 0, w_down, act, slope).astype(BF)
 
 
@@ -345,6 +454,7 @@
     branch = branch + branch_of(at[1], recv, w_out_own[...], pair_other[256:512])
     out = x[...] + branch + out_bias[0, 0:1] + out_bias[0, 1:2]
     stream[...] = out
+    flush(stream)
     normed, _ = norm_rows(out)
     attn_in = (normed * gain[1, 0:1] + bias[1, 0:1]).astype(BF)
     mlp_in = (normed * gain[1, 1:2] + bias[1, 1:2]).astype(BF)
@@ -356,6 +466,7 @@
             send[s * 4 + h, 3 * HEAD : 4 * HEAD, :] = d_ctx[
                 h * HEAD : (h + 1) * HEAD, s * BLK : (s + 1) * BLK
             ].astype(BF)
+    flush(send)
     d_sum[...] = jnp.sum(cot[...], 0, keepdims=True)
     parts[0:256] = feed_forward(mlp_in, w_up, b_up, 1, w_down, act, slope).astype(BF)
     parts[256:512] = feed_back(
@@ -412,12 +523,14 @@
     branch = parts[0:256].astype(F32) + parts_other[0:256].astype(F32)
     branch = branch + branch_of(t, recv, w_out[...], out_other(others))
     block_out[...] = stream[...] + branch + out_bias[1, 0:1] + out_bias[1, 1:2]
+    flush(block_out)
     d_mlp_in = parts[256:512].astype(F32) + parts_other[256:512].astype(F32)
     g = norm_back(
         t, stream[...], cot[...], d_mlp_in, recv, HEAD, w_qkv, others, cs, gain, bias, 1,
         pack_qkv(grads, 0), d_b_qkv, d_norm,
     )
     g_out[...] = g
+    flush(g_out)
     g_b = g.astype(BF)
     d_sum[...] = jnp.sum(g, 0, keepdims=True)
     d_ctx = mm(w_out_first[...], g_b, 1, 1)
@@ -431,6 +544,7 @@
             send[q, 64 + 64 * c : 128 + 64 * c] = sums_a[
                 64 * q : 64 * (q + 1), BLK * c : BLK * (c + 1)
             ]
+    flush(send)
     pack_out(grads, 704, own_ctx(t, recv), cot[...].astype(BF))
     pack_out(grads, 768, own_ctx(t, recv_first), g_b)
     normed, _ = norm_rows(x[...])
@@ -473,6 +587,7 @@
         have = rows[p] if p < len(rows) else []
         fill = [jnp.zeros((16 - len(have), 256), F32)]
         grads[p, 192:208, :] = jnp.concatenate(have + fill, 0).astype(BF)
+    flush(grads, slice(None), slice(192, 208))
 
 
 def chunk_body(at, w_qkv, w_out, out):
@@ -499,10 +614,6 @@
         compiler_params=pltpu.CompilerParams(vmem_limit_bytes=63 * 1024 * 1024),
         name="chunk",
     )(at, wq, w_out)
-
-
-def hand_on_body(value, _, out):
-    out[...] = value[...]
 
 
 def mix_body(got, early, first, out, first_out):
@@ -673,21 +784,22 @@
     send, pair, act, slope, cs = call(
         first_body,
         [
-            ((8, 208, BLK), BF),
-            ((2 * rows, width), BF),
-            ((rows, 1024), BF),
-            ((rows, 1024), F32),
+            Store((8, 208, BLK), BF),
+            Store((2 * rows, width), BF),
+            Store((rows, 1024), BF),
+            Store((rows, 1024), BF),
             ((2, 2, HALF, BLK), F32),
         ],
         (
-            at, positions, freqs, x, ln_gain, ln_bias, Layer(wq, 0), bq, Layer(w_up, 0), b_up,
-            Layer(w_down, 0), Layer(w_out, 0),
+            at, positions, freqs, Fetch(x), ln_gain, ln_bias, Fetch(wq, 0), bq, Fetch(w_up, 0), b_up,
+            Fetch(w_down, 0), Fetch(w_out, 0),
         ),
         "norm_qkv_feed",
         smem_first=True,
     )
     pair_other = swap(pair)
-    (chunk,) = call(hand_on_body, [(chunk.shape, BF)], (chunk, After(send)), "hand_on")
+    mark = send[0, 0, 0]
+    chunk = jnp.where(mark == mark, chunk, 0)
     others = lax.all_gather(chunk, "dp", axis=2, tiled=True)
     recv = exchange(send, "context")
     ctx_send, lse, ctx, start = call(
@@ -700,19 +812,20 @@
     stream, send, grads_a, parts, d_b_up1, d_sum1 = call(
         middle_body,
         [
-            ((rows, width), F32),
-            ((8, 256, BLK), BF),
-            ((8, 512, 256), BF),
-            ((2 * rows, width), BF),
+            Store((rows, width), F32),
+            Store((8, 256, BLK), BF),
+            Store((8, 512, 256), BF),
+            Store((2 * rows, width), BF),
             ((1, 1024), F32),
             ((1, width), F32),
         ],
         (
-            at, x, pair, pair_other, recv_ctx, Layer(w_out, 0), out_bias, ln_gain, ln_bias,
-            Layer(wq, 1), bq, Layer(w_up, 1), b_up, Layer(w_down, 1), Layer(w_out, 1), cot, cs,
+            at, Fetch(x), Fetch(pair), Fetch(pair_other), Fetch(recv_ctx), Fetch(w_out, 0), out_bias,
+            ln_gain, ln_bias, Fetch(wq, 1), bq, Fetch(w_up, 1), b_up, Fetch(w_down, 1),
+            Fetch(w_out, 1), Fetch(cot), cs,
         ),
         "middle",
-        scratch=[pltpu.VMEM((rows, 1024), BF), pltpu.VMEM((rows, 1024), F32)],
+        scratch=[pltpu.VMEM((rows, 1024), BF), pltpu.VMEM((rows, 1024), BF)],
         smem_first=True,
     )
     sums_a = lax.psum_scatter(grads_a, "dp", scatter_dimension=0)
@@ -729,20 +842,21 @@
     block_out, g, send, grads_b, part_g, d_b_up0, d_b_qkv1, d_norm1, d_sum0 = call(
         turn_point_body,
         [
-            ((rows, width), F32),
-            ((rows, width), F32),
-            ((8, 192, BLK), BF),
-            ((8, 832, 256), BF),
-            ((rows, width), BF),
+            Store((rows, width), F32),
+            Store((rows, width), F32),
+            Store((8, 192, BLK), BF),
+            Store((8, 832, 256), BF),
+            Store((rows, width), BF),
             ((1, 1024), F32),
             ((3, 256), F32),
             ((4, width), F32),
             ((1, width), F32),
         ],
         (
-            at, stream, parts, parts_other, recv_grad, Layer(w_out, 1), Layer(wq, 1), Layer(others, 1),
-            out_bias, ln_gain, ln_bias, cot, cs, x, act, slope, Layer(w_up, 0), Layer(w_down, 0),
-            Layer(w_out, 0), recv_ctx, sums_a,
+            at, Fetch(stream), Fetch(parts), Fetch(parts_other), Fetch(recv_grad), Fetch(w_out, 1),
+            Fetch(wq, 1), Fetch(others, 1), out_bias, ln_gain, ln_bias, Fetch(cot), cs, Fetch(x),
+            Fetch(act), Fetch(slope), Fetch(w_up, 0), Fetch(w_down, 0), Fetch(w_out, 0),
+            Fetch(recv_ctx), Fetch(sums_a),
         ),
         "turn_point",
         smem_first=True,
@@ -761,14 +875,15 @@
     in_grad, grads_c, sums_a, _, _ = call(
         last_body,
         [
-            ((rows, width), F32),
-            ((8, 208, 256), BF),
-            ((512, 256), BF),
+            Store((rows, width), F32),
+            Store((8, 208, 256), BF),
+            Store((512, 256), BF),
             ((3, 256), F32),
             ((4, width), F32),
         ],
         (
-            at, x, g, part_g, part_g_other, recv_grad0, Layer(wq, 0), Layer(others, 0), cs,
+            at, Fetch(x), Fetch(g), Fetch(part_g), Fetch(part_g_other), Fetch(recv_grad0), Fetch(wq, 0),
+            Fetch(others, 0), cs,
             ln_gain, ln_bias, d_b_up0, d_b_up1, d_b_qkv1, d_norm1, d_sum0, d_sum1,
         ),
         "last",

time: 255 us -> 259 us (1.016)
  starting transfers between devices: 23.4 us -> 19.7 us
  Pallas kernels: 59.4 us -> 62.9 us
    pallas_call x10 -> x9, Pallas kernels: 46.8 us -> 50.3 us  [call(): pl.pallas_call(run, grid=(1,), out_shape=[jax.ShapeDtypeStruct(s, d) for...]
    all_to_all x3, waiting for transfers between devices: 8.7 us -> 11.5 us  [exchange(): return lax.all_to_all(value, axes, 0, 0)]
  transfers between devices with their start and end apart: 12 -> 12, of which waited for: 7 -> 5; matrix products, arithmetic and copies ran while one was open for 0% -> 0% of each run, Pallas kernels for 15% -> 16%
where the time goes in v7:
time: 259 us; the launch traced here: 258 us
  blocking collectives  104 us (40%)
  Pallas kernels  62.9 us (24%)
  waiting for transfers between devices  49.2 us (19%)
  starting transfers between devices  19.7 us (8%)
  between operations  15.2 us (6%)
  local copies, waits for them, and re-layouts  5.26 us (2%)
    all_to_all x6, blocking collectives, exchange(): return lax.all_to_all(value, axes, 0, 0)  104 us
    pallas_call x9, Pallas kernels, call(): pl.pallas_call(run, grid=(1,), out_shape=[jax.ShapeDtypeStruct(s, d) for...  50.3 us
    all_gather x1, waiting for transfers between devices, shards(): full_bc = lax.all_gather(exchange(summed, 'context'), 'dp')  28.6 us
    all_to_all x3, starting transfers between devices, exchange(): return lax.all_to_all(value, axes, 0, 0)  12.5 us
    all_to_all x3, waiting for transfers between devices, exchange(): return lax.all_to_all(value, axes, 0, 0)  11.5 us
    ppermute x4, waiting for transfers between devices, swap(): return lax.ppermute(value, 'tensor', [(0, 1), (1, 0)])  9.02 us
    ppermute x4, starting transfers between devices, swap(): return lax.ppermute(value, 'tensor', [(0, 1), (1, 0)])  7.06 us
    pallas_call x1, Pallas kernels, unpack(): pl.pallas_call(unpack_rest_body, grid=(4,), out_shape=[jax.ShapeDtypeStru...  6.11 us
  transfers between devices with their start and end apart: 12, of which 5 were waited for; matrix products, arithmetic and copies ran while one was open for 0% of the time, Pallas kernels for 16%

profile of v7, /device:TPU:1, one launch (start us, length us, event | category | flops | bytes accessed | tf_op | source)
XLA Modules:
  0.0 257.8 jit_solution(14798393738310543935)
XLA Ops:
  7.9 2.3 chunk.1
  10.2 4.4 %collective-permute-start.2 = (bf16[2,4,64,256]{3,2,1,0:T(8,128)(2,1)}, bf16[2,4,64,256]{3,2,1,0:T(8,128)(2,1)S(1)}, u32[]{:S(2)}, u32[]{:S(2)}) collective-permute-start(bf16[2,4,64,256]{3,2,1,0:T(8,128)(2,1)} %chunk.1), channel_id=1, source_target_pairs={{0,1},{1,0},{2,3},{3,2},{4,5},{5,4},{6,7},{7,6},{8,9},{9,8},{10,11... | collective-permute-start | bytes 786440 | tf_op jit(solution)/shard_map/ppermute | solution.py:759
  14.6 5.9 %norm_qkv_feed.1 = (bf16[8,208,128]{2,1,0:T(8,128)(2,1)}, bf16[512,512]{1,0:T(8,128)(2,1)}, bf16[256,1024]{1,0:T(8,128)(2,1)}, bf16[256,1024]{1,0:T(8,128)(2,1)}, f32[2,2,8,128]{3,2,1,0:T(8,128)}) custom-call(s32[3]{0:T(128)} %pad_add_fusion.refs_0_.at, s32[2,128]{1,0:T(2,128)} %refs_1_.1, f32[8,1]{1,0:T(8,128)} %constant.21.refs_2_, f32[256,512]{1,0:T(8,128)} %bitcast.27, ...), custom_call_target="tpu_custom_call" | custom-call | tf_op jit(solution)/shard_map/norm_qkv_feed/pallas_call | solution.py:154
  23.8 4.7 %all-to-all-start = ((bf16[8,208,128]{2,1,0:T(8,128)(2,1)}), bf16[8,208,128]{2,1,0:T(8,128)(2,1)S(1)}, u32[]{:S(2)}, u32[]{:S(2)}) async-start(bf16[8,208,128]{2,1,0:T(8,128)(2,1)} %get-tuple-element.52), calls=%async_computation | async-start | bytes 851968 | tf_op jit(solution)/shard_map/all_to_all | solution.py:763
  29.5 6.1 %all-to-all-done.refs_0_ = bf16[8,208,128]{2,1,0:T(8,128)(2,1)S(1)} async-done(((bf16[8,208,128]{2,1,0:T(8,128)(2,1)}), bf16[8,208,128]{2,1,0:T(8,128)(2,1)S(1)}, u32[]{:S(2)}, u32[]{:S(2)}) %all-to-all-start) | async-done | bytes 426016 | tf_op jit(solution)/shard_map/all_to_all | solution.py:763
  36.5 3.8 %attend.1 = (bf16[8,2,64,128]{3,2,1,0:T(8,128)(2,1)}, f32[1,1024]{1,0:T(1,128)}, f32[64,1024]{1,0:T(8,128)}, s32[1,1024]{1,0:T(1,128)}) custom-call(bf16[8,208,128]{2,1,0:T(8,128)(2,1)} %copy-done), custom_call_target="tpu_custom_call" | custom-call | tf_op jit(solution)/shard_map/attend/pallas_call | solution.py:154
  40.3 4.2 %all-to-all-start.1 = ((bf16[16,64,128]{2,1,0:T(8,128)(2,1)}), bf16[16,64,128]{2,1,0:T(8,128)(2,1)S(1)}, u32[]{:S(2)}, u32[]{:S(2)}) async-start(bf16[16,64,128]{2,1,0:T(8,128)(2,1)} %bitcast.42), calls=%async_computation.1 | async-start | bytes 524288 | tf_op jit(solution)/shard_map/all_to_all | solution.py:763
  46.9 5.3 %all-to-all-done.1 = bf16[16,64,128]{2,1,0:T(8,128)(2,1)S(1)} async-done(((bf16[16,64,128]{2,1,0:T(8,128)(2,1)}), bf16[16,64,128]{2,1,0:T(8,128)(2,1)S(1)}, u32[]{:S(2)}, u32[]{:S(2)}) %all-to-all-start.1) | async-done | bytes 262176 | tf_op jit(solution)/shard_map/all_to_all | solution.py:763
  52.9 8.7 %middle.1 = (f32[256,512]{1,0:T(8,128)}, bf16[8,256,128]{2,1,0:T(8,128)(2,1)}, bf16[8,512,256]{2,1,0:T(8,128)(2,1)}, bf16[512,512]{1,0:T(8,128)(2,1)}, f32[1,1024]{1,0:T(1,128)}, /*index=5*/f32[1,512]{1,0:T(1,128)}) custom-call(s32[3]{0:T(128)} %pad_add_fusion.refs_0_.at, f32[256,512]{1,0:T(8,128)} %bitcast.28, bf16[512,512]{1,0:T(8,128)(2,1)} %get-tuple-element.51.refs_2_, ...), custom_call_target="tpu_custom_call" | custom-call | tf_op jit(solution)/shard_map/middle/pallas_call | solution.py:154
  63.0 15.3 %all_to_all.45.refs_0_ = bf16[8,256,128]{2,1,0:T(8,128)(2,1)} all-to-all(bf16[8,256,128]{2,1,0:T(8,128)(2,1)S(1)} %copy-done.6), channel_id=1, replica_groups=mesh['dp'=8,'context'=8,'tensor'=2] {'context'}, dimensions={0} | all-to-all | bytes 1048576 | tf_op jit(solution)/shard_map/all_to_all | solution.py:763
  79.1 6.2 %attend_both.1 = bf16[8,2,256,128]{3,2,1,0:T(8,128)(2,1)} custom-call(bf16[8,256,128]{2,1,0:T(8,128)(2,1)} %all_to_all.45.refs_0_, s32[1,1024]{1,0:T(1,128)} %get-tuple-element.58.refs_1_.refs_2_, bf16[512,512]{1,0:T(8,128)(2,1)} %copy-done.2), custom_call_target="tpu_custom_call" | custom-call | tf_op jit(solution)/shard_map/attend_both/pallas_call | solution.py:154
  85.3 16.9 %all_to_all.46 = bf16[16,256,128]{2,1,0:T(8,128)(2,1)} all-to-all(bf16[16,256,128]{2,1,0:T(8,128)(2,1)} %bitcast.34), channel_id=1, replica_groups=mesh['dp'=8,'context'=8,'tensor'=2] {'context','tensor'}, dimensions={0} | all-to-all | bytes 2097152 | tf_op jit(solution)/shard_map/all_to_all | solution.py:763
  102.2 10.6 %turn_point.1 = (f32[256,512]{1,0:T(8,128)}, f32[256,512]{1,0:T(8,128)}, bf16[8,192,128]{2,1,0:T(8,128)(2,1)}, bf16[8,832,256]{2,1,0:T(8,128)(2,1)}, bf16[256,51...) custom-call(s32[3]{0:T(128)} %pad_add_fusion.refs_0_.at, ...), custom_call_target="tpu_custom_call" | custom-call | tf_op jit(solution)/shard_map/turn_point/pallas_call | solution.py:154
  112.9 3.6 %all-to-all-start.4 = ((bf16[8,192,128]{2,1,0:T(8,128)(2,1)}), bf16[8,192,128]{2,1,0:T(8,128)(2,1)S(1)}, u32[]{:S(2)}, u32[]{:S(2)}) async-start(bf16[8,192,128]{2,1,0:T(8,128)(2,1)} %get-tuple-element.65), calls=%async_computation.5 | async-start | bytes 786432 | tf_op jit(solution)/shard_map/all_to_all | solution.py:763
  117.7 6.7 %collective-permute-done.3.refs_5_.refs_4_ = bf16[256,512]{1,0:T(8,128)(2,1)S(1)} collective-permute-done((bf16[256,512]{1,0:T(8,128)(2,1)S(1)}, bf16[256,512]{1,0:T(8,128)(2,1)S(1)}, u32[]{:S(2)}, u32[]{:S(2)}) %collective-permute-start.3) | collective-permute-done | bytes 262176 | tf_op jit(solution)/shard_map/ppermute | solution.py:759
  125.2 4.6 %attend_back.1 = bf16[8,2,320,128]{3,2,1,0:T(8,128)(2,1)} custom-call(bf16[8,208,128]{2,1,0:T(8,128)(2,1)} %copy-done, bf16[8,192,128]{2,1,0:T(8,128)(2,1)} %copy-done.3, s32[1,1024]{1,0:T(1,128)} %get-tuple-element.58.refs_1_.refs_2_, f32[1,1024]{1,0:T(1,128)} %get-tuple-element.66.refs_3_, f32[64,1024]{1,0:T(8,128)} %get-tuple-element.67.refs_4_, ...), custom_call_target="tpu_custom_call" | custom-call | tf_op jit(solution)/shard_map/attend_back/pallas_call | solution.py:154
  129.8 19.3 %all_to_all.47 = bf16[16,320,128]{2,1,0:T(8,128)(2,1)} all-to-all(bf16[16,320,128]{2,1,0:T(8,128)(2,1)} %bitcast.31), channel_id=1, replica_groups=mesh['dp'=8,'context'=8,'tensor'=2] {'context','tensor'}, dimensions={0} | all-to-all | bytes 2621440 | tf_op jit(solution)/shard_map/all_to_all | solution.py:763
  149.1 6.3 %last.1 = (f32[256,512]{1,0:T(8,128)}, bf16[8,208,256]{2,1,0:T(8,128)(2,1)}, bf16[512,256]{1,0:T(8,128)(2,1)}, f32[3,256]{1,0:T(4,128)}, f32[4,512]{1,0:T(4,128)}) custom-call(s32[3]{0:T(128)} %pad_add_fusion.refs_0_.at, f32[256,512]{1,0:T(8,128)} %bitcast.30, f32[256,512]{1,0:T(8,128)} %get-tuple-element.63.refs_2_, ...), custom_call_target="tpu_custom_call" | custom-call | tf_op jit(solution)/shard_map/last/pallas_call | solution.py:154
  155.4 25.8 %all_to_all.48.refs_0_ = bf16[8,208,256]{2,1,0:T(8,128)(2,1)} all-to-all(bf16[8,208,256]{2,1,0:T(8,128)(2,1)} %get-tuple-element.75), channel_id=1, replica_groups=mesh['dp'=8,'context'=8,'tensor'=2] {'dp'}, dimensions={0} | all-to-all | bytes 1703936 | tf_op jit(solution)/shard_map/all_to_all | solution.py:763
  183.6 14.1 %all_to_all.49.refs_0_ = bf16[8,144,256]{2,1,0:T(8,128)(2,1)} all-to-all(bf16[8,144,256]{2,1,0:T(8,128)(2,1)} %get-tuple-element.78), channel_id=1, replica_groups=mesh['dp'=8,'context'=8,'tensor'=2] {'context'}, dimensions={0} | all-to-all | bytes 1179648 | tf_op jit(solution)/shard_map/all_to_all | solution.py:763
  199.7 12.6 %all_to_all.50 = bf16[8,144,256]{2,1,0:T(8,128)(2,1)} all-to-all(bf16[8,144,256]{2,1,0:T(8,128)(2,1)} %sum.1), channel_id=1, replica_groups=mesh['dp'=8,'context'=8,'tensor'=2] {'context'}, dimensions={0} | all-to-all | bytes 1179648 | tf_op jit(solution)/shard_map/all_to_all | solution.py:763
  212.4 4.2 %unpack_first.1 = (f32[2,512,1024]{2,1,0:T(8,128)}, f32[2,1024,512]{2,1,0:T(8,128)}) custom-call(bf16[8,512,256]{2,1,0:T(8,128)(2,1)} %bitcast.38), custom_call_target="tpu_custom_call" | custom-call | tf_op jit(solution)/shard_map/unpack_first/pallas_call | solution.py:724
  216.5 28.6 %all-gather.8.cloned.1.call-done = bf16[64,144,256]{2,1,0:T(8,128)(2,1)} async-done(((bf16[8,144,256]{2,1,0:T(8,128)(2,1)}), bf16[64,144,256]{2,1,0:T(8,128)(2,1)}) %all-gather.8.cloned.1.call-update) | async-done | bytes 4718608 | tf_op jit(solution)/shard_map/all_gather | solution.py:900
  245.1 6.1 %unpack_rest.1 = (f32[2,512,1024]{2,1,0:T(8,128)}, f32[2,1024,512]{2,1,0:T(8,128)}, f32[2,3,512,256]{3,2,1,0:T(8,128)}, f32[2,256,512]{2,1,0:T(8,128)}, f32[2,10...) custom-call(bf16[8,8,144,256]{3,2,1,0:T(8,128)(2,1)} %bitcast.33, ...), custom_call_target="tpu_custom_call", output_to_operand_aliasing={{0}: (1, {}), {1}: (2, {})} | custom-call | tf_op jit(solution)/shard_map/unpack_rest/pallas_call | solution.py:742
  (44 shorter events, 16.2 us)
Async XLA Ops:
  7.2 95.1 %all-gather.6.cloned.1.call-start = ((), (), s32[]{:S(2)}) async-start(), calls=%async_computation.11 | async-start | bytes 2359296 | tf_op jit(solution)/shard_map/all_gather | solution.py:803
  10.2 12.8 %collective-permute-start.2 = (bf16[2,4,64,256]{3,2,1,0:T(8,128)(2,1)}, bf16[2,4,64,256]{3,2,1,0:T(8,128)(2,1)S(1)}, u32[]{:S(2)}, u32[]{:S(2)}) collective-permute-start(bf16[2,4,64,256]{3,2,1,0:T(8,128)(2,1)} %chunk.1), channel_id=1, source_target_pairs={{0,1},{1,0},{2,3},{3,2},{4,5},{5,4},{6,7},{7,6},{8,9},{9,8},{10,11... | collective-permute-start | bytes 786440 | tf_op jit(solution)/shard_map/ppermute | solution.py:759
  23.8 11.9 %all-to-all-start = ((bf16[8,208,128]{2,1,0:T(8,128)(2,1)}), bf16[8,208,128]{2,1,0:T(8,128)(2,1)S(1)}, u32[]{:S(2)}, u32[]{:S(2)}) async-start(bf16[8,208,128]{2,1,0:T(8,128)(2,1)} %get-tuple-element.52), calls=%async_computation | async-start | bytes 851968 | tf_op jit(solution)/shard_map/all_to_all | solution.py:763
  28.5 18.4 %collective-permute-start = (bf16[512,512]{1,0:T(8,128)(2,1)}, bf16[512,512]{1,0:T(8,128)(2,1)S(1)}, u32[]{:S(2)}, u32[]{:S(2)}) collective-permute-start(bf16[512,512]{1,0:T(8,128)(2,1)} %get-tuple-element.51.refs_2_), channel_id=1, source_target_pairs={{0,1},{1,0},{2,3},{3,2},{4,5},{5,4},{6,7},{7,6},{8,9},{9,8},{10,11... | collective-permute-start | bytes 1572872 | tf_op jit(solution)/shard_map/ppermute | solution.py:759
  35.7 0.8 copy-start
  40.3 11.9 %all-to-all-start.1 = ((bf16[16,64,128]{2,1,0:T(8,128)(2,1)}), bf16[16,64,128]{2,1,0:T(8,128)(2,1)S(1)}, u32[]{:S(2)}, u32[]{:S(2)}) async-start(bf16[16,64,128]{2,1,0:T(8,128)(2,1)} %bitcast.42), calls=%async_computation.1 | async-start | bytes 524288 | tf_op jit(solution)/shard_map/all_to_all | solution.py:763
  44.5 57.7 %reduce-scatter.3.cloned.1.call-start = ((), (), s32[]{:S(2)}) async-start(), calls=%async_computation.12 | async-start | bytes 2359296 | tf_op jit(solution)/shard_map/reduce_scatter | solution.py:831
  46.9 5.3 %copy-start.5 = (bf16[512,512]{1,0:T(8,128)(2,1)}, bf16[512,512]{1,0:T(8,128)(2,1)S(1)}, u32[]{:S(2)}) copy-start(bf16[512,512]{1,0:T(8,128)(2,1)S(1)} %collective-permute-done.refs_3_) | copy-start | bytes 1572868
  52.2 0.7 copy-start.1
  61.5 1.0 copy-start.7
  61.6 1.5 copy-start.6
  61.6 119.6 %reduce-scatter.5.cloned.1.call-start = ((), (), s32[]{:S(2)}) async-start(), calls=%async_computation.13 | async-start | bytes 3833856 | tf_op jit(solution)/shard_map/reduce_scatter | solution.py:864
  62.6 15.7 %collective-permute-start.1 = (bf16[512,512]{1,0:T(8,128)(2,1)S(1)}, bf16[512,512]{1,0:T(8,128)(2,1)S(1)}, u32[]{:S(2)}, u32[]{:S(2)}) collective-permute-start(bf16[512,512]{1,0:T(8,128)(2,1)S(1)} %copy-done.7), channel_id=1, source_target_pairs={{0,1},{1,0},{2,3},{3,2},{4,5},{5,4},{6,7},{7,6},{8,9},{9,8},{10,11... | collective-permute-start | bytes 1572872 | tf_op jit(solution)/shard_map/ppermute | solution.py:759
  78.3 0.8 copy-start.2
  112.9 3.7 %copy-start.8 = (bf16[256,512]{1,0:T(8,128)(2,1)S(1)}, bf16[256,512]{1,0:T(8,128)(2,1)}, u32[]{:S(2)}) copy-start(bf16[256,512]{1,0:T(8,128)(2,1)} %get-tuple-element.64.refs_3_) | copy-start | bytes 786436
  112.9 11.5 %all-to-all-start.4 = ((bf16[8,192,128]{2,1,0:T(8,128)(2,1)}), bf16[8,192,128]{2,1,0:T(8,128)(2,1)S(1)}, u32[]{:S(2)}, u32[]{:S(2)}) async-start(bf16[8,192,128]{2,1,0:T(8,128)(2,1)} %get-tuple-element.65), calls=%async_computation.5 | async-start | bytes 786432 | tf_op jit(solution)/shard_map/all_to_all | solution.py:763
  116.5 95.8 %all-gather.10.cloned.1.call-start = ((), (), s32[]{:S(2)}) async-start(), calls=%async_computation.15 | async-start | bytes 2359296 | tf_op jit(solution)/shard_map/all_gather | solution.py:898
  116.6 7.9 %collective-permute-start.3 = (bf16[256,512]{1,0:T(8,128)(2,1)S(1)}, bf16[256,512]{1,0:T(8,128)(2,1)S(1)}, u32[]{:S(2)}, u32[]{:S(2)}) collective-permute-start(bf16[256,512]{1,0:T(8,128)(2,1)S(1)} %copy-done.8), channel_id=1, source_target_pairs={{0,1},{1,0},{2,3},{3,2},{4,5},{5,4},{6,7},{7,6},{8,9},{9,8},{10,11... | collective-permute-start | bytes 786440 | tf_op jit(solution)/shard_map/ppermute | solution.py:759
  124.4 0.7 copy-start.4
  124.4 0.8 copy-start.3
  183.6 61.6 %all-gather.8.cloned.1.call-start = ((), (), s32[]{:S(2)}) async-start(), calls=%async_computation.14 | async-start | bytes 5308416 | tf_op jit(solution)/shard_map/all_gather | solution.py:900
Sparse Core Ops, SparseCore 0:
  23.9 25.6 all-gather.5
  61.7 31.3 reduce-scatter.2
  113.0 36.3 reduce-scatter.4
  183.7 21.4 all-gather.9
  212.4 32.6 all-gather.7

commit v8 on v7

--- a/solution.py
+++ b/solution.py
@@ -161,7 +161,7 @@
             for o in out_shape
         ],
         scratch_shapes=list(scratch) + buffers + sems,
-        compiler_params=pltpu.CompilerParams(vmem_limit_bytes=63 * 1024 * 1024),
+        compiler_params=pltpu.CompilerParams(vmem_limit_bytes=32 * 1024 * 1024),
         name=name,
     )(*arrays)
 
@@ -611,7 +611,7 @@
             ],
             out_specs=pl.BlockSpec((2, 4, 64, 256), lambda i, at: (0, 0, 0, 0)),
         ),
-        compiler_params=pltpu.CompilerParams(vmem_limit_bytes=63 * 1024 * 1024),
+        compiler_params=pltpu.CompilerParams(vmem_limit_bytes=32 * 1024 * 1024),
         name="chunk",
     )(at, wq, w_out)
 
@@ -720,7 +720,7 @@
             pl.BlockSpec((1, 256, 512), lambda p: (layer, p, 0)),
         ]
 
-    params = pltpu.CompilerParams(vmem_limit_bytes=63 * 1024 * 1024)
+    params = pltpu.CompilerParams(vmem_limit_bytes=32 * 1024 * 1024)
     g_up, g_down = pl.pallas_call(
         unpack_first_body,
         grid=(4,),

time: 259 us -> 275 us (1.062)
  local copies, waits for them, and re-layouts: 5.26 us -> 41.8 us
  Pallas kernels: 62.9 us -> 44.3 us
  blocking collectives: 104 us -> 100 us
    unnamed x18 -> x100, local copies, waits for them, and re-layouts: 4.07 us -> 40.5 us
    pallas_call x9, Pallas kernels: 50.3 us -> 37.9 us  [call(): pl.pallas_call(run, grid=(1,), out_shape=[jax.ShapeDtypeStruct(s, d) for...]
    all_to_all x6, blocking collectives: 104 us -> 100 us  [exchange(): return lax.all_to_all(value, axes, 0, 0)]
  transfers between devices with their start and end apart: 12 -> 12, of which waited for: 5 -> 5; matrix products, arithmetic and copies ran while one was open for 0% -> 0% of each run, Pallas kernels for 16% -> 11%
where the time goes in v8:
time: 275 us; the launch traced here: 273 us
  blocking collectives  100 us (36%)
  waiting for transfers between devices  50.3 us (18%)
  Pallas kernels  44.3 us (16%)
  local copies, waits for them, and re-layouts  41.8 us (15%)
  starting transfers between devices  20.4 us (7%)
  between operations  15.4 us (6%)
    all_to_all x6, blocking collectives, exchange(): return lax.all_to_all(value, axes, 0, 0)  100 us
    unnamed x100, local copies, waits for them, and re-layouts  40.5 us
    pallas_call x9, Pallas kernels, call(): pl.pallas_call(run, grid=(1,), out_shape=[jax.ShapeDtypeStruct(s, d) for...  37.9 us
    all_gather x1, waiting for transfers between devices, shards(): full_bc = lax.all_gather(exchange(summed, 'context'), 'dp')  29.8 us
    all_to_all x3, starting transfers between devices, exchange(): return lax.all_to_all(value, axes, 0, 0)  12.7 us
    ppermute x4, waiting for transfers between devices, swap(): return lax.ppermute(value, 'tensor', [(0, 1), (1, 0)])  10.8 us
    all_to_all x3, waiting for transfers between devices, exchange(): return lax.all_to_all(value, axes, 0, 0)  9.56 us
    ppermute x4, starting transfers between devices, swap(): return lax.ppermute(value, 'tensor', [(0, 1), (1, 0)])  7.53 us
  transfers between devices with their start and end apart: 12, of which 5 were waited for; matrix products, arithmetic and copies ran while one was open for 0% of the time, Pallas kernels for 11%

profile of v8, /device:TPU:1, one launch (start us, length us, event | category | flops | bytes accessed | tf_op | source)
XLA Modules:
  0.0 273.3 jit_solution(850506456958534990)
XLA Ops:
  10.4 4.5 %collective-permute-start.2 = (bf16[2,4,64,256]{3,2,1,0:T(8,128)(2,1)S(1)}, bf16[2,4,64,256]{3,2,1,0:T(8,128)(2,1)S(1)}, u32[]{:S(2)}, u32[]{:S(2)}) collective-permute-start(bf16[2,4,64,256]{3,2,1,0:T(8,128)(2,1)S(1)} %chunk.1), channel_id=1, source_target_pairs={{0,1},{1,0},{2,3},{3,2},{4,5},{5,4},{6,7},{7,6},{8,9},{9,8},{10,11... | collective-permute-start | bytes 786440 | tf_op jit(solution)/shard_map/ppermute | solution.py:759
  18.1 4.1 %norm_qkv_feed.1 = (bf16[8,208,128]{2,1,0:T(8,128)(2,1)}, bf16[512,512]{1,0:T(8,128)(2,1)S(1)}, bf16[256,1024]{1,0:T(8,128)(2,1)S(1)}, bf16[256,1024]{1,0:T(8,128)(2,1)S(1)}, f32[2,2,8,128]{3,2,1,0:T(8,128)S(1)}) custom-call(s32[3]{0:T(128)S(1)} %pad_add_fusion.refs_0_.at, s32[2,128]{1,0:T(2,128)S(1)} %copy-done.49, f32[8,1]{1,0:T(8,128)S(1)} %copy-done.48, ...), custom_call_target="tpu_custom_call" | custom-call | tf_op jit(solution)/shard_map/norm_qkv_feed/pallas_call | solution.py:154
  27.9 4.7 %all-to-all-start = ((bf16[8,208,128]{2,1,0:T(8,128)(2,1)}), bf16[8,208,128]{2,1,0:T(8,128)(2,1)S(1)}, u32[]{:S(2)}, u32[]{:S(2)}) async-start(bf16[8,208,128]{2,1,0:T(8,128)(2,1)} %get-tuple-element.52), calls=%async_computation | async-start | bytes 851968 | tf_op jit(solution)/shard_map/all_to_all | solution.py:763
  34.0 5.8 %all-to-all-done.refs_0_ = bf16[8,208,128]{2,1,0:T(8,128)(2,1)S(1)} async-done(((bf16[8,208,128]{2,1,0:T(8,128)(2,1)}), bf16[8,208,128]{2,1,0:T(8,128)(2,1)S(1)}, u32[]{:S(2)}, u32[]{:S(2)}) %all-to-all-start) | async-done | bytes 426016 | tf_op jit(solution)/shard_map/all_to_all | solution.py:763
  43.1 4.5 %all-to-all-start.1 = ((bf16[16,64,128]{2,1,0:T(8,128)(2,1)}), bf16[16,64,128]{2,1,0:T(8,128)(2,1)S(1)}, u32[]{:S(2)}, u32[]{:S(2)}) async-start(bf16[16,64,128]{2,1,0:T(8,128)(2,1)} %bitcast.42), calls=%async_computation.1 | async-start | bytes 524288 | tf_op jit(solution)/shard_map/all_to_all | solution.py:763
  47.6 3.9 %collective-permute-done.refs_3_ = bf16[512,512]{1,0:T(8,128)(2,1)} collective-permute-done((bf16[512,512]{1,0:T(8,128)(2,1)}, bf16[512,512]{1,0:T(8,128)(2,1)}, u32[]{:S(2)}, u32[]{:S(2)}) %collective-permute-start) | collective-permute-done | bytes 524320 | tf_op jit(solution)/shard_map/ppermute | solution.py:759
  51.5 3.7 %all-to-all-done.1 = bf16[16,64,128]{2,1,0:T(8,128)(2,1)S(1)} async-done(((bf16[16,64,128]{2,1,0:T(8,128)(2,1)}), bf16[16,64,128]{2,1,0:T(8,128)(2,1)S(1)}, u32[]{:S(2)}, u32[]{:S(2)}) %all-to-all-start.1) | async-done | bytes 262176 | tf_op jit(solution)/shard_map/all_to_all | solution.py:763
  60.5 9.4 %middle.1 = (f32[256,512]{1,0:T(8,128)S(1)}, bf16[8,256,128]{2,1,0:T(8,128)(2,1)S(1)}, bf16[8,512,256]{2,1,0:T(8,128)(2,1)S(1)}, bf16[512,512]{1,0:T(8,128)(2,1)...) custom-call(s32[3]{0:T(128)S(1)} %pad_add_fusion.refs_0_.at, f32[256,512]{1,0:T(8,128)S(1)} %bitcast.28, ...), custom_call_target="tpu_custom_call" | custom-call | tf_op jit(solution)/shard_map/middle/pallas_call | solution.py:154
  74.2 15.6 %all_to_all.45.refs_0_ = bf16[8,256,128]{2,1,0:T(8,128)(2,1)S(1)} all-to-all(bf16[8,256,128]{2,1,0:T(8,128)(2,1)} %copy-done.24), channel_id=1, replica_groups=mesh['dp'=8,'context'=8,'tensor'=2] {'context'}, dimensions={0} | all-to-all | bytes 1048576 | tf_op jit(solution)/shard_map/all_to_all | solution.py:763
  89.9 4.2 %attend_both.1 = bf16[8,2,256,128]{3,2,1,0:T(8,128)(2,1)S(1)} custom-call(bf16[8,256,128]{2,1,0:T(8,128)(2,1)S(1)} %all_to_all.45.refs_0_, s32[1,1024]{1,0:T(1,128)S(1)} %get-tuple-element.58.refs_1_.refs_2_, bf16[512,512]{1,0:T(8,128)(2,1)S(1)} %collective-permute-done.1.refs_2_.refs_3_), custom_call_target="tpu_custom_call" | custom-call | tf_op jit(solution)/shard_map/attend_both/pallas_call | solution.py:154
  94.1 16.6 %all_to_all.46 = bf16[16,256,128]{2,1,0:T(8,128)(2,1)} all-to-all(bf16[16,256,128]{2,1,0:T(8,128)(2,1)S(1)} %bitcast.34), channel_id=1, replica_groups=mesh['dp'=8,'context'=8,'tensor'=2] {'context','tensor'}, dimensions={0} | all-to-all | bytes 2097152 | tf_op jit(solution)/shard_map/all_to_all | solution.py:763
  123.9 10.1 %turn_point.1 = (f32[256,512]{1,0:T(8,128)}, f32[256,512]{1,0:T(8,128)S(1)}, bf16[8,192,128]{2,1,0:T(8,128)(2,1)S(1)}, bf16[8,832,256]{2,1,0:T(8,128)(2,1)S(1)},...) custom-call(s32[3]{0:T(128)S(1)} %pad_add_fusion.refs_0_.at, ...), custom_call_target="tpu_custom_call" | custom-call | tf_op jit(solution)/shard_map/turn_point/pallas_call | solution.py:154
  138.0 3.6 %all-to-all-start.4 = ((bf16[8,192,128]{2,1,0:T(8,128)(2,1)}), bf16[8,192,128]{2,1,0:T(8,128)(2,1)S(1)}, u32[]{:S(2)}, u32[]{:S(2)}) async-start(bf16[8,192,128]{2,1,0:T(8,128)(2,1)} %copy-done.36), calls=%async_computation.5 | async-start | bytes 786432 | tf_op jit(solution)/shard_map/all_to_all | solution.py:763
  142.8 7.0 %collective-permute-done.3.refs_5_.refs_4_ = bf16[256,512]{1,0:T(8,128)(2,1)S(1)} collective-permute-done((bf16[256,512]{1,0:T(8,128)(2,1)}, bf16[256,512]{1,0:T(8,128)(2,1)S(1)}, u32[]{:S(2)}, u32[]{:S(2)}) %collective-permute-start.3) | collective-permute-done | bytes 262176 | tf_op jit(solution)/shard_map/ppermute | solution.py:759
  149.8 2.2 attend_back.1
  152.0 18.7 %all_to_all.47 = bf16[16,320,128]{2,1,0:T(8,128)(2,1)S(1)} all-to-all(bf16[16,320,128]{2,1,0:T(8,128)(2,1)S(1)} %bitcast.31), channel_id=1, replica_groups=mesh['dp'=8,'context'=8,'tensor'=2] {'context','tensor'}, dimensions={0} | all-to-all | bytes 2621440 | tf_op jit(solution)/shard_map/all_to_all | solution.py:763
  170.8 5.1 %last.1 = (f32[256,512]{1,0:T(8,128)}, bf16[8,208,256]{2,1,0:T(8,128)(2,1)S(1)}, bf16[512,256]{1,0:T(8,128)(2,1)S(1)}, f32[3,256]{1,0:T(4,128)}, f32[4,512]{1,0:T(4,128)}) custom-call(s32[3]{0:T(128)S(1)} %pad_add_fusion.refs_0_.at, f32[256,512]{1,0:T(8,128)S(1)} %bitcast.30, f32[256,512]{1,0:T(8,128)S(1)} %copy-done.26, bf16[256,512]{1,0:T(8,128)(2,1)S(1)} %copy-done.41, ...), custom_call_target="tpu_custom_call" | custom-call | tf_op jit(solution)/shard_map/last/pallas_call | solution.py:154
  175.8 25.5 %all_to_all.48.refs_0_ = bf16[8,208,256]{2,1,0:T(8,128)(2,1)S(1)} all-to-all(bf16[8,208,256]{2,1,0:T(8,128)(2,1)S(1)} %get-tuple-element.75), channel_id=1, replica_groups=mesh['dp'=8,'context'=8,'tensor'=2] {'dp'}, dimensions={0} | all-to-all | bytes 1703936 | tf_op jit(solution)/shard_map/all_to_all | solution.py:763
  203.2 12.2 %all_to_all.49.refs_0_ = bf16[8,144,256]{2,1,0:T(8,128)(2,1)S(1)} all-to-all(bf16[8,144,256]{2,1,0:T(8,128)(2,1)S(1)} %get-tuple-element.78), channel_id=1, replica_groups=mesh['dp'=8,'context'=8,'tensor'=2] {'context'}, dimensions={0} | all-to-all | bytes 1179648 | tf_op jit(solution)/shard_map/all_to_all | solution.py:763
  215.5 11.6 %all_to_all.50 = bf16[8,144,256]{2,1,0:T(8,128)(2,1)} all-to-all(bf16[8,144,256]{2,1,0:T(8,128)(2,1)S(1)} %sum.1), channel_id=1, replica_groups=mesh['dp'=8,'context'=8,'tensor'=2] {'context'}, dimensions={0} | all-to-all | bytes 1179648 | tf_op jit(solution)/shard_map/all_to_all | solution.py:763
  228.8 2.4 unpack_first.1
  231.1 29.8 %all-gather.8.cloned.1.call-done = bf16[64,144,256]{2,1,0:T(8,128)(2,1)} async-done(((bf16[8,144,256]{2,1,0:T(8,128)(2,1)}), bf16[64,144,256]{2,1,0:T(8,128)(2,1)}) %all-gather.8.cloned.1.call-update) | async-done | bytes 4718608 | tf_op jit(solution)/shard_map/all_gather | solution.py:900
  260.9 2.3 copy-done.13
  263.3 3.5 %unpack_rest.1 = (f32[2,512,1024]{2,1,0:T(8,128)}, f32[2,1024,512]{2,1,0:T(8,128)}, f32[2,3,512,256]{3,2,1,0:T(8,128)}, f32[2,256,512]{2,1,0:T(8,128)}, f32[2,10...) custom-call(bf16[8,8,144,256]{3,2,1,0:T(8,128)(2,1)S(1)} %bitcast.33, ...), custom_call_target="tpu_custom_call", output_to_operand_aliasing={{0}: (1, {}), {1}: (2, {})} | custom-call | tf_op jit(solution)/shard_map/unpack_rest/pallas_call | solution.py:742
  (126 shorter events, 46.9 us)
Async XLA Ops:
  7.2 7.7 %copy-start.44 = (f32[2,2,512]{2,1,0:T(2,128)S(1)}, f32[2,2,512]{2,1,0:T(2,128)}, u32[]{:S(2)}) copy-start(f32[2,2,512]{2,1,0:T(2,128)} %refs_10_.5) | copy-start | bytes 24580
  7.2 7.7 %copy-start.43 = (f32[2,2,512]{2,1,0:T(2,128)S(1)}, f32[2,2,512]{2,1,0:T(2,128)}, u32[]{:S(2)}) copy-start(f32[2,2,512]{2,1,0:T(2,128)} %refs_9_.5) | copy-start | bytes 24580
  7.2 7.7 %copy-start.45 = (f32[2,1024]{1,0:T(2,128)S(1)}, f32[2,1024]{1,0:T(2,128)}, u32[]{:S(2)}) copy-start(f32[2,1024]{1,0:T(2,128)} %refs_12_.1) | copy-start | bytes 24580
  7.2 7.7 %copy-start.49 = (s32[2,128]{1,0:T(2,128)S(1)}, s32[2,128]{1,0:T(2,128)}, u32[]{:S(2)}) copy-start(s32[2,128]{1,0:T(2,128)} %refs_1_.1) | copy-start | bytes 3076
  7.2 103.5 %all-gather.6.cloned.1.call-start = ((), (), s32[]{:S(2)}) async-start(), calls=%async_computation.11 | async-start | bytes 2359296 | tf_op jit(solution)/shard_map/all_gather | solution.py:803
  9.8 5.1 %copy-start.47 = (f32[2,3,256]{2,0,1:T(2,128)S(1)}, f32[2,3,256]{2,0,1:T(2,128)}, u32[]{:S(2)}) copy-start(f32[2,3,256]{2,0,1:T(2,128)} %param.17) | copy-start | bytes 18436
  9.8 5.1 %copy-start.48 = (f32[8,1]{1,0:T(8,128)S(1)}, f32[8,1]{1,0:T(8,128)}, u32[]{:S(2)}) copy-start(f32[8,1]{1,0:T(8,128)} %constant.21.refs_2_) | copy-start | bytes 100
  10.4 16.8 %collective-permute-start.2 = (bf16[2,4,64,256]{3,2,1,0:T(8,128)(2,1)S(1)}, bf16[2,4,64,256]{3,2,1,0:T(8,128)(2,1)S(1)}, u32[]{:S(2)}, u32[]{:S(2)}) collective-permute-start(bf16[2,4,64,256]{3,2,1,0:T(8,128)(2,1)S(1)} %chunk.1), channel_id=1, source_target_pairs={{0,1},{1,0},{2,3},{3,2},{4,5},{5,4},{6,7},{7,6},{8,9},{9,8},{10,11... | collective-permute-start | bytes 786440 | tf_op jit(solution)/shard_map/ppermute | solution.py:759
  24.6 30.6 %copy-start.9 = (bf16[2,256,512]{2,1,0:T(8,128)(2,1)S(1)}, bf16[2,256,512]{2,1,0:T(8,128)(2,1)}, u32[]{:S(2)}) copy-start(bf16[2,256,512]{2,1,0:T(8,128)(2,1)} %refs_18_.1) | copy-start | bytes 1572868
  24.6 30.6 %copy-start.46 = (f32[2,2,512]{2,1,0:T(2,128)S(1)}, f32[2,2,512]{2,1,0:T(2,128)}, u32[]{:S(2)}) copy-start(f32[2,2,512]{2,1,0:T(2,128)} %refs_8_.5) | copy-start | bytes 24580
  27.9 11.9 %all-to-all-start = ((bf16[8,208,128]{2,1,0:T(8,128)(2,1)}), bf16[8,208,128]{2,1,0:T(8,128)(2,1)S(1)}, u32[]{:S(2)}, u32[]{:S(2)}) async-start(bf16[8,208,128]{2,1,0:T(8,128)(2,1)} %get-tuple-element.52), calls=%async_computation | async-start | bytes 851968 | tf_op jit(solution)/shard_map/all_to_all | solution.py:763
  32.6 18.9 %collective-permute-start = (bf16[512,512]{1,0:T(8,128)(2,1)}, bf16[512,512]{1,0:T(8,128)(2,1)}, u32[]{:S(2)}, u32[]{:S(2)}) collective-permute-start(bf16[512,512]{1,0:T(8,128)(2,1)} %copy-done.22), channel_id=1, source_target_pairs={{0,1},{1,0},{2,3},{3,2},{4,5},{5,4},{6,7},{7,6},{8,9},{9,8},{10,11... | collective-permute-start | bytes 1572872 | tf_op jit(solution)/shard_map/ppermute | solution.py:759
  43.1 12.1 %all-to-all-start.1 = ((bf16[16,64,128]{2,1,0:T(8,128)(2,1)}), bf16[16,64,128]{2,1,0:T(8,128)(2,1)S(1)}, u32[]{:S(2)}, u32[]{:S(2)}) async-start(bf16[16,64,128]{2,1,0:T(8,128)(2,1)} %bitcast.42), calls=%async_computation.1 | async-start | bytes 524288 | tf_op jit(solution)/shard_map/all_to_all | solution.py:763
  47.6 63.1 %reduce-scatter.3.cloned.1.call-start = ((), (), s32[]{:S(2)}) async-start(), calls=%async_computation.12 | async-start | bytes 2359296 | tf_op jit(solution)/shard_map/reduce_scatter | solution.py:831
  73.7 127.7 %reduce-scatter.5.cloned.1.call-start = ((), (), s32[]{:S(2)}) async-start(), calls=%async_computation.13 | async-start | bytes 3833856 | tf_op jit(solution)/shard_map/reduce_scatter | solution.py:864
  73.7 16.2 %collective-permute-start.1 = (bf16[512,512]{1,0:T(8,128)(2,1)}, bf16[512,512]{1,0:T(8,128)(2,1)S(1)}, u32[]{:S(2)}, u32[]{:S(2)}) collective-permute-start(bf16[512,512]{1,0:T(8,128)(2,1)} %copy-done.33), channel_id=1, source_target_pairs={{0,1},{1,0},{2,3},{3,2},{4,5},{5,4},{6,7},{7,6},{8,9},{9,8},{10,11... | collective-permute-start | bytes 1572872 | tf_op jit(solution)/shard_map/ppermute | solution.py:759
  138.0 11.8 %copy-start.39 = (f32[64,1024]{1,0:T(8,128)S(1)}, f32[64,1024]{1,0:T(8,128)}, u32[]{:S(2)}) copy-start(f32[64,1024]{1,0:T(8,128)} %copy-done.38) | copy-start | bytes 786436
  138.0 11.7 %all-to-all-start.4 = ((bf16[8,192,128]{2,1,0:T(8,128)(2,1)}), bf16[8,192,128]{2,1,0:T(8,128)(2,1)S(1)}, u32[]{:S(2)}, u32[]{:S(2)}) async-start(bf16[8,192,128]{2,1,0:T(8,128)(2,1)} %copy-done.36), calls=%async_computation.5 | async-start | bytes 786432 | tf_op jit(solution)/shard_map/all_to_all | solution.py:763
  141.6 85.5 %all-gather.10.cloned.1.call-start = ((), (), s32[]{:S(2)}) async-start(), calls=%async_computation.15 | async-start | bytes 2359296 | tf_op jit(solution)/shard_map/all_gather | solution.py:898
  141.7 8.1 %collective-permute-start.3 = (bf16[256,512]{1,0:T(8,128)(2,1)}, bf16[256,512]{1,0:T(8,128)(2,1)S(1)}, u32[]{:S(2)}, u32[]{:S(2)}) collective-permute-start(bf16[256,512]{1,0:T(8,128)(2,1)} %copy-done.40), channel_id=1, source_target_pairs={{0,1},{1,0},{2,3},{3,2},{4,5},{5,4},{6,7},{7,6},{8,9},{9,8},{10,11... | collective-permute-start | bytes 786440 | tf_op jit(solution)/shard_map/ppermute | solution.py:759
  149.8 21.0 %copy-start.11 = (bf16[2,4,512,256]{3,2,1,0:T(8,128)(2,1)S(1)}, bf16[2,4,512,256]{3,2,1,0:T(8,128)(2,1)}, u32[]{:S(2)}) copy-start(bf16[2,4,512,256]{3,2,1,0:T(8,128)(2,1)} %all-gather.6.cloned.1.call-done.refs_7_) | copy-start | bytes 6291460
  149.8 21.0 %copy-start.26 = (f32[256,512]{1,0:T(8,128)S(1)}, f32[256,512]{1,0:T(8,128)}, u32[]{:S(2)}) copy-start(f32[256,512]{1,0:T(8,128)} %copy-done.25) | copy-start | bytes 1572868
  149.8 21.0 %copy-start.41 = (bf16[256,512]{1,0:T(8,128)(2,1)S(1)}, bf16[256,512]{1,0:T(8,128)(2,1)}, u32[]{:S(2)}) copy-start(bf16[256,512]{1,0:T(8,128)(2,1)} %copy-done.40) | copy-start | bytes 786436
  203.2 57.7 %all-gather.8.cloned.1.call-start = ((), (), s32[]{:S(2)}) async-start(), calls=%async_computation.14 | async-start | bytes 5308416 | tf_op jit(solution)/shard_map/all_gather | solution.py:900
  (38 other events, 54.9 us)
Sparse Core Ops, SparseCore 0:
  28.0 25.1 all-gather.5
  73.8 31.3 reduce-scatter.2
  138.2 36.2 reduce-scatter.4
  203.3 21.4 all-gather.9
  227.3 33.6 all-gather.7

commit v9 on v6

--- a/solution.py
+++ b/solution.py
@@ -35,7 +35,7 @@
 
 class Layer:
     def __init__(self, array, index):
-        self.array, self.index = array, index
+        self.array, self.index = far(array), index
 
     def spec(self):
         rest = self.array.shape[1:]
@@ -43,25 +43,40 @@
         return pl.BlockSpec((None,) + rest, lambda i: place)
 
 
+class Far:
+    def __init__(self, array):
+        self.array = far(array)
+
+    def spec(self):
+        return whole(self.array.shape)
+
+
+Kept = type(pltpu.HBM((8, 128), F32))
+
+
+def far(array):
+    return pltpu.with_memory_space_constraint(array, pltpu.HBM)
+
+
 def whole(shape):
     return pl.BlockSpec(shape, lambda i: (0,) * len(shape))
 
 
 def call(body, out_shape, args, name, scratch=(), smem_first=False):
     specs = [
-        a.spec() if isinstance(a, (Layer, After)) else whole(a.shape) for a in args
+        a.spec() if isinstance(a, (Layer, Far, After)) else whole(a.shape) for a in args
     ]
-    args = [a.array if isinstance(a, (Layer, After)) else a for a in args]
+    args = [a.array if isinstance(a, (Layer, Far, After)) else a for a in args]
     if smem_first:
         specs[0] = pl.BlockSpec(memory_space=pltpu.SMEM)
     return pl.pallas_call(
         body,
         grid=(1,),
-        out_shape=[jax.ShapeDtypeStruct(s, d) for s, d in out_shape],
+        out_shape=[o if isinstance(o, Kept) else jax.ShapeDtypeStruct(*o) for o in out_shape],
         in_specs=specs,
-        out_specs=[whole(s) for s, _ in out_shape],
+        out_specs=[whole(o.shape if isinstance(o, Kept) else o[0]) for o in out_shape],
         scratch_shapes=list(scratch),
-        compiler_params=pltpu.CompilerParams(vmem_limit_bytes=63 * 1024 * 1024),
+        compiler_params=pltpu.CompilerParams(vmem_limit_bytes=40 * 1024 * 1024),
         name=name,
     )(*args)
 
@@ -107,7 +122,8 @@
         cdf = 0.5 + 0.5 * lax.erf(pre * np.float32(0.7071067811865476))
         a = (pre * cdf).astype(BF)
         act[:, cols] = a
-        slope[:, cols] = cdf + pre * (jnp.exp(-0.5 * pre * pre) * np.float32(0.3989422804014327))
+        tail = pre * (jnp.exp(-0.5 * pre * pre) * np.float32(0.3989422804014327))
+        slope[:, cols] = (cdf + tail).astype(BF)
         term = mm(a, w_down[cols, :])
         total = term if total is None else total + term
     return total
@@ -120,7 +136,7 @@
     for c in range(0, width, 256):
         cols = slice(c, c + 256)
         d_act = mm(g_b, w_down[cols, :], 1, 1)
-        d_pre = d_act * slope[:, cols]
+        d_pre = d_act * slope[:, cols].astype(F32)
         d_pre_b = d_pre.astype(BF)
         d_b_up[:, cols] = jnp.sum(d_pre_b.astype(F32), 0, keepdims=True)
         d_up(c // 256, mm(mlp_t, d_pre_b))
@@ -496,13 +512,9 @@
             ],
             out_specs=pl.BlockSpec((2, 4, 64, 256), lambda i, at: (0, 0, 0, 0)),
         ),
-        compiler_params=pltpu.CompilerParams(vmem_limit_bytes=63 * 1024 * 1024),
+        compiler_params=pltpu.CompilerParams(vmem_limit_bytes=40 * 1024 * 1024),
         name="chunk",
-    )(at, wq, w_out)
-
-
-def hand_on_body(value, _, out):
-    out[...] = value[...]
+    )(at, far(wq), far(w_out))
 
 
 def mix_body(got, early, first, out, first_out):
@@ -609,16 +621,16 @@
             pl.BlockSpec((1, 256, 512), lambda p: (layer, p, 0)),
         ]
 
-    params = pltpu.CompilerParams(vmem_limit_bytes=63 * 1024 * 1024)
+    params = pltpu.CompilerParams(vmem_limit_bytes=40 * 1024 * 1024)
     g_up, g_down = pl.pallas_call(
         unpack_first_body,
         grid=(4,),
-        out_shape=[jax.ShapeDtypeStruct(UP, F32), jax.ShapeDtypeStruct(DOWN, F32)],
+        out_shape=[pltpu.HBM(UP, F32), pltpu.HBM(DOWN, F32)],
         in_specs=[pl.BlockSpec((2, 512, 256), lambda p: (p, 0, 0))],
         out_specs=place(1),
         compiler_params=params,
         name="unpack_first",
-    )(first)
+    )(far(first))
     outs = [
         ((2, 3, 512, 256), pl.BlockSpec((2, 3, 128, 256), lambda p: (0, 0, p, 0))),
         ((2, 256, 512), pl.BlockSpec((2, 64, 512), lambda p: (0, p, 0))),
@@ -631,7 +643,7 @@
     return pl.pallas_call(
         unpack_rest_body,
         grid=(4,),
-        out_shape=[jax.ShapeDtypeStruct(shape, F32) for shape in [UP, DOWN] + [o[0] for o in outs]],
+        out_shape=[pltpu.HBM(shape, F32) for shape in [UP, DOWN] + [o[0] for o in outs]],
         in_specs=[
             pl.BlockSpec((2, 8, 144, 256), lambda p: (p, 0, 0, 0)),
             pl.BlockSpec(memory_space=pl.ANY),
@@ -641,7 +653,7 @@
         input_output_aliases={1: 0, 2: 1},
         compiler_params=params,
         name="unpack_rest",
-    )(rest, g_up, g_down)
+    )(far(rest), far(g_up), far(g_down))
 
 
 def swap(value):
@@ -675,19 +687,20 @@
         [
             ((8, 208, BLK), BF),
             ((2 * rows, width), BF),
-            ((rows, 1024), BF),
-            ((rows, 1024), F32),
+            pltpu.HBM((rows, 1024), BF),
+            pltpu.HBM((rows, 1024), BF),
             ((2, 2, HALF, BLK), F32),
         ],
         (
-            at, positions, freqs, x, ln_gain, ln_bias, Layer(wq, 0), bq, Layer(w_up, 0), b_up,
+            at, positions, freqs, Far(x), ln_gain, ln_bias, Layer(wq, 0), bq, Layer(w_up, 0), b_up,
             Layer(w_down, 0), Layer(w_out, 0),
         ),
         "norm_qkv_feed",
         smem_first=True,
     )
     pair_other = swap(pair)
-    (chunk,) = call(hand_on_body, [(chunk.shape, BF)], (chunk, After(send)), "hand_on")
+    mark = send[0, 0, 0]
+    chunk = jnp.where(mark == mark, chunk, 0)
     others = lax.all_gather(chunk, "dp", axis=2, tiled=True)
     recv = exchange(send, "context")
     ctx_send, lse, ctx, start = call(
@@ -700,19 +713,19 @@
     stream, send, grads_a, parts, d_b_up1, d_sum1 = call(
         middle_body,
         [
-            ((rows, width), F32),
+            pltpu.HBM((rows, width), F32),
             ((8, 256, BLK), BF),
-            ((8, 512, 256), BF),
+            pltpu.HBM((8, 512, 256), BF),
             ((2 * rows, width), BF),
             ((1, 1024), F32),
             ((1, width), F32),
         ],
         (
-            at, x, pair, pair_other, recv_ctx, Layer(w_out, 0), out_bias, ln_gain, ln_bias,
-            Layer(wq, 1), bq, Layer(w_up, 1), b_up, Layer(w_down, 1), Layer(w_out, 1), cot, cs,
+            at, Far(x), pair, pair_other, recv_ctx, Layer(w_out, 0), out_bias, ln_gain, ln_bias,
+            Layer(wq, 1), bq, Layer(w_up, 1), b_up, Layer(w_down, 1), Layer(w_out, 1), Far(cot), cs,
         ),
         "middle",
-        scratch=[pltpu.VMEM((rows, 1024), BF), pltpu.VMEM((rows, 1024), F32)],
+        scratch=[pltpu.VMEM((rows, 1024), BF), pltpu.VMEM((rows, 1024), BF)],
         smem_first=True,
     )
     sums_a = lax.psum_scatter(grads_a, "dp", scatter_dimension=0)
@@ -729,10 +742,10 @@
     block_out, g, send, grads_b, part_g, d_b_up0, d_b_qkv1, d_norm1, d_sum0 = call(
         turn_point_body,
         [
-            ((rows, width), F32),
-            ((rows, width), F32),
+            pltpu.HBM((rows, width), F32),
+            pltpu.HBM((rows, width), F32),
             ((8, 192, BLK), BF),
-            ((8, 832, 256), BF),
+            pltpu.HBM((8, 832, 256), BF),
             ((rows, width), BF),
             ((1, 1024), F32),
             ((3, 256), F32),
@@ -740,9 +753,9 @@
             ((1, width), F32),
         ],
         (
-            at, stream, parts, parts_other, recv_grad, Layer(w_out, 1), Layer(wq, 1), Layer(others, 1),
-            out_bias, ln_gain, ln_bias, cot, cs, x, act, slope, Layer(w_up, 0), Layer(w_down, 0),
-            Layer(w_out, 0), recv_ctx, sums_a,
+            at, Far(stream), parts, parts_other, recv_grad, Layer(w_out, 1), Layer(wq, 1),
+            Layer(others, 1), out_bias, ln_gain, ln_bias, Far(cot), cs, Far(x), Far(act), Far(slope),
+            Layer(w_up, 0), Layer(w_down, 0), Layer(w_out, 0), recv_ctx, Far(sums_a),
         ),
         "turn_point",
         smem_first=True,
@@ -761,14 +774,14 @@
     in_grad, grads_c, sums_a, _, _ = call(
         last_body,
         [
-            ((rows, width), F32),
+            pltpu.HBM((rows, width), F32),
             ((8, 208, 256), BF),
-            ((512, 256), BF),
+            pltpu.HBM((512, 256), BF),
             ((3, 256), F32),
             ((4, width), F32),
         ],
         (
-            at, x, g, part_g, part_g_other, recv_grad0, Layer(wq, 0), Layer(others, 0), cs,
+            at, Far(x), Far(g), part_g, part_g_other, recv_grad0, Layer(wq, 0), Layer(others, 0), cs,
             ln_gain, ln_bias, d_b_up0, d_b_up1, d_b_qkv1, d_norm1, d_sum0, d_sum1,
         ),
         "last",
@@ -776,8 +789,8 @@
     )
     mixed, sums_a = call(
         mix_body,
-        [((8, 144, 256), BF), ((512, 256), BF)],
-        (exchange(grads_c, "dp"), sums_b, sums_a),
+        [((8, 144, 256), BF), pltpu.HBM((512, 256), BF)],
+        (exchange(grads_c, "dp"), Far(sums_b), Far(sums_a)),
         "mix",
     )
     full_a = lax.all_gather(sums_a, "dp")

time: 255 us -> 235 us (0.922)
  Pallas kernels: 59.4 us -> 46 us
  blocking collectives: 103 us -> 98 us
  local copies, waits for them, and re-layouts: 4.77 us -> 1.93 us
    pallas_call x12 -> x11, Pallas kernels: 57.1 us -> 44.5 us  [the longest x9 34.3 us: call(): pl.pallas_call(body, grid=(1,), out_shape=[o if isinstance(o, Kept) else...]
    all_to_all x6, blocking collectives: 103 us -> 98 us  [exchange(): return lax.all_to_all(value, axes, 0, 0)]
    unnamed x20 -> x18, local copies, waits for them, and re-layouts: 4.77 us -> 0.72 us
  transfers between devices with their start and end apart: 12 -> 12, of which waited for: 7 -> 6; matrix products, arithmetic and copies ran while one was open for 0% -> 1% of each run, Pallas kernels for 15% -> 12%
where the time goes in v9:
time: 235 us; the launch traced here: 234 us
  blocking collectives  98 us (42%)
  waiting for transfers between devices  48.2 us (21%)
  Pallas kernels  46 us (20%)
  starting transfers between devices  23.7 us (10%)
  between operations  15.2 us (6%)
    all_to_all x6, blocking collectives, exchange(): return lax.all_to_all(value, axes, 0, 0)  98 us
    pallas_call x9, Pallas kernels, call(): pl.pallas_call(body, grid=(1,), out_shape=[o if isinstance(o, Kept) else...  34.3 us
    all_gather x1, waiting for transfers between devices, shards(): full_bc = lax.all_gather(exchange(summed, 'context'), 'dp')  29.6 us
    all_to_all x3, starting transfers between devices, exchange(): return lax.all_to_all(value, axes, 0, 0)  13.5 us
    ppermute x4, starting transfers between devices, swap(): return lax.ppermute(value, 'tensor', [(0, 1), (1, 0)])  10 us
    ppermute x4, waiting for transfers between devices, swap(): return lax.ppermute(value, 'tensor', [(0, 1), (1, 0)])  9.31 us
    all_to_all x3, waiting for transfers between devices, exchange(): return lax.all_to_all(value, axes, 0, 0)  9.22 us
    pallas_call x1, Pallas kernels, unpack(): pl.pallas_call(unpack_rest_body, grid=(4,), out_shape=[pltpu.HBM(shape, F...  6.11 us
  transfers between devices with their start and end apart: 12, of which 6 were waited for; matrix products, arithmetic and copies ran while one was open for 1% of the time, Pallas kernels for 12%

profile of v9, /device:TPU:1, one launch (start us, length us, event | category | flops | bytes accessed | tf_op | source)
XLA Modules:
  0.0 233.9 jit_solution(5173545341456245206)
XLA Ops:
  8.9 4.5 %collective-permute-start.2 = (bf16[2,4,64,256]{3,2,1,0:T(8,128)(2,1)S(1)}, bf16[2,4,64,256]{3,2,1,0:T(8,128)(2,1)S(1)}, u32[]{:S(2)}, u32[]{:S(2)}) collective-permute-start(bf16[2,4,64,256]{3,2,1,0:T(8,128)(2,1)S(1)} %chunk.1), channel_id=1, source_target_pairs={{0,1},{1,0},{2,3},{3,2},{4,5},{5,4},{6,7},{7,6},{8,9},{9,8},{10,11... | collective-permute-start | bytes 786440 | tf_op jit(solution)/shard_map/ppermute | solution.py:660
  13.4 4.4 %norm_qkv_feed.1 = (bf16[8,208,128]{2,1,0:T(8,128)(2,1)}, bf16[512,512]{1,0:T(8,128)(2,1)S(1)}, bf16[256,1024]{1,0:T(8,128)(2,1)}, bf16[256,1024]{1,0:T(8,128)(2,1)}, f32[2,2,8,128]{3,2,1,0:T(8,128)S(1)}) custom-call(s32[3]{0:T(128)S(1)} %pad_add_fusion.at, s32[2,128]{1,0:T(2,128)S(1)} %copy-done.8, f32[8,1]{1,0:T(8,128)S(1)} %copy-done.7, ...), custom_call_target="tpu_custom_call" | custom-call | tf_op jit(solution)/shard_map/norm_qkv_feed/pallas_call | solution.py:72
  21.1 4.7 %all-to-all-start = ((bf16[8,208,128]{2,1,0:T(8,128)(2,1)}), bf16[8,208,128]{2,1,0:T(8,128)(2,1)S(1)}, u32[]{:S(2)}, u32[]{:S(2)}) async-start(bf16[8,208,128]{2,1,0:T(8,128)(2,1)} %get-tuple-element.52), calls=%async_computation | async-start | bytes 851968 | tf_op jit(solution)/shard_map/all_to_all | solution.py:664
  28.1 4.9 %all-to-all-done.recv = bf16[8,208,128]{2,1,0:T(8,128)(2,1)S(1)} async-done(((bf16[8,208,128]{2,1,0:T(8,128)(2,1)}), bf16[8,208,128]{2,1,0:T(8,128)(2,1)S(1)}, u32[]{:S(2)}, u32[]{:S(2)}) %all-to-all-start) | async-done | bytes 426016 | tf_op jit(solution)/shard_map/all_to_all | solution.py:664
  33.0 2.6 %attend.1 = (bf16[8,2,64,128]{3,2,1,0:T(8,128)(2,1)}, f32[1,1024]{1,0:T(1,128)S(1)}, f32[64,1024]{1,0:T(8,128)S(1)}, s32[1,1024]{1,0:T(1,128)S(1)}) custom-call(bf16[8,208,128]{2,1,0:T(8,128)(2,1)S(1)} %all-to-all-done.recv), custom_call_target="tpu_custom_call" | custom-call | tf_op jit(solution)/shard_map/attend/pallas_call | solution.py:72
  36.3 4.2 %all-to-all-start.1 = ((bf16[16,64,128]{2,1,0:T(8,128)(2,1)}), bf16[16,64,128]{2,1,0:T(8,128)(2,1)S(1)}, u32[]{:S(2)}, u32[]{:S(2)}) async-start(bf16[16,64,128]{2,1,0:T(8,128)(2,1)} %bitcast.6), calls=%async_computation.1 | async-start | bytes 524288 | tf_op jit(solution)/shard_map/all_to_all | solution.py:664
  40.5 3.3 %collective-permute-done.pair_other = bf16[512,512]{1,0:T(8,128)(2,1)S(1)} collective-permute-done((bf16[512,512]{1,0:T(8,128)(2,1)S(1)}, bf16[512,512]{1,0:T(8,128)(2,1)S(1)}, u32[]{:S(2)}, u32[]{:S(2)}) %collective-permute-start) | collective-permute-done | bytes 524320 | tf_op jit(solution)/shard_map/ppermute | solution.py:660
  43.8 4.3 %all-to-all-done.1 = bf16[16,64,128]{2,1,0:T(8,128)(2,1)S(1)} async-done(((bf16[16,64,128]{2,1,0:T(8,128)(2,1)}), bf16[16,64,128]{2,1,0:T(8,128)(2,1)S(1)}, u32[]{:S(2)}, u32[]{:S(2)}) %all-to-all-start.1) | async-done | bytes 262176 | tf_op jit(solution)/shard_map/all_to_all | solution.py:664
  48.1 6.8 %middle.1 = (f32[256,512]{1,0:T(8,128)}, bf16[8,256,128]{2,1,0:T(8,128)(2,1)S(1)}, bf16[8,512,256]{2,1,0:T(8,128)(2,1)}, bf16[512,512]{1,0:T(8,128)(2,1)S(1)}, f...) custom-call(s32[3]{0:T(128)S(1)} %pad_add_fusion.at, f32[256,512]{1,0:T(8,128)} %bitcast.36, ...), custom_call_target="tpu_custom_call" | custom-call | tf_op jit(solution)/shard_map/middle/pallas_call | solution.py:72
  55.6 11.8 %all_to_all.45.recv = bf16[8,256,128]{2,1,0:T(8,128)(2,1)S(1)} all-to-all(bf16[8,256,128]{2,1,0:T(8,128)(2,1)S(1)} %get-tuple-element.57), channel_id=1, replica_groups=mesh['dp'=8,'context'=8,'tensor'=2] {'context'}, dimensions={0} | all-to-all | bytes 1048576 | tf_op jit(solution)/shard_map/all_to_all | solution.py:664
  67.5 4.2 %attend_both.1 = bf16[8,2,256,128]{3,2,1,0:T(8,128)(2,1)S(1)} custom-call(bf16[8,256,128]{2,1,0:T(8,128)(2,1)S(1)} %all_to_all.45.recv, s32[1,1024]{1,0:T(1,128)S(1)} %get-tuple-element.58.start, bf16[512,512]{1,0:T(8,128)(2,1)S(1)} %collective-permute-done.1._.parts_other), custom_call_target="tpu_custom_call" | custom-call | tf_op jit(solution)/shard_map/attend_both/pallas_call | solution.py:72
  71.7 16.7 %all_to_all.46 = bf16[16,256,128]{2,1,0:T(8,128)(2,1)S(1)} all-to-all(bf16[16,256,128]{2,1,0:T(8,128)(2,1)S(1)} %bitcast.24), channel_id=1, replica_groups=mesh['dp'=8,'context'=8,'tensor'=2] {'context','tensor'}, dimensions={0} | all-to-all | bytes 2097152 | tf_op jit(solution)/shard_map/all_to_all | solution.py:664
  88.4 8.2 %turn_point.1 = (f32[256,512]{1,0:T(8,128)}, f32[256,512]{1,0:T(8,128)}, bf16[8,192,128]{2,1,0:T(8,128)(2,1)}, bf16[8,832,256]{2,1,0:T(8,128)(2,1)}, bf16[256,51...) custom-call(s32[3]{0:T(128)S(1)} %pad_add_fusion.at, ...), custom_call_target="tpu_custom_call" | custom-call | tf_op jit(solution)/shard_map/turn_point/pallas_call | solution.py:72
  96.6 4.6 %all-to-all-start.4 = ((bf16[8,192,128]{2,1,0:T(8,128)(2,1)}), bf16[8,192,128]{2,1,0:T(8,128)(2,1)S(1)}, u32[]{:S(2)}, u32[]{:S(2)}) async-start(bf16[8,192,128]{2,1,0:T(8,128)(2,1)} %get-tuple-element.65), calls=%async_computation.5 | async-start | bytes 786432 | tf_op jit(solution)/shard_map/all_to_all | solution.py:664
  101.2 2.6 %collective-permute-start.3 = (bf16[256,512]{1,0:T(8,128)(2,1)S(1)}, bf16[256,512]{1,0:T(8,128)(2,1)S(1)}, u32[]{:S(2)}, u32[]{:S(2)}) collective-permute-start(bf16[256,512]{1,0:T(8,128)(2,1)S(1)} %get-tuple-element.64.part), channel_id=1, source_target_pairs={{0,1},{1,0},{2,3},{3,2},{4,5},{5,4},{6,7},{7,6},{8,9},{9,8},{10,11... | collective-permute-start | bytes 786440 | tf_op jit(solution)/shard_map/ppermute | solution.py:660
  103.9 5.9 %collective-permute-done.3._.part_other = bf16[256,512]{1,0:T(8,128)(2,1)S(1)} collective-permute-done((bf16[256,512]{1,0:T(8,128)(2,1)S(1)}, bf16[256,512]{1,0:T(8,128)(2,1)S(1)}, u32[]{:S(2)}, u32[]{:S(2)}) %collective-permute-start.3) | collective-permute-done | bytes 262176 | tf_op jit(solution)/shard_map/ppermute | solution.py:660
  112.1 18.2 %all_to_all.47 = bf16[16,320,128]{2,1,0:T(8,128)(2,1)S(1)} all-to-all(bf16[16,320,128]{2,1,0:T(8,128)(2,1)S(1)} %bitcast.22), channel_id=1, replica_groups=mesh['dp'=8,'context'=8,'tensor'=2] {'context','tensor'}, dimensions={0} | all-to-all | bytes 2621440 | tf_op jit(solution)/shard_map/all_to_all | solution.py:664
  130.3 3.9 %last.1 = (f32[256,512]{1,0:T(8,128)}, bf16[8,208,256]{2,1,0:T(8,128)(2,1)S(1)}, bf16[512,256]{1,0:T(8,128)(2,1)}, f32[3,256]{1,0:T(4,128)}, f32[4,512]{1,0:T(4,128)}) custom-call(s32[3]{0:T(128)S(1)} %pad_add_fusion.at, f32[256,512]{1,0:T(8,128)} %bitcast.38, f32[256,512]{1,0:T(8,128)} %get-tuple-element.63.g, bf16[256,512]{1,0:T(8,128)(2,1)S(1)} %get-tuple-element.64.part, ...), custom_call_target="tpu_custom_call" | custom-call | tf_op jit(solution)/shard_map/last/pallas_call | solution.py:72
  134.2 27.5 %all_to_all.48.got = bf16[8,208,256]{2,1,0:T(8,128)(2,1)S(1)} all-to-all(bf16[8,208,256]{2,1,0:T(8,128)(2,1)S(1)} %get-tuple-element.75), channel_id=1, replica_groups=mesh['dp'=8,'context'=8,'tensor'=2] {'dp'}, dimensions={0} | all-to-all | bytes 1703936 | tf_op jit(solution)/shard_map/all_to_all | solution.py:664
  163.6 12.2 %all_to_all.49.got = bf16[8,144,256]{2,1,0:T(8,128)(2,1)S(1)} all-to-all(bf16[8,144,256]{2,1,0:T(8,128)(2,1)S(1)} %get-tuple-element.78), channel_id=1, replica_groups=mesh['dp'=8,'context'=8,'tensor'=2] {'context'}, dimensions={0} | all-to-all | bytes 1179648 | tf_op jit(solution)/shard_map/all_to_all | solution.py:664
  175.9 11.6 %all_to_all.50 = bf16[8,144,256]{2,1,0:T(8,128)(2,1)} all-to-all(bf16[8,144,256]{2,1,0:T(8,128)(2,1)S(1)} %sum.1), channel_id=1, replica_groups=mesh['dp'=8,'context'=8,'tensor'=2] {'context'}, dimensions={0} | all-to-all | bytes 1179648 | tf_op jit(solution)/shard_map/all_to_all | solution.py:664
  187.5 4.2 %unpack_first.1 = (f32[2,512,1024]{2,1,0:T(8,128)}, f32[2,1024,512]{2,1,0:T(8,128)}) custom-call(bf16[8,512,256]{2,1,0:T(8,128)(2,1)} %bitcast.40), custom_call_target="tpu_custom_call" | custom-call | tf_op jit(solution)/shard_map/unpack_first/pallas_call | solution.py:625
  191.7 29.6 %all-gather.8.cloned.1.call-done = bf16[64,144,256]{2,1,0:T(8,128)(2,1)} async-done(((bf16[8,144,256]{2,1,0:T(8,128)(2,1)}), bf16[64,144,256]{2,1,0:T(8,128)(2,1)}) %all-gather.8.cloned.1.call-update) | async-done | bytes 4718608 | tf_op jit(solution)/shard_map/all_gather | solution.py:798
  221.3 6.1 %unpack_rest.1 = (f32[2,512,1024]{2,1,0:T(8,128)}, f32[2,1024,512]{2,1,0:T(8,128)}, f32[2,3,512,256]{3,2,1,0:T(8,128)}, f32[2,256,512]{2,1,0:T(8,128)}, f32[2,10...) custom-call(bf16[8,8,144,256]{3,2,1,0:T(8,128)(2,1)} %bitcast.39, ...), custom_call_target="tpu_custom_call", output_to_operand_aliasing={{0}: (1, {}), {1}: (2, {})} | custom-call | tf_op jit(solution)/shard_map/unpack_rest/pallas_call | solution.py:643
  (44 shorter events, 11.6 us)
Async XLA Ops:
  7.2 6.2 %copy-start.7 = (f32[8,1]{1,0:T(8,128)S(1)}, f32[8,1]{1,0:T(8,128)}, u32[]{:S(2)}) copy-start(f32[8,1]{1,0:T(8,128)} %constant.21.freqs) | copy-start | bytes 100
  7.2 6.2 %copy-start.3 = (f32[2,2,512]{2,1,0:T(2,128)S(1)}, f32[2,2,512]{2,1,0:T(2,128)}, u32[]{:S(2)}) copy-start(f32[2,2,512]{2,1,0:T(2,128)} %bias.7) | copy-start | bytes 24580
  7.2 6.2 %copy-start.2 = (f32[2,2,512]{2,1,0:T(2,128)S(1)}, f32[2,2,512]{2,1,0:T(2,128)}, u32[]{:S(2)}) copy-start(f32[2,2,512]{2,1,0:T(2,128)} %gain.7) | copy-start | bytes 24580
  7.2 6.2 %copy-start.4 = (f32[2,1024]{1,0:T(2,128)S(1)}, f32[2,1024]{1,0:T(2,128)}, u32[]{:S(2)}) copy-start(f32[2,1024]{1,0:T(2,128)} %b_up.3) | copy-start | bytes 24580
  7.2 6.2 %copy-start.6 = (f32[2,3,256]{2,0,1:T(2,128)S(1)}, f32[2,3,256]{2,0,1:T(2,128)}, u32[]{:S(2)}) copy-start(f32[2,3,256]{2,0,1:T(2,128)} %param.17) | copy-start | bytes 18436
  7.2 6.2 %copy-start.8 = (s32[2,128]{1,0:T(2,128)S(1)}, s32[2,128]{1,0:T(2,128)}, u32[]{:S(2)}) copy-start(s32[2,128]{1,0:T(2,128)} %pos.1) | copy-start | bytes 3076
  7.2 81.2 %all-gather.6.cloned.1.call-start = ((), (), s32[]{:S(2)}) async-start(), calls=%async_computation.11 | async-start | bytes 2359296 | tf_op jit(solution)/shard_map/all_gather | solution.py:704
  8.9 11.4 %collective-permute-start.2 = (bf16[2,4,64,256]{3,2,1,0:T(8,128)(2,1)S(1)}, bf16[2,4,64,256]{3,2,1,0:T(8,128)(2,1)S(1)}, u32[]{:S(2)}, u32[]{:S(2)}) collective-permute-start(bf16[2,4,64,256]{3,2,1,0:T(8,128)(2,1)S(1)} %chunk.1), channel_id=1, source_target_pairs={{0,1},{1,0},{2,3},{3,2},{4,5},{5,4},{6,7},{7,6},{8,9},{9,8},{10,11... | collective-permute-start | bytes 786440 | tf_op jit(solution)/shard_map/ppermute | solution.py:660
  17.8 30.3 %copy-start.5 = (f32[2,2,512]{2,1,0:T(2,128)S(1)}, f32[2,2,512]{2,1,0:T(2,128)}, u32[]{:S(2)}) copy-start(f32[2,2,512]{2,1,0:T(2,128)} %out_bias.3) | copy-start | bytes 24580
  21.1 11.9 %all-to-all-start = ((bf16[8,208,128]{2,1,0:T(8,128)(2,1)}), bf16[8,208,128]{2,1,0:T(8,128)(2,1)S(1)}, u32[]{:S(2)}, u32[]{:S(2)}) async-start(bf16[8,208,128]{2,1,0:T(8,128)(2,1)} %get-tuple-element.52), calls=%async_computation | async-start | bytes 851968 | tf_op jit(solution)/shard_map/all_to_all | solution.py:664
  25.7 18.1 %collective-permute-start = (bf16[512,512]{1,0:T(8,128)(2,1)S(1)}, bf16[512,512]{1,0:T(8,128)(2,1)S(1)}, u32[]{:S(2)}, u32[]{:S(2)}) collective-permute-start(bf16[512,512]{1,0:T(8,128)(2,1)S(1)} %get-tuple-element.51.pair), channel_id=1, source_target_pairs={{0,1},{1,0},{2,3},{3,2},{4,5},{5,4},{6,7},{7,6},{8,9},{9,8},{10,11... | collective-permute-start | bytes 1572872 | tf_op jit(solution)/shard_map/ppermute | solution.py:660
  35.6 0.7 copy-start
  36.3 11.9 %all-to-all-start.1 = ((bf16[16,64,128]{2,1,0:T(8,128)(2,1)}), bf16[16,64,128]{2,1,0:T(8,128)(2,1)S(1)}, u32[]{:S(2)}, u32[]{:S(2)}) async-start(bf16[16,64,128]{2,1,0:T(8,128)(2,1)} %bitcast.6), calls=%async_computation.1 | async-start | bytes 524288 | tf_op jit(solution)/shard_map/all_to_all | solution.py:664
  40.5 47.9 %reduce-scatter.3.cloned.1.call-start = ((), (), s32[]{:S(2)}) async-start(), calls=%async_computation.12 | async-start | bytes 2359296 | tf_op jit(solution)/shard_map/reduce_scatter | solution.py:731
  55.0 106.7 %reduce-scatter.5.cloned.1.call-start = ((), (), s32[]{:S(2)}) async-start(), calls=%async_computation.13 | async-start | bytes 3833856 | tf_op jit(solution)/shard_map/reduce_scatter | solution.py:763
  55.1 12.4 %collective-permute-start.1 = (bf16[512,512]{1,0:T(8,128)(2,1)S(1)}, bf16[512,512]{1,0:T(8,128)(2,1)S(1)}, u32[]{:S(2)}, u32[]{:S(2)}) collective-permute-start(bf16[512,512]{1,0:T(8,128)(2,1)S(1)} %get-tuple-element.56.parts), channel_id=1, source_target_pairs={{0,1},{1,0},{2,3},{3,2},{4,5},{5,4},{6,7},{7,6},{8,9},{9,8},{10,11... | collective-permute-start | bytes 1572872 | tf_op jit(solution)/shard_map/ppermute | solution.py:660
  96.6 13.2 %copy-start.1 = (f32[64,1024]{1,0:T(8,128)S(1)}, f32[64,1024]{1,0:T(8,128)}, u32[]{:S(2)}) copy-start(f32[64,1024]{1,0:T(8,128)} %copy-done) | copy-start | bytes 786436
  96.6 13.2 %all-to-all-start.4 = ((bf16[8,192,128]{2,1,0:T(8,128)(2,1)}), bf16[8,192,128]{2,1,0:T(8,128)(2,1)S(1)}, u32[]{:S(2)}, u32[]{:S(2)}) async-start(bf16[8,192,128]{2,1,0:T(8,128)(2,1)} %get-tuple-element.65), calls=%async_computation.5 | async-start | bytes 786432 | tf_op jit(solution)/shard_map/all_to_all | solution.py:664
  101.2 86.3 %all-gather.10.cloned.1.call-start = ((), (), s32[]{:S(2)}) async-start(), calls=%async_computation.15 | async-start | bytes 2359296 | tf_op jit(solution)/shard_map/all_gather | solution.py:796
  101.2 8.6 %collective-permute-start.3 = (bf16[256,512]{1,0:T(8,128)(2,1)S(1)}, bf16[256,512]{1,0:T(8,128)(2,1)S(1)}, u32[]{:S(2)}, u32[]{:S(2)}) collective-permute-start(bf16[256,512]{1,0:T(8,128)(2,1)S(1)} %get-tuple-element.64.part), channel_id=1, source_target_pairs={{0,1},{1,0},{2,3},{3,2},{4,5},{5,4},{6,7},{7,6},{8,9},{9,8},{10,11... | collective-permute-start | bytes 786440 | tf_op jit(solution)/shard_map/ppermute | solution.py:660
  163.5 57.7 %all-gather.8.cloned.1.call-start = ((), (), s32[]{:S(2)}) async-start(), calls=%async_computation.14 | async-start | bytes 5308416 | tf_op jit(solution)/shard_map/all_gather | solution.py:798
Sparse Core Ops, SparseCore 0:
  21.2 26.9 all-gather.5
  55.1 32.6 reduce-scatter.2
  96.7 39.3 reduce-scatter.4
  163.7 21.4 all-gather.9
  187.6 33.6 all-gather.7

commit v10 on v9

--- a/solution.py
+++ b/solution.py
@@ -132,7 +132,7 @@
 def feed_back(g_b, act, slope, mlp_in, w_up, w_down, d_up, d_down, d_b_up):
     width = w_up.shape[1]
     total = None
-    mlp_t = mlp_in.astype(F32).T.astype(BF)
+    mlp_t = mlp_in.T
     for c in range(0, width, 256):
         cols = slice(c, c + 256)
         d_act = mm(g_b, w_down[cols, :], 1, 1)
@@ -140,7 +140,7 @@
         d_pre_b = d_pre.astype(BF)
         d_b_up[:, cols] = jnp.sum(d_pre_b.astype(F32), 0, keepdims=True)
         d_up(c // 256, mm(mlp_t, d_pre_b))
-        d_down(c, mm(act[:, cols].astype(F32).T.astype(BF), g_b))
+        d_down(c, mm(act[:, cols].T, g_b))
         term = mm(d_pre_b, w_up[:, cols], 1, 1)
         total = term if total is None else total + term
     return total
@@ -232,7 +232,7 @@
     q = load_rows(recv, 0, HEAD)
     k_t = load_rows(recv, HEAD, 2 * HEAD)
     v_t = load_rows(recv, 2 * HEAD, 3 * HEAD)
-    k = k_t.astype(F32).T.astype(BF)
+    k = k_t.T
     start = starts_of(recv).astype(jnp.int32)
     start_out[...] = start
     for c in range(4):
@@ -257,8 +257,8 @@
     k_t = load_rows(recv, HEAD, 2 * HEAD)
     v_t = load_rows(recv, 2 * HEAD, 3 * HEAD)
     d_ctx = load_rows(recv, 3 * HEAD, 4 * HEAD)
-    k = k_t.astype(F32).T.astype(BF)
-    v = v_t.astype(F32).T.astype(BF)
+    k = k_t.T
+    v = v_t.T
     dk[...] = jnp.zeros_like(dk)
     dv[...] = jnp.zeros_like(dv)
     for c in range(4):
@@ -309,8 +309,8 @@
     k_t = load_rows(recv, HEAD, 2 * HEAD)
     v_t = load_rows(recv, 2 * HEAD, 3 * HEAD)
     d_ctx = load_rows(recv_d, 0, HEAD)
-    k = k_t.astype(F32).T.astype(BF)
-    v = v_t.astype(F32).T.astype(BF)
+    k = k_t.T
+    v = v_t.T
     dk[...] = jnp.zeros_like(dk)
     dv[...] = jnp.zeros_like(dv)
     for c in range(4):
@@ -348,7 +348,7 @@
     w = jnp.concatenate([first, second], 0)
     rows = []
     for s in range(2):
-        rows.append(mm(gather_ctx(recv, s).astype(F32).T.astype(BF), w))
+        rows.append(mm(gather_ctx(recv, s).T, w))
     return jnp.concatenate(rows, 0)
 
 
@@ -384,7 +384,7 @@
 ):
     normed, inv = norm_rows(x)
     attn_in = (normed * gain[layer, 0:1] + bias[layer, 0:1]).astype(BF)
-    attn_t = attn_in.astype(F32).T.astype(BF)
+    attn_t = attn_in.T
     d_attn_t = None
     for e in range(3):
         halves = []
@@ -517,14 +517,18 @@
     )(at, far(wq), far(w_out))
 
 
+def hand_on_body(value, _, out):
+    out[...] = value[...]
+
+
 def mix_body(got, early, first, out, first_out):
     total = got[0].astype(F32)
     for i in range(1, 8):
         total = total + got[i].astype(F32)
     for q in range(8):
-        mine = [early[104 * q : 104 * (q + 1)].astype(F32), total[24 * q : 24 * (q + 1)]]
-        out[q, 0:128] = jnp.concatenate(mine, 0).astype(BF)
-        out[q, 128:144] = total[192:208].astype(BF) if q == 0 else jnp.zeros((16, 256), BF)
+        tiny = total[192 + 8 * q : 200 + 8 * q] if q < 2 else jnp.zeros((8, 256), F32)
+        mine = [early[104 * q : 104 * (q + 1)].astype(F32), total[24 * q : 24 * (q + 1)], tiny]
+        out[q] = jnp.concatenate(mine, 0).astype(BF)
     first_out[...] = first[...]
 
 
@@ -551,7 +555,7 @@
     p = pl.program_id(0)
     for k in range(2):
         for q in range(8):
-            block = rest[k, q, 0:128].astype(F32)
+            block = rest[k, q].astype(F32)
             for i in range(16):
                 value = block[8 * i : 8 * (i + 1)]
                 row = 104 * q + 8 * i
@@ -575,7 +579,7 @@
                     r += 32 * k
                     g_out[1 - (row - 704) // 64, r : r + 8, 256 * c : 256 * (c + 1)] = value
 
-    tiny = [rest[k, 0, 128:144].astype(F32) for k in range(2)]
+    tiny = [jnp.concatenate([rest[k, q].astype(F32)[128:136] for q in range(2)], 0) for k in range(2)]
 
     @pl.when(p == 0)
     def _():
@@ -645,7 +649,7 @@
         grid=(4,),
         out_shape=[pltpu.HBM(shape, F32) for shape in [UP, DOWN] + [o[0] for o in outs]],
         in_specs=[
-            pl.BlockSpec((2, 8, 144, 256), lambda p: (p, 0, 0, 0)),
+            pl.BlockSpec((2, 8, 136, 256), lambda p: (p, 0, 0, 0)),
             pl.BlockSpec(memory_space=pl.ANY),
             pl.BlockSpec(memory_space=pl.ANY),
         ],
@@ -685,7 +689,7 @@
     send, pair, act, slope, cs = call(
         first_body,
         [
-            ((8, 208, BLK), BF),
+            pltpu.VMEM((8, 208, BLK), BF),
             ((2 * rows, width), BF),
             pltpu.HBM((rows, 1024), BF),
             pltpu.HBM((rows, 1024), BF),
@@ -699,13 +703,14 @@
         smem_first=True,
     )
     pair_other = swap(pair)
-    mark = send[0, 0, 0]
-    chunk = jnp.where(mark == mark, chunk, 0)
+    (chunk,) = call(
+        hand_on_body, [pltpu.HBM(chunk.shape, BF)], (chunk, After(send)), "hand_on"
+    )
     others = lax.all_gather(chunk, "dp", axis=2, tiled=True)
     recv = exchange(send, "context")
     ctx_send, lse, ctx, start = call(
         attend_body,
-        [((8, 2, HEAD, BLK), BF), ((1, 1024), F32), ((HEAD, 1024), F32), ((1, 1024), jnp.int32)],
+        [((8, 2, HEAD, BLK), BF), ((1, 1024), F32), pltpu.HBM((HEAD, 1024), F32), ((1, 1024), jnp.int32)],
         (recv,),
         "attend",
     )
@@ -744,7 +749,7 @@
         [
             pltpu.HBM((rows, width), F32),
             pltpu.HBM((rows, width), F32),
-            ((8, 192, BLK), BF),
+            pltpu.VMEM((8, 192, BLK), BF),
             pltpu.HBM((8, 832, 256), BF),
             ((rows, width), BF),
             ((1, 1024), F32),
@@ -789,12 +794,12 @@
     )
     mixed, sums_a = call(
         mix_body,
-        [((8, 144, 256), BF), pltpu.HBM((512, 256), BF)],
+        [((8, 136, 256), BF), pltpu.HBM((512, 256), BF)],
         (exchange(grads_c, "dp"), Far(sums_b), Far(sums_a)),
         "mix",
     )
     full_a = lax.all_gather(sums_a, "dp")
-    (summed,) = call(sum_body, [((8, 144, 256), BF)], (exchange(mixed, "context"),), "sum")
+    (summed,) = call(sum_body, [((8, 136, 256), BF)], (exchange(mixed, "context"),), "sum")
     full_bc = lax.all_gather(exchange(summed, "context"), "dp")
     g_up, g_down, g_qkv, g_out, g_b_up, g_b_qkv, g_sum, g_gain, g_bias = unpack(full_a, full_bc)
     return (

time: 235 us -> 234 us (level)
    ppermute x4, waiting for transfers between devices: 9.31 us -> 12.4 us  [swap(): return lax.ppermute(value, 'tensor', [(0, 1), (1, 0)])]
    all_to_all x3, waiting for transfers between devices: 9.22 us -> 6.77 us  [exchange(): return lax.all_to_all(value, axes, 0, 0)]
    pallas_call x9 -> x10, Pallas kernels: 34.3 us -> 35 us  [call(): pl.pallas_call(body, grid=(1,), out_shape=[o if isinstance(o, Kept) else...]
  transfers between devices with their start and end apart: 12 -> 12, of which waited for: 6 -> 6; matrix products, arithmetic and copies ran while one was open for 1% -> 0% of each run, Pallas kernels for 12% -> 12%
where the time goes in v10:
time: 234 us; the launch traced here: 233 us
  blocking collectives  100 us (43%)
  waiting for transfers between devices  48 us (21%)
  Pallas kernels  46.7 us (20%)
  starting transfers between devices  23.7 us (10%)
  between operations  13.9 us (6%)
    all_to_all x6, blocking collectives, exchange(): return lax.all_to_all(value, axes, 0, 0)  100 us
    pallas_call x10, Pallas kernels, call(): pl.pallas_call(body, grid=(1,), out_shape=[o if isinstance(o, Kept) else...  35 us
    all_gather x1, waiting for transfers between devices, shards(): full_bc = lax.all_gather(exchange(summed, 'context'), 'dp')  28.7 us
    all_to_all x3, starting transfers between devices, exchange(): return lax.all_to_all(value, axes, 0, 0)  14.1 us
    ppermute x4, waiting for transfers between devices, swap(): return lax.ppermute(value, 'tensor', [(0, 1), (1, 0)])  12.4 us
    ppermute x4, starting transfers between devices, swap(): return lax.ppermute(value, 'tensor', [(0, 1), (1, 0)])  9.44 us
    all_to_all x3, waiting for transfers between devices, exchange(): return lax.all_to_all(value, axes, 0, 0)  6.77 us
    pallas_call x1, Pallas kernels, unpack(): pl.pallas_call(unpack_rest_body, grid=(4,), out_shape=[pltpu.HBM(shape, F...  6.04 us
  transfers between devices with their start and end apart: 12, of which 6 were waited for; matrix products, arithmetic and copies ran while one was open for 0% of the time, Pallas kernels for 12%

profile of v10, /device:TPU:1, one launch (start us, length us, event | category | flops | bytes accessed | tf_op | source)
XLA Modules:
  0.0 232.7 jit_solution(4135598649045973839)
XLA Ops:
  8.9 4.5 %collective-permute-start.2 = (bf16[2,4,64,256]{3,2,1,0:T(8,128)(2,1)S(1)}, bf16[2,4,64,256]{3,2,1,0:T(8,128)(2,1)S(1)}, u32[]{:S(2)}, u32[]{:S(2)}) collective-permute-start(bf16[2,4,64,256]{3,2,1,0:T(8,128)(2,1)S(1)} %chunk.1), channel_id=1, source_target_pairs={{0,1},{1,0},{2,3},{3,2},{4,5},{5,4},{6,7},{7,6},{8,9},{9,8},{10,11... | collective-permute-start | bytes 786440 | tf_op jit(solution)/shard_map/ppermute | solution.py:664
  13.4 4.4 %norm_qkv_feed.1 = (bf16[8,208,128]{2,1,0:T(8,128)(2,1)}, bf16[512,512]{1,0:T(8,128)(2,1)S(1)}, bf16[256,1024]{1,0:T(8,128)(2,1)}, bf16[256,1024]{1,0:T(8,128)(2,1)}, f32[2,2,8,128]{3,2,1,0:T(8,128)S(1)}) custom-call(s32[3]{0:T(128)S(1)} %pad_add_fusion.at, s32[2,128]{1,0:T(2,128)S(1)} %copy-done.7, f32[8,1]{1,0:T(8,128)S(1)} %copy-done.6, ...), custom_call_target="tpu_custom_call" | custom-call | tf_op jit(solution)/shard_map/norm_qkv_feed/pallas_call | solution.py:72
  20.2 4.6 %all-to-all-start = ((bf16[8,208,128]{2,1,0:T(8,128)(2,1)}), bf16[8,208,128]{2,1,0:T(8,128)(2,1)S(1)}, u32[]{:S(2)}, u32[]{:S(2)}) async-start(bf16[8,208,128]{2,1,0:T(8,128)(2,1)} %get-tuple-element.52._), calls=%async_computation | async-start | bytes 851968 | tf_op jit(solution)/shard_map/all_to_all | solution.py:668
  24.8 3.3 %collective-permute-start = (bf16[512,512]{1,0:T(8,128)(2,1)S(1)}, bf16[512,512]{1,0:T(8,128)(2,1)S(1)}, u32[]{:S(2)}, u32[]{:S(2)}) collective-permute-start(bf16[512,512]{1,0:T(8,128)(2,1)S(1)} %get-tuple-element.51.pair), channel_id=1, source_target_pairs={{0,1},{1,0},{2,3},{3,2},{4,5},{5,4},{6,7},{7,6},{8,9},{9,8},{10,11... | collective-permute-start | bytes 1572872 | tf_op jit(solution)/shard_map/ppermute | solution.py:664
  28.1 3.2 %all-to-all-done.recv = bf16[8,208,128]{2,1,0:T(8,128)(2,1)S(1)} async-done(((bf16[8,208,128]{2,1,0:T(8,128)(2,1)}), bf16[8,208,128]{2,1,0:T(8,128)(2,1)S(1)}, u32[]{:S(2)}, u32[]{:S(2)}) %all-to-all-start) | async-done | bytes 426016 | tf_op jit(solution)/shard_map/all_to_all | solution.py:668
  31.2 2.7 %attend.1 = (bf16[8,2,64,128]{3,2,1,0:T(8,128)(2,1)}, f32[1,1024]{1,0:T(1,128)S(1)}, f32[64,1024]{1,0:T(8,128)}, s32[1,1024]{1,0:T(1,128)S(1)}) custom-call(bf16[8,208,128]{2,1,0:T(8,128)(2,1)S(1)} %all-to-all-done.recv), custom_call_target="tpu_custom_call" | custom-call | tf_op jit(solution)/shard_map/attend/pallas_call | solution.py:72
  33.9 5.9 %all-to-all-start.1 = ((bf16[16,64,128]{2,1,0:T(8,128)(2,1)}), bf16[16,64,128]{2,1,0:T(8,128)(2,1)S(1)}, u32[]{:S(2)}, u32[]{:S(2)}) async-start(bf16[16,64,128]{2,1,0:T(8,128)(2,1)} %bitcast.6), calls=%async_computation.1 | async-start | bytes 524288 | tf_op jit(solution)/shard_map/all_to_all | solution.py:668
  39.8 4.0 %collective-permute-done.pair_other = bf16[512,512]{1,0:T(8,128)(2,1)S(1)} collective-permute-done((bf16[512,512]{1,0:T(8,128)(2,1)S(1)}, bf16[512,512]{1,0:T(8,128)(2,1)S(1)}, u32[]{:S(2)}, u32[]{:S(2)}) %collective-permute-start) | collective-permute-done | bytes 524320 | tf_op jit(solution)/shard_map/ppermute | solution.py:664
  43.8 3.6 %all-to-all-done.1 = bf16[16,64,128]{2,1,0:T(8,128)(2,1)S(1)} async-done(((bf16[16,64,128]{2,1,0:T(8,128)(2,1)}), bf16[16,64,128]{2,1,0:T(8,128)(2,1)S(1)}, u32[]{:S(2)}, u32[]{:S(2)}) %all-to-all-start.1) | async-done | bytes 262176 | tf_op jit(solution)/shard_map/all_to_all | solution.py:668
  47.4 6.8 %middle.1 = (f32[256,512]{1,0:T(8,128)}, bf16[8,256,128]{2,1,0:T(8,128)(2,1)S(1)}, bf16[8,512,256]{2,1,0:T(8,128)(2,1)}, bf16[512,512]{1,0:T(8,128)(2,1)S(1)}, f...) custom-call(s32[3]{0:T(128)S(1)} %pad_add_fusion.at, f32[256,512]{1,0:T(8,128)} %bitcast.35, ...), custom_call_target="tpu_custom_call" | custom-call | tf_op jit(solution)/shard_map/middle/pallas_call | solution.py:72
  54.9 12.1 %all_to_all.45.recv = bf16[8,256,128]{2,1,0:T(8,128)(2,1)S(1)} all-to-all(bf16[8,256,128]{2,1,0:T(8,128)(2,1)S(1)} %get-tuple-element.57), channel_id=1, replica_groups=mesh['dp'=8,'context'=8,'tensor'=2] {'context'}, dimensions={0} | all-to-all | bytes 1048576 | tf_op jit(solution)/shard_map/all_to_all | solution.py:668
  66.9 4.2 %attend_both.1 = bf16[8,2,256,128]{3,2,1,0:T(8,128)(2,1)S(1)} custom-call(bf16[8,256,128]{2,1,0:T(8,128)(2,1)S(1)} %all_to_all.45.recv, s32[1,1024]{1,0:T(1,128)S(1)} %get-tuple-element.58.start, bf16[512,512]{1,0:T(8,128)(2,1)S(1)} %collective-permute-done.1._.parts_other), custom_call_target="tpu_custom_call" | custom-call | tf_op jit(solution)/shard_map/attend_both/pallas_call | solution.py:72
  71.2 19.5 %all_to_all.46 = bf16[16,256,128]{2,1,0:T(8,128)(2,1)S(1)} all-to-all(bf16[16,256,128]{2,1,0:T(8,128)(2,1)S(1)} %bitcast.23), channel_id=1, replica_groups=mesh['dp'=8,'context'=8,'tensor'=2] {'context','tensor'}, dimensions={0} | all-to-all | bytes 2097152 | tf_op jit(solution)/shard_map/all_to_all | solution.py:668
  90.7 8.2 %turn_point.1 = (f32[256,512]{1,0:T(8,128)}, f32[256,512]{1,0:T(8,128)}, bf16[8,192,128]{2,1,0:T(8,128)(2,1)}, bf16[8,832,256]{2,1,0:T(8,128)(2,1)}, bf16[256,51...) custom-call(s32[3]{0:T(128)S(1)} %pad_add_fusion.at, ...), custom_call_target="tpu_custom_call" | custom-call | tf_op jit(solution)/shard_map/turn_point/pallas_call | solution.py:72
  98.9 3.6 %all-to-all-start.4 = ((bf16[8,192,128]{2,1,0:T(8,128)(2,1)}), bf16[8,192,128]{2,1,0:T(8,128)(2,1)S(1)}, u32[]{:S(2)}, u32[]{:S(2)}) async-start(bf16[8,192,128]{2,1,0:T(8,128)(2,1)} %get-tuple-element.65), calls=%async_computation.5 | async-start | bytes 786432 | tf_op jit(solution)/shard_map/all_to_all | solution.py:668
  103.6 6.8 %collective-permute-done.3._.part_other = bf16[256,512]{1,0:T(8,128)(2,1)S(1)} collective-permute-done((bf16[256,512]{1,0:T(8,128)(2,1)S(1)}, bf16[256,512]{1,0:T(8,128)(2,1)S(1)}, u32[]{:S(2)}, u32[]{:S(2)}) %collective-permute-start.3) | collective-permute-done | bytes 262176 | tf_op jit(solution)/shard_map/ppermute | solution.py:664
  112.6 18.8 %all_to_all.47 = bf16[16,320,128]{2,1,0:T(8,128)(2,1)S(1)} all-to-all(bf16[16,320,128]{2,1,0:T(8,128)(2,1)S(1)} %bitcast.21), channel_id=1, replica_groups=mesh['dp'=8,'context'=8,'tensor'=2] {'context','tensor'}, dimensions={0} | all-to-all | bytes 2621440 | tf_op jit(solution)/shard_map/all_to_all | solution.py:668
  131.4 3.9 %last.1 = (f32[256,512]{1,0:T(8,128)}, bf16[8,208,256]{2,1,0:T(8,128)(2,1)S(1)}, bf16[512,256]{1,0:T(8,128)(2,1)}, f32[3,256]{1,0:T(4,128)}, f32[4,512]{1,0:T(4,128)}) custom-call(s32[3]{0:T(128)S(1)} %pad_add_fusion.at, f32[256,512]{1,0:T(8,128)} %bitcast.37, f32[256,512]{1,0:T(8,128)} %get-tuple-element.63.g, bf16[256,512]{1,0:T(8,128)(2,1)S(1)} %get-tuple-element.64.part, ...), custom_call_target="tpu_custom_call" | custom-call | tf_op jit(solution)/shard_map/last/pallas_call | solution.py:72
  135.3 26.3 %all_to_all.48.got = bf16[8,208,256]{2,1,0:T(8,128)(2,1)S(1)} all-to-all(bf16[8,208,256]{2,1,0:T(8,128)(2,1)S(1)} %get-tuple-element.75), channel_id=1, replica_groups=mesh['dp'=8,'context'=8,'tensor'=2] {'dp'}, dimensions={0} | all-to-all | bytes 1703936 | tf_op jit(solution)/shard_map/all_to_all | solution.py:668
  163.5 12.1 %all_to_all.49.got = bf16[8,136,256]{2,1,0:T(8,128)(2,1)S(1)} all-to-all(bf16[8,136,256]{2,1,0:T(8,128)(2,1)S(1)} %get-tuple-element.78), channel_id=1, replica_groups=mesh['dp'=8,'context'=8,'tensor'=2] {'context'}, dimensions={0} | all-to-all | bytes 1114112 | tf_op jit(solution)/shard_map/all_to_all | solution.py:668
  175.7 11.5 %all_to_all.50 = bf16[8,136,256]{2,1,0:T(8,128)(2,1)} all-to-all(bf16[8,136,256]{2,1,0:T(8,128)(2,1)S(1)} %sum.1), channel_id=1, replica_groups=mesh['dp'=8,'context'=8,'tensor'=2] {'context'}, dimensions={0} | all-to-all | bytes 1114112 | tf_op jit(solution)/shard_map/all_to_all | solution.py:668
  187.2 4.2 %unpack_first.1 = (f32[2,512,1024]{2,1,0:T(8,128)}, f32[2,1024,512]{2,1,0:T(8,128)}) custom-call(bf16[8,512,256]{2,1,0:T(8,128)(2,1)} %bitcast.39), custom_call_target="tpu_custom_call" | custom-call | tf_op jit(solution)/shard_map/unpack_first/pallas_call | solution.py:629
  191.4 28.7 %all-gather.8.cloned.1.call-done = bf16[64,136,256]{2,1,0:T(8,128)(2,1)} async-done(((bf16[8,136,256]{2,1,0:T(8,128)(2,1)}), bf16[64,136,256]{2,1,0:T(8,128)(2,1)}) %all-gather.8.cloned.1.call-update) | async-done | bytes 4456464 | tf_op jit(solution)/shard_map/all_gather | solution.py:803
  220.1 6.0 %unpack_rest.1 = (f32[2,512,1024]{2,1,0:T(8,128)}, f32[2,1024,512]{2,1,0:T(8,128)}, f32[2,3,512,256]{3,2,1,0:T(8,128)}, f32[2,256,512]{2,1,0:T(8,128)}, f32[2,10...) custom-call(bf16[8,8,136,256]{3,2,1,0:T(8,128)(2,1)} %bitcast.38, ...), custom_call_target="tpu_custom_call", output_to_operand_aliasing={{0}: (1, {}), {1}: (2, {})} | custom-call | tf_op jit(solution)/shard_map/unpack_rest/pallas_call | solution.py:647
  (41 shorter events, 10.0 us)
Async XLA Ops:
  7.2 6.2 %copy-start.6 = (f32[8,1]{1,0:T(8,128)S(1)}, f32[8,1]{1,0:T(8,128)}, u32[]{:S(2)}) copy-start(f32[8,1]{1,0:T(8,128)} %constant.18.freqs) | copy-start | bytes 100
  7.2 6.2 %copy-start.2 = (f32[2,2,512]{2,1,0:T(2,128)S(1)}, f32[2,2,512]{2,1,0:T(2,128)}, u32[]{:S(2)}) copy-start(f32[2,2,512]{2,1,0:T(2,128)} %bias.7) | copy-start | bytes 24580
  7.2 6.2 %copy-start.1 = (f32[2,2,512]{2,1,0:T(2,128)S(1)}, f32[2,2,512]{2,1,0:T(2,128)}, u32[]{:S(2)}) copy-start(f32[2,2,512]{2,1,0:T(2,128)} %gain.7) | copy-start | bytes 24580
  7.2 6.2 %copy-start.3 = (f32[2,1024]{1,0:T(2,128)S(1)}, f32[2,1024]{1,0:T(2,128)}, u32[]{:S(2)}) copy-start(f32[2,1024]{1,0:T(2,128)} %b_up.3) | copy-start | bytes 24580
  7.2 6.2 %copy-start.5 = (f32[2,3,256]{2,0,1:T(2,128)S(1)}, f32[2,3,256]{2,0,1:T(2,128)}, u32[]{:S(2)}) copy-start(f32[2,3,256]{2,0,1:T(2,128)} %param.17) | copy-start | bytes 18436
  7.2 6.2 %copy-start.7 = (s32[2,128]{1,0:T(2,128)S(1)}, s32[2,128]{1,0:T(2,128)}, u32[]{:S(2)}) copy-start(s32[2,128]{1,0:T(2,128)} %pos.1) | copy-start | bytes 3076
  7.2 83.4 %all-gather.6.cloned.1.call-start = ((), (), s32[]{:S(2)}) async-start(), calls=%async_computation.11 | async-start | bytes 2359296 | tf_op jit(solution)/shard_map/all_gather | solution.py:709
  8.9 10.5 %collective-permute-start.2 = (bf16[2,4,64,256]{3,2,1,0:T(8,128)(2,1)S(1)}, bf16[2,4,64,256]{3,2,1,0:T(8,128)(2,1)S(1)}, u32[]{:S(2)}, u32[]{:S(2)}) collective-permute-start(bf16[2,4,64,256]{3,2,1,0:T(8,128)(2,1)S(1)} %chunk.1), channel_id=1, source_target_pairs={{0,1},{1,0},{2,3},{3,2},{4,5},{5,4},{6,7},{7,6},{8,9},{9,8},{10,11... | collective-permute-start | bytes 786440 | tf_op jit(solution)/shard_map/ppermute | solution.py:664
  17.8 29.6 %copy-start.4 = (f32[2,2,512]{2,1,0:T(2,128)S(1)}, f32[2,2,512]{2,1,0:T(2,128)}, u32[]{:S(2)}) copy-start(f32[2,2,512]{2,1,0:T(2,128)} %out_bias.3) | copy-start | bytes 24580
  20.2 11.1 %all-to-all-start = ((bf16[8,208,128]{2,1,0:T(8,128)(2,1)}), bf16[8,208,128]{2,1,0:T(8,128)(2,1)S(1)}, u32[]{:S(2)}, u32[]{:S(2)}) async-start(bf16[8,208,128]{2,1,0:T(8,128)(2,1)} %get-tuple-element.52._), calls=%async_computation | async-start | bytes 851968 | tf_op jit(solution)/shard_map/all_to_all | solution.py:668
  24.8 19.1 %collective-permute-start = (bf16[512,512]{1,0:T(8,128)(2,1)S(1)}, bf16[512,512]{1,0:T(8,128)(2,1)S(1)}, u32[]{:S(2)}, u32[]{:S(2)}) collective-permute-start(bf16[512,512]{1,0:T(8,128)(2,1)S(1)} %get-tuple-element.51.pair), channel_id=1, source_target_pairs={{0,1},{1,0},{2,3},{3,2},{4,5},{5,4},{6,7},{7,6},{8,9},{9,8},{10,11... | collective-permute-start | bytes 1572872 | tf_op jit(solution)/shard_map/ppermute | solution.py:664
  33.9 13.5 %all-to-all-start.1 = ((bf16[16,64,128]{2,1,0:T(8,128)(2,1)}), bf16[16,64,128]{2,1,0:T(8,128)(2,1)S(1)}, u32[]{:S(2)}, u32[]{:S(2)}) async-start(bf16[16,64,128]{2,1,0:T(8,128)(2,1)} %bitcast.6), calls=%async_computation.1 | async-start | bytes 524288 | tf_op jit(solution)/shard_map/all_to_all | solution.py:668
  39.8 50.9 %reduce-scatter.3.cloned.1.call-start = ((), (), s32[]{:S(2)}) async-start(), calls=%async_computation.12 | async-start | bytes 2359296 | tf_op jit(solution)/shard_map/reduce_scatter | solution.py:736
  54.2 107.4 %reduce-scatter.5.cloned.1.call-start = ((), (), s32[]{:S(2)}) async-start(), calls=%async_computation.13 | async-start | bytes 3833856 | tf_op jit(solution)/shard_map/reduce_scatter | solution.py:768
  54.3 12.7 %collective-permute-start.1 = (bf16[512,512]{1,0:T(8,128)(2,1)S(1)}, bf16[512,512]{1,0:T(8,128)(2,1)S(1)}, u32[]{:S(2)}, u32[]{:S(2)}) collective-permute-start(bf16[512,512]{1,0:T(8,128)(2,1)S(1)} %get-tuple-element.56.parts), channel_id=1, source_target_pairs={{0,1},{1,0},{2,3},{3,2},{4,5},{5,4},{6,7},{7,6},{8,9},{9,8},{10,11... | collective-permute-start | bytes 1572872 | tf_op jit(solution)/shard_map/ppermute | solution.py:664
  98.8 11.5 %copy-start = (f32[64,1024]{1,0:T(8,128)S(1)}, f32[64,1024]{1,0:T(8,128)}, u32[]{:S(2)}) copy-start(f32[64,1024]{1,0:T(8,128)} %get-tuple-element.67.ctx) | copy-start | bytes 786436
  98.9 11.5 %all-to-all-start.4 = ((bf16[8,192,128]{2,1,0:T(8,128)(2,1)}), bf16[8,192,128]{2,1,0:T(8,128)(2,1)S(1)}, u32[]{:S(2)}, u32[]{:S(2)}) async-start(bf16[8,192,128]{2,1,0:T(8,128)(2,1)} %get-tuple-element.65), calls=%async_computation.5 | async-start | bytes 786432 | tf_op jit(solution)/shard_map/all_to_all | solution.py:668
  102.5 84.7 %all-gather.10.cloned.1.call-start = ((), (), s32[]{:S(2)}) async-start(), calls=%async_computation.15 | async-start | bytes 2359296 | tf_op jit(solution)/shard_map/all_gather | solution.py:801
  102.5 7.9 %collective-permute-start.3 = (bf16[256,512]{1,0:T(8,128)(2,1)S(1)}, bf16[256,512]{1,0:T(8,128)(2,1)S(1)}, u32[]{:S(2)}, u32[]{:S(2)}) collective-permute-start(bf16[256,512]{1,0:T(8,128)(2,1)S(1)} %get-tuple-element.64.part), channel_id=1, source_target_pairs={{0,1},{1,0},{2,3},{3,2},{4,5},{5,4},{6,7},{7,6},{8,9},{9,8},{10,11... | collective-permute-start | bytes 786440 | tf_op jit(solution)/shard_map/ppermute | solution.py:664
  163.4 56.6 %all-gather.8.cloned.1.call-start = ((), (), s32[]{:S(2)}) async-start(), calls=%async_computation.14 | async-start | bytes 5013504 | tf_op jit(solution)/shard_map/all_gather | solution.py:803
Sparse Core Ops, SparseCore 0:
  20.3 27.8 all-gather.5
  54.4 32.7 reduce-scatter.2
  99.0 37.0 reduce-scatter.4
  163.6 21.4 all-gather.9
  187.3 32.7 all-gather.7

commit v11 on v10

--- a/solution.py
+++ b/solution.py
@@ -43,6 +43,24 @@
         return pl.BlockSpec((None,) + rest, lambda i: place)
 
 
+class Quarter:
+    def __init__(self, array, at):
+        self.array, self.at = far(array), at
+
+    def spec(self):
+        rest = self.array.shape[1:]
+        place = (self.at,) + (0,) * len(rest)
+        return pl.BlockSpec((4,) + rest, lambda i: place)
+
+
+class Raw:
+    def __init__(self, array):
+        self.array = far(array)
+
+    def spec(self):
+        return pl.BlockSpec(memory_space=pltpu.HBM)
+
+
 class Far:
     def __init__(self, array):
         self.array = far(array)
@@ -64,9 +82,9 @@
 
 def call(body, out_shape, args, name, scratch=(), smem_first=False):
     specs = [
-        a.spec() if isinstance(a, (Layer, Far, After)) else whole(a.shape) for a in args
+        a.spec() if isinstance(a, (Layer, Quarter, Raw, Far, After)) else whole(a.shape) for a in args
     ]
-    args = [a.array if isinstance(a, (Layer, Far, After)) else a for a in args]
+    args = [a.array if isinstance(a, (Layer, Quarter, Raw, Far, After)) else a for a in args]
     if smem_first:
         specs[0] = pl.BlockSpec(memory_space=pltpu.SMEM)
     return pl.pallas_call(
@@ -98,7 +116,7 @@
     return jnp.concatenate([a * cos + b * sin, b * cos - a * sin, u[2 * HALF :]], 0)
 
 
-def send_qkv(send, attn_in, w_qkv, b_qkv, layer, cs):
+def send_qkv(send, attn_in, w_qkv, b_qkv, layer, cs, plane=None):
     for e in range(3):
         turned = (mm(attn_in, w_qkv[e]) + b_qkv[e, layer : layer + 1]).T
         for s in range(2):
@@ -110,7 +128,11 @@
                     part = turn(part, cos, sin)
                 if e == 0:
                     part = part * (HEAD**-0.5)
-                send[j, e * HEAD : (e + 1) * HEAD, :] = part.astype(BF)
+                rows = slice(e * HEAD, (e + 1) * HEAD)
+                if plane is None:
+                    send[j, rows, :] = part.astype(BF)
+                else:
+                    send[j, plane, rows, :] = part.astype(BF)
 
 
 def feed_forward(mlp_in, w_up, b_up, layer, w_down, act, slope):
@@ -188,9 +210,21 @@
 
 
 def first_body(
-    at, pos, freqs, x, gain, bias, w_qkv, b_qkv, w_up, b_up, w_down, w_out,
-    send, pair, act, slope, cs,
+    at, pos, freqs, x, gain, bias, w_qkv, b_qkv, w_up, b_up, w_down, w_out, all_qkv, all_out,
+    send, pair, act, slope, cs, piece_a, piece_b, sems,
 ):
+    matrix, part_of = at[2], at[0]
+    rows_a = pl.ds(pl.multiple_of(part_of * 64, 64), 64)
+    rows_b = pl.ds(pl.multiple_of(part_of % 4 * 64, 64), 64)
+    cols_b = pl.ds(pl.multiple_of(part_of // 4 * 256, 256), 256)
+    copies = [
+        pltpu.make_async_copy(
+            all_qkv.at[matrix // 4, jnp.minimum(matrix % 4, 2), rows_a], piece_a, sems.at[0]
+        ),
+        pltpu.make_async_copy(all_out.at[matrix // 4, rows_b, cols_b], piece_b, sems.at[1]),
+    ]
+    for copy in copies:
+        copy.start()
     pair[256:512] = w_out[...]
     for s in range(2):
         p = pos[s : s + 1, :].astype(F32)
@@ -200,7 +234,14 @@
     normed, _ = norm_rows(x[...])
     attn_in = (normed * gain[0, 0:1] + bias[0, 0:1]).astype(BF)
     mlp_in = (normed * gain[0, 1:2] + bias[0, 1:2]).astype(BF)
-    send_qkv(send, attn_in, w_qkv, b_qkv, 0, cs)
+    send_qkv(send, attn_in, w_qkv, b_qkv, 0, cs, at[1])
+    for copy in copies:
+        copy.wait()
+    piece = jnp.where(matrix % 4 == 3, piece_b[...], piece_a[...])
+    for j in range(8):
+        send[j, 1 - at[1], 0:64, :] = piece[:, 0:BLK]
+        send[j, 1 - at[1], 64:128, :] = piece[:, BLK : 2 * BLK]
+        send[j, 1 - at[1], 128:208, :] = jnp.zeros((80, BLK), BF)
     row = lax.broadcasted_iota(jnp.int32, (16, BLK), 0)
     token = at[0] * BLK + lax.broadcasted_iota(jnp.int32, (1, BLK), 1)
     for s in range(2):
@@ -209,16 +250,18 @@
         low = (start % 8).astype(F32)
         block = jnp.where(row == 0, high, jnp.where(row == 1, low, 0.0)).astype(BF)
         for h in range(4):
-            send[s * 4 + h, 3 * HEAD : 3 * HEAD + 16, :] = block
+            send[s * 4 + h, at[1], 3 * HEAD : 3 * HEAD + 16, :] = block
     pair[0:256] = feed_forward(mlp_in, w_up, b_up, 0, w_down, act, slope).astype(BF)
 
 
-def load_rows(recv, lo, hi):
+def load_rows(recv, lo, hi, plane=None):
+    if plane is not None:
+        return jnp.concatenate([recv[i, plane, lo:hi, :] for i in range(8)], 1)
     return jnp.concatenate([recv[i, lo:hi, :] for i in range(8)], 1)
 
 
-def starts_of(recv):
-    rows = load_rows(recv, 3 * HEAD, 3 * HEAD + 16).astype(F32)
+def starts_of(recv, plane):
+    rows = load_rows(recv, 3 * HEAD, 3 * HEAD + 16, plane).astype(F32)
     return rows[0:1] * 8.0 + rows[1:2]
 
 
@@ -228,12 +271,14 @@
     return (key <= query) & (key >= start[:, c * CHUNK : (c + 1) * CHUNK])
 
 
-def attend_body(recv, send, lse, ctx, start_out):
-    q = load_rows(recv, 0, HEAD)
-    k_t = load_rows(recv, HEAD, 2 * HEAD)
-    v_t = load_rows(recv, 2 * HEAD, 3 * HEAD)
+def attend_body(at, recv, send, lse, ctx, start_out, pieces):
+    for b in range(8):
+        pieces[b] = recv[b, 1 - at[1], 0 : 2 * HEAD, :]
+    q = load_rows(recv, 0, HEAD, at[1])
+    k_t = load_rows(recv, HEAD, 2 * HEAD, at[1])
+    v_t = load_rows(recv, 2 * HEAD, 3 * HEAD, at[1])
     k = k_t.T
-    start = starts_of(recv).astype(jnp.int32)
+    start = starts_of(recv, at[1]).astype(jnp.int32)
     start_out[...] = start
     for c in range(4):
         cols = slice(c * CHUNK, (c + 1) * CHUNK)
@@ -297,7 +342,7 @@
             send[b, t, row + HEAD : row + 2 * HEAD] = dv[:, b * BLK : (b + 1) * BLK].astype(BF)
 
 
-def attend_back_body(recv, recv_d, start, lse, ctx, _, send, dk, dv):
+def attend_back_body(at, recv, recv_d, start, lse, ctx, _, send, dk, dv):
     ride = recv_d[0, 64:192].astype(F32)
     for i in range(1, 8):
         ride = ride + recv_d[i, 64:192].astype(F32)
@@ -305,9 +350,9 @@
     for b in range(8):
         for t in range(2):
             send[b, t, 192:320] = ride
-    q = load_rows(recv, 0, HEAD)
-    k_t = load_rows(recv, HEAD, 2 * HEAD)
-    v_t = load_rows(recv, 2 * HEAD, 3 * HEAD)
+    q = load_rows(recv, 0, HEAD, at[1])
+    k_t = load_rows(recv, HEAD, 2 * HEAD, at[1])
+    v_t = load_rows(recv, 2 * HEAD, 3 * HEAD, at[1])
     d_ctx = load_rows(recv_d, 0, HEAD)
     k = k_t.T
     v = v_t.T
@@ -335,12 +380,16 @@
     return jnp.where(t == 0, own, other), jnp.where(t == 0, other, own)
 
 
+def other_matrix(others, m):
+    rows = [
+        jnp.concatenate([others[m, c, 0:64, :], others[m, c, 64:128, :]], 1) for c in range(8)
+    ]
+    return jnp.concatenate(rows, 0)
+
+
 def out_other(others):
-    halves = [
-        jnp.concatenate([others[3, 64 * p + 32 * c : 64 * p + 32 * (c + 1), :] for p in range(8)], 0)
-        for c in range(2)
-    ]
-    return jnp.concatenate(halves, 1)
+    stacked = other_matrix(others, 3)
+    return jnp.concatenate([stacked[0:256], stacked[256:512]], 1)
 
 
 def branch_of(t, recv, w_own, w_other):
@@ -400,7 +449,7 @@
                     pieces.append(u)
                 blocks.append(jnp.concatenate(pieces, 1))
             halves.append(jnp.concatenate(blocks, 0))
-        first, second = ordered(t, w_own[e], others[e])
+        first, second = ordered(t, w_own[e], other_matrix(others, e))
         term = mm(first, halves[0]) + mm(second, halves[1])
         d_attn_t = term if d_attn_t is None else d_attn_t + term
         own = jnp.where(t == 0, halves[0], halves[1])
@@ -489,36 +538,6 @@
         have = rows[p] if p < len(rows) else []
         fill = [jnp.zeros((16 - len(have), 256), F32)]
         grads[p, 192:208, :] = jnp.concatenate(have + fill, 0).astype(BF)
-
-
-def chunk_body(at, w_qkv, w_out, out):
-    for layer in range(2):
-        for e in range(3):
-            out[layer, e] = w_qkv[layer, e]
-        out[layer, 3, 0:32] = w_out[layer, :, 0:256]
-        out[layer, 3, 32:64] = w_out[layer, :, 256:512]
-
-
-def chunk_of(at, wq, w_out):
-    return pl.pallas_call(
-        chunk_body,
-        out_shape=jax.ShapeDtypeStruct((2, 4, 64, 256), BF),
-        grid_spec=pltpu.PrefetchScalarGridSpec(
-            num_scalar_prefetch=1,
-            grid=(1,),
-            in_specs=[
-                pl.BlockSpec((2, 3, 64, 256), lambda i, at: (0, 0, at[2], 0)),
-                pl.BlockSpec((2, 32, 512), lambda i, at: (0, at[2], 0)),
-            ],
-            out_specs=pl.BlockSpec((2, 4, 64, 256), lambda i, at: (0, 0, 0, 0)),
-        ),
-        compiler_params=pltpu.CompilerParams(vmem_limit_bytes=40 * 1024 * 1024),
-        name="chunk",
-    )(at, far(wq), far(w_out))
-
-
-def hand_on_body(value, _, out):
-    out[...] = value[...]
 
 
 def mix_body(got, early, first, out, first_out):
@@ -685,35 +704,40 @@
         [lax.axis_index("context"), lax.axis_index("tensor"), lax.axis_index("dp")]
     ).astype(jnp.int32)
     freqs = jnp.asarray(FREQS).reshape(HALF, 1)
-    chunk = swap(chunk_of(at, wq, w_out))
     send, pair, act, slope, cs = call(
         first_body,
         [
-            pltpu.VMEM((8, 208, BLK), BF),
+            pltpu.VMEM((8, 2, 208, BLK), BF),
             ((2 * rows, width), BF),
             pltpu.HBM((rows, 1024), BF),
             pltpu.HBM((rows, 1024), BF),
             ((2, 2, HALF, BLK), F32),
         ],
         (
-            at, positions, freqs, Far(x), ln_gain, ln_bias, Layer(wq, 0), bq, Layer(w_up, 0), b_up,
-            Layer(w_down, 0), Layer(w_out, 0),
+            at, Far(positions), Far(freqs), Far(x), Far(ln_gain), Far(ln_bias), Layer(wq, 0), Far(bq),
+            Layer(w_up, 0), Far(b_up),
+            Layer(w_down, 0), Layer(w_out, 0), Raw(wq), Raw(w_out),
         ),
         "norm_qkv_feed",
+        scratch=[
+            pltpu.VMEM((64, 256), BF),
+            pltpu.VMEM((64, 256), BF),
+            pltpu.SemaphoreType.DMA((2,)),
+        ],
         smem_first=True,
     )
     pair_other = swap(pair)
-    (chunk,) = call(
-        hand_on_body, [pltpu.HBM(chunk.shape, BF)], (chunk, After(send)), "hand_on"
-    )
-    others = lax.all_gather(chunk, "dp", axis=2, tiled=True)
-    recv = exchange(send, "context")
-    ctx_send, lse, ctx, start = call(
+    recv = both(send)
+    ctx_send, lse, ctx, start, pieces = call(
         attend_body,
-        [((8, 2, HEAD, BLK), BF), ((1, 1024), F32), pltpu.HBM((HEAD, 1024), F32), ((1, 1024), jnp.int32)],
-        (recv,),
+        [((8, 2, HEAD, BLK), BF), ((1, 1024), F32), pltpu.HBM((HEAD, 1024), F32), ((1, 1024), jnp.int32),
+            pltpu.HBM((8, 2 * HEAD, BLK), BF),
+        ],
+        (at, recv),
         "attend",
-    )
+        smem_first=True,
+    )
+    others = lax.all_gather(pieces, "dp")
     recv_ctx = both(ctx_send)
     stream, send, grads_a, parts, d_b_up1, d_sum1 = call(
         middle_body,
@@ -759,7 +783,7 @@
         ],
         (
             at, Far(stream), parts, parts_other, recv_grad, Layer(w_out, 1), Layer(wq, 1),
-            Layer(others, 1), out_bias, ln_gain, ln_bias, Far(cot), cs, Far(x), Far(act), Far(slope),
+            Quarter(others, 1), out_bias, ln_gain, ln_bias, Far(cot), cs, Far(x), Far(act), Far(slope),
             Layer(w_up, 0), Layer(w_down, 0), Layer(w_out, 0), recv_ctx, Far(sums_a),
         ),
         "turn_point",
@@ -771,8 +795,9 @@
     (back_send,) = call(
         attend_back_body,
         [((8, 2, 320, BLK), BF)],
-        (recv, recv_d, start, lse, ctx, After(part_g_other)),
+        (at, recv, recv_d, start, lse, ctx, After(part_g_other)),
         "attend_back",
+        smem_first=True,
         scratch=[pltpu.VMEM((HEAD, 1024), F32), pltpu.VMEM((HEAD, 1024), F32)],
     )
     recv_grad0 = both(back_send)
@@ -786,7 +811,7 @@
             ((4, width), F32),
         ],
         (
-            at, Far(x), Far(g), part_g, part_g_other, recv_grad0, Layer(wq, 0), Layer(others, 0), cs,
+            at, Far(x), Far(g), part_g, part_g_other, recv_grad0, Layer(wq, 0), Quarter(others, 0), cs,
             ln_gain, ln_bias, d_b_up0, d_b_up1, d_b_qkv1, d_norm1, d_sum0, d_sum1,
         ),
         "last",

time: 234 us -> 245 us (1.047)
  blocking collectives: 100 us -> 123 us
  starting transfers between devices: 23.7 us -> 12.4 us
    all_to_all x6 -> x7, blocking collectives: 100 us -> 123 us  [exchange(): return lax.all_to_all(value, axes, 0, 0)]
    all_to_all x3 -> x2, starting transfers between devices: 14.1 us -> 8.11 us  [exchange(): return lax.all_to_all(value, axes, 0, 0)]
    all_to_all x3 -> x2, waiting for transfers between devices: 6.77 us -> 0.88 us  [exchange(): return lax.all_to_all(value, axes, 0, 0)]
    ppermute x4 -> x3, starting transfers between devices: 9.44 us -> 4.09 us  [swap(): return lax.ppermute(value, 'tensor', [(0, 1), (1, 0)])]
    ppermute x4 -> x3, waiting for transfers between devices: 12.4 us -> 16.1 us  [swap(): return lax.ppermute(value, 'tensor', [(0, 1), (1, 0)])]
    pallas_call x10 -> x9, Pallas kernels: 35 us -> 36.5 us  [call(): pl.pallas_call(body, grid=(1,), out_shape=[o if isinstance(o, Kept) else...]
  transfers between devices with their start and end apart: 12 -> 10, of which waited for: 6 -> 4; matrix products, arithmetic and copies ran while one was open for 0% -> 0% of each run, Pallas kernels for 12% -> 9%
where the time goes in v11:
time: 245 us; the launch traced here: 244 us
  blocking collectives  123 us (50%)
  Pallas kernels  46.8 us (19%)
  waiting for transfers between devices  45.7 us (19%)
  between operations  13.9 us (6%)
  starting transfers between devices  12.4 us (5%)
    all_to_all x7, blocking collectives, exchange(): return lax.all_to_all(value, axes, 0, 0)  123 us
    pallas_call x9, Pallas kernels, call(): pl.pallas_call(body, grid=(1,), out_shape=[o if isinstance(o, Kept) else...  36.5 us
    all_gather x1, waiting for transfers between devices, shards(): full_bc = lax.all_gather(exchange(summed, 'context'), 'dp')  28.7 us
    ppermute x3, waiting for transfers between devices, swap(): return lax.ppermute(value, 'tensor', [(0, 1), (1, 0)])  16.1 us
    all_to_all x2, starting transfers between devices, exchange(): return lax.all_to_all(value, axes, 0, 0)  8.11 us
    pallas_call x1, Pallas kernels, unpack(): pl.pallas_call(unpack_rest_body, grid=(4,), out_shape=[pltpu.HBM(shape, F...  6.04 us
  transfers between devices with their start and end apart: 10, of which 4 were waited for; matrix products, arithmetic and copies ran while one was open for 0% of the time, Pallas kernels for 9%

profile of v11, /device:TPU:1, one launch (start us, length us, event | category | flops | bytes accessed | tf_op | source)
XLA Modules:
  0.0 243.5 jit_solution(1759098612430280711)
XLA Ops:
  7.3 5.3 %norm_qkv_feed.1 = (bf16[8,2,208,128]{3,2,1,0:T(8,128)(2,1)S(1)}, bf16[512,512]{1,0:T(8,128)(2,1)S(1)}, bf16[256,1024]{1,0:T(8,128)(2,1)}, bf16[256,1024]{1,0:T(8,128)(2,1)}, f32[2,2,8,128]{3,2,1,0:T(8,128)S(1)}) custom-call(s32[3]{0:T(128)S(1)} %pad_add_fusion.at, s32[2,128]{1,0:T(2,128)} %pos.1, f32[8,1]{1,0:T(8,128)} %constant.18.freqs, ...), custom_call_target="tpu_custom_call" | custom-call | tf_op jit(solution)/shard_map/norm_qkv_feed/pallas_call | solution.py:90
  12.6 22.6 %all_to_all.45 = bf16[16,208,128]{2,1,0:T(8,128)(2,1)S(1)} all-to-all(bf16[16,208,128]{2,1,0:T(8,128)(2,1)S(1)} %bitcast.32), channel_id=1, replica_groups=mesh['dp'=8,'context'=8,'tensor'=2] {'context','tensor'}, dimensions={0} | all-to-all | bytes 1703936 | tf_op jit(solution)/shard_map/all_to_all | solution.py:687
  35.2 3.3 %attend.1 = (bf16[8,2,64,128]{3,2,1,0:T(8,128)(2,1)}, f32[1,1024]{1,0:T(1,128)S(1)}, f32[64,1024]{1,0:T(8,128)}, s32[1,1024]{1,0:T(1,128)S(1)}, bf16[8,128,128]{2,1,0:T(8,128)(2,1)}) custom-call(s32[3]{0:T(128)S(1)} %pad_add_fusion.at, bf16[8,2,208,128]{3,2,1,0:T(8,128)(2,1)S(1)} %bitcast.24), custom_call_target="tpu_custom_call" | custom-call | tf_op jit(solution)/shard_map/attend/pallas_call | solution.py:90
  39.3 4.5 %all-to-all-start.1 = ((bf16[16,64,128]{2,1,0:T(8,128)(2,1)}), bf16[16,64,128]{2,1,0:T(8,128)(2,1)S(1)}, u32[]{:S(2)}, u32[]{:S(2)}) async-start(bf16[16,64,128]{2,1,0:T(8,128)(2,1)} %bitcast.8), calls=%async_computation.1 | async-start | bytes 524288 | tf_op jit(solution)/shard_map/all_to_all | solution.py:687
  43.8 9.0 %collective-permute-done.pair_other = bf16[512,512]{1,0:T(8,128)(2,1)S(1)} collective-permute-done((bf16[512,512]{1,0:T(8,128)(2,1)S(1)}, bf16[512,512]{1,0:T(8,128)(2,1)S(1)}, u32[]{:S(2)}, u32[]{:S(2)}) %collective-permute-start) | collective-permute-done | bytes 524320 | tf_op jit(solution)/shard_map/ppermute | solution.py:683
  53.7 6.9 %middle.1 = (f32[256,512]{1,0:T(8,128)}, bf16[8,256,128]{2,1,0:T(8,128)(2,1)S(1)}, bf16[8,512,256]{2,1,0:T(8,128)(2,1)}, bf16[512,512]{1,0:T(8,128)(2,1)S(1)}, f...) custom-call(s32[3]{0:T(128)S(1)} %pad_add_fusion.at, f32[256,512]{1,0:T(8,128)} %bitcast.43, ...), custom_call_target="tpu_custom_call" | custom-call | tf_op jit(solution)/shard_map/middle/pallas_call | solution.py:90
  62.5 2.0 collective-permute-start.1
  64.5 15.1 %all_to_all.46.recv = bf16[8,256,128]{2,1,0:T(8,128)(2,1)S(1)} all-to-all(bf16[8,256,128]{2,1,0:T(8,128)(2,1)S(1)} %get-tuple-element.58), channel_id=1, replica_groups=mesh['dp'=8,'context'=8,'tensor'=2] {'context'}, dimensions={0} | all-to-all | bytes 1048576 | tf_op jit(solution)/shard_map/all_to_all | solution.py:687
  79.6 4.2 %attend_both.1 = bf16[8,2,256,128]{3,2,1,0:T(8,128)(2,1)S(1)} custom-call(bf16[8,256,128]{2,1,0:T(8,128)(2,1)S(1)} %all_to_all.46.recv, s32[1,1024]{1,0:T(1,128)S(1)} %get-tuple-element.59.start, bf16[512,512]{1,0:T(8,128)(2,1)S(1)} %collective-permute-done.1._.parts_other), custom_call_target="tpu_custom_call" | custom-call | tf_op jit(solution)/shard_map/attend_both/pallas_call | solution.py:90
  83.8 18.6 %all_to_all.47 = bf16[16,256,128]{2,1,0:T(8,128)(2,1)S(1)} all-to-all(bf16[16,256,128]{2,1,0:T(8,128)(2,1)S(1)} %bitcast.28), channel_id=1, replica_groups=mesh['dp'=8,'context'=8,'tensor'=2] {'context','tensor'}, dimensions={0} | all-to-all | bytes 2097152 | tf_op jit(solution)/shard_map/all_to_all | solution.py:687
  102.5 8.2 %turn_point.1 = (f32[256,512]{1,0:T(8,128)}, f32[256,512]{1,0:T(8,128)}, bf16[8,192,128]{2,1,0:T(8,128)(2,1)}, bf16[8,832,256]{2,1,0:T(8,128)(2,1)}, bf16[256,51...) custom-call(s32[3]{0:T(128)S(1)} %pad_add_fusion.at, ...), custom_call_target="tpu_custom_call" | custom-call | tf_op jit(solution)/shard_map/turn_point/pallas_call | solution.py:90
  110.7 3.6 %all-to-all-start.4 = ((bf16[8,192,128]{2,1,0:T(8,128)(2,1)}), bf16[8,192,128]{2,1,0:T(8,128)(2,1)S(1)}, u32[]{:S(2)}, u32[]{:S(2)}) async-start(bf16[8,192,128]{2,1,0:T(8,128)(2,1)} %get-tuple-element.67), calls=%async_computation.5 | async-start | bytes 786432 | tf_op jit(solution)/shard_map/all_to_all | solution.py:687
  114.4 1.3 collective-permute-start.2
  115.7 7.1 %collective-permute-done.2._.part_other = bf16[256,512]{1,0:T(8,128)(2,1)S(1)} collective-permute-done((bf16[256,512]{1,0:T(8,128)(2,1)S(1)}, bf16[256,512]{1,0:T(8,128)(2,1)S(1)}, u32[]{:S(2)}, u32[]{:S(2)}) %collective-permute-start.2) | collective-permute-done | bytes 262176 | tf_op jit(solution)/shard_map/ppermute | solution.py:683
  122.8 2.8 %attend_back.1 = bf16[8,2,320,128]{3,2,1,0:T(8,128)(2,1)S(1)} custom-call(s32[3]{0:T(128)S(1)} %pad_add_fusion.at, bf16[8,2,208,128]{3,2,1,0:T(8,128)(2,1)S(1)} %bitcast.25, bf16[8,192,128]{2,1,0:T(8,128)(2,1)S(1)} %all-to-all-done.4.recv_d, s32[1,1024]{1,0:T(1,128)S(1)} %get-tuple-element.59.start, f32[1,1024]{1,0:T(1,128)S(1)} %get-tuple-element.68.lse, ...), custom_call_target="tpu_custom_call" | custom-call | tf_op jit(solution)/shard_map/attend_back/pallas_call | solution.py:90
  125.6 18.8 %all_to_all.48 = bf16[16,320,128]{2,1,0:T(8,128)(2,1)S(1)} all-to-all(bf16[16,320,128]{2,1,0:T(8,128)(2,1)S(1)} %bitcast.26), channel_id=1, replica_groups=mesh['dp'=8,'context'=8,'tensor'=2] {'context','tensor'}, dimensions={0} | all-to-all | bytes 2621440 | tf_op jit(solution)/shard_map/all_to_all | solution.py:687
  144.4 4.0 %last.1 = (f32[256,512]{1,0:T(8,128)}, bf16[8,208,256]{2,1,0:T(8,128)(2,1)S(1)}, bf16[512,256]{1,0:T(8,128)(2,1)}, f32[3,256]{1,0:T(4,128)}, f32[4,512]{1,0:T(4,128)}) custom-call(s32[3]{0:T(128)S(1)} %pad_add_fusion.at, f32[256,512]{1,0:T(8,128)} %bitcast.45, f32[256,512]{1,0:T(8,128)} %get-tuple-element.65.g, bf16[256,512]{1,0:T(8,128)(2,1)S(1)} %get-tuple-element.66.part, ...), custom_call_target="tpu_custom_call" | custom-call | tf_op jit(solution)/shard_map/last/pallas_call | solution.py:90
  148.4 24.1 %all_to_all.49.got = bf16[8,208,256]{2,1,0:T(8,128)(2,1)S(1)} all-to-all(bf16[8,208,256]{2,1,0:T(8,128)(2,1)S(1)} %get-tuple-element.77), channel_id=1, replica_groups=mesh['dp'=8,'context'=8,'tensor'=2] {'dp'}, dimensions={0} | all-to-all | bytes 1703936 | tf_op jit(solution)/shard_map/all_to_all | solution.py:687
  172.5 1.8 mix.1
  174.4 12.1 %all_to_all.50.got = bf16[8,136,256]{2,1,0:T(8,128)(2,1)S(1)} all-to-all(bf16[8,136,256]{2,1,0:T(8,128)(2,1)S(1)} %get-tuple-element.80), channel_id=1, replica_groups=mesh['dp'=8,'context'=8,'tensor'=2] {'context'}, dimensions={0} | all-to-all | bytes 1114112 | tf_op jit(solution)/shard_map/all_to_all | solution.py:687
  186.6 11.5 %all_to_all.51 = bf16[8,136,256]{2,1,0:T(8,128)(2,1)} all-to-all(bf16[8,136,256]{2,1,0:T(8,128)(2,1)S(1)} %sum.1), channel_id=1, replica_groups=mesh['dp'=8,'context'=8,'tensor'=2] {'context'}, dimensions={0} | all-to-all | bytes 1114112 | tf_op jit(solution)/shard_map/all_to_all | solution.py:687
  198.1 4.2 %unpack_first.1 = (f32[2,512,1024]{2,1,0:T(8,128)}, f32[2,1024,512]{2,1,0:T(8,128)}) custom-call(bf16[8,512,256]{2,1,0:T(8,128)(2,1)} %bitcast.47), custom_call_target="tpu_custom_call" | custom-call | tf_op jit(solution)/shard_map/unpack_first/pallas_call | solution.py:648
  202.3 28.7 %all-gather.9.cloned.1.call-done = bf16[64,136,256]{2,1,0:T(8,128)(2,1)} async-done(((bf16[8,136,256]{2,1,0:T(8,128)(2,1)}), bf16[64,136,256]{2,1,0:T(8,128)(2,1)}) %all-gather.9.cloned.1.call-update) | async-done | bytes 4456464 | tf_op jit(solution)/shard_map/all_gather | solution.py:828
  231.0 6.0 %unpack_rest.1 = (f32[2,512,1024]{2,1,0:T(8,128)}, f32[2,1024,512]{2,1,0:T(8,128)}, f32[2,3,512,256]{3,2,1,0:T(8,128)}, f32[2,256,512]{2,1,0:T(8,128)}, f32[2,10...) custom-call(bf16[8,8,136,256]{3,2,1,0:T(8,128)(2,1)} %bitcast.46, ...), custom_call_target="tpu_custom_call", output_to_operand_aliasing={{0}: (1, {}), {1}: (2, {})} | custom-call | tf_op jit(solution)/shard_map/unpack_rest/pallas_call | solution.py:666
  (38 shorter events, 3.9 us)
Async XLA Ops:
  7.2 95.3 %all-gather.7.cloned.1.call-start = ((), (), s32[]{:S(2)}) async-start(), calls=%async_computation.13 | async-start | bytes 2359296 | tf_op jit(solution)/shard_map/all_gather | solution.py:740
  12.6 41.1 %copy-start.4 = (f32[2,2,512]{2,1,0:T(2,128)S(1)}, f32[2,2,512]{2,1,0:T(2,128)}, u32[]{:S(2)}) copy-start(f32[2,2,512]{2,1,0:T(2,128)} %gain.7) | copy-start | bytes 24580
  12.6 41.1 %copy-start.5 = (f32[2,2,512]{2,1,0:T(2,128)S(1)}, f32[2,2,512]{2,1,0:T(2,128)}, u32[]{:S(2)}) copy-start(f32[2,2,512]{2,1,0:T(2,128)} %bias.7) | copy-start | bytes 24580
  12.6 41.1 %copy-start.6 = (f32[2,2,512]{2,1,0:T(2,128)S(1)}, f32[2,2,512]{2,1,0:T(2,128)}, u32[]{:S(2)}) copy-start(f32[2,2,512]{2,1,0:T(2,128)} %out_bias.3) | copy-start | bytes 24580
  12.6 41.1 %copy-start.7 = (f32[2,1024]{1,0:T(2,128)S(1)}, f32[2,1024]{1,0:T(2,128)}, u32[]{:S(2)}) copy-start(f32[2,1024]{1,0:T(2,128)} %b_up.3) | copy-start | bytes 24580
  12.6 41.1 %copy-start.8 = (f32[2,3,256]{2,0,1:T(2,128)S(1)}, f32[2,3,256]{2,0,1:T(2,128)}, u32[]{:S(2)}) copy-start(f32[2,3,256]{2,0,1:T(2,128)} %param.17) | copy-start | bytes 18436
  38.5 14.3 %collective-permute-start = (bf16[512,512]{1,0:T(8,128)(2,1)S(1)}, bf16[512,512]{1,0:T(8,128)(2,1)S(1)}, u32[]{:S(2)}, u32[]{:S(2)}) collective-permute-start(bf16[512,512]{1,0:T(8,128)(2,1)S(1)} %get-tuple-element.52.pair), channel_id=1, source_target_pairs={{0,1},{1,0},{2,3},{3,2},{4,5},{5,4},{6,7},{7,6},{8,9},{9,8},{10,11... | collective-permute-start | bytes 1572872 | tf_op jit(solution)/shard_map/ppermute | solution.py:683
  39.3 14.4 %all-to-all-start.1 = ((bf16[16,64,128]{2,1,0:T(8,128)(2,1)}), bf16[16,64,128]{2,1,0:T(8,128)(2,1)S(1)}, u32[]{:S(2)}, u32[]{:S(2)}) async-start(bf16[16,64,128]{2,1,0:T(8,128)(2,1)} %bitcast.8), calls=%async_computation.1 | async-start | bytes 524288 | tf_op jit(solution)/shard_map/all_to_all | solution.py:687
  43.8 58.7 %reduce-scatter.3.cloned.1.call-start = ((), (), s32[]{:S(2)}) async-start(), calls=%async_computation.11 | async-start | bytes 2359296 | tf_op jit(solution)/shard_map/reduce_scatter | solution.py:760
  60.6 0.8 copy-start
  61.4 1.0 copy-start.1
  61.4 111.0 %reduce-scatter.5.cloned.1.call-start = ((), (), s32[]{:S(2)}) async-start(), calls=%async_computation.12 | async-start | bytes 3833856 | tf_op jit(solution)/shard_map/reduce_scatter | solution.py:792
  62.5 17.2 %collective-permute-start.1 = (bf16[512,512]{1,0:T(8,128)(2,1)S(1)}, bf16[512,512]{1,0:T(8,128)(2,1)S(1)}, u32[]{:S(2)}, u32[]{:S(2)}) collective-permute-start(bf16[512,512]{1,0:T(8,128)(2,1)S(1)} %copy-done.1), channel_id=1, source_target_pairs={{0,1},{1,0},{2,3},{3,2},{4,5},{5,4},{6,7},{7,6},{8,9},{9,8},{10,11... | collective-permute-start | bytes 1572872 | tf_op jit(solution)/shard_map/ppermute | solution.py:683
  79.6 22.8 %copy-start.2 = (bf16[512,512]{1,0:T(8,128)(2,1)S(1)}, bf16[512,512]{1,0:T(8,128)(2,1)}, u32[]{:S(2)}) copy-start(bf16[512,512]{1,0:T(8,128)(2,1)} %copy-done) | copy-start | bytes 1572868
  110.7 12.1 %copy-start.3 = (f32[64,1024]{1,0:T(8,128)S(1)}, f32[64,1024]{1,0:T(8,128)}, u32[]{:S(2)}) copy-start(f32[64,1024]{1,0:T(8,128)} %get-tuple-element.69.ctx) | copy-start | bytes 786436
  110.7 12.1 %all-to-all-start.4 = ((bf16[8,192,128]{2,1,0:T(8,128)(2,1)}), bf16[8,192,128]{2,1,0:T(8,128)(2,1)S(1)}, u32[]{:S(2)}, u32[]{:S(2)}) async-start(bf16[8,192,128]{2,1,0:T(8,128)(2,1)} %get-tuple-element.67), calls=%async_computation.5 | async-start | bytes 786432 | tf_op jit(solution)/shard_map/all_to_all | solution.py:687
  114.3 83.8 %all-gather.11.cloned.1.call-start = ((), (), s32[]{:S(2)}) async-start(), calls=%async_computation.15 | async-start | bytes 2359296 | tf_op jit(solution)/shard_map/all_gather | solution.py:826
  114.4 8.4 %collective-permute-start.2 = (bf16[256,512]{1,0:T(8,128)(2,1)S(1)}, bf16[256,512]{1,0:T(8,128)(2,1)S(1)}, u32[]{:S(2)}, u32[]{:S(2)}) collective-permute-start(bf16[256,512]{1,0:T(8,128)(2,1)S(1)} %get-tuple-element.66.part), channel_id=1, source_target_pairs={{0,1},{1,0},{2,3},{3,2},{4,5},{5,4},{6,7},{7,6},{8,9},{9,8},{10,11... | collective-permute-start | bytes 786440 | tf_op jit(solution)/shard_map/ppermute | solution.py:683
  174.3 56.6 %all-gather.9.cloned.1.call-start = ((), (), s32[]{:S(2)}) async-start(), calls=%async_computation.14 | async-start | bytes 5013504 | tf_op jit(solution)/shard_map/all_gather | solution.py:828
Sparse Core Ops, SparseCore 0:
  38.6 24.6 all-gather.6
  66.3 30.8 reduce-scatter.2
  110.8 34.9 reduce-scatter.4
  174.4 21.4 all-gather.10
  198.2 32.7 all-gather.8

commit v12 on v10

--- a/solution.py
+++ b/solution.py
@@ -58,27 +58,125 @@
     return pltpu.with_memory_space_constraint(array, pltpu.HBM)
 
 
+class Fetch:
+    def __init__(self, array, layer=None):
+        self.array, self.layer = far(array), layer
+        self.shape = array.shape if layer is None else array.shape[1:]
+
+    def spec(self):
+        return pl.BlockSpec(memory_space=pltpu.HBM)
+
+    def source(self, ref):
+        return ref if self.layer is None else ref.at[self.layer]
+
+
+class Lazy:
+    def __init__(self, ref, copy):
+        self.ref, self.copy, self.shape = ref, copy, ref.shape
+
+    def __getitem__(self, index):
+        if self.copy is not None:
+            self.copy.wait()
+            self.copy = None
+        return self.ref[index]
+
+
+class Store:
+    def __init__(self, shape, dtype):
+        self.shape, self.dtype = shape, dtype
+
+
+class Out:
+    def __init__(self, ref, target, sems, copies):
+        self.ref, self.target, self.sems, self.copies, self.done = ref, target, sems, copies, False
+
+    def __setitem__(self, index, value):
+        self.ref[index] = value
+
+    def __getitem__(self, index):
+        return self.ref[index]
+
+    def flush(self, *place):
+        source, target = self.ref, self.target
+        if place:
+            source, target = source.at[place], target.at[place]
+        copy = pltpu.make_async_copy(source, target, self.sems.at[len(self.copies)])
+        copy.start()
+        self.copies.append(copy)
+        self.done = True
+
+
+FLUSHES = 40
+
+
+def flush(ref, *place):
+    if isinstance(ref, Out):
+        ref.flush(*place)
+
+
 def whole(shape):
     return pl.BlockSpec(shape, lambda i: (0,) * len(shape))
 
 
 def call(body, out_shape, args, name, scratch=(), smem_first=False):
-    specs = [
-        a.spec() if isinstance(a, (Layer, Far, After)) else whole(a.shape) for a in args
-    ]
-    args = [a.array if isinstance(a, (Layer, Far, After)) else a for a in args]
+    own = (Layer, Far, After, Fetch)
+    specs = [a.spec() if isinstance(a, own) else whole(a.shape) for a in args]
+    fetched = [i for i, a in enumerate(args) if isinstance(a, Fetch)]
+    stored = [i for i, o in enumerate(out_shape) if isinstance(o, Store)]
+    plans = list(args)
+    arrays = [a.array if isinstance(a, own) else a for a in args]
     if smem_first:
         specs[0] = pl.BlockSpec(memory_space=pltpu.SMEM)
+    shapes, out_specs = [], []
+    for o in out_shape:
+        if isinstance(o, Store):
+            shapes.append(pltpu.HBM(o.shape, o.dtype))
+            out_specs.append(pl.BlockSpec(memory_space=pltpu.HBM))
+        else:
+            shapes.append(o if isinstance(o, Kept) else jax.ShapeDtypeStruct(*o))
+            out_specs.append(whole(o.shape if isinstance(o, Kept) else o[0]))
+    buffers = [pltpu.VMEM(plans[i].shape, arrays[i].dtype) for i in fetched]
+    buffers += [pltpu.VMEM(out_shape[i].shape, out_shape[i].dtype) for i in stored]
+    sems = []
+    if fetched:
+        sems.append(pltpu.SemaphoreType.DMA((len(fetched),)))
+    if stored:
+        sems.append(pltpu.SemaphoreType.DMA((FLUSHES,)))
+    n_in, n_out, n_scratch = len(args), len(out_shape), len(scratch)
+
+    def run(*refs):
+        ins, outs = list(refs[:n_in]), list(refs[n_in : n_in + n_out])
+        rest = list(refs[n_in + n_out :])
+        mine, rest = rest[:n_scratch], rest[n_scratch:]
+        for k, i in enumerate(fetched):
+            copy = pltpu.make_async_copy(
+                plans[i].source(ins[i]), rest[k], rest[len(buffers)].at[k]
+            )
+            copy.start()
+            ins[i] = Lazy(rest[k], copy)
+        copies = []
+        for k, i in enumerate(stored):
+            outs[i] = Out(rest[len(fetched) + k], outs[i], rest[-1], copies)
+        body(*ins, *outs, *mine)
+        for i in fetched:
+            if ins[i].copy is not None:
+                ins[i].copy.wait()
+        for i in stored:
+            if not outs[i].done:
+                outs[i].flush()
+        for copy in copies:
+            copy.wait()
+
     return pl.pallas_call(
-        body,
+        run,
         grid=(1,),
-        out_shape=[o if isinstance(o, Kept) else jax.ShapeDtypeStruct(*o) for o in out_shape],
+        out_shape=shapes,
         in_specs=specs,
-        out_specs=[whole(o.shape if isinstance(o, Kept) else o[0]) for o in out_shape],
-        scratch_shapes=list(scratch),
+        out_specs=out_specs,
+        scratch_shapes=list(scratch) + buffers + sems,
         compiler_params=pltpu.CompilerParams(vmem_limit_bytes=40 * 1024 * 1024),
         name=name,
-    )(*args)
+    )(*arrays)
 
 
 def norm_rows(x):
@@ -150,6 +248,8 @@
     def put(c, value):
         for p in range(8):
             out[p, row + 64 * c : row + 64 * (c + 1), :] = value[64 * p : 64 * (p + 1)].astype(BF)
+        if c % 2 == 1:
+            flush(out, slice(None), slice(row + 64 * (c - 1), row + 64 * (c + 1)))
 
     return put
 
@@ -161,6 +261,8 @@
                 out[c // 128 + k, row + 128 * half : row + 128 * (half + 1), :] = value[
                     128 * k : 128 * (k + 1), 256 * half : 256 * (half + 1)
                 ].astype(BF)
+        if c % 512 == 256:
+            flush(out, slice(c // 128 - 2, c // 128 + 2), slice(row, row + 256))
 
     return put
 
@@ -449,6 +551,8 @@
             ]
     pack_out(grads, 704, own_ctx(t, recv), cot[...].astype(BF))
     pack_out(grads, 768, own_ctx(t, recv_first), g_b)
+    flush(grads, slice(None), slice(0, 192))
+    flush(grads, slice(None), slice(704, 832))
     normed, _ = norm_rows(x[...])
     mlp_in = (normed * gain[0, 1:2] + bias[0, 1:2]).astype(BF)
     part[...] = feed_back(
@@ -696,8 +800,8 @@
             ((2, 2, HALF, BLK), F32),
         ],
         (
-            at, positions, freqs, Far(x), ln_gain, ln_bias, Layer(wq, 0), bq, Layer(w_up, 0), b_up,
-            Layer(w_down, 0), Layer(w_out, 0),
+            at, positions, freqs, Far(x), ln_gain, ln_bias, Layer(wq, 0), bq, Fetch(w_up, 0), b_up,
+            Fetch(w_down, 0), Layer(w_out, 0),
         ),
         "norm_qkv_feed",
         smem_first=True,
@@ -720,14 +824,14 @@
         [
             pltpu.HBM((rows, width), F32),
             ((8, 256, BLK), BF),
-            pltpu.HBM((8, 512, 256), BF),
+            Store((8, 512, 256), BF),
             ((2 * rows, width), BF),
             ((1, 1024), F32),
             ((1, width), F32),
         ],
         (
             at, Far(x), pair, pair_other, recv_ctx, Layer(w_out, 0), out_bias, ln_gain, ln_bias,
-            Layer(wq, 1), bq, Layer(w_up, 1), b_up, Layer(w_down, 1), Layer(w_out, 1), Far(cot), cs,
+            Layer(wq, 1), bq, Fetch(w_up, 1), b_up, Fetch(w_down, 1), Layer(w_out, 1), Far(cot), cs,
         ),
         "middle",
         scratch=[pltpu.VMEM((rows, 1024), BF), pltpu.VMEM((rows, 1024), BF)],
@@ -750,7 +854,7 @@
             pltpu.HBM((rows, width), F32),
             pltpu.HBM((rows, width), F32),
             pltpu.VMEM((8, 192, BLK), BF),
-            pltpu.HBM((8, 832, 256), BF),
+            Store((8, 832, 256), BF),
             ((rows, width), BF),
             ((1, 1024), F32),
             ((3, 256), F32),
@@ -759,8 +863,8 @@
         ],
         (
             at, Far(stream), parts, parts_other, recv_grad, Layer(w_out, 1), Layer(wq, 1),
-            Layer(others, 1), out_bias, ln_gain, ln_bias, Far(cot), cs, Far(x), Far(act), Far(slope),
-            Layer(w_up, 0), Layer(w_down, 0), Layer(w_out, 0), recv_ctx, Far(sums_a),
+            Layer(others, 1), out_bias, ln_gain, ln_bias, Far(cot), cs, Fetch(x), Fetch(act), Fetch(slope),
+            Fetch(w_up, 0), Fetch(w_down, 0), Layer(w_out, 0), recv_ctx, Far(sums_a),
         ),
         "turn_point",
         smem_first=True,

time: 234 us -> 237 us (1.013)
  Pallas kernels: 46.7 us -> 51.1 us
    pallas_call x10, Pallas kernels: 35 us -> 39.4 us  [call(): pl.pallas_call(run, grid=(1,), out_shape=shapes, in_specs=specs, out_spec...]
  transfers between devices with their start and end apart: 12 -> 12, of which waited for: 6 -> 6; matrix products, arithmetic and copies ran while one was open for 0% -> 0% of each run, Pallas kernels for 12% -> 13%
where the time goes in v12:
time: 237 us; the launch traced here: 236 us
  blocking collectives  100 us (42%)
  Pallas kernels  51.1 us (22%)
  waiting for transfers between devices  47.1 us (20%)
  starting transfers between devices  23.7 us (10%)
  between operations  14 us (6%)
    all_to_all x6, blocking collectives, exchange(): return lax.all_to_all(value, axes, 0, 0)  100 us
    pallas_call x10, Pallas kernels, call(): pl.pallas_call(run, grid=(1,), out_shape=shapes, in_specs=specs, out_spec...  39.4 us
    all_gather x1, waiting for transfers between devices, shards(): full_bc = lax.all_gather(exchange(summed, 'context'), 'dp')  28.7 us
    all_to_all x3, starting transfers between devices, exchange(): return lax.all_to_all(value, axes, 0, 0)  14.1 us
    ppermute x4, waiting for transfers between devices, swap(): return lax.ppermute(value, 'tensor', [(0, 1), (1, 0)])  11.5 us
    ppermute x4, starting transfers between devices, swap(): return lax.ppermute(value, 'tensor', [(0, 1), (1, 0)])  9.43 us
    all_to_all x3, waiting for transfers between devices, exchange(): return lax.all_to_all(value, axes, 0, 0)  6.77 us
    pallas_call x1, Pallas kernels, unpack(): pl.pallas_call(unpack_rest_body, grid=(4,), out_shape=[pltpu.HBM(shape, F...  6.04 us
  transfers between devices with their start and end apart: 12, of which 6 were waited for; matrix products, arithmetic and copies ran while one was open for 0% of the time, Pallas kernels for 13%

profile of v12, /device:TPU:1, one launch (start us, length us, event | category | flops | bytes accessed | tf_op | source)
XLA Modules:
  0.0 236.3 jit_solution(6891072919649428623)
XLA Ops:
  8.9 4.5 %collective-permute-start.2 = (bf16[2,4,64,256]{3,2,1,0:T(8,128)(2,1)S(1)}, bf16[2,4,64,256]{3,2,1,0:T(8,128)(2,1)S(1)}, u32[]{:S(2)}, u32[]{:S(2)}) collective-permute-start(bf16[2,4,64,256]{3,2,1,0:T(8,128)(2,1)S(1)} %chunk.1), channel_id=1, source_target_pairs={{0,1},{1,0},{2,3},{3,2},{4,5},{5,4},{6,7},{7,6},{8,9},{9,8},{10,11... | collective-permute-start | bytes 786440 | tf_op jit(solution)/shard_map/ppermute | solution.py:768
  13.4 5.3 %norm_qkv_feed.1 = (bf16[8,208,128]{2,1,0:T(8,128)(2,1)}, bf16[512,512]{1,0:T(8,128)(2,1)S(1)}, bf16[256,1024]{1,0:T(8,128)(2,1)}, bf16[256,1024]{1,0:T(8,128)(2,1)}, f32[2,2,8,128]{3,2,1,0:T(8,128)S(1)}) custom-call(s32[3]{0:T(128)S(1)} %pad_add_fusion.refs_0_.at, s32[2,128]{1,0:T(2,128)S(1)} %copy-done.7, f32[8,1]{1,0:T(8,128)S(1)} %copy-done.6, ...), custom_call_target="tpu_custom_call" | custom-call | tf_op jit(solution)/shard_map/norm_qkv_feed/pallas_call | solution.py:170
  20.2 4.6 %all-to-all-start = ((bf16[8,208,128]{2,1,0:T(8,128)(2,1)}), bf16[8,208,128]{2,1,0:T(8,128)(2,1)S(1)}, u32[]{:S(2)}, u32[]{:S(2)}) async-start(bf16[8,208,128]{2,1,0:T(8,128)(2,1)} %get-tuple-element.52.refs_1_), calls=%async_computation | async-start | bytes 851968 | tf_op jit(solution)/shard_map/all_to_all | solution.py:772
  24.8 3.3 %collective-permute-start = (bf16[512,512]{1,0:T(8,128)(2,1)S(1)}, bf16[512,512]{1,0:T(8,128)(2,1)S(1)}, u32[]{:S(2)}, u32[]{:S(2)}) collective-permute-start(bf16[512,512]{1,0:T(8,128)(2,1)S(1)} %get-tuple-element.51.refs_2_), channel_id=1, source_target_pairs={{0,1},{1,0},{2,3},{3,2},{4,5},{5,4},{6,7},{7,6},{8,9},{9,8},{10,11... | collective-permute-start | bytes 1572872 | tf_op jit(solution)/shard_map/ppermute | solution.py:768
  28.1 3.2 %all-to-all-done.refs_0_ = bf16[8,208,128]{2,1,0:T(8,128)(2,1)S(1)} async-done(((bf16[8,208,128]{2,1,0:T(8,128)(2,1)}), bf16[8,208,128]{2,1,0:T(8,128)(2,1)S(1)}, u32[]{:S(2)}, u32[]{:S(2)}) %all-to-all-start) | async-done | bytes 426016 | tf_op jit(solution)/shard_map/all_to_all | solution.py:772
  31.2 2.7 %attend.1 = (bf16[8,2,64,128]{3,2,1,0:T(8,128)(2,1)}, f32[1,1024]{1,0:T(1,128)S(1)}, f32[64,1024]{1,0:T(8,128)}, s32[1,1024]{1,0:T(1,128)S(1)}) custom-call(bf16[8,208,128]{2,1,0:T(8,128)(2,1)S(1)} %all-to-all-done.refs_0_), custom_call_target="tpu_custom_call" | custom-call | tf_op jit(solution)/shard_map/attend/pallas_call | solution.py:170
  33.9 5.9 %all-to-all-start.1 = ((bf16[16,64,128]{2,1,0:T(8,128)(2,1)}), bf16[16,64,128]{2,1,0:T(8,128)(2,1)S(1)}, u32[]{:S(2)}, u32[]{:S(2)}) async-start(bf16[16,64,128]{2,1,0:T(8,128)(2,1)} %bitcast.6), calls=%async_computation.1 | async-start | bytes 524288 | tf_op jit(solution)/shard_map/all_to_all | solution.py:772
  39.8 4.0 %collective-permute-done.refs_3_ = bf16[512,512]{1,0:T(8,128)(2,1)S(1)} collective-permute-done((bf16[512,512]{1,0:T(8,128)(2,1)S(1)}, bf16[512,512]{1,0:T(8,128)(2,1)S(1)}, u32[]{:S(2)}, u32[]{:S(2)}) %collective-permute-start) | collective-permute-done | bytes 524320 | tf_op jit(solution)/shard_map/ppermute | solution.py:768
  43.8 3.6 %all-to-all-done.1 = bf16[16,64,128]{2,1,0:T(8,128)(2,1)S(1)} async-done(((bf16[16,64,128]{2,1,0:T(8,128)(2,1)}), bf16[16,64,128]{2,1,0:T(8,128)(2,1)S(1)}, u32[]{:S(2)}, u32[]{:S(2)}) %all-to-all-start.1) | async-done | bytes 262176 | tf_op jit(solution)/shard_map/all_to_all | solution.py:772
  47.4 8.0 %middle.1 = (f32[256,512]{1,0:T(8,128)}, bf16[8,256,128]{2,1,0:T(8,128)(2,1)S(1)}, bf16[8,512,256]{2,1,0:T(8,128)(2,1)}, bf16[512,512]{1,0:T(8,128)(2,1)S(1)}, f...) custom-call(s32[3]{0:T(128)S(1)} %pad_add_fusion.refs_0_.at, f32[256,512]{1,0:T(8,128)} %bitcast.35, ...), custom_call_target="tpu_custom_call" | custom-call | tf_op jit(solution)/shard_map/middle/pallas_call | solution.py:170
  56.0 12.1 %all_to_all.45.refs_0_ = bf16[8,256,128]{2,1,0:T(8,128)(2,1)S(1)} all-to-all(bf16[8,256,128]{2,1,0:T(8,128)(2,1)S(1)} %get-tuple-element.57), channel_id=1, replica_groups=mesh['dp'=8,'context'=8,'tensor'=2] {'context'}, dimensions={0} | all-to-all | bytes 1048576 | tf_op jit(solution)/shard_map/all_to_all | solution.py:772
  68.1 4.2 %attend_both.1 = bf16[8,2,256,128]{3,2,1,0:T(8,128)(2,1)S(1)} custom-call(bf16[8,256,128]{2,1,0:T(8,128)(2,1)S(1)} %all_to_all.45.refs_0_, s32[1,1024]{1,0:T(1,128)S(1)} %get-tuple-element.58.refs_1_.refs_2_, bf16[512,512]{1,0:T(8,128)(2,1)S(1)} %collective-permute-done.1.refs_2_.refs_3_), custom_call_target="tpu_custom_call" | custom-call | tf_op jit(solution)/shard_map/attend_both/pallas_call | solution.py:170
  72.3 19.5 %all_to_all.46 = bf16[16,256,128]{2,1,0:T(8,128)(2,1)S(1)} all-to-all(bf16[16,256,128]{2,1,0:T(8,128)(2,1)S(1)} %bitcast.23), channel_id=1, replica_groups=mesh['dp'=8,'context'=8,'tensor'=2] {'context','tensor'}, dimensions={0} | all-to-all | bytes 2097152 | tf_op jit(solution)/shard_map/all_to_all | solution.py:772
  91.8 10.6 %turn_point.1 = (f32[256,512]{1,0:T(8,128)}, f32[256,512]{1,0:T(8,128)}, bf16[8,192,128]{2,1,0:T(8,128)(2,1)}, bf16[8,832,256]{2,1,0:T(8,128)(2,1)}, bf16[256,51...) custom-call(s32[3]{0:T(128)S(1)} %pad_add_fusion.refs_0_.at, ...), custom_call_target="tpu_custom_call" | custom-call | tf_op jit(solution)/shard_map/turn_point/pallas_call | solution.py:170
  102.4 3.6 %all-to-all-start.4 = ((bf16[8,192,128]{2,1,0:T(8,128)(2,1)}), bf16[8,192,128]{2,1,0:T(8,128)(2,1)S(1)}, u32[]{:S(2)}, u32[]{:S(2)}) async-start(bf16[8,192,128]{2,1,0:T(8,128)(2,1)} %get-tuple-element.65), calls=%async_computation.5 | async-start | bytes 786432 | tf_op jit(solution)/shard_map/all_to_all | solution.py:772
  107.1 6.8 %collective-permute-done.3.refs_5_.refs_4_ = bf16[256,512]{1,0:T(8,128)(2,1)S(1)} collective-permute-done((bf16[256,512]{1,0:T(8,128)(2,1)S(1)}, bf16[256,512]{1,0:T(8,128)(2,1)S(1)}, u32[]{:S(2)}, u32[]{:S(2)}) %collective-permute-start.3) | collective-permute-done | bytes 262176 | tf_op jit(solution)/shard_map/ppermute | solution.py:768
  116.2 18.8 %all_to_all.47 = bf16[16,320,128]{2,1,0:T(8,128)(2,1)S(1)} all-to-all(bf16[16,320,128]{2,1,0:T(8,128)(2,1)S(1)} %bitcast.21), channel_id=1, replica_groups=mesh['dp'=8,'context'=8,'tensor'=2] {'context','tensor'}, dimensions={0} | all-to-all | bytes 2621440 | tf_op jit(solution)/shard_map/all_to_all | solution.py:772
  135.0 3.9 %last.1 = (f32[256,512]{1,0:T(8,128)}, bf16[8,208,256]{2,1,0:T(8,128)(2,1)S(1)}, bf16[512,256]{1,0:T(8,128)(2,1)}, f32[3,256]{1,0:T(4,128)}, f32[4,512]{1,0:T(4,128)}) custom-call(s32[3]{0:T(128)S(1)} %pad_add_fusion.refs_0_.at, f32[256,512]{1,0:T(8,128)} %bitcast.37, f32[256,512]{1,0:T(8,128)} %get-tuple-element.63.refs_2_, ...), custom_call_target="tpu_custom_call" | custom-call | tf_op jit(solution)/shard_map/last/pallas_call | solution.py:170
  138.9 26.3 %all_to_all.48.refs_0_ = bf16[8,208,256]{2,1,0:T(8,128)(2,1)S(1)} all-to-all(bf16[8,208,256]{2,1,0:T(8,128)(2,1)S(1)} %get-tuple-element.75), channel_id=1, replica_groups=mesh['dp'=8,'context'=8,'tensor'=2] {'dp'}, dimensions={0} | all-to-all | bytes 1703936 | tf_op jit(solution)/shard_map/all_to_all | solution.py:772
  167.1 12.1 %all_to_all.49.refs_0_ = bf16[8,136,256]{2,1,0:T(8,128)(2,1)S(1)} all-to-all(bf16[8,136,256]{2,1,0:T(8,128)(2,1)S(1)} %get-tuple-element.78), channel_id=1, replica_groups=mesh['dp'=8,'context'=8,'tensor'=2] {'context'}, dimensions={0} | all-to-all | bytes 1114112 | tf_op jit(solution)/shard_map/all_to_all | solution.py:772
  179.3 11.5 %all_to_all.50 = bf16[8,136,256]{2,1,0:T(8,128)(2,1)} all-to-all(bf16[8,136,256]{2,1,0:T(8,128)(2,1)S(1)} %sum.1), channel_id=1, replica_groups=mesh['dp'=8,'context'=8,'tensor'=2] {'context'}, dimensions={0} | all-to-all | bytes 1114112 | tf_op jit(solution)/shard_map/all_to_all | solution.py:772
  190.8 4.2 %unpack_first.1 = (f32[2,512,1024]{2,1,0:T(8,128)}, f32[2,1024,512]{2,1,0:T(8,128)}) custom-call(bf16[8,512,256]{2,1,0:T(8,128)(2,1)} %bitcast.39), custom_call_target="tpu_custom_call" | custom-call | tf_op jit(solution)/shard_map/unpack_first/pallas_call | solution.py:733
  195.0 28.7 %all-gather.8.cloned.1.call-done = bf16[64,136,256]{2,1,0:T(8,128)(2,1)} async-done(((bf16[8,136,256]{2,1,0:T(8,128)(2,1)}), bf16[64,136,256]{2,1,0:T(8,128)(2,1)}) %all-gather.8.cloned.1.call-update) | async-done | bytes 4456464 | tf_op jit(solution)/shard_map/all_gather | solution.py:907
  223.7 6.0 %unpack_rest.1 = (f32[2,512,1024]{2,1,0:T(8,128)}, f32[2,1024,512]{2,1,0:T(8,128)}, f32[2,3,512,256]{3,2,1,0:T(8,128)}, f32[2,256,512]{2,1,0:T(8,128)}, f32[2,10...) custom-call(bf16[8,8,136,256]{3,2,1,0:T(8,128)(2,1)} %bitcast.38, ...), custom_call_target="tpu_custom_call", output_to_operand_aliasing={{0}: (1, {}), {1}: (2, {})} | custom-call | tf_op jit(solution)/shard_map/unpack_rest/pallas_call | solution.py:751
  (41 shorter events, 9.1 us)
Async XLA Ops:
  7.2 6.2 %copy-start.6 = (f32[8,1]{1,0:T(8,128)S(1)}, f32[8,1]{1,0:T(8,128)}, u32[]{:S(2)}) copy-start(f32[8,1]{1,0:T(8,128)} %constant.18.refs_2_) | copy-start | bytes 100
  7.2 6.2 %copy-start.2 = (f32[2,2,512]{2,1,0:T(2,128)S(1)}, f32[2,2,512]{2,1,0:T(2,128)}, u32[]{:S(2)}) copy-start(f32[2,2,512]{2,1,0:T(2,128)} %refs_10_.5) | copy-start | bytes 24580
  7.2 6.2 %copy-start.1 = (f32[2,2,512]{2,1,0:T(2,128)S(1)}, f32[2,2,512]{2,1,0:T(2,128)}, u32[]{:S(2)}) copy-start(f32[2,2,512]{2,1,0:T(2,128)} %refs_9_.5) | copy-start | bytes 24580
  7.2 6.2 %copy-start.3 = (f32[2,1024]{1,0:T(2,128)S(1)}, f32[2,1024]{1,0:T(2,128)}, u32[]{:S(2)}) copy-start(f32[2,1024]{1,0:T(2,128)} %refs_12_.1) | copy-start | bytes 24580
  7.2 6.2 %copy-start.5 = (f32[2,3,256]{2,0,1:T(2,128)S(1)}, f32[2,3,256]{2,0,1:T(2,128)}, u32[]{:S(2)}) copy-start(f32[2,3,256]{2,0,1:T(2,128)} %param.17) | copy-start | bytes 18436
  7.2 6.2 %copy-start.7 = (s32[2,128]{1,0:T(2,128)S(1)}, s32[2,128]{1,0:T(2,128)}, u32[]{:S(2)}) copy-start(s32[2,128]{1,0:T(2,128)} %refs_1_.1) | copy-start | bytes 3076
  7.2 84.6 %all-gather.6.cloned.1.call-start = ((), (), s32[]{:S(2)}) async-start(), calls=%async_computation.11 | async-start | bytes 2359296 | tf_op jit(solution)/shard_map/all_gather | solution.py:813
  8.9 10.5 %collective-permute-start.2 = (bf16[2,4,64,256]{3,2,1,0:T(8,128)(2,1)S(1)}, bf16[2,4,64,256]{3,2,1,0:T(8,128)(2,1)S(1)}, u32[]{:S(2)}, u32[]{:S(2)}) collective-permute-start(bf16[2,4,64,256]{3,2,1,0:T(8,128)(2,1)S(1)} %chunk.1), channel_id=1, source_target_pairs={{0,1},{1,0},{2,3},{3,2},{4,5},{5,4},{6,7},{7,6},{8,9},{9,8},{10,11... | collective-permute-start | bytes 786440 | tf_op jit(solution)/shard_map/ppermute | solution.py:768
  18.7 28.7 %copy-start.4 = (f32[2,2,512]{2,1,0:T(2,128)S(1)}, f32[2,2,512]{2,1,0:T(2,128)}, u32[]{:S(2)}) copy-start(f32[2,2,512]{2,1,0:T(2,128)} %refs_8_.5) | copy-start | bytes 24580
  20.2 11.1 %all-to-all-start = ((bf16[8,208,128]{2,1,0:T(8,128)(2,1)}), bf16[8,208,128]{2,1,0:T(8,128)(2,1)S(1)}, u32[]{:S(2)}, u32[]{:S(2)}) async-start(bf16[8,208,128]{2,1,0:T(8,128)(2,1)} %get-tuple-element.52.refs_1_), calls=%async_computation | async-start | bytes 851968 | tf_op jit(solution)/shard_map/all_to_all | solution.py:772
  24.8 19.1 %collective-permute-start = (bf16[512,512]{1,0:T(8,128)(2,1)S(1)}, bf16[512,512]{1,0:T(8,128)(2,1)S(1)}, u32[]{:S(2)}, u32[]{:S(2)}) collective-permute-start(bf16[512,512]{1,0:T(8,128)(2,1)S(1)} %get-tuple-element.51.refs_2_), channel_id=1, source_target_pairs={{0,1},{1,0},{2,3},{3,2},{4,5},{5,4},{6,7},{7,6},{8,9},{9,8},{10,11... | collective-permute-start | bytes 1572872 | tf_op jit(solution)/shard_map/ppermute | solution.py:768
  33.9 13.5 %all-to-all-start.1 = ((bf16[16,64,128]{2,1,0:T(8,128)(2,1)}), bf16[16,64,128]{2,1,0:T(8,128)(2,1)S(1)}, u32[]{:S(2)}, u32[]{:S(2)}) async-start(bf16[16,64,128]{2,1,0:T(8,128)(2,1)} %bitcast.6), calls=%async_computation.1 | async-start | bytes 524288 | tf_op jit(solution)/shard_map/all_to_all | solution.py:772
  39.8 52.1 %reduce-scatter.3.cloned.1.call-start = ((), (), s32[]{:S(2)}) async-start(), calls=%async_computation.12 | async-start | bytes 2359296 | tf_op jit(solution)/shard_map/reduce_scatter | solution.py:840
  55.4 109.8 %reduce-scatter.5.cloned.1.call-start = ((), (), s32[]{:S(2)}) async-start(), calls=%async_computation.13 | async-start | bytes 3833856 | tf_op jit(solution)/shard_map/reduce_scatter | solution.py:872
  55.5 12.7 %collective-permute-start.1 = (bf16[512,512]{1,0:T(8,128)(2,1)S(1)}, bf16[512,512]{1,0:T(8,128)(2,1)S(1)}, u32[]{:S(2)}, u32[]{:S(2)}) collective-permute-start(bf16[512,512]{1,0:T(8,128)(2,1)S(1)} %get-tuple-element.56.refs_2_), channel_id=1, source_target_pairs={{0,1},{1,0},{2,3},{3,2},{4,5},{5,4},{6,7},{7,6},{8,9},{9,8},{10,11... | collective-permute-start | bytes 1572872 | tf_op jit(solution)/shard_map/ppermute | solution.py:768
  102.4 11.6 %copy-start = (f32[64,1024]{1,0:T(8,128)S(1)}, f32[64,1024]{1,0:T(8,128)}, u32[]{:S(2)}) copy-start(f32[64,1024]{1,0:T(8,128)} %get-tuple-element.67.refs_4_) | copy-start | bytes 786436
  102.4 11.5 %all-to-all-start.4 = ((bf16[8,192,128]{2,1,0:T(8,128)(2,1)}), bf16[8,192,128]{2,1,0:T(8,128)(2,1)S(1)}, u32[]{:S(2)}, u32[]{:S(2)}) async-start(bf16[8,192,128]{2,1,0:T(8,128)(2,1)} %get-tuple-element.65), calls=%async_computation.5 | async-start | bytes 786432 | tf_op jit(solution)/shard_map/all_to_all | solution.py:772
  106.0 84.8 %all-gather.10.cloned.1.call-start = ((), (), s32[]{:S(2)}) async-start(), calls=%async_computation.15 | async-start | bytes 2359296 | tf_op jit(solution)/shard_map/all_gather | solution.py:905
  106.1 7.9 %collective-permute-start.3 = (bf16[256,512]{1,0:T(8,128)(2,1)S(1)}, bf16[256,512]{1,0:T(8,128)(2,1)S(1)}, u32[]{:S(2)}, u32[]{:S(2)}) collective-permute-start(bf16[256,512]{1,0:T(8,128)(2,1)S(1)} %get-tuple-element.64.refs_3_), channel_id=1, source_target_pairs={{0,1},{1,0},{2,3},{3,2},{4,5},{5,4},{6,7},{7,6},{8,9},{9,8},{10,11... | collective-permute-start | bytes 786440 | tf_op jit(solution)/shard_map/ppermute | solution.py:768
  167.0 56.6 %all-gather.8.cloned.1.call-start = ((), (), s32[]{:S(2)}) async-start(), calls=%async_computation.14 | async-start | bytes 5013504 | tf_op jit(solution)/shard_map/all_gather | solution.py:907
Sparse Core Ops, SparseCore 0:
  20.3 27.8 all-gather.5
  55.5 32.7 reduce-scatter.2
  102.6 36.9 reduce-scatter.4
  167.2 21.4 all-gather.9
  190.9 32.7 all-gather.7

commit v13 on v10

--- a/solution.py
+++ b/solution.py
@@ -54,6 +54,45 @@
 Kept = type(pltpu.HBM((8, 128), F32))
 
 
+class Near:
+    def __init__(self, array):
+        self.array = pltpu.with_memory_space_constraint(array, pltpu.VMEM)
+
+    def spec(self):
+        return whole(self.array.shape)
+
+
+def bring(items, after, name):
+    pairs = [i if isinstance(i, tuple) else (i, None) for i in items]
+    shapes = [a.shape if layer is None else a.shape[1:] for a, layer in pairs]
+    count = len(pairs)
+
+    def body(*refs):
+        sems = refs[-1]
+        copies = []
+        for k, (_, layer) in enumerate(pairs):
+            source = refs[k] if layer is None else refs[k].at[layer]
+            copies.append(pltpu.make_async_copy(source, refs[count + 1 + k], sems.at[k]))
+        for copy in copies:
+            copy.start()
+        for copy in copies:
+            copy.wait()
+
+    size = sum(int(np.prod(shape)) * a.dtype.itemsize for (a, _), shape in zip(pairs, shapes))
+    outs = pl.pallas_call(
+        body,
+        out_shape=[pltpu.VMEM(shape, a.dtype) for (a, _), shape in zip(pairs, shapes)],
+        in_specs=[pl.BlockSpec(memory_space=pltpu.HBM)] * count
+        + [pl.BlockSpec(memory_space=pl.ANY)],
+        out_specs=[pl.BlockSpec(memory_space=pltpu.VMEM)] * count,
+        scratch_shapes=[pltpu.SemaphoreType.DMA((count,))],
+        compiler_params=pltpu.CompilerParams(vmem_limit_bytes=16 * 1024 * 1024),
+        cost_estimate=pl.CostEstimate(flops=0, bytes_accessed=2 * size, transcendentals=0),
+        name=name,
+    )(*[far(a) for a, _ in pairs], after)
+    return [Near(o) for o in outs]
+
+
 def far(array):
     return pltpu.with_memory_space_constraint(array, pltpu.HBM)
 
@@ -64,9 +103,9 @@
 
 def call(body, out_shape, args, name, scratch=(), smem_first=False):
     specs = [
-        a.spec() if isinstance(a, (Layer, Far, After)) else whole(a.shape) for a in args
+        a.spec() if isinstance(a, (Layer, Far, Near, After)) else whole(a.shape) for a in args
     ]
-    args = [a.array if isinstance(a, (Layer, Far, After)) else a for a in args]
+    args = [a.array if isinstance(a, (Layer, Far, Near, After)) else a for a in args]
     if smem_first:
         specs[0] = pl.BlockSpec(memory_space=pltpu.SMEM)
     return pl.pallas_call(
@@ -715,6 +754,9 @@
         "attend",
     )
     recv_ctx = both(ctx_send)
+    x_n, w_out0_n, wq1_n, w_up1_n, w_down1_n, w_out1_n, cot_n = bring(
+        [x, (w_out, 0), (wq, 1), (w_up, 1), (w_down, 1), (w_out, 1), cot], ctx_send, "bring_middle"
+    )
     stream, send, grads_a, parts, d_b_up1, d_sum1 = call(
         middle_body,
         [
@@ -726,8 +768,8 @@
             ((1, width), F32),
         ],
         (
-            at, Far(x), pair, pair_other, recv_ctx, Layer(w_out, 0), out_bias, ln_gain, ln_bias,
-            Layer(wq, 1), bq, Layer(w_up, 1), b_up, Layer(w_down, 1), Layer(w_out, 1), Far(cot), cs,
+            at, x_n, pair, pair_other, recv_ctx, w_out0_n, out_bias, ln_gain, ln_bias,
+            wq1_n, bq, w_up1_n, b_up, w_down1_n, w_out1_n, cot_n, cs,
         ),
         "middle",
         scratch=[pltpu.VMEM((rows, 1024), BF), pltpu.VMEM((rows, 1024), BF)],
@@ -744,6 +786,14 @@
         scratch=[pltpu.VMEM((HEAD, 1024), F32), pltpu.VMEM((HEAD, 1024), F32)],
     )
     recv_grad = both(both_send)
+    near = bring(
+        [
+            (w_out, 1), (wq, 1), (others, 1), cot, x, act, slope, (w_up, 0), (w_down, 0), (w_out, 0),
+            stream,
+        ],
+        both_send,
+        "bring_turn_point",
+    )
     block_out, g, send, grads_b, part_g, d_b_up0, d_b_qkv1, d_norm1, d_sum0 = call(
         turn_point_body,
         [
@@ -758,9 +808,9 @@
             ((1, width), F32),
         ],
         (
-            at, Far(stream), parts, parts_other, recv_grad, Layer(w_out, 1), Layer(wq, 1),
-            Layer(others, 1), out_bias, ln_gain, ln_bias, Far(cot), cs, Far(x), Far(act), Far(slope),
-            Layer(w_up, 0), Layer(w_down, 0), Layer(w_out, 0), recv_ctx, Far(sums_a),
+            at, near[10], parts, parts_other, recv_grad, near[0], near[1], near[2], out_bias, ln_gain,
+            ln_bias, near[3], cs, near[4], near[5], near[6], near[7], near[8], near[9], recv_ctx,
+            Far(sums_a),
         ),
         "turn_point",
         smem_first=True,
@@ -776,6 +826,7 @@
         scratch=[pltpu.VMEM((HEAD, 1024), F32), pltpu.VMEM((HEAD, 1024), F32)],
     )
     recv_grad0 = both(back_send)
+    x_n, g_n, wq0_n, others0_n = bring([x, g, (wq, 0), (others, 0)], back_send, "bring_last")
     in_grad, grads_c, sums_a, _, _ = call(
         last_body,
         [
@@ -786,7 +837,7 @@
             ((4, width), F32),
         ],
         (
-            at, Far(x), Far(g), part_g, part_g_other, recv_grad0, Layer(wq, 0), Layer(others, 0), cs,
+            at, x_n, g_n, part_g, part_g_other, recv_grad0, wq0_n, others0_n, cs,
             ln_gain, ln_bias, d_b_up0, d_b_up1, d_b_qkv1, d_norm1, d_sum0, d_sum1,
         ),
         "last",

time: 234 us -> 263 us (1.12)
  blocking collectives: 100 us -> 57.7 us
  local copies, waits for them, and re-layouts: 0.04 us -> 36.1 us
  starting transfers between devices: 23.7 us -> 44.8 us
  waiting for transfers between devices: 48 us -> 56.7 us
  Pallas kernels: 46.7 us -> 51.8 us
    all_to_all x6 -> x4, blocking collectives: 100 us -> 57.7 us  [exchange(): return lax.all_to_all(value, axes, 0, 0)]
    unnamed x16 -> x102, local copies, waits for them, and re-layouts: 0.04 us -> 36.1 us
    all_to_all x3 -> x5, starting transfers between devices: 14.1 us -> 34.8 us  [exchange(): return lax.all_to_all(value, axes, 0, 0)]
    all_to_all x3 -> x5, waiting for transfers between devices: 6.77 us -> 18 us  [exchange(): return lax.all_to_all(value, axes, 0, 0)]
    pallas_call x0 -> x3, Pallas kernels: none -> 7.45 us  [bring(): pl.pallas_call(body, out_shape=[pltpu.VMEM(shape, a.dtype) for (a, _), sh...]
    ppermute x4, waiting for transfers between devices: 12.4 us -> 9.17 us  [swap(): return lax.ppermute(value, 'tensor', [(0, 1), (1, 0)])]
  transfers between devices with their start and end apart: 12 -> 14, of which waited for: 6 -> 7; matrix products, arithmetic and copies ran while one was open for 0% -> 0% of each run, Pallas kernels for 12% -> 14%
where the time goes in v13:
time: 263 us; the launch traced here: 261 us
  blocking collectives  57.7 us (22%)
  waiting for transfers between devices  56.7 us (22%)
  Pallas kernels  51.8 us (20%)
  starting transfers between devices  44.8 us (17%)
  local copies, waits for them, and re-layouts  36.1 us (14%)
  between operations  14.1 us (5%)
    all_to_all x4, blocking collectives, exchange(): return lax.all_to_all(value, axes, 0, 0)  57.7 us
    unnamed x102, local copies, waits for them, and re-layouts  36.1 us
    all_to_all x5, starting transfers between devices, exchange(): return lax.all_to_all(value, axes, 0, 0)  34.8 us
    pallas_call x10, Pallas kernels, call(): pl.pallas_call(body, grid=(1,), out_shape=[o if isinstance(o, Kept) else...  32.6 us
    all_gather x1, waiting for transfers between devices, shards(): full_bc = lax.all_gather(exchange(summed, 'context'), 'dp')  29.4 us
    all_to_all x5, waiting for transfers between devices, exchange(): return lax.all_to_all(value, axes, 0, 0)  18 us
    ppermute x4, starting transfers between devices, swap(): return lax.ppermute(value, 'tensor', [(0, 1), (1, 0)])  9.53 us
    ppermute x4, waiting for transfers between devices, swap(): return lax.ppermute(value, 'tensor', [(0, 1), (1, 0)])  9.17 us
  transfers between devices with their start and end apart: 14, of which 7 were waited for; matrix products, arithmetic and copies ran while one was open for 0% of the time, Pallas kernels for 14%

profile of v13, /device:TPU:1, one launch (start us, length us, event | category | flops | bytes accessed | tf_op | source)
XLA Modules:
  0.0 261.2 jit_solution(8156312806560645242)
XLA Ops:
  8.9 4.5 %collective-permute-start = (bf16[2,4,64,256]{3,2,1,0:T(8,128)(2,1)S(1)}, bf16[2,4,64,256]{3,2,1,0:T(8,128)(2,1)S(1)}, u32[]{:S(2)}, u32[]{:S(2)}) collective-permute-start(bf16[2,4,64,256]{3,2,1,0:T(8,128)(2,1)S(1)} %chunk.1), channel_id=1, source_target_pairs={{0,1},{1,0},{2,3},{3,2},{4,5},{5,4},{6,7},{7,6},{8,9},{9,8},{10,11... | collective-permute-start | bytes 786440 | tf_op jit(solution)/shard_map/ppermute | solution.py:703
  13.4 4.4 %norm_qkv_feed.1 = (bf16[8,208,128]{2,1,0:T(8,128)(2,1)}, bf16[512,512]{1,0:T(8,128)(2,1)S(1)}, bf16[256,1024]{1,0:T(8,128)(2,1)}, bf16[256,1024]{1,0:T(8,128)(2,1)}, f32[2,2,8,128]{3,2,1,0:T(8,128)S(1)}) custom-call(s32[3]{0:T(128)S(1)} %pad_add_fusion.at, s32[2,128]{1,0:T(2,128)S(1)} %copy-done.50, f32[8,1]{1,0:T(8,128)S(1)} %copy-done.49, ...), custom_call_target="tpu_custom_call" | custom-call | tf_op jit(solution)/shard_map/norm_qkv_feed/pallas_call | solution.py:111
  20.1 4.6 %all-to-all-start = ((bf16[8,208,128]{2,1,0:T(8,128)(2,1)}), bf16[8,208,128]{2,1,0:T(8,128)(2,1)S(1)}, u32[]{:S(2)}, u32[]{:S(2)}) async-start(bf16[8,208,128]{2,1,0:T(8,128)(2,1)} %get-tuple-element.73._), calls=%async_computation | async-start | bytes 851968 | tf_op jit(solution)/shard_map/all_to_all | solution.py:707
  24.8 3.3 %collective-permute-start.1 = (bf16[512,512]{1,0:T(8,128)(2,1)S(1)}, bf16[512,512]{1,0:T(8,128)(2,1)}, u32[]{:S(2)}, u32[]{:S(2)}) collective-permute-start(bf16[512,512]{1,0:T(8,128)(2,1)S(1)} %get-tuple-element.78.pair), channel_id=1, source_target_pairs={{0,1},{1,0},{2,3},{3,2},{4,5},{5,4},{6,7},{7,6},{8,9},{9,8},{10,11... | collective-permute-start | bytes 1572872 | tf_op jit(solution)/shard_map/ppermute | solution.py:703
  28.1 3.2 %all-to-all-done.recv = bf16[8,208,128]{2,1,0:T(8,128)(2,1)S(1)} async-done(((bf16[8,208,128]{2,1,0:T(8,128)(2,1)}), bf16[8,208,128]{2,1,0:T(8,128)(2,1)S(1)}, u32[]{:S(2)}, u32[]{:S(2)}) %all-to-all-start) | async-done | bytes 426016 | tf_op jit(solution)/shard_map/all_to_all | solution.py:707
  31.2 2.7 %attend.1 = (bf16[8,2,64,128]{3,2,1,0:T(8,128)(2,1)}, f32[1,1024]{1,0:T(1,128)S(1)}, f32[64,1024]{1,0:T(8,128)}, s32[1,1024]{1,0:T(1,128)S(1)}) custom-call(bf16[8,208,128]{2,1,0:T(8,128)(2,1)S(1)} %all-to-all-done.recv), custom_call_target="tpu_custom_call" | custom-call | tf_op jit(solution)/shard_map/attend/pallas_call | solution.py:111
  33.9 5.9 %all-to-all-start.1 = ((bf16[16,64,128]{2,1,0:T(8,128)(2,1)}), bf16[16,64,128]{2,1,0:T(8,128)(2,1)S(1)}, u32[]{:S(2)}, u32[]{:S(2)}) async-start(bf16[16,64,128]{2,1,0:T(8,128)(2,1)} %bitcast.7), calls=%async_computation.1 | async-start | bytes 524288 | tf_op jit(solution)/shard_map/all_to_all | solution.py:707
  53.6 5.7 %middle.1 = (f32[256,512]{1,0:T(8,128)}, bf16[8,256,128]{2,1,0:T(8,128)(2,1)S(1)}, bf16[8,512,256]{2,1,0:T(8,128)(2,1)}, bf16[512,512]{1,0:T(8,128)(2,1)S(1)}, f...) custom-call(s32[3]{0:T(128)S(1)} %pad_add_fusion.at, f32[256,512]{1,0:T(8,128)S(1)} %copy-done.27, ...), custom_call_target="tpu_custom_call" | custom-call | tf_op jit(solution)/shard_map/middle/pallas_call | solution.py:111
  61.7 11.4 %all_to_all.45.recv = bf16[8,256,128]{2,1,0:T(8,128)(2,1)S(1)} all-to-all(bf16[8,256,128]{2,1,0:T(8,128)(2,1)S(1)} %copy-done.31), channel_id=1, replica_groups=mesh['dp'=8,'context'=8,'tensor'=2] {'context'}, dimensions={0} | all-to-all | bytes 1048576 | tf_op jit(solution)/shard_map/all_to_all | solution.py:707
  73.1 5.2 %attend_both.1.refs_11_ = bf16[8,2,256,128]{3,2,1,0:T(8,128)(2,1)} custom-call(bf16[8,256,128]{2,1,0:T(8,128)(2,1)S(1)} %all_to_all.45.recv, s32[1,1024]{1,0:T(1,128)S(1)} %get-tuple-element.88.start, bf16[512,512]{1,0:T(8,128)(2,1)S(1)} %collective-permute-done.2._.parts_other), custom_call_target="tpu_custom_call" | custom-call | tf_op jit(solution)/shard_map/attend_both/pallas_call | solution.py:111
  78.3 7.7 %all-to-all-start.3 = ((bf16[16,256,128]{2,1,0:T(8,128)(2,1)}), bf16[16,256,128]{2,1,0:T(8,128)(2,1)S(1)}, u32[]{:S(2)}, u32[]{:S(2)}) async-start(bf16[16,256,128]{2,1,0:T(8,128)(2,1)} %bitcast.9), calls=%async_computation.3 | async-start | bytes 2097152 | tf_op jit(solution)/shard_map/all_to_all | solution.py:707
  86.2 3.2 %bring_turn_point.1 = (bf16[256,512]{1,0:T(8,128)(2,1)S(1)}, bf16[3,512,256]{2,1,0:T(8,128)(2,1)S(1)}, bf16[4,512,256]{2,1,0:T(8,128)(2,1)S(1)}, f32[256,512]{1,...) custom-call(bf16[2,256,512]{2,1,0:T(8,128)(2,1)} %refs_9_.1, ...), custom_call_target="tpu_custom_call" | custom-call | bytes 14155776 | tf_op jit(solution)/shard_map/bring_turn_point/pallas_call | solution.py:82
  110.0 6.2 %turn_point.1 = (f32[256,512]{1,0:T(8,128)}, f32[256,512]{1,0:T(8,128)}, bf16[8,192,128]{2,1,0:T(8,128)(2,1)}, bf16[8,832,256]{2,1,0:T(8,128)(2,1)}, bf16[256,51...) custom-call(s32[3]{0:T(128)S(1)} %pad_add_fusion.at, ...), custom_call_target="tpu_custom_call" | custom-call | tf_op jit(solution)/shard_map/turn_point/pallas_call | solution.py:111
  117.0 7.6 %all-to-all-start.4 = ((bf16[8,192,128]{2,1,0:T(8,128)(2,1)}), bf16[8,192,128]{2,1,0:T(8,128)(2,1)S(1)}, u32[]{:S(2)}, u32[]{:S(2)}) async-start(bf16[8,192,128]{2,1,0:T(8,128)(2,1)} %get-tuple-element.104), calls=%async_computation.5 | async-start | bytes 786432 | tf_op jit(solution)/shard_map/all_to_all | solution.py:707
  124.7 7.6 %collective-permute-done.3._.part_other = bf16[256,512]{1,0:T(8,128)(2,1)S(1)} collective-permute-done((bf16[256,512]{1,0:T(8,128)(2,1)S(1)}, bf16[256,512]{1,0:T(8,128)(2,1)S(1)}, u32[]{:S(2)}, u32[]{:S(2)}) %collective-permute-start.3) | collective-permute-done | bytes 262176 | tf_op jit(solution)/shard_map/ppermute | solution.py:703
  132.3 3.3 %attend_back.1.refs_4_ = bf16[8,2,320,128]{3,2,1,0:T(8,128)(2,1)} custom-call(bf16[8,208,128]{2,1,0:T(8,128)(2,1)S(1)} %all-to-all-done.recv, bf16[8,192,128]{2,1,0:T(8,128)(2,1)S(1)} %all-to-all-done.4.recv_d, s32[1,1024]{1,0:T(1,128)S(1)} %get-tuple-element.88.start, f32[1,1024]{1,0:T(1,128)S(1)} %get-tuple-element.105.lse, f32[64,1024]{1,0:T(8,128)S(1)} %copy-done.43, ...), custom_call_target="tpu_custom_call" | custom-call | tf_op jit(solution)/shard_map/attend_back/pallas_call | solution.py:111
  135.6 9.1 %all-to-all-start.5 = ((bf16[16,320,128]{2,1,0:T(8,128)(2,1)}), bf16[16,320,128]{2,1,0:T(8,128)(2,1)S(1)}, u32[]{:S(2)}, u32[]{:S(2)}) async-start(bf16[16,320,128]{2,1,0:T(8,128)(2,1)} %bitcast.13), calls=%async_computation.6 | async-start | bytes 2621440 | tf_op jit(solution)/shard_map/all_to_all | solution.py:707
  148.2 12.8 %all-to-all-done.5 = bf16[16,320,128]{2,1,0:T(8,128)(2,1)S(1)} async-done(((bf16[16,320,128]{2,1,0:T(8,128)(2,1)}), bf16[16,320,128]{2,1,0:T(8,128)(2,1)S(1)}, u32[]{:S(2)}, u32[]{:S(2)}) %all-to-all-start.5) | async-done | bytes 1310752 | tf_op jit(solution)/shard_map/all_to_all | solution.py:707
  166.7 22.3 %all_to_all.46.got = bf16[8,208,256]{2,1,0:T(8,128)(2,1)S(1)} all-to-all(bf16[8,208,256]{2,1,0:T(8,128)(2,1)S(1)} %get-tuple-element.119), channel_id=1, replica_groups=mesh['dp'=8,'context'=8,'tensor'=2] {'dp'}, dimensions={0} | all-to-all | bytes 1703936 | tf_op jit(solution)/shard_map/all_to_all | solution.py:707
  190.9 12.7 %all_to_all.47.got = bf16[8,136,256]{2,1,0:T(8,128)(2,1)S(1)} all-to-all(bf16[8,136,256]{2,1,0:T(8,128)(2,1)S(1)} %get-tuple-element.122), channel_id=1, replica_groups=mesh['dp'=8,'context'=8,'tensor'=2] {'context'}, dimensions={0} | all-to-all | bytes 1114112 | tf_op jit(solution)/shard_map/all_to_all | solution.py:707
  203.7 11.3 %all_to_all.48 = bf16[8,136,256]{2,1,0:T(8,128)(2,1)} all-to-all(bf16[8,136,256]{2,1,0:T(8,128)(2,1)S(1)} %sum.1), channel_id=1, replica_groups=mesh['dp'=8,'context'=8,'tensor'=2] {'context'}, dimensions={0} | all-to-all | bytes 1114112 | tf_op jit(solution)/shard_map/all_to_all | solution.py:707
  215.0 4.2 %unpack_first.1 = (f32[2,512,1024]{2,1,0:T(8,128)}, f32[2,1024,512]{2,1,0:T(8,128)}) custom-call(bf16[8,512,256]{2,1,0:T(8,128)(2,1)} %bitcast.39), custom_call_target="tpu_custom_call" | custom-call | tf_op jit(solution)/shard_map/unpack_first/pallas_call | solution.py:668
  219.2 29.4 %all-gather.8.cloned.1.call-done = bf16[64,136,256]{2,1,0:T(8,128)(2,1)} async-done(((bf16[8,136,256]{2,1,0:T(8,128)(2,1)}), bf16[64,136,256]{2,1,0:T(8,128)(2,1)}) %all-gather.8.cloned.1.call-update) | async-done | bytes 4456464 | tf_op jit(solution)/shard_map/all_gather | solution.py:854
  248.6 6.0 %unpack_rest.1 = (f32[2,512,1024]{2,1,0:T(8,128)}, f32[2,1024,512]{2,1,0:T(8,128)}, f32[2,3,512,256]{3,2,1,0:T(8,128)}, f32[2,256,512]{2,1,0:T(8,128)}, f32[2,10...) custom-call(bf16[8,8,136,256]{3,2,1,0:T(8,128)(2,1)} %bitcast.36, ...), custom_call_target="tpu_custom_call", output_to_operand_aliasing={{0}: (1, {}), {1}: (2, {})} | custom-call | tf_op jit(solution)/shard_map/unpack_rest/pallas_call | solution.py:686
  (132 shorter events, 53.0 us)
Async XLA Ops:
  7.2 6.2 %copy-start.49 = (f32[8,1]{1,0:T(8,128)S(1)}, f32[8,1]{1,0:T(8,128)}, u32[]{:S(2)}) copy-start(f32[8,1]{1,0:T(8,128)} %constant.18.freqs) | copy-start | bytes 100
  7.2 6.2 %copy-start.45 = (f32[2,2,512]{2,1,0:T(2,128)S(1)}, f32[2,2,512]{2,1,0:T(2,128)}, u32[]{:S(2)}) copy-start(f32[2,2,512]{2,1,0:T(2,128)} %bias.7) | copy-start | bytes 24580
  7.2 6.2 %copy-start.44 = (f32[2,2,512]{2,1,0:T(2,128)S(1)}, f32[2,2,512]{2,1,0:T(2,128)}, u32[]{:S(2)}) copy-start(f32[2,2,512]{2,1,0:T(2,128)} %gain.7) | copy-start | bytes 24580
  7.2 6.2 %copy-start.46 = (f32[2,1024]{1,0:T(2,128)S(1)}, f32[2,1024]{1,0:T(2,128)}, u32[]{:S(2)}) copy-start(f32[2,1024]{1,0:T(2,128)} %b_up.3) | copy-start | bytes 24580
  7.2 6.2 %copy-start.48 = (f32[2,3,256]{2,0,1:T(2,128)S(1)}, f32[2,3,256]{2,0,1:T(2,128)}, u32[]{:S(2)}) copy-start(f32[2,3,256]{2,0,1:T(2,128)} %param.17) | copy-start | bytes 18436
  7.2 78.9 %all-gather.6.cloned.1.call-start = ((), (), s32[]{:S(2)}) async-start(), calls=%async_computation.11 | async-start | bytes 2359296 | tf_op jit(solution)/shard_map/all_gather | solution.py:748
  8.9 10.5 %collective-permute-start = (bf16[2,4,64,256]{3,2,1,0:T(8,128)(2,1)S(1)}, bf16[2,4,64,256]{3,2,1,0:T(8,128)(2,1)S(1)}, u32[]{:S(2)}, u32[]{:S(2)}) collective-permute-start(bf16[2,4,64,256]{3,2,1,0:T(8,128)(2,1)S(1)} %chunk.1), channel_id=1, source_target_pairs={{0,1},{1,0},{2,3},{3,2},{4,5},{5,4},{6,7},{7,6},{8,9},{9,8},{10,11... | collective-permute-start | bytes 786440 | tf_op jit(solution)/shard_map/ppermute | solution.py:703
  17.8 24.4 %copy-start.10 = (bf16[512,512]{1,0:T(8,128)(2,1)}, bf16[512,512]{1,0:T(8,128)(2,1)S(1)}, u32[]{:S(2)}) copy-start(bf16[512,512]{1,0:T(8,128)(2,1)S(1)} %get-tuple-element.78.pair) | copy-start | bytes 1572868
  20.1 11.1 %all-to-all-start = ((bf16[8,208,128]{2,1,0:T(8,128)(2,1)}), bf16[8,208,128]{2,1,0:T(8,128)(2,1)S(1)}, u32[]{:S(2)}, u32[]{:S(2)}) async-start(bf16[8,208,128]{2,1,0:T(8,128)(2,1)} %get-tuple-element.73._), calls=%async_computation | async-start | bytes 851968 | tf_op jit(solution)/shard_map/all_to_all | solution.py:707
  24.8 21.3 %collective-permute-start.1 = (bf16[512,512]{1,0:T(8,128)(2,1)S(1)}, bf16[512,512]{1,0:T(8,128)(2,1)}, u32[]{:S(2)}, u32[]{:S(2)}) collective-permute-start(bf16[512,512]{1,0:T(8,128)(2,1)S(1)} %get-tuple-element.78.pair), channel_id=1, source_target_pairs={{0,1},{1,0},{2,3},{3,2},{4,5},{5,4},{6,7},{7,6},{8,9},{9,8},{10,11... | collective-permute-start | bytes 1572872 | tf_op jit(solution)/shard_map/ppermute | solution.py:703
  33.9 13.5 %all-to-all-start.1 = ((bf16[16,64,128]{2,1,0:T(8,128)(2,1)}), bf16[16,64,128]{2,1,0:T(8,128)(2,1)S(1)}, u32[]{:S(2)}, u32[]{:S(2)}) async-start(bf16[16,64,128]{2,1,0:T(8,128)(2,1)} %bitcast.7), calls=%async_computation.1 | async-start | bytes 524288 | tf_op jit(solution)/shard_map/all_to_all | solution.py:707
  39.8 58.5 %reduce-scatter.3.cloned.1.call-start = ((), (), s32[]{:S(2)}) async-start(), calls=%async_computation.12 | async-start | bytes 2359296 | tf_op jit(solution)/shard_map/reduce_scatter | solution.py:778
  39.8 7.6 %copy-start.47 = (f32[2,2,512]{2,1,0:T(2,128)S(1)}, f32[2,2,512]{2,1,0:T(2,128)}, u32[]{:S(2)}) copy-start(f32[2,2,512]{2,1,0:T(2,128)} %out_bias.3) | copy-start | bytes 24580
  60.0 18.2 %copy-start.8 = (bf16[512,512]{1,0:T(8,128)(2,1)}, bf16[512,512]{1,0:T(8,128)(2,1)S(1)}, u32[]{:S(2)}) copy-start(bf16[512,512]{1,0:T(8,128)(2,1)S(1)} %get-tuple-element.89.parts) | copy-start | bytes 1572868
  60.1 13.0 %collective-permute-start.2 = (bf16[512,512]{1,0:T(8,128)(2,1)S(1)}, bf16[512,512]{1,0:T(8,128)(2,1)S(1)}, u32[]{:S(2)}, u32[]{:S(2)}) collective-permute-start(bf16[512,512]{1,0:T(8,128)(2,1)S(1)} %get-tuple-element.89.parts), channel_id=1, source_target_pairs={{0,1},{1,0},{2,3},{3,2},{4,5},{5,4},{6,7},{7,6},{8,9},{9,8},{10,11... | collective-permute-start | bytes 1572872 | tf_op jit(solution)/shard_map/ppermute | solution.py:703
  78.3 20.0 %all-to-all-start.3 = ((bf16[16,256,128]{2,1,0:T(8,128)(2,1)}), bf16[16,256,128]{2,1,0:T(8,128)(2,1)S(1)}, u32[]{:S(2)}, u32[]{:S(2)}) async-start(bf16[16,256,128]{2,1,0:T(8,128)(2,1)} %bitcast.9), calls=%async_computation.3 | async-start | bytes 2097152 | tf_op jit(solution)/shard_map/all_to_all | solution.py:707
  85.9 103.1 %reduce-scatter.5.cloned.1.call-start = ((), (), s32[]{:S(2)}) async-start(), calls=%async_computation.13 | async-start | bytes 3833856 | tf_op jit(solution)/shard_map/reduce_scatter | solution.py:818
  117.0 7.7 %copy-start.33 = (bf16[256,512]{1,0:T(8,128)(2,1)S(1)}, bf16[256,512]{1,0:T(8,128)(2,1)}, u32[]{:S(2)}) copy-start(bf16[256,512]{1,0:T(8,128)(2,1)} %copy-done.32) | copy-start | bytes 786436
  117.0 15.3 %copy-start.43 = (f32[64,1024]{1,0:T(8,128)S(1)}, f32[64,1024]{1,0:T(8,128)}, u32[]{:S(2)}) copy-start(f32[64,1024]{1,0:T(8,128)} %get-tuple-element.106.ctx) | copy-start | bytes 786436
  117.0 15.3 %all-to-all-start.4 = ((bf16[8,192,128]{2,1,0:T(8,128)(2,1)}), bf16[8,192,128]{2,1,0:T(8,128)(2,1)S(1)}, u32[]{:S(2)}, u32[]{:S(2)}) async-start(bf16[8,192,128]{2,1,0:T(8,128)(2,1)} %get-tuple-element.104), calls=%async_computation.5 | async-start | bytes 786432 | tf_op jit(solution)/shard_map/all_to_all | solution.py:707
  124.6 7.7 %collective-permute-start.3 = (bf16[256,512]{1,0:T(8,128)(2,1)S(1)}, bf16[256,512]{1,0:T(8,128)(2,1)S(1)}, u32[]{:S(2)}, u32[]{:S(2)}) collective-permute-start(bf16[256,512]{1,0:T(8,128)(2,1)S(1)} %copy-done.33), channel_id=1, source_target_pairs={{0,1},{1,0},{2,3},{3,2},{4,5},{5,4},{6,7},{7,6},{8,9},{9,8},{10,11... | collective-permute-start | bytes 786440 | tf_op jit(solution)/shard_map/ppermute | solution.py:703
  135.6 25.5 %all-to-all-start.5 = ((bf16[16,320,128]{2,1,0:T(8,128)(2,1)}), bf16[16,320,128]{2,1,0:T(8,128)(2,1)S(1)}, u32[]{:S(2)}, u32[]{:S(2)}) async-start(bf16[16,320,128]{2,1,0:T(8,128)(2,1)} %bitcast.13), calls=%async_computation.6 | async-start | bytes 2621440 | tf_op jit(solution)/shard_map/all_to_all | solution.py:707
  144.7 70.3 %all-gather.10.cloned.1.call-start = ((), (), s32[]{:S(2)}) async-start(), calls=%async_computation.15 | async-start | bytes 2359296 | tf_op jit(solution)/shard_map/all_gather | solution.py:852
  190.9 57.8 %all-gather.8.cloned.1.call-start = ((), (), s32[]{:S(2)}) async-start(), calls=%async_computation.14 | async-start | bytes 5013504 | tf_op jit(solution)/shard_map/all_gather | solution.py:854
  (41 other events, 44.0 us)
Sparse Core Ops, SparseCore 0:
  20.3 27.8 all-gather.5
  60.2 34.1 reduce-scatter.2
  117.1 39.2 reduce-scatter.4
  191.0 22.5 all-gather.9
  215.1 33.4 all-gather.7

commit v14 on v10

--- a/solution.py
+++ b/solution.py
@@ -187,11 +187,7 @@
             ].astype(BF)
 
 
-def first_body(
-    at, pos, freqs, x, gain, bias, w_qkv, b_qkv, w_up, b_up, w_down, w_out,
-    send, pair, act, slope, cs,
-):
-    pair[256:512] = w_out[...]
+def first_body(at, pos, freqs, x, gain, bias, w_qkv, b_qkv, send, cs):
     for s in range(2):
         p = pos[s : s + 1, :].astype(F32)
         angle = freqs[...] * p
@@ -199,7 +195,6 @@
         cs[s, 1] = jnp.sin(angle)
     normed, _ = norm_rows(x[...])
     attn_in = (normed * gain[0, 0:1] + bias[0, 0:1]).astype(BF)
-    mlp_in = (normed * gain[0, 1:2] + bias[0, 1:2]).astype(BF)
     send_qkv(send, attn_in, w_qkv, b_qkv, 0, cs)
     row = lax.broadcasted_iota(jnp.int32, (16, BLK), 0)
     token = at[0] * BLK + lax.broadcasted_iota(jnp.int32, (1, BLK), 1)
@@ -210,6 +205,12 @@
         block = jnp.where(row == 0, high, jnp.where(row == 1, low, 0.0)).astype(BF)
         for h in range(4):
             send[s * 4 + h, 3 * HEAD : 3 * HEAD + 16, :] = block
+
+
+def feed_body(x, gain, bias, w_up, b_up, w_down, w_out, _, pair, act, slope):
+    normed, _ = norm_rows(x[...])
+    mlp_in = (normed * gain[0, 1:2] + bias[0, 1:2]).astype(BF)
+    pair[256:512] = w_out[...]
     pair[0:256] = feed_forward(mlp_in, w_up, b_up, 0, w_down, act, slope).astype(BF)
 
 
@@ -222,10 +223,16 @@
     return rows[0:1] * 8.0 + rows[1:2]
 
 
-def visible_of(start, c, length):
-    key = lax.broadcasted_iota(jnp.int32, (length, CHUNK), 0)
-    query = lax.broadcasted_iota(jnp.int32, (length, CHUNK), 1) + c * CHUNK
-    return (key <= query) & (key >= start[:, c * CHUNK : (c + 1) * CHUNK])
+def masked(scores, start, c, length):
+    own = start[:, c * CHUNK : (c + 1) * CHUNK]
+    past = length - CHUNK
+    key = lax.broadcasted_iota(jnp.int32, (CHUNK, CHUNK), 0)
+    query = lax.broadcasted_iota(jnp.int32, (CHUNK, CHUNK), 1)
+    near = jnp.where((key <= query) & (key + past >= own), scores[past:], NEG)
+    if past == 0:
+        return near
+    key = lax.broadcasted_iota(jnp.int32, (past, CHUNK), 0)
+    return jnp.concatenate([jnp.where(key >= own, scores[:past], NEG), near], 0)
 
 
 def attend_body(recv, send, lse, ctx, start_out):
@@ -239,7 +246,7 @@
         cols = slice(c * CHUNK, (c + 1) * CHUNK)
         length = (c + 1) * CHUNK
         scores = mm(k[:length], q[:, cols])
-        scores = jnp.where(visible_of(start, c, length), scores, NEG)
+        scores = masked(scores, start, c, length)
         peak = jnp.max(scores, 0, keepdims=True)
         shifted = jnp.exp(scores - peak)
         total = jnp.sum(shifted, 0, keepdims=True)
@@ -265,7 +272,7 @@
         cols = slice(c * CHUNK, (c + 1) * CHUNK)
         length = (c + 1) * CHUNK
         scores = mm(k[:length], q[:, cols])
-        scores = jnp.where(visible_of(start[...], c, length), scores, NEG)
+        scores = masked(scores, start[...], c, length)
         peak = jnp.max(scores, 0, keepdims=True)
         shifted = jnp.exp(scores - peak)
         probs = shifted * (1.0 / jnp.sum(shifted, 0, keepdims=True))
@@ -317,7 +324,7 @@
         cols = slice(c * CHUNK, (c + 1) * CHUNK)
         length = (c + 1) * CHUNK
         scores = mm(k[:length], q[:, cols])
-        scores = jnp.where(visible_of(start[...], c, length), scores, NEG)
+        scores = masked(scores, start[...], c, length)
         probs = jnp.exp(scores - lse[:, cols])
         probs_b = probs.astype(BF)
         dq = backward_chunk(q, k_t, v, d_ctx, probs, probs_b, ctx[:, cols], cols, length, dk, dv)
@@ -686,25 +693,29 @@
     ).astype(jnp.int32)
     freqs = jnp.asarray(FREQS).reshape(HALF, 1)
     chunk = swap(chunk_of(at, wq, w_out))
-    send, pair, act, slope, cs = call(
+    send, cs = call(
         first_body,
+        [pltpu.VMEM((8, 208, BLK), BF), ((2, 2, HALF, BLK), F32)],
+        (at, positions, freqs, Far(x), ln_gain, ln_bias, Layer(wq, 0), bq),
+        "norm_qkv",
+        smem_first=True,
+    )
+    pair, act, slope = call(
+        feed_body,
         [
-            pltpu.VMEM((8, 208, BLK), BF),
             ((2 * rows, width), BF),
             pltpu.HBM((rows, 1024), BF),
             pltpu.HBM((rows, 1024), BF),
-            ((2, 2, HALF, BLK), F32),
         ],
         (
-            at, positions, freqs, Far(x), ln_gain, ln_bias, Layer(wq, 0), bq, Layer(w_up, 0), b_up,
-            Layer(w_down, 0), Layer(w_out, 0),
+            Far(x), ln_gain, ln_bias, Layer(w_up, 0), b_up, Layer(w_down, 0), Layer(w_out, 0),
+            After(send),
         ),
-        "norm_qkv_feed",
-        smem_first=True,
+        "feed",
     )
     pair_other = swap(pair)
     (chunk,) = call(
-        hand_on_body, [pltpu.HBM(chunk.shape, BF)], (chunk, After(send)), "hand_on"
+        hand_on_body, [pltpu.HBM(chunk.shape, BF)], (chunk, After(act)), "hand_on"
     )
     others = lax.all_gather(chunk, "dp", axis=2, tiled=True)
     recv = exchange(send, "context")

time: 234 us -> 235 us (level)
  Pallas kernels: 46.7 us -> 49.2 us
  starting transfers between devices: 23.7 us -> 21.2 us
    pallas_call x10 -> x11, Pallas kernels: 35 us -> 37.5 us  [call(): pl.pallas_call(body, grid=(1,), out_shape=[o if isinstance(o, Kept) else...]
  transfers between devices with their start and end apart: 12 -> 12, of which waited for: 6 -> 5; matrix products, arithmetic and copies ran while one was open for 0% -> 0% of each run, Pallas kernels for 12% -> 13%
where the time goes in v14:
time: 235 us; the launch traced here: 234 us
  blocking collectives  100 us (43%)
  Pallas kernels  49.2 us (21%)
  waiting for transfers between devices  48.1 us (20%)
  starting transfers between devices  21.2 us (9%)
  between operations  13.9 us (6%)
    all_to_all x6, blocking collectives, exchange(): return lax.all_to_all(value, axes, 0, 0)  100 us
    pallas_call x11, Pallas kernels, call(): pl.pallas_call(body, grid=(1,), out_shape=[o if isinstance(o, Kept) else...  37.5 us
    all_gather x1, waiting for transfers between devices, shards(): full_bc = lax.all_gather(exchange(summed, 'context'), 'dp')  28.7 us
    all_to_all x3, starting transfers between devices, exchange(): return lax.all_to_all(value, axes, 0, 0)  12.5 us
    ppermute x4, waiting for transfers between devices, swap(): return lax.ppermute(value, 'tensor', [(0, 1), (1, 0)])  10.8 us
    ppermute x4, starting transfers between devices, swap(): return lax.ppermute(value, 'tensor', [(0, 1), (1, 0)])  8.51 us
    all_to_all x3, waiting for transfers between devices, exchange(): return lax.all_to_all(value, axes, 0, 0)  8.5 us
    pallas_call x1, Pallas kernels, unpack(): pl.pallas_call(unpack_rest_body, grid=(4,), out_shape=[pltpu.HBM(shape, F...  6.04 us
  transfers between devices with their start and end apart: 12, of which 5 were waited for; matrix products, arithmetic and copies ran while one was open for 0% of the time, Pallas kernels for 13%

profile of v14, /device:TPU:1, one launch (start us, length us, event | category | flops | bytes accessed | tf_op | source)
XLA Modules:
  0.0 233.7 jit_solution(15329958600193186555)
XLA Ops:
  8.9 4.5 %collective-permute-start.2 = (bf16[2,4,64,256]{3,2,1,0:T(8,128)(2,1)S(1)}, bf16[2,4,64,256]{3,2,1,0:T(8,128)(2,1)S(1)}, u32[]{:S(2)}, u32[]{:S(2)}) collective-permute-start(bf16[2,4,64,256]{3,2,1,0:T(8,128)(2,1)S(1)} %chunk.1), channel_id=1, source_target_pairs={{0,1},{1,0},{2,3},{3,2},{4,5},{5,4},{6,7},{7,6},{8,9},{9,8},{10,11... | collective-permute-start | bytes 786440 | tf_op jit(solution)/shard_map/ppermute | solution.py:671
  13.4 2.7 %norm_qkv.1 = (bf16[8,208,128]{2,1,0:T(8,128)(2,1)}, f32[2,2,8,128]{3,2,1,0:T(8,128)S(1)}) custom-call(s32[3]{0:T(128)S(1)} %pad_add_fusion.at, s32[2,128]{1,0:T(2,128)S(1)} %copy-done.8, f32[8,1]{1,0:T(8,128)S(1)} %copy-done.7, f32[256,512]{1,0:T(8,128)} %bitcast.34, f32[2,2,512]{2,1,0:T(2,128)S(1)} %copy-done.2, f32[2,2,512]{2,1,0:T(2,128)S(1)} %copy-done.3, ...), custom_call_target="tpu_custom_call" | custom-call | tf_op jit(solution)/shard_map/norm_qkv/pallas_call | solution.py:72
  16.1 4.1 %feed.1 = (bf16[512,512]{1,0:T(8,128)(2,1)S(1)}, bf16[256,1024]{1,0:T(8,128)(2,1)}, bf16[256,1024]{1,0:T(8,128)(2,1)}) custom-call(f32[256,512]{1,0:T(8,128)} %bitcast.35, f32[2,2,512]{2,1,0:T(2,128)S(1)} %copy-done.2, f32[2,2,512]{2,1,0:T(2,128)S(1)} %copy-done.3, bf16[2,512,1024]{2,1,0:T(8,128)(2,1)} %w_up.5, f32[2,1024]{1,0:T(2,128)S(1)} %copy-done.4, ...), custom_call_target="tpu_custom_call" | custom-call | tf_op jit(solution)/shard_map/feed/pallas_call | solution.py:72
  22.1 4.7 %all-to-all-start = ((bf16[8,208,128]{2,1,0:T(8,128)(2,1)}), bf16[8,208,128]{2,1,0:T(8,128)(2,1)S(1)}, u32[]{:S(2)}, u32[]{:S(2)}) async-start(bf16[8,208,128]{2,1,0:T(8,128)(2,1)} %get-tuple-element.51._), calls=%async_computation | async-start | bytes 851968 | tf_op jit(solution)/shard_map/all_to_all | solution.py:675
  29.1 4.8 %all-to-all-done.recv = bf16[8,208,128]{2,1,0:T(8,128)(2,1)S(1)} async-done(((bf16[8,208,128]{2,1,0:T(8,128)(2,1)}), bf16[8,208,128]{2,1,0:T(8,128)(2,1)S(1)}, u32[]{:S(2)}, u32[]{:S(2)}) %all-to-all-start) | async-done | bytes 426016 | tf_op jit(solution)/shard_map/all_to_all | solution.py:675
  33.9 2.7 %attend.1 = (bf16[8,2,64,128]{3,2,1,0:T(8,128)(2,1)}, f32[1,1024]{1,0:T(1,128)S(1)}, f32[64,1024]{1,0:T(8,128)}, s32[1,1024]{1,0:T(1,128)S(1)}) custom-call(bf16[8,208,128]{2,1,0:T(8,128)(2,1)S(1)} %all-to-all-done.recv), custom_call_target="tpu_custom_call" | custom-call | tf_op jit(solution)/shard_map/attend/pallas_call | solution.py:72
  36.6 4.2 %all-to-all-start.1 = ((bf16[16,64,128]{2,1,0:T(8,128)(2,1)}), bf16[16,64,128]{2,1,0:T(8,128)(2,1)S(1)}, u32[]{:S(2)}, u32[]{:S(2)}) async-start(bf16[16,64,128]{2,1,0:T(8,128)(2,1)} %bitcast.6), calls=%async_computation.1 | async-start | bytes 524288 | tf_op jit(solution)/shard_map/all_to_all | solution.py:675
  40.9 4.0 %collective-permute-done.pair_other = bf16[512,512]{1,0:T(8,128)(2,1)S(1)} collective-permute-done((bf16[512,512]{1,0:T(8,128)(2,1)S(1)}, bf16[512,512]{1,0:T(8,128)(2,1)S(1)}, u32[]{:S(2)}, u32[]{:S(2)}) %collective-permute-start) | collective-permute-done | bytes 524320 | tf_op jit(solution)/shard_map/ppermute | solution.py:671
  44.8 3.7 %all-to-all-done.1 = bf16[16,64,128]{2,1,0:T(8,128)(2,1)S(1)} async-done(((bf16[16,64,128]{2,1,0:T(8,128)(2,1)}), bf16[16,64,128]{2,1,0:T(8,128)(2,1)S(1)}, u32[]{:S(2)}, u32[]{:S(2)}) %all-to-all-start.1) | async-done | bytes 262176 | tf_op jit(solution)/shard_map/all_to_all | solution.py:675
  48.5 6.8 %middle.1 = (f32[256,512]{1,0:T(8,128)}, bf16[8,256,128]{2,1,0:T(8,128)(2,1)S(1)}, bf16[8,512,256]{2,1,0:T(8,128)(2,1)}, bf16[512,512]{1,0:T(8,128)(2,1)S(1)}, f...) custom-call(s32[3]{0:T(128)S(1)} %pad_add_fusion.at, f32[256,512]{1,0:T(8,128)} %bitcast.36, ...), custom_call_target="tpu_custom_call" | custom-call | tf_op jit(solution)/shard_map/middle/pallas_call | solution.py:72
  55.9 12.7 %all_to_all.45.recv = bf16[8,256,128]{2,1,0:T(8,128)(2,1)S(1)} all-to-all(bf16[8,256,128]{2,1,0:T(8,128)(2,1)S(1)} %get-tuple-element.57), channel_id=1, replica_groups=mesh['dp'=8,'context'=8,'tensor'=2] {'context'}, dimensions={0} | all-to-all | bytes 1048576 | tf_op jit(solution)/shard_map/all_to_all | solution.py:675
  68.7 4.2 %attend_both.1 = bf16[8,2,256,128]{3,2,1,0:T(8,128)(2,1)S(1)} custom-call(bf16[8,256,128]{2,1,0:T(8,128)(2,1)S(1)} %all_to_all.45.recv, s32[1,1024]{1,0:T(1,128)S(1)} %get-tuple-element.58.start, bf16[512,512]{1,0:T(8,128)(2,1)S(1)} %collective-permute-done.1._.parts_other), custom_call_target="tpu_custom_call" | custom-call | tf_op jit(solution)/shard_map/attend_both/pallas_call | solution.py:72
  72.9 18.8 %all_to_all.46 = bf16[16,256,128]{2,1,0:T(8,128)(2,1)S(1)} all-to-all(bf16[16,256,128]{2,1,0:T(8,128)(2,1)S(1)} %bitcast.23), channel_id=1, replica_groups=mesh['dp'=8,'context'=8,'tensor'=2] {'context','tensor'}, dimensions={0} | all-to-all | bytes 2097152 | tf_op jit(solution)/shard_map/all_to_all | solution.py:675
  91.6 8.2 %turn_point.1 = (f32[256,512]{1,0:T(8,128)}, f32[256,512]{1,0:T(8,128)}, bf16[8,192,128]{2,1,0:T(8,128)(2,1)}, bf16[8,832,256]{2,1,0:T(8,128)(2,1)}, bf16[256,51...) custom-call(s32[3]{0:T(128)S(1)} %pad_add_fusion.at, ...), custom_call_target="tpu_custom_call" | custom-call | tf_op jit(solution)/shard_map/turn_point/pallas_call | solution.py:72
  99.8 3.6 %all-to-all-start.4 = ((bf16[8,192,128]{2,1,0:T(8,128)(2,1)}), bf16[8,192,128]{2,1,0:T(8,128)(2,1)S(1)}, u32[]{:S(2)}, u32[]{:S(2)}) async-start(bf16[8,192,128]{2,1,0:T(8,128)(2,1)} %get-tuple-element.65), calls=%async_computation.5 | async-start | bytes 786432 | tf_op jit(solution)/shard_map/all_to_all | solution.py:675
  104.6 6.8 %collective-permute-done.3._.part_other = bf16[256,512]{1,0:T(8,128)(2,1)S(1)} collective-permute-done((bf16[256,512]{1,0:T(8,128)(2,1)S(1)}, bf16[256,512]{1,0:T(8,128)(2,1)S(1)}, u32[]{:S(2)}, u32[]{:S(2)}) %collective-permute-start.3) | collective-permute-done | bytes 262176 | tf_op jit(solution)/shard_map/ppermute | solution.py:671
  113.6 18.8 %all_to_all.47 = bf16[16,320,128]{2,1,0:T(8,128)(2,1)S(1)} all-to-all(bf16[16,320,128]{2,1,0:T(8,128)(2,1)S(1)} %bitcast.21), channel_id=1, replica_groups=mesh['dp'=8,'context'=8,'tensor'=2] {'context','tensor'}, dimensions={0} | all-to-all | bytes 2621440 | tf_op jit(solution)/shard_map/all_to_all | solution.py:675
  132.4 3.9 %last.1 = (f32[256,512]{1,0:T(8,128)}, bf16[8,208,256]{2,1,0:T(8,128)(2,1)S(1)}, bf16[512,256]{1,0:T(8,128)(2,1)}, f32[3,256]{1,0:T(4,128)}, f32[4,512]{1,0:T(4,128)}) custom-call(s32[3]{0:T(128)S(1)} %pad_add_fusion.at, f32[256,512]{1,0:T(8,128)} %bitcast.38, f32[256,512]{1,0:T(8,128)} %get-tuple-element.63.g, bf16[256,512]{1,0:T(8,128)(2,1)S(1)} %get-tuple-element.64.part, ...), custom_call_target="tpu_custom_call" | custom-call | tf_op jit(solution)/shard_map/last/pallas_call | solution.py:72
  136.3 26.3 %all_to_all.48.got = bf16[8,208,256]{2,1,0:T(8,128)(2,1)S(1)} all-to-all(bf16[8,208,256]{2,1,0:T(8,128)(2,1)S(1)} %get-tuple-element.75), channel_id=1, replica_groups=mesh['dp'=8,'context'=8,'tensor'=2] {'dp'}, dimensions={0} | all-to-all | bytes 1703936 | tf_op jit(solution)/shard_map/all_to_all | solution.py:675
  164.5 12.1 %all_to_all.49.got = bf16[8,136,256]{2,1,0:T(8,128)(2,1)S(1)} all-to-all(bf16[8,136,256]{2,1,0:T(8,128)(2,1)S(1)} %get-tuple-element.78), channel_id=1, replica_groups=mesh['dp'=8,'context'=8,'tensor'=2] {'context'}, dimensions={0} | all-to-all | bytes 1114112 | tf_op jit(solution)/shard_map/all_to_all | solution.py:675
  176.7 11.5 %all_to_all.50 = bf16[8,136,256]{2,1,0:T(8,128)(2,1)} all-to-all(bf16[8,136,256]{2,1,0:T(8,128)(2,1)S(1)} %sum.1), channel_id=1, replica_groups=mesh['dp'=8,'context'=8,'tensor'=2] {'context'}, dimensions={0} | all-to-all | bytes 1114112 | tf_op jit(solution)/shard_map/all_to_all | solution.py:675
  188.2 4.2 %unpack_first.1 = (f32[2,512,1024]{2,1,0:T(8,128)}, f32[2,1024,512]{2,1,0:T(8,128)}) custom-call(bf16[8,512,256]{2,1,0:T(8,128)(2,1)} %bitcast.40), custom_call_target="tpu_custom_call" | custom-call | tf_op jit(solution)/shard_map/unpack_first/pallas_call | solution.py:636
  192.4 28.7 %all-gather.8.cloned.1.call-done = bf16[64,136,256]{2,1,0:T(8,128)(2,1)} async-done(((bf16[8,136,256]{2,1,0:T(8,128)(2,1)}), bf16[64,136,256]{2,1,0:T(8,128)(2,1)}) %all-gather.8.cloned.1.call-update) | async-done | bytes 4456464 | tf_op jit(solution)/shard_map/all_gather | solution.py:814
  221.1 6.0 %unpack_rest.1 = (f32[2,512,1024]{2,1,0:T(8,128)}, f32[2,1024,512]{2,1,0:T(8,128)}, f32[2,3,512,256]{3,2,1,0:T(8,128)}, f32[2,256,512]{2,1,0:T(8,128)}, f32[2,10...) custom-call(bf16[8,8,136,256]{3,2,1,0:T(8,128)(2,1)} %bitcast.39, ...), custom_call_target="tpu_custom_call", output_to_operand_aliasing={{0}: (1, {}), {1}: (2, {})} | custom-call | tf_op jit(solution)/shard_map/unpack_rest/pallas_call | solution.py:654
  (44 shorter events, 11.9 us)
Async XLA Ops:
  7.2 6.2 %copy-start.7 = (f32[8,1]{1,0:T(8,128)S(1)}, f32[8,1]{1,0:T(8,128)}, u32[]{:S(2)}) copy-start(f32[8,1]{1,0:T(8,128)} %constant.18.freqs) | copy-start | bytes 100
  7.2 6.2 %copy-start.3 = (f32[2,2,512]{2,1,0:T(2,128)S(1)}, f32[2,2,512]{2,1,0:T(2,128)}, u32[]{:S(2)}) copy-start(f32[2,2,512]{2,1,0:T(2,128)} %bias.9) | copy-start | bytes 24580
  7.2 6.2 %copy-start.2 = (f32[2,2,512]{2,1,0:T(2,128)S(1)}, f32[2,2,512]{2,1,0:T(2,128)}, u32[]{:S(2)}) copy-start(f32[2,2,512]{2,1,0:T(2,128)} %gain.9) | copy-start | bytes 24580
  7.2 6.2 %copy-start.6 = (f32[2,3,256]{2,0,1:T(2,128)S(1)}, f32[2,3,256]{2,0,1:T(2,128)}, u32[]{:S(2)}) copy-start(f32[2,3,256]{2,0,1:T(2,128)} %param.17) | copy-start | bytes 18436
  7.2 6.2 %copy-start.8 = (s32[2,128]{1,0:T(2,128)S(1)}, s32[2,128]{1,0:T(2,128)}, u32[]{:S(2)}) copy-start(s32[2,128]{1,0:T(2,128)} %pos.1) | copy-start | bytes 3076
  7.2 84.4 %all-gather.6.cloned.1.call-start = ((), (), s32[]{:S(2)}) async-start(), calls=%async_computation.11 | async-start | bytes 2359296 | tf_op jit(solution)/shard_map/all_gather | solution.py:720
  7.4 8.8 %copy-start.4 = (f32[2,1024]{1,0:T(2,128)S(1)}, f32[2,1024]{1,0:T(2,128)}, u32[]{:S(2)}) copy-start(f32[2,1024]{1,0:T(2,128)} %b_up.3) | copy-start | bytes 24580
  8.9 11.4 %collective-permute-start.2 = (bf16[2,4,64,256]{3,2,1,0:T(8,128)(2,1)S(1)}, bf16[2,4,64,256]{3,2,1,0:T(8,128)(2,1)S(1)}, u32[]{:S(2)}, u32[]{:S(2)}) collective-permute-start(bf16[2,4,64,256]{3,2,1,0:T(8,128)(2,1)S(1)} %chunk.1), channel_id=1, source_target_pairs={{0,1},{1,0},{2,3},{3,2},{4,5},{5,4},{6,7},{7,6},{8,9},{9,8},{10,11... | collective-permute-start | bytes 786440 | tf_op jit(solution)/shard_map/ppermute | solution.py:671
  16.1 32.4 %copy-start.5 = (f32[2,2,512]{2,1,0:T(2,128)S(1)}, f32[2,2,512]{2,1,0:T(2,128)}, u32[]{:S(2)}) copy-start(f32[2,2,512]{2,1,0:T(2,128)} %out_bias.3) | copy-start | bytes 24580
  20.3 1.0 copy-start
  22.1 11.9 %all-to-all-start = ((bf16[8,208,128]{2,1,0:T(8,128)(2,1)}), bf16[8,208,128]{2,1,0:T(8,128)(2,1)S(1)}, u32[]{:S(2)}, u32[]{:S(2)}) async-start(bf16[8,208,128]{2,1,0:T(8,128)(2,1)} %get-tuple-element.51._), calls=%async_computation | async-start | bytes 851968 | tf_op jit(solution)/shard_map/all_to_all | solution.py:675
  26.7 18.1 %collective-permute-start = (bf16[512,512]{1,0:T(8,128)(2,1)S(1)}, bf16[512,512]{1,0:T(8,128)(2,1)S(1)}, u32[]{:S(2)}, u32[]{:S(2)}) collective-permute-start(bf16[512,512]{1,0:T(8,128)(2,1)S(1)} %get-tuple-element.52.pair), channel_id=1, source_target_pairs={{0,1},{1,0},{2,3},{3,2},{4,5},{5,4},{6,7},{7,6},{8,9},{9,8},{10,11... | collective-permute-start | bytes 1572872 | tf_op jit(solution)/shard_map/ppermute | solution.py:671
  36.6 11.9 %all-to-all-start.1 = ((bf16[16,64,128]{2,1,0:T(8,128)(2,1)}), bf16[16,64,128]{2,1,0:T(8,128)(2,1)S(1)}, u32[]{:S(2)}, u32[]{:S(2)}) async-start(bf16[16,64,128]{2,1,0:T(8,128)(2,1)} %bitcast.6), calls=%async_computation.1 | async-start | bytes 524288 | tf_op jit(solution)/shard_map/all_to_all | solution.py:675
  40.8 50.8 %reduce-scatter.3.cloned.1.call-start = ((), (), s32[]{:S(2)}) async-start(), calls=%async_computation.12 | async-start | bytes 2359296 | tf_op jit(solution)/shard_map/reduce_scatter | solution.py:747
  55.3 107.3 %reduce-scatter.5.cloned.1.call-start = ((), (), s32[]{:S(2)}) async-start(), calls=%async_computation.13 | async-start | bytes 3833856 | tf_op jit(solution)/shard_map/reduce_scatter | solution.py:779
  55.4 13.3 %collective-permute-start.1 = (bf16[512,512]{1,0:T(8,128)(2,1)S(1)}, bf16[512,512]{1,0:T(8,128)(2,1)S(1)}, u32[]{:S(2)}, u32[]{:S(2)}) collective-permute-start(bf16[512,512]{1,0:T(8,128)(2,1)S(1)} %get-tuple-element.56.parts), channel_id=1, source_target_pairs={{0,1},{1,0},{2,3},{3,2},{4,5},{5,4},{6,7},{7,6},{8,9},{9,8},{10,11... | collective-permute-start | bytes 1572872 | tf_op jit(solution)/shard_map/ppermute | solution.py:671
  99.8 11.5 %copy-start.1 = (f32[64,1024]{1,0:T(8,128)S(1)}, f32[64,1024]{1,0:T(8,128)}, u32[]{:S(2)}) copy-start(f32[64,1024]{1,0:T(8,128)} %get-tuple-element.67.ctx) | copy-start | bytes 786436
  99.8 11.5 %all-to-all-start.4 = ((bf16[8,192,128]{2,1,0:T(8,128)(2,1)}), bf16[8,192,128]{2,1,0:T(8,128)(2,1)S(1)}, u32[]{:S(2)}, u32[]{:S(2)}) async-start(bf16[8,192,128]{2,1,0:T(8,128)(2,1)} %get-tuple-element.65), calls=%async_computation.5 | async-start | bytes 786432 | tf_op jit(solution)/shard_map/all_to_all | solution.py:675
  103.4 84.8 %all-gather.10.cloned.1.call-start = ((), (), s32[]{:S(2)}) async-start(), calls=%async_computation.15 | async-start | bytes 2359296 | tf_op jit(solution)/shard_map/all_gather | solution.py:812
  103.5 7.9 %collective-permute-start.3 = (bf16[256,512]{1,0:T(8,128)(2,1)S(1)}, bf16[256,512]{1,0:T(8,128)(2,1)S(1)}, u32[]{:S(2)}, u32[]{:S(2)}) collective-permute-start(bf16[256,512]{1,0:T(8,128)(2,1)S(1)} %get-tuple-element.64.part), channel_id=1, source_target_pairs={{0,1},{1,0},{2,3},{3,2},{4,5},{5,4},{6,7},{7,6},{8,9},{9,8},{10,11... | collective-permute-start | bytes 786440 | tf_op jit(solution)/shard_map/ppermute | solution.py:671
  164.4 56.6 %all-gather.8.cloned.1.call-start = ((), (), s32[]{:S(2)}) async-start(), calls=%async_computation.14 | async-start | bytes 5013504 | tf_op jit(solution)/shard_map/all_gather | solution.py:814
Sparse Core Ops, SparseCore 0:
  22.2 26.9 all-gather.5
  55.4 32.7 reduce-scatter.2
  100.0 36.9 reduce-scatter.4
  164.6 21.4 all-gather.9
  188.3 32.7 all-gather.7

commit v15 on v14

--- a/solution.py
+++ b/solution.py
@@ -714,11 +714,11 @@
         "feed",
     )
     pair_other = swap(pair)
+    recv = exchange(send, "context")
     (chunk,) = call(
-        hand_on_body, [pltpu.HBM(chunk.shape, BF)], (chunk, After(act)), "hand_on"
+        hand_on_body, [pltpu.HBM(chunk.shape, BF)], (chunk, After(recv)), "hand_on"
     )
     others = lax.all_gather(chunk, "dp", axis=2, tiled=True)
-    recv = exchange(send, "context")
     ctx_send, lse, ctx, start = call(
         attend_body,
         [((8, 2, HEAD, BLK), BF), ((1, 1024), F32), pltpu.HBM((HEAD, 1024), F32), ((1, 1024), jnp.int32)],

time: 235 us -> 254 us (1.081)
  waiting for transfers between devices: 48.1 us -> 57.4 us
  blocking collectives: 100 us -> 106 us
    ppermute x4, waiting for transfers between devices: 10.8 us -> 25.2 us  [swap(): return lax.ppermute(value, 'tensor', [(0, 1), (1, 0)])]
    all_to_all x6, blocking collectives: 100 us -> 106 us  [exchange(): return lax.all_to_all(value, axes, 0, 0)]
    all_to_all x3, waiting for transfers between devices: 8.5 us -> 3.36 us  [exchange(): return lax.all_to_all(value, axes, 0, 0)]
    all_to_all x3, starting transfers between devices: 12.5 us -> 16.9 us  [exchange(): return lax.all_to_all(value, axes, 0, 0)]
  transfers between devices with their start and end apart: 12 -> 12, of which waited for: 5 -> 6; matrix products, arithmetic and copies ran while one was open for 0% -> 0% of each run, Pallas kernels for 13% -> 12%
where the time goes in v15:
time: 254 us; the launch traced here: 253 us
  blocking collectives  106 us (42%)
  waiting for transfers between devices  57.4 us (23%)
  Pallas kernels  49.1 us (19%)
  starting transfers between devices  23.1 us (9%)
  between operations  13.9 us (5%)
  local copies, waits for them, and re-layouts  3.48 us (1%)
    all_to_all x6, blocking collectives, exchange(): return lax.all_to_all(value, axes, 0, 0)  106 us
    pallas_call x11, Pallas kernels, call(): pl.pallas_call(body, grid=(1,), out_shape=[o if isinstance(o, Kept) else...  37.4 us
    all_gather x1, waiting for transfers between devices, shards(): full_bc = lax.all_gather(exchange(summed, 'context'), 'dp')  28.7 us
    ppermute x4, waiting for transfers between devices, swap(): return lax.ppermute(value, 'tensor', [(0, 1), (1, 0)])  25.2 us
    all_to_all x3, starting transfers between devices, exchange(): return lax.all_to_all(value, axes, 0, 0)  16.9 us
    pallas_call x1, Pallas kernels, unpack(): pl.pallas_call(unpack_rest_body, grid=(4,), out_shape=[pltpu.HBM(shape, F...  6.04 us
    ppermute x4, starting transfers between devices, swap(): return lax.ppermute(value, 'tensor', [(0, 1), (1, 0)])  5.97 us
  transfers between devices with their start and end apart: 12, of which 6 were waited for; matrix products, arithmetic and copies ran while one was open for 0% of the time, Pallas kernels for 12%

profile of v15, /device:TPU:1, one launch (start us, length us, event | category | flops | bytes accessed | tf_op | source)
XLA Modules:
  0.0 253.0 jit_solution(3446189369706824782)
XLA Ops:
  10.7 2.7 %norm_qkv.1 = (bf16[8,208,128]{2,1,0:T(8,128)(2,1)}, f32[2,2,8,128]{3,2,1,0:T(8,128)S(1)}) custom-call(s32[3]{0:T(128)S(1)} %pad_add_fusion.at, s32[2,128]{1,0:T(2,128)S(1)} %copy-done.10, f32[8,1]{1,0:T(8,128)S(1)} %copy-done.9, f32[256,512]{1,0:T(8,128)} %bitcast.34, f32[2,2,512]{2,1,0:T(2,128)S(1)} %copy-done.1, f32[2,2,512]{2,1,0:T(2,128)S(1)} %copy-done.3, ...), custom_call_target="tpu_custom_call" | custom-call | tf_op jit(solution)/shard_map/norm_qkv/pallas_call | solution.py:72
  13.5 6.5 %all-to-all-start = ((bf16[8,208,128]{2,1,0:T(8,128)(2,1)}), bf16[8,208,128]{2,1,0:T(8,128)(2,1)S(1)}, u32[]{:S(2)}, u32[]{:S(2)}) async-start(bf16[8,208,128]{2,1,0:T(8,128)(2,1)} %get-tuple-element.51._), calls=%async_computation | async-start | bytes 851968 | tf_op jit(solution)/shard_map/all_to_all | solution.py:675
  21.5 3.4 %collective-permute-start.2 = (bf16[2,4,64,256]{3,2,1,0:T(8,128)(2,1)S(1)}, bf16[2,4,64,256]{3,2,1,0:T(8,128)(2,1)S(1)}, u32[]{:S(2)}, u32[]{:S(2)}) collective-permute-start(bf16[2,4,64,256]{3,2,1,0:T(8,128)(2,1)S(1)} %chunk.1), channel_id=1, source_target_pairs={{0,1},{1,0},{2,3},{3,2},{4,5},{5,4},{6,7},{7,6},{8,9},{9,8},{10,11... | collective-permute-start | bytes 786440 | tf_op jit(solution)/shard_map/ppermute | solution.py:671
  24.9 10.1 %collective-permute-done.2.value = bf16[2,4,64,256]{3,2,1,0:T(8,128)(2,1)S(1)} collective-permute-done((bf16[2,4,64,256]{3,2,1,0:T(8,128)(2,1)S(1)}, bf16[2,4,64,256]{3,2,1,0:T(8,128)(2,1)S(1)}, u32[]{:S(2)}, u32[]{:S(2)}) %collective-permute-start.2) | collective-permute-done | bytes 262176 | tf_op jit(solution)/shard_map/ppermute | solution.py:671
  35.8 4.1 %feed.1 = (bf16[512,512]{1,0:T(8,128)(2,1)S(1)}, bf16[256,1024]{1,0:T(8,128)(2,1)}, bf16[256,1024]{1,0:T(8,128)(2,1)}) custom-call(f32[256,512]{1,0:T(8,128)} %bitcast.35, f32[2,2,512]{2,1,0:T(2,128)S(1)} %copy-done.2, f32[2,2,512]{2,1,0:T(2,128)S(1)} %copy-done.4, bf16[2,512,1024]{2,1,0:T(8,128)(2,1)} %w_up.5, f32[2,1024]{1,0:T(2,128)S(1)} %copy-done.5, ...), custom_call_target="tpu_custom_call" | custom-call | tf_op jit(solution)/shard_map/feed/pallas_call | solution.py:72
  40.0 2.7 %attend.1 = (bf16[8,2,64,128]{3,2,1,0:T(8,128)(2,1)}, f32[1,1024]{1,0:T(1,128)S(1)}, f32[64,1024]{1,0:T(8,128)}, s32[1,1024]{1,0:T(1,128)S(1)}) custom-call(bf16[8,208,128]{2,1,0:T(8,128)(2,1)S(1)} %all-to-all-done.recv._), custom_call_target="tpu_custom_call" | custom-call | tf_op jit(solution)/shard_map/attend/pallas_call | solution.py:72
  42.6 6.8 %all-to-all-start.1 = ((bf16[16,64,128]{2,1,0:T(8,128)(2,1)}), bf16[16,64,128]{2,1,0:T(8,128)(2,1)S(1)}, u32[]{:S(2)}, u32[]{:S(2)}) async-start(bf16[16,64,128]{2,1,0:T(8,128)(2,1)} %bitcast.6), calls=%async_computation.1 | async-start | bytes 524288 | tf_op jit(solution)/shard_map/all_to_all | solution.py:675
  49.5 4.6 %collective-permute-done.pair_other = bf16[512,512]{1,0:T(8,128)(2,1)S(1)} collective-permute-done((bf16[512,512]{1,0:T(8,128)(2,1)S(1)}, bf16[512,512]{1,0:T(8,128)(2,1)S(1)}, u32[]{:S(2)}, u32[]{:S(2)}) %collective-permute-start) | collective-permute-done | bytes 524320 | tf_op jit(solution)/shard_map/ppermute | solution.py:671
  54.1 3.4 %all-to-all-done.1 = bf16[16,64,128]{2,1,0:T(8,128)(2,1)S(1)} async-done(((bf16[16,64,128]{2,1,0:T(8,128)(2,1)}), bf16[16,64,128]{2,1,0:T(8,128)(2,1)S(1)}, u32[]{:S(2)}, u32[]{:S(2)}) %all-to-all-start.1) | async-done | bytes 262176 | tf_op jit(solution)/shard_map/all_to_all | solution.py:675
  57.5 6.8 %middle.1 = (f32[256,512]{1,0:T(8,128)}, bf16[8,256,128]{2,1,0:T(8,128)(2,1)S(1)}, bf16[8,512,256]{2,1,0:T(8,128)(2,1)}, bf16[512,512]{1,0:T(8,128)(2,1)S(1)}, f...) custom-call(s32[3]{0:T(128)S(1)} %pad_add_fusion.at, f32[256,512]{1,0:T(8,128)} %bitcast.36, ...), custom_call_target="tpu_custom_call" | custom-call | tf_op jit(solution)/shard_map/middle/pallas_call | solution.py:72
  64.7 16.2 %all_to_all.45.recv = bf16[8,256,128]{2,1,0:T(8,128)(2,1)S(1)} all-to-all(bf16[8,256,128]{2,1,0:T(8,128)(2,1)S(1)} %get-tuple-element.57), channel_id=1, replica_groups=mesh['dp'=8,'context'=8,'tensor'=2] {'context'}, dimensions={0} | all-to-all | bytes 1048576 | tf_op jit(solution)/shard_map/all_to_all | solution.py:675
  81.7 4.2 %attend_both.1 = bf16[8,2,256,128]{3,2,1,0:T(8,128)(2,1)S(1)} custom-call(bf16[8,256,128]{2,1,0:T(8,128)(2,1)S(1)} %all_to_all.45.recv, s32[1,1024]{1,0:T(1,128)S(1)} %get-tuple-element.58.start, bf16[512,512]{1,0:T(8,128)(2,1)S(1)} %collective-permute-done.1._.parts_other), custom_call_target="tpu_custom_call" | custom-call | tf_op jit(solution)/shard_map/attend_both/pallas_call | solution.py:72
  85.9 22.7 %all_to_all.46 = bf16[16,256,128]{2,1,0:T(8,128)(2,1)S(1)} all-to-all(bf16[16,256,128]{2,1,0:T(8,128)(2,1)S(1)} %bitcast.23), channel_id=1, replica_groups=mesh['dp'=8,'context'=8,'tensor'=2] {'context','tensor'}, dimensions={0} | all-to-all | bytes 2097152 | tf_op jit(solution)/shard_map/all_to_all | solution.py:675
  108.6 8.2 %turn_point.1 = (f32[256,512]{1,0:T(8,128)}, f32[256,512]{1,0:T(8,128)}, bf16[8,192,128]{2,1,0:T(8,128)(2,1)}, bf16[8,832,256]{2,1,0:T(8,128)(2,1)}, bf16[256,51...) custom-call(s32[3]{0:T(128)S(1)} %pad_add_fusion.at, ...), custom_call_target="tpu_custom_call" | custom-call | tf_op jit(solution)/shard_map/turn_point/pallas_call | solution.py:72
  116.8 3.6 %all-to-all-start.4 = ((bf16[8,192,128]{2,1,0:T(8,128)(2,1)}), bf16[8,192,128]{2,1,0:T(8,128)(2,1)S(1)}, u32[]{:S(2)}, u32[]{:S(2)}) async-start(bf16[8,192,128]{2,1,0:T(8,128)(2,1)} %get-tuple-element.65), calls=%async_computation.5 | async-start | bytes 786432 | tf_op jit(solution)/shard_map/all_to_all | solution.py:675
  122.6 9.7 %collective-permute-done.3._.part_other = bf16[256,512]{1,0:T(8,128)(2,1)S(1)} collective-permute-done((bf16[256,512]{1,0:T(8,128)(2,1)S(1)}, bf16[256,512]{1,0:T(8,128)(2,1)S(1)}, u32[]{:S(2)}, u32[]{:S(2)}) %collective-permute-start.3) | collective-permute-done | bytes 262176 | tf_op jit(solution)/shard_map/ppermute | solution.py:671
  134.6 23.2 %all_to_all.47 = bf16[16,320,128]{2,1,0:T(8,128)(2,1)S(1)} all-to-all(bf16[16,320,128]{2,1,0:T(8,128)(2,1)S(1)} %bitcast.21), channel_id=1, replica_groups=mesh['dp'=8,'context'=8,'tensor'=2] {'context','tensor'}, dimensions={0} | all-to-all | bytes 2621440 | tf_op jit(solution)/shard_map/all_to_all | solution.py:675
  157.8 3.9 %last.1 = (f32[256,512]{1,0:T(8,128)}, bf16[8,208,256]{2,1,0:T(8,128)(2,1)S(1)}, bf16[512,256]{1,0:T(8,128)(2,1)}, f32[3,256]{1,0:T(4,128)}, f32[4,512]{1,0:T(4,128)}) custom-call(s32[3]{0:T(128)S(1)} %pad_add_fusion.at, f32[256,512]{1,0:T(8,128)} %bitcast.38, f32[256,512]{1,0:T(8,128)} %get-tuple-element.63.g, bf16[256,512]{1,0:T(8,128)(2,1)S(1)} %get-tuple-element.64.part, ...), custom_call_target="tpu_custom_call" | custom-call | tf_op jit(solution)/shard_map/last/pallas_call | solution.py:72
  161.7 20.2 %all_to_all.48.got = bf16[8,208,256]{2,1,0:T(8,128)(2,1)S(1)} all-to-all(bf16[8,208,256]{2,1,0:T(8,128)(2,1)S(1)} %get-tuple-element.75), channel_id=1, replica_groups=mesh['dp'=8,'context'=8,'tensor'=2] {'dp'}, dimensions={0} | all-to-all | bytes 1703936 | tf_op jit(solution)/shard_map/all_to_all | solution.py:675
  183.8 12.0 %all_to_all.49.got = bf16[8,136,256]{2,1,0:T(8,128)(2,1)S(1)} all-to-all(bf16[8,136,256]{2,1,0:T(8,128)(2,1)S(1)} %get-tuple-element.78), channel_id=1, replica_groups=mesh['dp'=8,'context'=8,'tensor'=2] {'context'}, dimensions={0} | all-to-all | bytes 1114112 | tf_op jit(solution)/shard_map/all_to_all | solution.py:675
  195.8 11.6 %all_to_all.50 = bf16[8,136,256]{2,1,0:T(8,128)(2,1)} all-to-all(bf16[8,136,256]{2,1,0:T(8,128)(2,1)S(1)} %sum.1), channel_id=1, replica_groups=mesh['dp'=8,'context'=8,'tensor'=2] {'context'}, dimensions={0} | all-to-all | bytes 1114112 | tf_op jit(solution)/shard_map/all_to_all | solution.py:675
  207.5 4.2 %unpack_first.1 = (f32[2,512,1024]{2,1,0:T(8,128)}, f32[2,1024,512]{2,1,0:T(8,128)}) custom-call(bf16[8,512,256]{2,1,0:T(8,128)(2,1)} %bitcast.40), custom_call_target="tpu_custom_call" | custom-call | tf_op jit(solution)/shard_map/unpack_first/pallas_call | solution.py:636
  211.6 28.7 %all-gather.8.cloned.1.call-done = bf16[64,136,256]{2,1,0:T(8,128)(2,1)} async-done(((bf16[8,136,256]{2,1,0:T(8,128)(2,1)}), bf16[64,136,256]{2,1,0:T(8,128)(2,1)}) %all-gather.8.cloned.1.call-update) | async-done | bytes 4456464 | tf_op jit(solution)/shard_map/all_gather | solution.py:814
  240.4 6.0 %unpack_rest.1 = (f32[2,512,1024]{2,1,0:T(8,128)}, f32[2,1024,512]{2,1,0:T(8,128)}, f32[2,3,512,256]{3,2,1,0:T(8,128)}, f32[2,256,512]{2,1,0:T(8,128)}, f32[2,10...) custom-call(bf16[8,8,136,256]{3,2,1,0:T(8,128)(2,1)} %bitcast.39, ...), custom_call_target="tpu_custom_call", output_to_operand_aliasing={{0}: (1, {}), {1}: (2, {})} | custom-call | tf_op jit(solution)/shard_map/unpack_rest/pallas_call | solution.py:654
  (48 shorter events, 13.6 us)
Async XLA Ops:
  7.3 0.7 copy-start.1
  8.0 0.7 copy-start.3
  8.7 0.7 copy-start.7
  9.3 0.7 copy-start.9
  10.0 0.7 copy-start.10
  13.5 22.3 %copy-start.2 = (f32[2,2,512]{2,1,0:T(2,128)S(1)}, f32[2,2,512]{2,1,0:T(2,128)}, u32[]{:S(2)}) copy-start(f32[2,2,512]{2,1,0:T(2,128)} %gain.9) | copy-start | bytes 24580
  13.5 22.4 %copy-start.4 = (f32[2,2,512]{2,1,0:T(2,128)S(1)}, f32[2,2,512]{2,1,0:T(2,128)}, u32[]{:S(2)}) copy-start(f32[2,2,512]{2,1,0:T(2,128)} %bias.9) | copy-start | bytes 24580
  13.5 22.4 %copy-start.5 = (f32[2,1024]{1,0:T(2,128)S(1)}, f32[2,1024]{1,0:T(2,128)}, u32[]{:S(2)}) copy-start(f32[2,1024]{1,0:T(2,128)} %b_up.3) | copy-start | bytes 24580
  13.5 21.6 %all-to-all-start = ((bf16[8,208,128]{2,1,0:T(8,128)(2,1)}), bf16[8,208,128]{2,1,0:T(8,128)(2,1)S(1)}, u32[]{:S(2)}, u32[]{:S(2)}) async-start(bf16[8,208,128]{2,1,0:T(8,128)(2,1)} %get-tuple-element.51._), calls=%async_computation | async-start | bytes 851968 | tf_op jit(solution)/shard_map/all_to_all | solution.py:675
  20.0 88.6 %all-gather.6.cloned.1.call-start = ((), (), s32[]{:S(2)}) async-start(), calls=%async_computation.11 | async-start | bytes 2359296 | tf_op jit(solution)/shard_map/all_gather | solution.py:721
  21.5 13.5 %collective-permute-start.2 = (bf16[2,4,64,256]{3,2,1,0:T(8,128)(2,1)S(1)}, bf16[2,4,64,256]{3,2,1,0:T(8,128)(2,1)S(1)}, u32[]{:S(2)}, u32[]{:S(2)}) collective-permute-start(bf16[2,4,64,256]{3,2,1,0:T(8,128)(2,1)S(1)} %chunk.1), channel_id=1, source_target_pairs={{0,1},{1,0},{2,3},{3,2},{4,5},{5,4},{6,7},{7,6},{8,9},{9,8},{10,11... | collective-permute-start | bytes 786440 | tf_op jit(solution)/shard_map/ppermute | solution.py:671
  35.8 21.6 %copy-start.6 = (f32[2,2,512]{2,1,0:T(2,128)S(1)}, f32[2,2,512]{2,1,0:T(2,128)}, u32[]{:S(2)}) copy-start(f32[2,2,512]{2,1,0:T(2,128)} %out_bias.3) | copy-start | bytes 24580
  35.8 21.6 %copy-start.8 = (f32[2,3,256]{2,0,1:T(2,128)S(1)}, f32[2,3,256]{2,0,1:T(2,128)}, u32[]{:S(2)}) copy-start(f32[2,3,256]{2,0,1:T(2,128)} %param.17) | copy-start | bytes 18436
  40.0 14.1 %collective-permute-start = (bf16[512,512]{1,0:T(8,128)(2,1)S(1)}, bf16[512,512]{1,0:T(8,128)(2,1)S(1)}, u32[]{:S(2)}, u32[]{:S(2)}) collective-permute-start(bf16[512,512]{1,0:T(8,128)(2,1)S(1)} %get-tuple-element.52.pair), channel_id=1, source_target_pairs={{0,1},{1,0},{2,3},{3,2},{4,5},{5,4},{6,7},{7,6},{8,9},{9,8},{10,11... | collective-permute-start | bytes 1572872 | tf_op jit(solution)/shard_map/ppermute | solution.py:671
  42.6 14.8 %all-to-all-start.1 = ((bf16[16,64,128]{2,1,0:T(8,128)(2,1)}), bf16[16,64,128]{2,1,0:T(8,128)(2,1)S(1)}, u32[]{:S(2)}, u32[]{:S(2)}) async-start(bf16[16,64,128]{2,1,0:T(8,128)(2,1)} %bitcast.6), calls=%async_computation.1 | async-start | bytes 524288 | tf_op jit(solution)/shard_map/all_to_all | solution.py:675
  49.5 59.1 %reduce-scatter.3.cloned.1.call-start = ((), (), s32[]{:S(2)}) async-start(), calls=%async_computation.12 | async-start | bytes 2359296 | tf_op jit(solution)/shard_map/reduce_scatter | solution.py:747
  64.3 117.6 %reduce-scatter.5.cloned.1.call-start = ((), (), s32[]{:S(2)}) async-start(), calls=%async_computation.13 | async-start | bytes 3833856 | tf_op jit(solution)/shard_map/reduce_scatter | solution.py:779
  64.4 17.3 %collective-permute-start.1 = (bf16[512,512]{1,0:T(8,128)(2,1)S(1)}, bf16[512,512]{1,0:T(8,128)(2,1)S(1)}, u32[]{:S(2)}, u32[]{:S(2)}) collective-permute-start(bf16[512,512]{1,0:T(8,128)(2,1)S(1)} %get-tuple-element.56.parts), channel_id=1, source_target_pairs={{0,1},{1,0},{2,3},{3,2},{4,5},{5,4},{6,7},{7,6},{8,9},{9,8},{10,11... | collective-permute-start | bytes 1572872 | tf_op jit(solution)/shard_map/ppermute | solution.py:671
  116.7 15.6 %copy-start = (f32[64,1024]{1,0:T(8,128)S(1)}, f32[64,1024]{1,0:T(8,128)}, u32[]{:S(2)}) copy-start(f32[64,1024]{1,0:T(8,128)} %get-tuple-element.67.ctx) | copy-start | bytes 786436
  116.8 15.6 %all-to-all-start.4 = ((bf16[8,192,128]{2,1,0:T(8,128)(2,1)}), bf16[8,192,128]{2,1,0:T(8,128)(2,1)S(1)}, u32[]{:S(2)}, u32[]{:S(2)}) async-start(bf16[8,192,128]{2,1,0:T(8,128)(2,1)} %get-tuple-element.65), calls=%async_computation.5 | async-start | bytes 786432 | tf_op jit(solution)/shard_map/all_to_all | solution.py:675
  120.4 87.1 %all-gather.10.cloned.1.call-start = ((), (), s32[]{:S(2)}) async-start(), calls=%async_computation.15 | async-start | bytes 2359296 | tf_op jit(solution)/shard_map/all_gather | solution.py:812
  120.4 11.9 %collective-permute-start.3 = (bf16[256,512]{1,0:T(8,128)(2,1)S(1)}, bf16[256,512]{1,0:T(8,128)(2,1)S(1)}, u32[]{:S(2)}, u32[]{:S(2)}) collective-permute-start(bf16[256,512]{1,0:T(8,128)(2,1)S(1)} %get-tuple-element.64.part), channel_id=1, source_target_pairs={{0,1},{1,0},{2,3},{3,2},{4,5},{5,4},{6,7},{7,6},{8,9},{9,8},{10,11... | collective-permute-start | bytes 786440 | tf_op jit(solution)/shard_map/ppermute | solution.py:671
  183.7 56.6 %all-gather.8.cloned.1.call-start = ((), (), s32[]{:S(2)}) async-start(), calls=%async_computation.14 | async-start | bytes 5013504 | tf_op jit(solution)/shard_map/all_gather | solution.py:814
Sparse Core Ops, SparseCore 0:
  35.9 24.3 all-gather.5
  64.4 30.5 reduce-scatter.2
  116.9 33.8 reduce-scatter.4
  183.9 21.4 all-gather.9
  207.6 32.7 all-gather.7

commit v16 on v10

--- a/solution.py
+++ b/solution.py
@@ -541,7 +541,7 @@
 
 
 def unpack_first_body(first, g_up, g_down):
-    for k in range(2):
+    for k in range(4):
         for c in range(4):
             cols = slice(256 * c, 256 * (c + 1))
             g_up[0, 64 * k : 64 * (k + 1), cols] = first[k, 64 * c : 64 * (c + 1)].astype(F32)
@@ -553,7 +553,7 @@
 
 def unpack_rest_body(rest, _, __, g_up, g_down, g_qkv, g_out, g_b_up, g_b_qkv, g_sum, g_gain, g_bias):
     p = pl.program_id(0)
-    for k in range(2):
+    for k in range(4):
         for q in range(8):
             block = rest[k, q].astype(F32)
             for i in range(16):
@@ -579,7 +579,7 @@
                     r += 32 * k
                     g_out[1 - (row - 704) // 64, r : r + 8, 256 * c : 256 * (c + 1)] = value
 
-    tiny = [jnp.concatenate([rest[k, q].astype(F32)[128:136] for q in range(2)], 0) for k in range(2)]
+    tiny = [jnp.concatenate([rest[k, q].astype(F32)[128:136] for q in range(2)], 0) for k in range(3)]
 
     @pl.when(p == 0)
     def _():
@@ -608,10 +608,7 @@
     @pl.when(p == 0)
     def _():
         norms(0, tiny[1], 4)
-
-    @pl.when(p == 1)
-    def _():
-        norms(1, tiny[0], 0)
+        norms(1, tiny[2], 0)
 
 
 UP = (2, 512, 1024)
@@ -621,23 +618,23 @@
 def unpack(first, rest):
     def place(layer):
         return [
-            pl.BlockSpec((1, 128, 1024), lambda p: (layer, p, 0)),
-            pl.BlockSpec((1, 256, 512), lambda p: (layer, p, 0)),
+            pl.BlockSpec((1, 256, 1024), lambda p: (layer, p, 0)),
+            pl.BlockSpec((1, 512, 512), lambda p: (layer, p, 0)),
         ]
 
     params = pltpu.CompilerParams(vmem_limit_bytes=40 * 1024 * 1024)
     g_up, g_down = pl.pallas_call(
         unpack_first_body,
-        grid=(4,),
+        grid=(2,),
         out_shape=[pltpu.HBM(UP, F32), pltpu.HBM(DOWN, F32)],
-        in_specs=[pl.BlockSpec((2, 512, 256), lambda p: (p, 0, 0))],
+        in_specs=[pl.BlockSpec((4, 512, 256), lambda p: (p, 0, 0))],
         out_specs=place(1),
         compiler_params=params,
         name="unpack_first",
     )(far(first))
     outs = [
-        ((2, 3, 512, 256), pl.BlockSpec((2, 3, 128, 256), lambda p: (0, 0, p, 0))),
-        ((2, 256, 512), pl.BlockSpec((2, 64, 512), lambda p: (0, p, 0))),
+        ((2, 3, 512, 256), pl.BlockSpec((2, 3, 256, 256), lambda p: (0, 0, p, 0))),
+        ((2, 256, 512), pl.BlockSpec((2, 128, 512), lambda p: (0, p, 0))),
         ((2, 1024), whole((2, 1024))),
         ((3, 2, 256), whole((3, 2, 256))),
         ((2, 2, 512), whole((2, 2, 512))),
@@ -646,10 +643,10 @@
     ]
     return pl.pallas_call(
         unpack_rest_body,
-        grid=(4,),
+        grid=(2,),
         out_shape=[pltpu.HBM(shape, F32) for shape in [UP, DOWN] + [o[0] for o in outs]],
         in_specs=[
-            pl.BlockSpec((2, 8, 136, 256), lambda p: (p, 0, 0, 0)),
+            pl.BlockSpec((4, 8, 136, 256), lambda p: (p, 0, 0, 0)),
             pl.BlockSpec(memory_space=pl.ANY),
             pl.BlockSpec(memory_space=pl.ANY),
         ],

time: 234 us -> 233 us (level)
  no operation moved by 1% of the time
where the time goes in v16:
time: 233 us; the launch traced here: 232 us
  blocking collectives  100 us (43%)
  waiting for transfers between devices  48.8 us (21%)
  Pallas kernels  45.1 us (19%)
  starting transfers between devices  23.7 us (10%)
  between operations  13.9 us (6%)
    all_to_all x6, blocking collectives, exchange(): return lax.all_to_all(value, axes, 0, 0)  100 us
    pallas_call x10, Pallas kernels, call(): pl.pallas_call(body, grid=(1,), out_shape=[o if isinstance(o, Kept) else...  35 us
    all_gather x1, waiting for transfers between devices, shards(): full_bc = lax.all_gather(exchange(summed, 'context'), 'dp')  29.5 us
    all_to_all x3, starting transfers between devices, exchange(): return lax.all_to_all(value, axes, 0, 0)  14.1 us
    ppermute x4, waiting for transfers between devices, swap(): return lax.ppermute(value, 'tensor', [(0, 1), (1, 0)])  12.4 us
    ppermute x4, starting transfers between devices, swap(): return lax.ppermute(value, 'tensor', [(0, 1), (1, 0)])  9.44 us
    all_to_all x3, waiting for transfers between devices, exchange(): return lax.all_to_all(value, axes, 0, 0)  6.77 us
    pallas_call x1, Pallas kernels, unpack(): pl.pallas_call(unpack_rest_body, grid=(2,), out_shape=[pltpu.HBM(shape, F...  5.19 us
  transfers between devices with their start and end apart: 12, of which 6 were waited for; matrix products, arithmetic and copies ran while one was open for 0% of the time, Pallas kernels for 12%

profile of v16, /device:TPU:1, one launch (start us, length us, event | category | flops | bytes accessed | tf_op | source)
XLA Modules:
  0.0 231.8 jit_solution(10164313004620419096)
XLA Ops:
  8.9 4.5 %collective-permute-start.2 = (bf16[2,4,64,256]{3,2,1,0:T(8,128)(2,1)S(1)}, bf16[2,4,64,256]{3,2,1,0:T(8,128)(2,1)S(1)}, u32[]{:S(2)}, u32[]{:S(2)}) collective-permute-start(bf16[2,4,64,256]{3,2,1,0:T(8,128)(2,1)S(1)} %chunk.1), channel_id=1, source_target_pairs={{0,1},{1,0},{2,3},{3,2},{4,5},{5,4},{6,7},{7,6},{8,9},{9,8},{10,11... | collective-permute-start | bytes 786440 | tf_op jit(solution)/shard_map/ppermute | solution.py:661
  13.4 4.4 %norm_qkv_feed.1 = (bf16[8,208,128]{2,1,0:T(8,128)(2,1)}, bf16[512,512]{1,0:T(8,128)(2,1)S(1)}, bf16[256,1024]{1,0:T(8,128)(2,1)}, bf16[256,1024]{1,0:T(8,128)(2,1)}, f32[2,2,8,128]{3,2,1,0:T(8,128)S(1)}) custom-call(s32[3]{0:T(128)S(1)} %pad_add_fusion.at, s32[2,128]{1,0:T(2,128)S(1)} %copy-done.7, f32[8,1]{1,0:T(8,128)S(1)} %copy-done.6, ...), custom_call_target="tpu_custom_call" | custom-call | tf_op jit(solution)/shard_map/norm_qkv_feed/pallas_call | solution.py:72
  20.2 4.6 %all-to-all-start = ((bf16[8,208,128]{2,1,0:T(8,128)(2,1)}), bf16[8,208,128]{2,1,0:T(8,128)(2,1)S(1)}, u32[]{:S(2)}, u32[]{:S(2)}) async-start(bf16[8,208,128]{2,1,0:T(8,128)(2,1)} %get-tuple-element.52._), calls=%async_computation | async-start | bytes 851968 | tf_op jit(solution)/shard_map/all_to_all | solution.py:665
  24.8 3.3 %collective-permute-start = (bf16[512,512]{1,0:T(8,128)(2,1)S(1)}, bf16[512,512]{1,0:T(8,128)(2,1)S(1)}, u32[]{:S(2)}, u32[]{:S(2)}) collective-permute-start(bf16[512,512]{1,0:T(8,128)(2,1)S(1)} %get-tuple-element.51.pair), channel_id=1, source_target_pairs={{0,1},{1,0},{2,3},{3,2},{4,5},{5,4},{6,7},{7,6},{8,9},{9,8},{10,11... | collective-permute-start | bytes 1572872 | tf_op jit(solution)/shard_map/ppermute | solution.py:661
  28.1 3.2 %all-to-all-done.recv = bf16[8,208,128]{2,1,0:T(8,128)(2,1)S(1)} async-done(((bf16[8,208,128]{2,1,0:T(8,128)(2,1)}), bf16[8,208,128]{2,1,0:T(8,128)(2,1)S(1)}, u32[]{:S(2)}, u32[]{:S(2)}) %all-to-all-start) | async-done | bytes 426016 | tf_op jit(solution)/shard_map/all_to_all | solution.py:665
  31.2 2.7 %attend.1 = (bf16[8,2,64,128]{3,2,1,0:T(8,128)(2,1)}, f32[1,1024]{1,0:T(1,128)S(1)}, f32[64,1024]{1,0:T(8,128)}, s32[1,1024]{1,0:T(1,128)S(1)}) custom-call(bf16[8,208,128]{2,1,0:T(8,128)(2,1)S(1)} %all-to-all-done.recv), custom_call_target="tpu_custom_call" | custom-call | tf_op jit(solution)/shard_map/attend/pallas_call | solution.py:72
  33.9 5.9 %all-to-all-start.1 = ((bf16[16,64,128]{2,1,0:T(8,128)(2,1)}), bf16[16,64,128]{2,1,0:T(8,128)(2,1)S(1)}, u32[]{:S(2)}, u32[]{:S(2)}) async-start(bf16[16,64,128]{2,1,0:T(8,128)(2,1)} %bitcast.6), calls=%async_computation.1 | async-start | bytes 524288 | tf_op jit(solution)/shard_map/all_to_all | solution.py:665
  39.8 4.0 %collective-permute-done.pair_other = bf16[512,512]{1,0:T(8,128)(2,1)S(1)} collective-permute-done((bf16[512,512]{1,0:T(8,128)(2,1)S(1)}, bf16[512,512]{1,0:T(8,128)(2,1)S(1)}, u32[]{:S(2)}, u32[]{:S(2)}) %collective-permute-start) | collective-permute-done | bytes 524320 | tf_op jit(solution)/shard_map/ppermute | solution.py:661
  43.8 3.6 %all-to-all-done.1 = bf16[16,64,128]{2,1,0:T(8,128)(2,1)S(1)} async-done(((bf16[16,64,128]{2,1,0:T(8,128)(2,1)}), bf16[16,64,128]{2,1,0:T(8,128)(2,1)S(1)}, u32[]{:S(2)}, u32[]{:S(2)}) %all-to-all-start.1) | async-done | bytes 262176 | tf_op jit(solution)/shard_map/all_to_all | solution.py:665
  47.4 6.8 %middle.1 = (f32[256,512]{1,0:T(8,128)}, bf16[8,256,128]{2,1,0:T(8,128)(2,1)S(1)}, bf16[8,512,256]{2,1,0:T(8,128)(2,1)}, bf16[512,512]{1,0:T(8,128)(2,1)S(1)}, f...) custom-call(s32[3]{0:T(128)S(1)} %pad_add_fusion.at, f32[256,512]{1,0:T(8,128)} %bitcast.35, ...), custom_call_target="tpu_custom_call" | custom-call | tf_op jit(solution)/shard_map/middle/pallas_call | solution.py:72
  54.9 12.1 %all_to_all.45.recv = bf16[8,256,128]{2,1,0:T(8,128)(2,1)S(1)} all-to-all(bf16[8,256,128]{2,1,0:T(8,128)(2,1)S(1)} %get-tuple-element.57), channel_id=1, replica_groups=mesh['dp'=8,'context'=8,'tensor'=2] {'context'}, dimensions={0} | all-to-all | bytes 1048576 | tf_op jit(solution)/shard_map/all_to_all | solution.py:665
  66.9 4.2 %attend_both.1 = bf16[8,2,256,128]{3,2,1,0:T(8,128)(2,1)S(1)} custom-call(bf16[8,256,128]{2,1,0:T(8,128)(2,1)S(1)} %all_to_all.45.recv, s32[1,1024]{1,0:T(1,128)S(1)} %get-tuple-element.58.start, bf16[512,512]{1,0:T(8,128)(2,1)S(1)} %collective-permute-done.1._.parts_other), custom_call_target="tpu_custom_call" | custom-call | tf_op jit(solution)/shard_map/attend_both/pallas_call | solution.py:72
  71.2 19.5 %all_to_all.46 = bf16[16,256,128]{2,1,0:T(8,128)(2,1)S(1)} all-to-all(bf16[16,256,128]{2,1,0:T(8,128)(2,1)S(1)} %bitcast.23), channel_id=1, replica_groups=mesh['dp'=8,'context'=8,'tensor'=2] {'context','tensor'}, dimensions={0} | all-to-all | bytes 2097152 | tf_op jit(solution)/shard_map/all_to_all | solution.py:665
  90.7 8.2 %turn_point.1 = (f32[256,512]{1,0:T(8,128)}, f32[256,512]{1,0:T(8,128)}, bf16[8,192,128]{2,1,0:T(8,128)(2,1)}, bf16[8,832,256]{2,1,0:T(8,128)(2,1)}, bf16[256,51...) custom-call(s32[3]{0:T(128)S(1)} %pad_add_fusion.at, ...), custom_call_target="tpu_custom_call" | custom-call | tf_op jit(solution)/shard_map/turn_point/pallas_call | solution.py:72
  98.9 3.6 %all-to-all-start.4 = ((bf16[8,192,128]{2,1,0:T(8,128)(2,1)}), bf16[8,192,128]{2,1,0:T(8,128)(2,1)S(1)}, u32[]{:S(2)}, u32[]{:S(2)}) async-start(bf16[8,192,128]{2,1,0:T(8,128)(2,1)} %get-tuple-element.65), calls=%async_computation.5 | async-start | bytes 786432 | tf_op jit(solution)/shard_map/all_to_all | solution.py:665
  103.6 6.8 %collective-permute-done.3._.part_other = bf16[256,512]{1,0:T(8,128)(2,1)S(1)} collective-permute-done((bf16[256,512]{1,0:T(8,128)(2,1)S(1)}, bf16[256,512]{1,0:T(8,128)(2,1)S(1)}, u32[]{:S(2)}, u32[]{:S(2)}) %collective-permute-start.3) | collective-permute-done | bytes 262176 | tf_op jit(solution)/shard_map/ppermute | solution.py:661
  112.6 18.8 %all_to_all.47 = bf16[16,320,128]{2,1,0:T(8,128)(2,1)S(1)} all-to-all(bf16[16,320,128]{2,1,0:T(8,128)(2,1)S(1)} %bitcast.21), channel_id=1, replica_groups=mesh['dp'=8,'context'=8,'tensor'=2] {'context','tensor'}, dimensions={0} | all-to-all | bytes 2621440 | tf_op jit(solution)/shard_map/all_to_all | solution.py:665
  131.4 3.9 %last.1 = (f32[256,512]{1,0:T(8,128)}, bf16[8,208,256]{2,1,0:T(8,128)(2,1)S(1)}, bf16[512,256]{1,0:T(8,128)(2,1)}, f32[3,256]{1,0:T(4,128)}, f32[4,512]{1,0:T(4,128)}) custom-call(s32[3]{0:T(128)S(1)} %pad_add_fusion.at, f32[256,512]{1,0:T(8,128)} %bitcast.37, f32[256,512]{1,0:T(8,128)} %get-tuple-element.63.g, bf16[256,512]{1,0:T(8,128)(2,1)S(1)} %get-tuple-element.64.part, ...), custom_call_target="tpu_custom_call" | custom-call | tf_op jit(solution)/shard_map/last/pallas_call | solution.py:72
  135.3 26.3 %all_to_all.48.got = bf16[8,208,256]{2,1,0:T(8,128)(2,1)S(1)} all-to-all(bf16[8,208,256]{2,1,0:T(8,128)(2,1)S(1)} %get-tuple-element.75), channel_id=1, replica_groups=mesh['dp'=8,'context'=8,'tensor'=2] {'dp'}, dimensions={0} | all-to-all | bytes 1703936 | tf_op jit(solution)/shard_map/all_to_all | solution.py:665
  163.5 12.1 %all_to_all.49.got = bf16[8,136,256]{2,1,0:T(8,128)(2,1)S(1)} all-to-all(bf16[8,136,256]{2,1,0:T(8,128)(2,1)S(1)} %get-tuple-element.78), channel_id=1, replica_groups=mesh['dp'=8,'context'=8,'tensor'=2] {'context'}, dimensions={0} | all-to-all | bytes 1114112 | tf_op jit(solution)/shard_map/all_to_all | solution.py:665
  175.7 11.5 %all_to_all.50 = bf16[8,136,256]{2,1,0:T(8,128)(2,1)} all-to-all(bf16[8,136,256]{2,1,0:T(8,128)(2,1)S(1)} %sum.1), channel_id=1, replica_groups=mesh['dp'=8,'context'=8,'tensor'=2] {'context'}, dimensions={0} | all-to-all | bytes 1114112 | tf_op jit(solution)/shard_map/all_to_all | solution.py:665
  187.2 3.4 %unpack_first.1 = (f32[2,512,1024]{2,1,0:T(8,128)}, f32[2,1024,512]{2,1,0:T(8,128)}) custom-call(bf16[8,512,256]{2,1,0:T(8,128)(2,1)} %bitcast.39), custom_call_target="tpu_custom_call" | custom-call | tf_op jit(solution)/shard_map/unpack_first/pallas_call | solution.py:626
  190.6 29.5 %all-gather.8.cloned.1.call-done = bf16[64,136,256]{2,1,0:T(8,128)(2,1)} async-done(((bf16[8,136,256]{2,1,0:T(8,128)(2,1)}), bf16[64,136,256]{2,1,0:T(8,128)(2,1)}) %all-gather.8.cloned.1.call-update) | async-done | bytes 4456464 | tf_op jit(solution)/shard_map/all_gather | solution.py:800
  220.1 5.2 %unpack_rest.1 = (f32[2,512,1024]{2,1,0:T(8,128)}, f32[2,1024,512]{2,1,0:T(8,128)}, f32[2,3,512,256]{3,2,1,0:T(8,128)}, f32[2,256,512]{2,1,0:T(8,128)}, f32[2,10...) custom-call(bf16[8,8,136,256]{3,2,1,0:T(8,128)(2,1)} %bitcast.38, ...), custom_call_target="tpu_custom_call", output_to_operand_aliasing={{0}: (1, {}), {1}: (2, {})} | custom-call | tf_op jit(solution)/shard_map/unpack_rest/pallas_call | solution.py:644
  (41 shorter events, 10.0 us)
Async XLA Ops:
  7.2 6.2 %copy-start.6 = (f32[8,1]{1,0:T(8,128)S(1)}, f32[8,1]{1,0:T(8,128)}, u32[]{:S(2)}) copy-start(f32[8,1]{1,0:T(8,128)} %constant.18.freqs) | copy-start | bytes 100
  7.2 6.2 %copy-start.2 = (f32[2,2,512]{2,1,0:T(2,128)S(1)}, f32[2,2,512]{2,1,0:T(2,128)}, u32[]{:S(2)}) copy-start(f32[2,2,512]{2,1,0:T(2,128)} %bias.7) | copy-start | bytes 24580
  7.2 6.2 %copy-start.1 = (f32[2,2,512]{2,1,0:T(2,128)S(1)}, f32[2,2,512]{2,1,0:T(2,128)}, u32[]{:S(2)}) copy-start(f32[2,2,512]{2,1,0:T(2,128)} %gain.7) | copy-start | bytes 24580
  7.2 6.2 %copy-start.3 = (f32[2,1024]{1,0:T(2,128)S(1)}, f32[2,1024]{1,0:T(2,128)}, u32[]{:S(2)}) copy-start(f32[2,1024]{1,0:T(2,128)} %b_up.3) | copy-start | bytes 24580
  7.2 6.2 %copy-start.5 = (f32[2,3,256]{2,0,1:T(2,128)S(1)}, f32[2,3,256]{2,0,1:T(2,128)}, u32[]{:S(2)}) copy-start(f32[2,3,256]{2,0,1:T(2,128)} %param.17) | copy-start | bytes 18436
  7.2 6.2 %copy-start.7 = (s32[2,128]{1,0:T(2,128)S(1)}, s32[2,128]{1,0:T(2,128)}, u32[]{:S(2)}) copy-start(s32[2,128]{1,0:T(2,128)} %pos.1) | copy-start | bytes 3076
  7.2 83.4 %all-gather.6.cloned.1.call-start = ((), (), s32[]{:S(2)}) async-start(), calls=%async_computation.11 | async-start | bytes 2359296 | tf_op jit(solution)/shard_map/all_gather | solution.py:706
  8.9 10.5 %collective-permute-start.2 = (bf16[2,4,64,256]{3,2,1,0:T(8,128)(2,1)S(1)}, bf16[2,4,64,256]{3,2,1,0:T(8,128)(2,1)S(1)}, u32[]{:S(2)}, u32[]{:S(2)}) collective-permute-start(bf16[2,4,64,256]{3,2,1,0:T(8,128)(2,1)S(1)} %chunk.1), channel_id=1, source_target_pairs={{0,1},{1,0},{2,3},{3,2},{4,5},{5,4},{6,7},{7,6},{8,9},{9,8},{10,11... | collective-permute-start | bytes 786440 | tf_op jit(solution)/shard_map/ppermute | solution.py:661
  17.8 29.6 %copy-start.4 = (f32[2,2,512]{2,1,0:T(2,128)S(1)}, f32[2,2,512]{2,1,0:T(2,128)}, u32[]{:S(2)}) copy-start(f32[2,2,512]{2,1,0:T(2,128)} %out_bias.3) | copy-start | bytes 24580
  20.2 11.1 %all-to-all-start = ((bf16[8,208,128]{2,1,0:T(8,128)(2,1)}), bf16[8,208,128]{2,1,0:T(8,128)(2,1)S(1)}, u32[]{:S(2)}, u32[]{:S(2)}) async-start(bf16[8,208,128]{2,1,0:T(8,128)(2,1)} %get-tuple-element.52._), calls=%async_computation | async-start | bytes 851968 | tf_op jit(solution)/shard_map/all_to_all | solution.py:665
  24.8 19.1 %collective-permute-start = (bf16[512,512]{1,0:T(8,128)(2,1)S(1)}, bf16[512,512]{1,0:T(8,128)(2,1)S(1)}, u32[]{:S(2)}, u32[]{:S(2)}) collective-permute-start(bf16[512,512]{1,0:T(8,128)(2,1)S(1)} %get-tuple-element.51.pair), channel_id=1, source_target_pairs={{0,1},{1,0},{2,3},{3,2},{4,5},{5,4},{6,7},{7,6},{8,9},{9,8},{10,11... | collective-permute-start | bytes 1572872 | tf_op jit(solution)/shard_map/ppermute | solution.py:661
  33.9 13.5 %all-to-all-start.1 = ((bf16[16,64,128]{2,1,0:T(8,128)(2,1)}), bf16[16,64,128]{2,1,0:T(8,128)(2,1)S(1)}, u32[]{:S(2)}, u32[]{:S(2)}) async-start(bf16[16,64,128]{2,1,0:T(8,128)(2,1)} %bitcast.6), calls=%async_computation.1 | async-start | bytes 524288 | tf_op jit(solution)/shard_map/all_to_all | solution.py:665
  39.8 50.9 %reduce-scatter.3.cloned.1.call-start = ((), (), s32[]{:S(2)}) async-start(), calls=%async_computation.12 | async-start | bytes 2359296 | tf_op jit(solution)/shard_map/reduce_scatter | solution.py:733
  54.2 107.4 %reduce-scatter.5.cloned.1.call-start = ((), (), s32[]{:S(2)}) async-start(), calls=%async_computation.13 | async-start | bytes 3833856 | tf_op jit(solution)/shard_map/reduce_scatter | solution.py:765
  54.3 12.7 %collective-permute-start.1 = (bf16[512,512]{1,0:T(8,128)(2,1)S(1)}, bf16[512,512]{1,0:T(8,128)(2,1)S(1)}, u32[]{:S(2)}, u32[]{:S(2)}) collective-permute-start(bf16[512,512]{1,0:T(8,128)(2,1)S(1)} %get-tuple-element.56.parts), channel_id=1, source_target_pairs={{0,1},{1,0},{2,3},{3,2},{4,5},{5,4},{6,7},{7,6},{8,9},{9,8},{10,11... | collective-permute-start | bytes 1572872 | tf_op jit(solution)/shard_map/ppermute | solution.py:661
  98.8 11.5 %copy-start = (f32[64,1024]{1,0:T(8,128)S(1)}, f32[64,1024]{1,0:T(8,128)}, u32[]{:S(2)}) copy-start(f32[64,1024]{1,0:T(8,128)} %get-tuple-element.67.ctx) | copy-start | bytes 786436
  98.9 11.5 %all-to-all-start.4 = ((bf16[8,192,128]{2,1,0:T(8,128)(2,1)}), bf16[8,192,128]{2,1,0:T(8,128)(2,1)S(1)}, u32[]{:S(2)}, u32[]{:S(2)}) async-start(bf16[8,192,128]{2,1,0:T(8,128)(2,1)} %get-tuple-element.65), calls=%async_computation.5 | async-start | bytes 786432 | tf_op jit(solution)/shard_map/all_to_all | solution.py:665
  102.5 84.7 %all-gather.10.cloned.1.call-start = ((), (), s32[]{:S(2)}) async-start(), calls=%async_computation.15 | async-start | bytes 2359296 | tf_op jit(solution)/shard_map/all_gather | solution.py:798
  102.5 7.9 %collective-permute-start.3 = (bf16[256,512]{1,0:T(8,128)(2,1)S(1)}, bf16[256,512]{1,0:T(8,128)(2,1)S(1)}, u32[]{:S(2)}, u32[]{:S(2)}) collective-permute-start(bf16[256,512]{1,0:T(8,128)(2,1)S(1)} %get-tuple-element.64.part), channel_id=1, source_target_pairs={{0,1},{1,0},{2,3},{3,2},{4,5},{5,4},{6,7},{7,6},{8,9},{9,8},{10,11... | collective-permute-start | bytes 786440 | tf_op jit(solution)/shard_map/ppermute | solution.py:661
  163.4 56.6 %all-gather.8.cloned.1.call-start = ((), (), s32[]{:S(2)}) async-start(), calls=%async_computation.14 | async-start | bytes 5013504 | tf_op jit(solution)/shard_map/all_gather | solution.py:800
Sparse Core Ops, SparseCore 0:
  20.3 27.8 all-gather.5
  54.4 32.7 reduce-scatter.2
  99.0 37.0 reduce-scatter.4
  163.6 21.4 all-gather.9
  187.3 32.7 all-gather.7

commit v17 on v16

--- a/solution.py
+++ b/solution.py
@@ -491,27 +491,33 @@
         grads[p, 192:208, :] = jnp.concatenate(have + fill, 0).astype(BF)
 
 
-def chunk_body(at, w_qkv, w_out, out):
+def chunk_body(at, w_qkv, w_out, out, buffer, sems):
+    rows = pl.ds(pl.multiple_of(at[2] * 64, 64), 64)
+    less = pl.ds(pl.multiple_of(at[2] * 32, 32), 32)
+    copies = [
+        pltpu.make_async_copy(w_qkv.at[:, :, rows], out.at[:, 0:3], sems.at[0]),
+        pltpu.make_async_copy(w_out.at[:, less], buffer, sems.at[1]),
+    ]
+    for copy in copies:
+        copy.start()
+    for copy in copies:
+        copy.wait()
     for layer in range(2):
-        for e in range(3):
-            out[layer, e] = w_qkv[layer, e]
-        out[layer, 3, 0:32] = w_out[layer, :, 0:256]
-        out[layer, 3, 32:64] = w_out[layer, :, 256:512]
+        out[layer, 3, 0:32] = buffer[layer, :, 0:256]
+        out[layer, 3, 32:64] = buffer[layer, :, 256:512]
 
 
 def chunk_of(at, wq, w_out):
     return pl.pallas_call(
         chunk_body,
-        out_shape=jax.ShapeDtypeStruct((2, 4, 64, 256), BF),
-        grid_spec=pltpu.PrefetchScalarGridSpec(
-            num_scalar_prefetch=1,
-            grid=(1,),
-            in_specs=[
-                pl.BlockSpec((2, 3, 64, 256), lambda i, at: (0, 0, at[2], 0)),
-                pl.BlockSpec((2, 32, 512), lambda i, at: (0, at[2], 0)),
-            ],
-            out_specs=pl.BlockSpec((2, 4, 64, 256), lambda i, at: (0, 0, 0, 0)),
-        ),
+        out_shape=pltpu.VMEM((2, 4, 64, 256), BF),
+        in_specs=[
+            pl.BlockSpec(memory_space=pltpu.SMEM),
+            pl.BlockSpec(memory_space=pltpu.HBM),
+            pl.BlockSpec(memory_space=pltpu.HBM),
+        ],
+        out_specs=pl.BlockSpec(memory_space=pltpu.VMEM),
+        scratch_shapes=[pltpu.VMEM((2, 32, 512), BF), pltpu.SemaphoreType.DMA((2,))],
         compiler_params=pltpu.CompilerParams(vmem_limit_bytes=40 * 1024 * 1024),
         name="chunk",
     )(at, far(wq), far(w_out))

time: 233 us -> 233 us (level)
  no operation moved by 1% of the time
where the time goes in v17:
time: 233 us; the launch traced here: 232 us
  blocking collectives  100 us (43%)
  waiting for transfers between devices  48.8 us (21%)
  Pallas kernels  45.1 us (19%)
  starting transfers between devices  23.7 us (10%)
  between operations  13.9 us (6%)
    all_to_all x6, blocking collectives, exchange(): return lax.all_to_all(value, axes, 0, 0)  100 us
    pallas_call x10, Pallas kernels, call(): pl.pallas_call(body, grid=(1,), out_shape=[o if isinstance(o, Kept) else...  35 us
    all_gather x1, waiting for transfers between devices, shards(): full_bc = lax.all_gather(exchange(summed, 'context'), 'dp')  29.5 us
    all_to_all x3, starting transfers between devices, exchange(): return lax.all_to_all(value, axes, 0, 0)  14.1 us
    ppermute x4, waiting for transfers between devices, swap(): return lax.ppermute(value, 'tensor', [(0, 1), (1, 0)])  12.4 us
    ppermute x4, starting transfers between devices, swap(): return lax.ppermute(value, 'tensor', [(0, 1), (1, 0)])  9.44 us
    all_to_all x3, waiting for transfers between devices, exchange(): return lax.all_to_all(value, axes, 0, 0)  6.77 us
    pallas_call x1, Pallas kernels, unpack(): pl.pallas_call(unpack_rest_body, grid=(2,), out_shape=[pltpu.HBM(shape, F...  5.19 us
  transfers between devices with their start and end apart: 12, of which 6 were waited for; matrix products, arithmetic and copies ran while one was open for 0% of the time, Pallas kernels for 12%

profile of v17, /device:TPU:1, one launch (start us, length us, event | category | flops | bytes accessed | tf_op | source)
XLA Modules:
  0.0 231.8 jit_solution(16041276056017586767)
XLA Ops:
  8.9 4.5 %collective-permute-start.2 = (bf16[2,4,64,256]{3,2,1,0:T(8,128)(2,1)S(1)}, bf16[2,4,64,256]{3,2,1,0:T(8,128)(2,1)S(1)}, u32[]{:S(2)}, u32[]{:S(2)}) collective-permute-start(bf16[2,4,64,256]{3,2,1,0:T(8,128)(2,1)S(1)} %chunk.1), channel_id=1, source_target_pairs={{0,1},{1,0},{2,3},{3,2},{4,5},{5,4},{6,7},{7,6},{8,9},{9,8},{10,11... | collective-permute-start | bytes 786440 | tf_op jit(solution)/shard_map/ppermute | solution.py:667
  13.4 4.4 %norm_qkv_feed.1 = (bf16[8,208,128]{2,1,0:T(8,128)(2,1)}, bf16[512,512]{1,0:T(8,128)(2,1)S(1)}, bf16[256,1024]{1,0:T(8,128)(2,1)}, bf16[256,1024]{1,0:T(8,128)(2,1)}, f32[2,2,8,128]{3,2,1,0:T(8,128)S(1)}) custom-call(s32[3]{0:T(128)S(1)} %pad_add_fusion.at, s32[2,128]{1,0:T(2,128)S(1)} %copy-done.7, f32[8,1]{1,0:T(8,128)S(1)} %copy-done.6, ...), custom_call_target="tpu_custom_call" | custom-call | tf_op jit(solution)/shard_map/norm_qkv_feed/pallas_call | solution.py:72
  20.2 4.6 %all-to-all-start = ((bf16[8,208,128]{2,1,0:T(8,128)(2,1)}), bf16[8,208,128]{2,1,0:T(8,128)(2,1)S(1)}, u32[]{:S(2)}, u32[]{:S(2)}) async-start(bf16[8,208,128]{2,1,0:T(8,128)(2,1)} %get-tuple-element.52._), calls=%async_computation | async-start | bytes 851968 | tf_op jit(solution)/shard_map/all_to_all | solution.py:671
  24.8 3.3 %collective-permute-start = (bf16[512,512]{1,0:T(8,128)(2,1)S(1)}, bf16[512,512]{1,0:T(8,128)(2,1)S(1)}, u32[]{:S(2)}, u32[]{:S(2)}) collective-permute-start(bf16[512,512]{1,0:T(8,128)(2,1)S(1)} %get-tuple-element.51.pair), channel_id=1, source_target_pairs={{0,1},{1,0},{2,3},{3,2},{4,5},{5,4},{6,7},{7,6},{8,9},{9,8},{10,11... | collective-permute-start | bytes 1572872 | tf_op jit(solution)/shard_map/ppermute | solution.py:667
  28.1 3.2 %all-to-all-done.recv = bf16[8,208,128]{2,1,0:T(8,128)(2,1)S(1)} async-done(((bf16[8,208,128]{2,1,0:T(8,128)(2,1)}), bf16[8,208,128]{2,1,0:T(8,128)(2,1)S(1)}, u32[]{:S(2)}, u32[]{:S(2)}) %all-to-all-start) | async-done | bytes 426016 | tf_op jit(solution)/shard_map/all_to_all | solution.py:671
  31.2 2.7 %attend.1 = (bf16[8,2,64,128]{3,2,1,0:T(8,128)(2,1)}, f32[1,1024]{1,0:T(1,128)S(1)}, f32[64,1024]{1,0:T(8,128)}, s32[1,1024]{1,0:T(1,128)S(1)}) custom-call(bf16[8,208,128]{2,1,0:T(8,128)(2,1)S(1)} %all-to-all-done.recv), custom_call_target="tpu_custom_call" | custom-call | tf_op jit(solution)/shard_map/attend/pallas_call | solution.py:72
  33.9 5.9 %all-to-all-start.1 = ((bf16[16,64,128]{2,1,0:T(8,128)(2,1)}), bf16[16,64,128]{2,1,0:T(8,128)(2,1)S(1)}, u32[]{:S(2)}, u32[]{:S(2)}) async-start(bf16[16,64,128]{2,1,0:T(8,128)(2,1)} %bitcast.6), calls=%async_computation.1 | async-start | bytes 524288 | tf_op jit(solution)/shard_map/all_to_all | solution.py:671
  39.8 4.0 %collective-permute-done.pair_other = bf16[512,512]{1,0:T(8,128)(2,1)S(1)} collective-permute-done((bf16[512,512]{1,0:T(8,128)(2,1)S(1)}, bf16[512,512]{1,0:T(8,128)(2,1)S(1)}, u32[]{:S(2)}, u32[]{:S(2)}) %collective-permute-start) | collective-permute-done | bytes 524320 | tf_op jit(solution)/shard_map/ppermute | solution.py:667
  43.8 3.6 %all-to-all-done.1 = bf16[16,64,128]{2,1,0:T(8,128)(2,1)S(1)} async-done(((bf16[16,64,128]{2,1,0:T(8,128)(2,1)}), bf16[16,64,128]{2,1,0:T(8,128)(2,1)S(1)}, u32[]{:S(2)}, u32[]{:S(2)}) %all-to-all-start.1) | async-done | bytes 262176 | tf_op jit(solution)/shard_map/all_to_all | solution.py:671
  47.4 6.8 %middle.1 = (f32[256,512]{1,0:T(8,128)}, bf16[8,256,128]{2,1,0:T(8,128)(2,1)S(1)}, bf16[8,512,256]{2,1,0:T(8,128)(2,1)}, bf16[512,512]{1,0:T(8,128)(2,1)S(1)}, f...) custom-call(s32[3]{0:T(128)S(1)} %pad_add_fusion.at, f32[256,512]{1,0:T(8,128)} %bitcast.35, ...), custom_call_target="tpu_custom_call" | custom-call | tf_op jit(solution)/shard_map/middle/pallas_call | solution.py:72
  54.9 12.1 %all_to_all.45.recv = bf16[8,256,128]{2,1,0:T(8,128)(2,1)S(1)} all-to-all(bf16[8,256,128]{2,1,0:T(8,128)(2,1)S(1)} %get-tuple-element.57), channel_id=1, replica_groups=mesh['dp'=8,'context'=8,'tensor'=2] {'context'}, dimensions={0} | all-to-all | bytes 1048576 | tf_op jit(solution)/shard_map/all_to_all | solution.py:671
  67.0 4.2 %attend_both.1 = bf16[8,2,256,128]{3,2,1,0:T(8,128)(2,1)S(1)} custom-call(bf16[8,256,128]{2,1,0:T(8,128)(2,1)S(1)} %all_to_all.45.recv, s32[1,1024]{1,0:T(1,128)S(1)} %get-tuple-element.58.start, bf16[512,512]{1,0:T(8,128)(2,1)S(1)} %collective-permute-done.1._.parts_other), custom_call_target="tpu_custom_call" | custom-call | tf_op jit(solution)/shard_map/attend_both/pallas_call | solution.py:72
  71.2 19.5 %all_to_all.46 = bf16[16,256,128]{2,1,0:T(8,128)(2,1)S(1)} all-to-all(bf16[16,256,128]{2,1,0:T(8,128)(2,1)S(1)} %bitcast.23), channel_id=1, replica_groups=mesh['dp'=8,'context'=8,'tensor'=2] {'context','tensor'}, dimensions={0} | all-to-all | bytes 2097152 | tf_op jit(solution)/shard_map/all_to_all | solution.py:671
  90.7 8.2 %turn_point.1 = (f32[256,512]{1,0:T(8,128)}, f32[256,512]{1,0:T(8,128)}, bf16[8,192,128]{2,1,0:T(8,128)(2,1)}, bf16[8,832,256]{2,1,0:T(8,128)(2,1)}, bf16[256,51...) custom-call(s32[3]{0:T(128)S(1)} %pad_add_fusion.at, ...), custom_call_target="tpu_custom_call" | custom-call | tf_op jit(solution)/shard_map/turn_point/pallas_call | solution.py:72
  98.9 3.6 %all-to-all-start.4 = ((bf16[8,192,128]{2,1,0:T(8,128)(2,1)}), bf16[8,192,128]{2,1,0:T(8,128)(2,1)S(1)}, u32[]{:S(2)}, u32[]{:S(2)}) async-start(bf16[8,192,128]{2,1,0:T(8,128)(2,1)} %get-tuple-element.65), calls=%async_computation.5 | async-start | bytes 786432 | tf_op jit(solution)/shard_map/all_to_all | solution.py:671
  103.6 6.8 %collective-permute-done.3._.part_other = bf16[256,512]{1,0:T(8,128)(2,1)S(1)} collective-permute-done((bf16[256,512]{1,0:T(8,128)(2,1)S(1)}, bf16[256,512]{1,0:T(8,128)(2,1)S(1)}, u32[]{:S(2)}, u32[]{:S(2)}) %collective-permute-start.3) | collective-permute-done | bytes 262176 | tf_op jit(solution)/shard_map/ppermute | solution.py:667
  112.6 18.8 %all_to_all.47 = bf16[16,320,128]{2,1,0:T(8,128)(2,1)S(1)} all-to-all(bf16[16,320,128]{2,1,0:T(8,128)(2,1)S(1)} %bitcast.21), channel_id=1, replica_groups=mesh['dp'=8,'context'=8,'tensor'=2] {'context','tensor'}, dimensions={0} | all-to-all | bytes 2621440 | tf_op jit(solution)/shard_map/all_to_all | solution.py:671
  131.4 3.9 %last.1 = (f32[256,512]{1,0:T(8,128)}, bf16[8,208,256]{2,1,0:T(8,128)(2,1)S(1)}, bf16[512,256]{1,0:T(8,128)(2,1)}, f32[3,256]{1,0:T(4,128)}, f32[4,512]{1,0:T(4,128)}) custom-call(s32[3]{0:T(128)S(1)} %pad_add_fusion.at, f32[256,512]{1,0:T(8,128)} %bitcast.37, f32[256,512]{1,0:T(8,128)} %get-tuple-element.63.g, bf16[256,512]{1,0:T(8,128)(2,1)S(1)} %get-tuple-element.64.part, ...), custom_call_target="tpu_custom_call" | custom-call | tf_op jit(solution)/shard_map/last/pallas_call | solution.py:72
  135.3 26.3 %all_to_all.48.got = bf16[8,208,256]{2,1,0:T(8,128)(2,1)S(1)} all-to-all(bf16[8,208,256]{2,1,0:T(8,128)(2,1)S(1)} %get-tuple-element.75), channel_id=1, replica_groups=mesh['dp'=8,'context'=8,'tensor'=2] {'dp'}, dimensions={0} | all-to-all | bytes 1703936 | tf_op jit(solution)/shard_map/all_to_all | solution.py:671
  163.5 12.1 %all_to_all.49.got = bf16[8,136,256]{2,1,0:T(8,128)(2,1)S(1)} all-to-all(bf16[8,136,256]{2,1,0:T(8,128)(2,1)S(1)} %get-tuple-element.78), channel_id=1, replica_groups=mesh['dp'=8,'context'=8,'tensor'=2] {'context'}, dimensions={0} | all-to-all | bytes 1114112 | tf_op jit(solution)/shard_map/all_to_all | solution.py:671
  175.7 11.5 %all_to_all.50 = bf16[8,136,256]{2,1,0:T(8,128)(2,1)} all-to-all(bf16[8,136,256]{2,1,0:T(8,128)(2,1)S(1)} %sum.1), channel_id=1, replica_groups=mesh['dp'=8,'context'=8,'tensor'=2] {'context'}, dimensions={0} | all-to-all | bytes 1114112 | tf_op jit(solution)/shard_map/all_to_all | solution.py:671
  187.2 3.4 %unpack_first.1 = (f32[2,512,1024]{2,1,0:T(8,128)}, f32[2,1024,512]{2,1,0:T(8,128)}) custom-call(bf16[8,512,256]{2,1,0:T(8,128)(2,1)} %bitcast.39), custom_call_target="tpu_custom_call" | custom-call | tf_op jit(solution)/shard_map/unpack_first/pallas_call | solution.py:632
  190.6 29.5 %all-gather.8.cloned.1.call-done = bf16[64,136,256]{2,1,0:T(8,128)(2,1)} async-done(((bf16[8,136,256]{2,1,0:T(8,128)(2,1)}), bf16[64,136,256]{2,1,0:T(8,128)(2,1)}) %all-gather.8.cloned.1.call-update) | async-done | bytes 4456464 | tf_op jit(solution)/shard_map/all_gather | solution.py:806
  220.1 5.2 %unpack_rest.1 = (f32[2,512,1024]{2,1,0:T(8,128)}, f32[2,1024,512]{2,1,0:T(8,128)}, f32[2,3,512,256]{3,2,1,0:T(8,128)}, f32[2,256,512]{2,1,0:T(8,128)}, f32[2,10...) custom-call(bf16[8,8,136,256]{3,2,1,0:T(8,128)(2,1)} %bitcast.38, ...), custom_call_target="tpu_custom_call", output_to_operand_aliasing={{0}: (1, {}), {1}: (2, {})} | custom-call | tf_op jit(solution)/shard_map/unpack_rest/pallas_call | solution.py:650
  (41 shorter events, 10.0 us)
Async XLA Ops:
  7.2 6.2 %copy-start.6 = (f32[8,1]{1,0:T(8,128)S(1)}, f32[8,1]{1,0:T(8,128)}, u32[]{:S(2)}) copy-start(f32[8,1]{1,0:T(8,128)} %constant.18.freqs) | copy-start | bytes 100
  7.2 6.2 %copy-start.2 = (f32[2,2,512]{2,1,0:T(2,128)S(1)}, f32[2,2,512]{2,1,0:T(2,128)}, u32[]{:S(2)}) copy-start(f32[2,2,512]{2,1,0:T(2,128)} %bias.7) | copy-start | bytes 24580
  7.2 6.2 %copy-start.1 = (f32[2,2,512]{2,1,0:T(2,128)S(1)}, f32[2,2,512]{2,1,0:T(2,128)}, u32[]{:S(2)}) copy-start(f32[2,2,512]{2,1,0:T(2,128)} %gain.7) | copy-start | bytes 24580
  7.2 6.2 %copy-start.3 = (f32[2,1024]{1,0:T(2,128)S(1)}, f32[2,1024]{1,0:T(2,128)}, u32[]{:S(2)}) copy-start(f32[2,1024]{1,0:T(2,128)} %b_up.3) | copy-start | bytes 24580
  7.2 6.2 %copy-start.5 = (f32[2,3,256]{2,0,1:T(2,128)S(1)}, f32[2,3,256]{2,0,1:T(2,128)}, u32[]{:S(2)}) copy-start(f32[2,3,256]{2,0,1:T(2,128)} %param.17) | copy-start | bytes 18436
  7.2 6.2 %copy-start.7 = (s32[2,128]{1,0:T(2,128)S(1)}, s32[2,128]{1,0:T(2,128)}, u32[]{:S(2)}) copy-start(s32[2,128]{1,0:T(2,128)} %pos.1) | copy-start | bytes 3076
  7.2 83.4 %all-gather.6.cloned.1.call-start = ((), (), s32[]{:S(2)}) async-start(), calls=%async_computation.11 | async-start | bytes 2359296 | tf_op jit(solution)/shard_map/all_gather | solution.py:712
  8.9 10.5 %collective-permute-start.2 = (bf16[2,4,64,256]{3,2,1,0:T(8,128)(2,1)S(1)}, bf16[2,4,64,256]{3,2,1,0:T(8,128)(2,1)S(1)}, u32[]{:S(2)}, u32[]{:S(2)}) collective-permute-start(bf16[2,4,64,256]{3,2,1,0:T(8,128)(2,1)S(1)} %chunk.1), channel_id=1, source_target_pairs={{0,1},{1,0},{2,3},{3,2},{4,5},{5,4},{6,7},{7,6},{8,9},{9,8},{10,11... | collective-permute-start | bytes 786440 | tf_op jit(solution)/shard_map/ppermute | solution.py:667
  17.8 29.6 %copy-start.4 = (f32[2,2,512]{2,1,0:T(2,128)S(1)}, f32[2,2,512]{2,1,0:T(2,128)}, u32[]{:S(2)}) copy-start(f32[2,2,512]{2,1,0:T(2,128)} %out_bias.3) | copy-start | bytes 24580
  20.2 11.1 %all-to-all-start = ((bf16[8,208,128]{2,1,0:T(8,128)(2,1)}), bf16[8,208,128]{2,1,0:T(8,128)(2,1)S(1)}, u32[]{:S(2)}, u32[]{:S(2)}) async-start(bf16[8,208,128]{2,1,0:T(8,128)(2,1)} %get-tuple-element.52._), calls=%async_computation | async-start | bytes 851968 | tf_op jit(solution)/shard_map/all_to_all | solution.py:671
  24.8 19.1 %collective-permute-start = (bf16[512,512]{1,0:T(8,128)(2,1)S(1)}, bf16[512,512]{1,0:T(8,128)(2,1)S(1)}, u32[]{:S(2)}, u32[]{:S(2)}) collective-permute-start(bf16[512,512]{1,0:T(8,128)(2,1)S(1)} %get-tuple-element.51.pair), channel_id=1, source_target_pairs={{0,1},{1,0},{2,3},{3,2},{4,5},{5,4},{6,7},{7,6},{8,9},{9,8},{10,11... | collective-permute-start | bytes 1572872 | tf_op jit(solution)/shard_map/ppermute | solution.py:667
  33.9 13.5 %all-to-all-start.1 = ((bf16[16,64,128]{2,1,0:T(8,128)(2,1)}), bf16[16,64,128]{2,1,0:T(8,128)(2,1)S(1)}, u32[]{:S(2)}, u32[]{:S(2)}) async-start(bf16[16,64,128]{2,1,0:T(8,128)(2,1)} %bitcast.6), calls=%async_computation.1 | async-start | bytes 524288 | tf_op jit(solution)/shard_map/all_to_all | solution.py:671
  39.8 50.9 %reduce-scatter.3.cloned.1.call-start = ((), (), s32[]{:S(2)}) async-start(), calls=%async_computation.12 | async-start | bytes 2359296 | tf_op jit(solution)/shard_map/reduce_scatter | solution.py:739
  54.2 107.4 %reduce-scatter.5.cloned.1.call-start = ((), (), s32[]{:S(2)}) async-start(), calls=%async_computation.13 | async-start | bytes 3833856 | tf_op jit(solution)/shard_map/reduce_scatter | solution.py:771
  54.3 12.7 %collective-permute-start.1 = (bf16[512,512]{1,0:T(8,128)(2,1)S(1)}, bf16[512,512]{1,0:T(8,128)(2,1)S(1)}, u32[]{:S(2)}, u32[]{:S(2)}) collective-permute-start(bf16[512,512]{1,0:T(8,128)(2,1)S(1)} %get-tuple-element.56.parts), channel_id=1, source_target_pairs={{0,1},{1,0},{2,3},{3,2},{4,5},{5,4},{6,7},{7,6},{8,9},{9,8},{10,11... | collective-permute-start | bytes 1572872 | tf_op jit(solution)/shard_map/ppermute | solution.py:667
  98.8 11.5 %copy-start = (f32[64,1024]{1,0:T(8,128)S(1)}, f32[64,1024]{1,0:T(8,128)}, u32[]{:S(2)}) copy-start(f32[64,1024]{1,0:T(8,128)} %get-tuple-element.67.ctx) | copy-start | bytes 786436
  98.9 11.5 %all-to-all-start.4 = ((bf16[8,192,128]{2,1,0:T(8,128)(2,1)}), bf16[8,192,128]{2,1,0:T(8,128)(2,1)S(1)}, u32[]{:S(2)}, u32[]{:S(2)}) async-start(bf16[8,192,128]{2,1,0:T(8,128)(2,1)} %get-tuple-element.65), calls=%async_computation.5 | async-start | bytes 786432 | tf_op jit(solution)/shard_map/all_to_all | solution.py:671
  102.5 84.7 %all-gather.10.cloned.1.call-start = ((), (), s32[]{:S(2)}) async-start(), calls=%async_computation.15 | async-start | bytes 2359296 | tf_op jit(solution)/shard_map/all_gather | solution.py:804
  102.5 7.9 %collective-permute-start.3 = (bf16[256,512]{1,0:T(8,128)(2,1)S(1)}, bf16[256,512]{1,0:T(8,128)(2,1)S(1)}, u32[]{:S(2)}, u32[]{:S(2)}) collective-permute-start(bf16[256,512]{1,0:T(8,128)(2,1)S(1)} %get-tuple-element.64.part), channel_id=1, source_target_pairs={{0,1},{1,0},{2,3},{3,2},{4,5},{5,4},{6,7},{7,6},{8,9},{9,8},{10,11... | collective-permute-start | bytes 786440 | tf_op jit(solution)/shard_map/ppermute | solution.py:667
  163.5 56.6 %all-gather.8.cloned.1.call-start = ((), (), s32[]{:S(2)}) async-start(), calls=%async_computation.14 | async-start | bytes 5013504 | tf_op jit(solution)/shard_map/all_gather | solution.py:806
Sparse Core Ops, SparseCore 0:
  20.3 27.8 all-gather.5
  54.4 32.7 reduce-scatter.2
  99.0 37.0 reduce-scatter.4
  163.6 21.4 all-gather.9
  187.3 32.7 all-gather.7
